TPU v7x, 32 devices: a whole 2x2x4 slice. The times are simulated.
32 devices in a mesh: obs: 16 (over z, x, core), ind: 2 (over y).
Axes of the slice: x: 2, y: 2, z: 4, core: 2. Of those that a mesh axis runs over, the one named last changes fastest.
Arguments:
- obs_coords: float32 [2, 32768], P(None, 'obs'), may hold values from 0 to 1
- obs_codes: int32 [32768], P('obs'), may hold values from 0 to 47
- route_plan: int32 [16, 16], replicated, may hold values from 0 to 1, as said below
- inducing_coords: float32 [2, 2048], P(None, 'ind'), may hold values from 0 to 1
- inducing_bands: int32 [2048], P('ind'), may hold values from 0 to 5
- band_mix: float32 [6, 6], replicated, may hold values from -2.4 to 2.4
- lengthscales: float32 [2], replicated, may hold values from 0.04 to 0.1
- class_scales: float32 [8], replicated, may hold values from 0.5 to 2
- prior_factor: bfloat16 [2048, 1024], P(('ind', 'obs')), may hold values from -0.046875 to 0.046875
- variational_chol: bfloat16 [2048, 1024], P(('ind', 'obs')), may hold values from -1 to 1, as said below
- variational_mean: bfloat16 [8, 2048], P(None, 'ind'), may hold values from -6 to 6
Outputs:
- class_probs: float32 [8, 32768], P(None, 'obs')
- grad_chol: float32 [2048, 1024], P(('ind', 'obs'))
- grad_mean: float32 [8, 2048], P(None, 'ind')
Inputs may be any that keep to these rules, and one draw needn't show every extreme that they name: `route_plan`: entry [s, d] is the number of 128-row blocks that reader s hands to device d; every column sums to 16; a reader's blocks go out in order of destination from the front of its buffer. `variational_chol`: each block's rows are lower triangular within the block, with diagonal entries of 0.3 to 1.
All inputs are finite; a program needn't handle non-finite values.
Results may differ from a plain program's by a relative error of at most 0.014.
Values may be sent and summed in bfloat16 or wider, within the bound.
No kernel may reach another device: no remote copies, remote signals or barrier semaphores. Data moves between devices by JAX's collectives and lax.ppermute only.
A program may use at most 64 MiB of HBM per device.

v0:
```python
import jax
import jax.numpy as jnp
from jax import lax
from jax.sharding import PartitionSpec as P

C = 8
NB = 6
ROWS_DEV = 2048


precise = lax.Precision.HIGHEST


def cross_cov(coords, band_ids, centers, center_bands, lengthscales, coupling):
    delta_t = (coords[0][:, None] - centers[0][None, :]) / lengthscales[0]
    delta_w = (coords[1][:, None] - centers[1][None, :]) / lengthscales[1]
    kinds = jnp.arange(NB, dtype=jnp.int32)
    row_hot = (band_ids[:, None] == kinds[None, :]).astype(jnp.float32)
    col_hot = (center_bands[:, None] == kinds[None, :]).astype(jnp.float32)
    mixing = jnp.dot(jnp.dot(row_hot, coupling, precision=precise), col_hot.T, precision=precise)
    return (jnp.exp(-0.5 * (delta_t * delta_t + delta_w * delta_w)) * mixing).astype(jnp.bfloat16)


def likelihood(mean_sum, variance, class_scales):
    logits = mean_sum + 0.5 * class_scales[:, None] * variance[None, :]
    weights = jnp.exp(logits)
    chances = weights / jnp.sum(weights, axis=0, keepdims=True)
    var_slope = -0.5 * jnp.sum(chances * class_scales[:, None], axis=0)
    return (chances, var_slope)


def body(
    obs_coords,
    obs_codes,
    route_plan,
    inducing_coords,
    inducing_bands,
    band_mix,
    lengthscales,
    class_scales,
    prior_factor,
    variational_chol,
    variational_mean,
):
    devices = lax.axis_size("obs")
    my_index = lax.axis_index("obs")
    slot_rows = 128
    blocks = route_plan * slot_rows
    send_start = jnp.cumsum(blocks, axis=1) - blocks
    recv_start = jnp.cumsum(blocks, axis=0) - blocks
    my_sends = lax.dynamic_index_in_dim(send_start, my_index, 0, keepdims=False)
    my_recvs = lax.dynamic_index_in_dim(recv_start, my_index, 1, keepdims=False)
    stacked = jnp.concatenate([obs_coords, obs_codes.astype(jnp.float32)[None, :]], axis=0)
    padded = jnp.concatenate([stacked, jnp.zeros((3, slot_rows), jnp.float32)], axis=1)
    outgoing = jax.vmap(lambda offset: lax.dynamic_slice_in_dim(padded, offset, slot_rows, 1))(
        my_sends
    )
    incoming = lax.all_to_all(outgoing, "obs", split_axis=0, concat_axis=0, tiled=True)
    position = jnp.arange(ROWS_DEV, dtype=jnp.int32)
    sources = jnp.arange(devices, dtype=jnp.int32)
    source = jnp.sum((my_recvs[None, :] <= position[:, None]).astype(jnp.int32), axis=1) - 1
    pick = (source[:, None] == sources[None, :]).astype(jnp.int32)
    begin_row = jnp.sum(pick * my_recvs[None, :], axis=1)
    arrived = incoming[source, :, position - begin_row].T
    coords = arrived[0:2]
    code_ids = arrived[2].astype(jnp.int32)
    band_ids = code_ids % NB
    labels = code_ids // NB
    coupling = jnp.eye(NB, dtype=jnp.float32) + jnp.dot(band_mix, band_mix.T, precision=precise)
    kinds = jnp.arange(NB, dtype=jnp.int32)
    row_hot = (band_ids[:, None] == kinds[None, :]).astype(jnp.float32)
    self_cov = jnp.sum(row_hot * jnp.dot(row_hot, coupling, precision=precise), axis=1)
    kernel_rows = cross_cov(
        coords, band_ids, inducing_coords, inducing_bands, lengthscales, coupling
    )
    prior_block, chol_block = (
        lax.all_gather(prior_factor, "obs", axis=0, tiled=True),
        lax.all_gather(variational_chol, "obs", axis=0, tiled=True),
    )
    whitened = jnp.dot(kernel_rows, prior_block, preferred_element_type=jnp.float32)
    whitened_bf = whitened.astype(jnp.bfloat16)
    covariant = jnp.dot(whitened_bf, chol_block, preferred_element_type=jnp.float32)
    mean_part = lax.dot_general(
        variational_mean, whitened_bf, (((1,), (1,)), ((), ())), preferred_element_type=jnp.float32
    )
    var_part = (jnp.sum(covariant * covariant, axis=1) - jnp.sum(whitened * whitened, axis=1))[
        None, :
    ]
    mean_sum, var_sum = lax.psum((mean_part, var_part), "ind")
    chances, var_slope = likelihood(mean_sum, self_cov + var_sum[0], class_scales)
    classes = jnp.arange(C, dtype=jnp.int32)
    mean_slope = ((labels[None, :] == classes[:, None]).astype(jnp.float32) - chances).astype(
        jnp.bfloat16
    )
    heavy = (2.0 * var_slope[:, None] * covariant).astype(jnp.bfloat16)
    piece_rows = variational_chol.shape[0]
    full_width = variational_chol.shape[1]
    column_ids = jnp.arange(full_width, dtype=jnp.int32)
    own_rows = my_index * piece_rows + jnp.arange(piece_rows, dtype=jnp.int32)[:, None]
    term = lax.dot_general(
        whitened_bf, heavy, (((0,), (0,)), ((), ())), preferred_element_type=jnp.float32
    )
    row_ids = jnp.arange(lax.axis_size("obs") * piece_rows, dtype=jnp.int32)[:, None]
    data_term = lax.psum_scatter(
        jnp.where(column_ids[None, :] <= row_ids, term, 0.0).astype(jnp.bfloat16),
        "obs",
        scatter_dimension=0,
        tiled=True,
    ).astype(jnp.float32)
    on_diag = column_ids[None, :] == own_rows
    own_chol = variational_chol.astype(jnp.float32)
    diagonal = jnp.sum(jnp.where(on_diag, own_chol, 0.0), axis=1, keepdims=True)
    grad_chol = data_term - own_chol + jnp.where(on_diag, 1.0 / diagonal, 0.0)
    mean_term = lax.dot_general(
        mean_slope, whitened_bf, (((1,), (0,)), ((), ())), preferred_element_type=jnp.float32
    )
    grad_mean = lax.psum(mean_term, "obs") - variational_mean.astype(jnp.float32)
    return (chances, grad_chol, grad_mean)


def solution(mesh):
    placed = (
        P(None, "obs"),
        P("obs"),
        P(),
        P(None, "ind"),
        P("ind"),
        P(),
        P(),
        P(),
        P(("ind", "obs"), None),
        P(("ind", "obs"), None),
        P(None, "ind"),
    )
    return jax.shard_map(
        body,
        mesh=mesh,
        in_specs=placed,
        out_specs=(P(None, "obs"), P(("ind", "obs"), None), P(None, "ind")),
        check_vma=False,
    )
```

profile of v0, /device:TPU:0, one launch (start us, length us, event | category | flops | bytes accessed | tf_op | source)
XLA Modules:
  0.0 205.6 jit_solution(10195719504383215228)
XLA Ops:
  7.2 0.7 all-gather.3.cloned.1.call-update
  7.9 0.7 convert_element_type.49
  8.6 0.7 broadcast_multiply_fusion.1
  9.5 0.7 select_maximum_fusion
  10.3 30.2 %while.1 = (s32[]{:T(128)}, f32[3,2176]{1,0:T(4,128)S(1)}, s32[16,2]{0,1:T(2,128)S(1)}, f32[16,3,128]{2,1,0:T(4,128)}, s32[]{:T(128)}) while((s32[]{:T(128)}, f32[3,2176]{1,0:T(4,128)S(1)}, s32[16,2]{0,1:T(2,128)S(1)}, f32[16,3,128]{2,1,0:T(4,128)}, s32[]{:T(128)}) %tuple.31), condition=%wide.while_cond, body=%wide.while_body.sunk | while | flops 2 | bytes 4197 | solution.py:55
  10.3 0.5 slice.63
  10.9 1.3 bitcast_dynamic-update-slice_fusion.2
  12.2 0.5 slice.63
  12.7 1.3 bitcast_dynamic-update-slice_fusion.2
  14.1 0.5 slice.63
  14.6 1.3 bitcast_dynamic-update-slice_fusion.2
  16.0 0.5 slice.63
  16.5 1.3 bitcast_dynamic-update-slice_fusion.2
  17.9 0.5 slice.63
  18.4 1.3 bitcast_dynamic-update-slice_fusion.2
  19.8 0.5 slice.63
  20.3 1.3 bitcast_dynamic-update-slice_fusion.2
  21.7 0.5 slice.63
  22.2 1.3 bitcast_dynamic-update-slice_fusion.2
  23.6 0.5 slice.63
  24.1 1.3 bitcast_dynamic-update-slice_fusion.2
  25.4 0.5 slice.63
  26.0 1.3 bitcast_dynamic-update-slice_fusion.2
  27.3 0.5 slice.63
  27.8 1.3 bitcast_dynamic-update-slice_fusion.2
  29.2 0.5 slice.63
  29.7 1.3 bitcast_dynamic-update-slice_fusion.2
  31.1 0.5 slice.63
  31.6 1.3 bitcast_dynamic-update-slice_fusion.2
  33.0 0.5 slice.63
  33.5 1.3 bitcast_dynamic-update-slice_fusion.2
  34.9 0.5 slice.63
  35.4 1.3 bitcast_dynamic-update-slice_fusion.2
  36.8 0.5 slice.63
  37.3 1.3 bitcast_dynamic-update-slice_fusion.2
  38.7 0.5 slice.63
  39.2 1.3 bitcast_dynamic-update-slice_fusion.2
  40.5 7.4 %all-to-all-start = ((f32[16,3,128]{2,1,0:T(4,128)}), f32[16,3,128]{2,1,0:T(4,128)S(1)}, u32[]{:S(2)}, u32[]{:S(2)}) async-start(f32[16,3,128]{2,1,0:T(4,128)} %get-tuple-element.10), calls=%async_computation | async-start | bytes 65536 | tf_op jit(solution)/shard_map/all_to_all | solution.py:58
  47.9 0.7 all-gather.5.cloned.1.call-update
  49.2 0.8 fusion.23
  50.0 0.7 broadcast_multiply_fusion.2
  50.7 1.3 fusion.24
  52.0 2.4 %all-to-all-done = f32[16,3,128]{2,1,0:T(4,128)S(1)} async-done(((f32[16,3,128]{2,1,0:T(4,128)}), f32[16,3,128]{2,1,0:T(4,128)S(1)}, u32[]{:S(2)}, u32[]{:S(2)}) %all-to-all-start) | async-done | bytes 24608 | tf_op jit(solution)/shard_map/all_to_all | solution.py:58
  54.5 0.4 copy.17
  54.8 13.0 %gather_fusion = f32[2048,3]{1,0:T(8,128)S(1)} fusion(f32[16,3,128]{1,2,0:T(8,128)S(1)} %copy.17, s32[2048]{0:T(1024)S(1)} %bitcast.38), kind=kCustom, calls=%fused_computation | custom fusion | bytes 65536 | tf_op jit(solution)/shard_map/gather | solution.py:64
  67.9 1.3 fusion.2
  69.2 0.9 slice_reduce_fusion.1
  70.1 0.2 select_reduce_fusion.1
  70.3 10.1 %multiply_convert_fusion.1 = bf16[2048,1024]{1,0:T(8,128)(2,1)} fusion(f32[2048,6]{0,1:T(8,128)S(1)} %get-tuple-element.35, f32[]{:T(128)} %bitcast.10, f32[1024]{0:T(1024)S(1)} %bitcast.50, f32[2048]{0:T(1024)S(1)} %get-tuple-element.14, f32[]{:T(128)} %bitcast.8, f32[1024]{0:T(1024)S(1)} %bitcast.49, f32[2048]{0:T(1024)S(1)} %get-tuple-element.13, ...), kind=kOutput, calls=%fused_computation.6 | convolution fusion | flops 171972608 | bytes 4272136 | tf_op jit(solution)/shard_map/dot_general | solution.py:20
  80.4 7.5 %multiply_reduce_fusion = (f32[2048]{0:T(1024)S(1)}, bf16[2048,1024]{0,1:T(8,128)(2,1)S(1)}) fusion(bf16[2048,1024]{1,0:T(8,128)(2,1)} %multiply_convert_fusion.1, bf16[1024,1024]{1,0:T(8,128)(2,1)} %all-gather.3.cloned.1.call-done), kind=kOutput, calls=%fused_computation.4 | convolution fusion | flops 4301256704 | bytes 10493952 | tf_op jit(solution)/shard_map/dot_general | solution.py:80
  87.9 2.0 copy-done.1
  89.9 1.3 convolution_bitcast_fusion
  91.2 0.2 reduce-scatter.2.cloned.1.call-start
  91.4 5.7 %all-gather.5.cloned.1.call-done = bf16[1024,1024]{1,0:T(8,128)(2,1)} async-done(((bf16[64,1024]{1,0:T(8,128)(2,1)}), bf16[1024,1024]{1,0:T(8,128)(2,1)}) %all-gather.5.cloned.1.call-update) | async-done | bytes 2097168 | tf_op jit(solution)/shard_map/all_gather | solution.py:78
  97.1 10.7 %multiply_reduce_fusion.1 = (f32[2048]{0:T(1024)S(1)}, f32[2048,1024]{0,1:T(8,128)}) fusion(bf16[2048,1024]{0,1:T(8,128)(2,1)} %copy-done.1, bf16[1024,1024]{1,0:T(8,128)(2,1)} %all-gather.5.cloned.1.call-done), kind=kOutput, calls=%fused_computation.5 | convolution fusion | flops 4299159552 | bytes 14688256 | tf_op jit(solution)/shard_map/dot_general | solution.py:82
  107.8 5.0 %psum.22 = f32[1,2048]{1,0:T(1,128)S(1)} all-reduce(f32[1,2048]{1,0:T(1,128)S(1)} %bitcast.44), channel_id=1, replica_groups=mesh['obs'=16,'ind'=2] {'ind'}, use_global_device_ids=true, to_apply=%region_8.9 | all-reduce | flops 2048 | bytes 16384 | tf_op jit(solution)/shard_map/psum | solution.py:89
  112.8 6.7 %all-reduce.4.cloned.1.call-done = f32[8,2048]{1,0:T(8,128)} async-done(((f32[8,2048]{1,0:T(8,128)}), f32[8,2048]{1,0:T(8,128)}) %all-reduce.4.cloned.1.call-update) | async-done | bytes 65552 | tf_op jit(solution)/shard_map/psum | solution.py:89
  119.5 0.9 fusion.11
  120.4 0.9 multiply_reduce_fusion.2
  121.4 10.7 %select_convert_fusion = bf16[1024,1024]{1,0:T(8,128)(2,1)} fusion(bf16[2048,1024]{0,1:T(8,128)(2,1)} %copy-done.1, f32[2048,1024]{0,1:T(8,128)} %get-tuple-element.37, f32[2048]{0:T(1024)S(1)} %broadcast_multiply_fusion), kind=kOutput, calls=%fused_computation.8 | convolution fusion | flops 4302307328 | bytes 14688256 | tf_op jit(solution)/shard_map/dot_general | solution.py:100
  132.4 3.4 %fusion.12 = f32[8,1024]{1,0:T(8,128)S(1)} fusion(bf16[2048,1024]{0,1:T(8,128)(2,1)} %copy-done.1, f32[8,2048]{1,0:T(8,128)S(1)} %get-tuple-element.24, s32[2048]{0:T(1024)S(1)} %get-tuple-element.11), kind=kOutput, calls=%fused_computation.46 | convolution fusion | flops 33619968 | bytes 4300800 | tf_op jit(solution)/shard_map/dot_general | solution.py:114
  135.7 61.0 %psum.23 = f32[8,1024]{1,0:T(8,128)S(1)} all-reduce(f32[8,1024]{1,0:T(8,128)S(1)} %fusion.12), channel_id=1, replica_groups=mesh['obs'=16,'ind'=2] {'obs'}, use_global_device_ids=true, to_apply=%region_13.14 | all-reduce | flops 8192 | bytes 65536 | tf_op jit(solution)/shard_map/psum | solution.py:117
  196.7 0.6 convert_subtract_fusion.1
  197.3 1.7 fusion.6
  (54 shorter events, 2.4 us)
Async XLA Ops:
  7.2 41.9 %copy-start = (f32[6,6]{1,0:T(8,128)S(1)}, f32[6,6]{1,0:T(8,128)}, u32[]{:S(2)}) copy-start(f32[6,6]{1,0:T(8,128)} %param.16) | copy-start | bytes 436
  7.2 73.2 %all-gather.3.cloned.1.call-start = ((), (), s32[]{:S(2)}) async-start(), calls=%async_computation.2 | async-start | bytes 2228224 | tf_op jit(solution)/shard_map/all_gather | solution.py:77
  40.5 14.0 %all-to-all-start = ((f32[16,3,128]{2,1,0:T(4,128)}), f32[16,3,128]{2,1,0:T(4,128)S(1)}, u32[]{:S(2)}, u32[]{:S(2)}) async-start(f32[16,3,128]{2,1,0:T(4,128)} %get-tuple-element.10), calls=%async_computation | async-start | bytes 65536 | tf_op jit(solution)/shard_map/all_to_all | solution.py:58
  47.8 49.3 %all-gather.5.cloned.1.call-start = ((), (), s32[]{:S(2)}) async-start(), calls=%async_computation.4 | async-start | bytes 2228224 | tf_op jit(solution)/shard_map/all_gather | solution.py:78
  48.6 70.9 %all-reduce.4.cloned.1.call-start = ((), (), s32[]{:S(2)}) async-start(), calls=%async_computation.3 | async-start | bytes 131072 | tf_op jit(solution)/shard_map/psum | solution.py:89
  54.8 15.5 %copy-start.6 = (s32[1024]{0:T(1024)S(1)}, s32[1024]{0:T(1024)}, u32[]{:S(2)}) copy-start(s32[1024]{0:T(1024)} %param.15) | copy-start | bytes 12292
  80.4 9.5 %copy-start.4 = (bf16[8,1024]{1,0:T(8,128)(2,1)S(1)}, bf16[8,1024]{1,0:T(8,128)(2,1)}, u32[]{:S(2)}) copy-start(bf16[8,1024]{1,0:T(8,128)(2,1)} %param.21) | copy-start | bytes 49156
  87.9 2.0 copy-start.1
  91.2 29.2 %copy-start.5 = (f32[8]{0:T(128)S(1)}, f32[8]{0:T(128)}, u32[]{:S(2)}) copy-start(f32[8]{0:T(128)} %param.18) | copy-start | bytes 100
  91.2 106.1 %reduce-scatter.2.cloned.1.call-start = ((), (), s32[]{:S(2)}) async-start(), calls=%async_computation.5 | async-start | bytes 2228224 | tf_op jit(solution)/shard_map/reduce_scatter | solution.py:104
  121.4 11.0 %copy-start.3 = (f32[8,2048]{1,0:T(8,128)}, f32[8,2048]{1,0:T(8,128)S(1)}, u32[]{:S(2)}) copy-start(f32[8,2048]{1,0:T(8,128)S(1)} %get-tuple-element.24) | copy-start | bytes 196612
  121.4 10.7 %copy-start.2 = (bf16[64,1024]{1,0:T(8,128)(2,1)S(1)}, bf16[64,1024]{1,0:T(8,128)(2,1)}, u32[]{:S(2)}) copy-start(bf16[64,1024]{1,0:T(8,128)(2,1)} %param.20) | copy-start | bytes 393220
Sparse Core Ops, SparseCore 0:
  10.2 44.4 all-gather.2
  56.9 40.2 all-gather.4
  99.9 19.5 all-reduce.3
  132.2 61.6 reduce-scatter.1
where the time goes:
time: 207 us; the launch traced here: 206 us
  blocking collectives  66 us (32%)
  local copies, waits for them, and re-layouts  48.6 us (23%)
  matrix products  43.9 us (21%)
  waiting for transfers between devices  16.3 us (8%)
  between operations  14 us (7%)
  other arithmetic  9.15 us (4%)
  starting transfers between devices  7.69 us (4%)
    psum x1, blocking collectives, body(): lax.psum(mean_term, 'obs') - variational_mean.astype(jnp.float32)  61 us
    gather x48, local copies, waits for them, and re-layouts  30.2 us
    gather x1, local copies, waits for them, and re-layouts, body(): arrived = incoming[source, :, position - begin_row].T  13 us
    dot_general x1, matrix products, body(): lax.dot_general(whitened_bf, heavy, (((0,), (0,)), ((), ())), preferred_e...  10.7 us
    dot_general x1, matrix products, body(): jnp.dot(whitened_bf, chol_block, preferred_element_type=jnp.float32)  10.7 us
    dot_general x1, matrix products, cross_cov(): jnp.dot(jnp.dot(row_hot, coupling, precision=precise), col_hot.T, precisi...  10.1 us
    dot_general x1, matrix products, body(): jnp.dot(kernel_rows, prior_block, preferred_element_type=jnp.float32)  7.48 us
    all_to_all x1, starting transfers between devices, body(): lax.all_to_all(outgoing, 'obs', split_axis=0, concat_axis=0, tiled=True)  7.35 us
  transfers between devices with their start and end apart: 5, of which 3 were waited for; matrix products, arithmetic and copies ran while one was open for 42% of the time, Pallas kernels for 0%

commit v1 on v0

v1 whole, which is shorter than its diff:
```python
import functools

import jax
import jax.numpy as jnp
from jax import lax
from jax.experimental import pallas as pl
from jax.experimental.pallas import tpu as pltpu
from jax.sharding import PartitionSpec as P

C = 8
NB = 6
ROWS_DEV = 2048
SLOT = 128
COL = 512

precise = lax.Precision.HIGHEST
f32 = jnp.float32
bf16 = jnp.bfloat16
SMEM = pl.BlockSpec(memory_space=pltpu.SMEM)
VMEM = pl.BlockSpec(memory_space=pltpu.VMEM)
ANY = pl.BlockSpec(memory_space=pl.ANY)


def dot(a, b):
    return jnp.dot(a, b, preferred_element_type=f32)


def dot_nt(a, b):
    return lax.dot_general(a, b, (((1,), (1,)), ((), ())), preferred_element_type=f32)


def swap(value, axis, bit):
    size = lax.axis_size(axis)
    return lax.ppermute(value, axis, [(i, i ^ bit) for i in range(size)])


def gather_pieces(own, nz):
    near = jnp.concatenate([own] + [swap(own, "obs", 4 * k) for k in range(1, nz)], axis=0)
    far = swap(near, "obs", 2)
    return near, far, swap(near, "obs", 1), swap(far, "obs", 1)


def load_pieces(me, groups, whole, sems, nz):
    rows = whole.shape[0] // (4 * nz)
    copies = []
    for g, group in enumerate(groups):
        for s in range(nz):
            piece = me ^ (4 * s) ^ (2 * (g % 2)) ^ (g // 2)
            copies.append(
                pltpu.make_async_copy(
                    group.at[pl.ds(rows * s, rows)],
                    whole.at[pl.ds(pl.multiple_of(rows * piece, rows), rows)],
                    sems.at[g, s],
                )
            )
    for copy in copies:
        copy.start()
    for copy in copies:
        copy.wait()


def whiten_kernel(nz, me, kt, g0, g1, g2, g3, means, ab, stats, whole, turned, sems):
    width = whole.shape[0]

    @pl.when(pl.program_id(0) == 0)
    def _():
        load_pieces(me[0], (g0, g1, g2, g3), whole, sems, nz)
        for j in range(0, width, 256):
            turned[:, j : j + 256] = whole[j : j + 256, :].T

    square = jnp.zeros((1, kt.shape[1]), f32)
    for k in range(0, width, 256):
        part = dot(turned[k : k + 256, :], kt[...])
        square = square + jnp.sum(part * part, axis=0, keepdims=True)
        ab[k : k + 256, :] = part.astype(bf16)
    stats[0:C, :] = dot(means[...], ab[...])
    stats[C : 2 * C, :] = jnp.broadcast_to(-square, (C, kt.shape[1]))


def covary_kernel(nz, me, ab, stats, g0, g1, g2, g3, bt, sums, whole, turned, sems):
    width = whole.shape[0]
    step = pl.program_id(0)

    @pl.when(step == 0)
    def _():
        load_pieces(me[0], (g0, g1, g2, g3), whole, sems, nz)
        for j in range(0, width, 256):
            turned[:, j : j + 256] = whole[j : j + 256, :].T

    square = stats[C : C + 1, :]
    for l in range(0, width, 256):
        part = dot(turned[l : l + 256, l:], ab[l:, :])
        square = square + jnp.sum(part * part, axis=0, keepdims=True)
        bt[l : l + 256, :] = part.astype(bf16)
    columns = pl.multiple_of(step * COL, COL)
    sums[:, pl.ds(columns, COL)] = stats[0:C, :]
    half = COL // 2
    sums[pl.ds(2 * step, 1), ROWS_DEV:] = square[:, :half]
    sums[pl.ds(2 * step + 1, 1), ROWS_DEV:] = square[:, half:]


def slope_kernel(
    nz, me, own, other, scales, labels, self_cov, ab, bt, chances_out, keep, send, heavy, slope, twice
):
    step = pl.program_id(0)
    core = me[0] % 2
    block = ab.shape[0]
    quarter = block // 4
    groups = quarter // 16

    @pl.when(step == 0)
    def _():
        total = own[...] + other[...]
        variance = jnp.concatenate(
            [total[i : i + 1, ROWS_DEV:] for i in range(C)], axis=1
        ) + self_cov[...]
        logits = total[:, :ROWS_DEV] + 0.5 * scales[...] * variance
        weights = jnp.exp(logits)
        chances = weights / jnp.sum(weights, axis=0, keepdims=True)
        chances_out[...] = chances
        twice[...] = -jnp.sum(chances * scales[...], axis=0, keepdims=True)
        classes = lax.broadcasted_iota(jnp.int32, chances.shape, 0)
        slope[...] = ((labels[...] == classes).astype(f32) - chances).astype(bf16)

    rows = pl.multiple_of(step * block, block)
    heavy[pl.ds(rows, block), :] = (bt[...].astype(f32) * twice[...]).astype(bf16)
    extra = block * nz * (nz + 1) // 2

    for z in range(nz):

        @pl.when(step == z)
        def _():
            wide = block * (z + 1)
            start = block * z * (z + 1) // 2
            term = dot_nt(ab[...], heavy[:wide, :])
            for x in range(2):
                first = term[2 * quarter * x : 2 * quarter * x + quarter, :]
                second = term[2 * quarter * x + quarter : 2 * quarter * (x + 1), :]
                keep[x, :, start : start + wide] = jnp.where(core == 0, first, second)
                send[x, :, start : start + wide] = jnp.where(core == 0, second, first).astype(bf16)
            mean = dot_nt(slope[...], ab[...])
            high = mean.astype(bf16).astype(f32)
            both = jnp.concatenate([high, mean - high], axis=0).astype(bf16)
            held = jnp.concatenate([mean, jnp.zeros_like(mean)], axis=0)
            top = 16 * (z % groups)
            left = extra + block * (z // groups)
            for x in range(2):
                keep[x, top : top + 16, left : left + block] = held
                send[x, top : top + 16, left : left + block] = both


def add_extra(kept, arrived, groups):
    parts = []
    for g in range(groups):
        top = kept[16 * g : 16 * g + 8] + arrived[16 * g : 16 * g + 8] + arrived[16 * g + 8 : 16 * g + 16]
        parts.append(top)
    return parts


def fold_extra(parts):
    held, sent = [], []
    for part in parts:
        high = part.astype(bf16).astype(f32)
        held += [part, jnp.zeros_like(part)]
        sent += [high, part - high]
    return jnp.concatenate(held, axis=0), jnp.concatenate(sent, axis=0).astype(bf16)


def pair_kernel(body_width, me, keep, arrived, kept, send):
    x = (me[0] // 2) % 2
    groups = keep.shape[1] // 16
    send[:, :body_width] = (
        keep[1 - x, :, :body_width] + arrived[1 - x, :, :body_width].astype(f32)
    ).astype(bf16)
    kept[:, :body_width] = keep[x, :, :body_width] + arrived[x, :, :body_width].astype(f32)
    parts = add_extra(
        keep[0, :, body_width:], arrived[0, :, body_width:].astype(f32), groups
    )
    held, sent = fold_extra(parts)
    kept[:, body_width:] = held
    send[:, body_width:] = sent


def chip_kernel(nz, body_width, me, kept, arrived, mine, *sends):
    z = me[0] // 4
    groups = kept.shape[0] // 16
    width = mine.shape[1] - (kept.shape[1] - body_width)
    block = width // nz
    parts = add_extra(kept[:, body_width:], arrived[:, body_width:].astype(f32), groups)
    held, sent = fold_extra(parts)
    for k in range(nz):
        target = z ^ k
        start = pl.multiple_of(block * (target * (target + 1) // 2), block)
        value = kept[:, pl.ds(start, width)] + arrived[:, pl.ds(start, width)].astype(f32)
        if k == 0:
            mine[:, :width] = value
            mine[:, width:] = held
        else:
            sends[k - 1][:, :width] = value.astype(bf16)
            sends[k - 1][:, width:] = sent


def finish_kernel(nz, me, mine, chol, means, *rest):
    arrived, grad_chol, grad_mean = rest[: nz - 1], rest[nz - 1], rest[nz]
    rows, width = chol.shape
    groups = rows // 16
    total = mine[:, :width]
    for piece in arrived:
        total = total + piece[:, :width].astype(f32)
    row_ids = me[0] * rows + lax.broadcasted_iota(jnp.int32, (rows, width), 0)
    column_ids = lax.broadcasted_iota(jnp.int32, (rows, width), 1)
    own = chol[...].astype(f32)
    on_diag = column_ids == row_ids
    diagonal = jnp.sum(jnp.where(on_diag, own, 0.0), axis=1, keepdims=True)
    grad_chol[...] = (
        jnp.where(column_ids <= row_ids, total, 0.0) - own + jnp.where(on_diag, 1.0 / diagonal, 0.0)
    )
    extra = mine[:, width:]
    parts = [extra[16 * g : 16 * g + 8] for g in range(groups)]
    for piece in arrived:
        values = piece[:, width:].astype(f32)
        parts = [
            part + values[16 * g : 16 * g + 8] + values[16 * g + 8 : 16 * g + 16]
            for g, part in enumerate(parts)
        ]
    block = width // nz
    for z in range(nz):
        part = parts[z % groups][:, block * (z // groups) : block * (z // groups + 1)]
        here = slice(block * z, block * (z + 1))
        grad_mean[:, here] = part - means[:, here].astype(f32)


def route(obs_coords, obs_codes, route_plan):
    devices = lax.axis_size("obs")
    stacked = jnp.concatenate([obs_coords, obs_codes.astype(f32)[None, :]], axis=0)
    if devices * SLOT == ROWS_DEV:
        return lax.all_to_all(stacked, "obs", split_axis=1, concat_axis=1, tiled=True)
    me = lax.axis_index("obs")
    blocks = route_plan * SLOT
    send_start = jnp.cumsum(blocks, axis=1) - blocks
    recv_start = jnp.cumsum(blocks, axis=0) - blocks
    my_sends = lax.dynamic_index_in_dim(send_start, me, 0, keepdims=False)
    my_recvs = lax.dynamic_index_in_dim(recv_start, me, 1, keepdims=False)
    padded = jnp.concatenate([stacked, jnp.zeros((3, SLOT), f32)], axis=1)
    outgoing = jax.vmap(lambda offset: lax.dynamic_slice_in_dim(padded, offset, SLOT, 1))(my_sends)
    incoming = lax.all_to_all(outgoing, "obs", split_axis=0, concat_axis=0, tiled=True)
    position = jnp.arange(ROWS_DEV, dtype=jnp.int32)
    sources = jnp.arange(devices, dtype=jnp.int32)
    source = jnp.sum((my_recvs[None, :] <= position[:, None]).astype(jnp.int32), axis=1) - 1
    pick = (source[:, None] == sources[None, :]).astype(jnp.int32)
    begin_row = jnp.sum(pick * my_recvs[None, :], axis=1)
    return incoming[source, :, position - begin_row].T


def body(
    obs_coords,
    obs_codes,
    route_plan,
    inducing_coords,
    inducing_bands,
    band_mix,
    lengthscales,
    class_scales,
    prior_factor,
    variational_chol,
    variational_mean,
):
    n = lax.axis_size("obs")
    nz = n // 4
    me = lax.axis_index("obs").astype(jnp.int32)[None]
    rows, width = variational_chol.shape
    steps = ROWS_DEV // COL
    block = width // nz
    body_width = block * nz * (nz + 1) // 2
    extra_width = 16 * width // rows
    packed = body_width + extra_width

    prior_groups = gather_pieces(prior_factor, nz)
    arrived = route(obs_coords, obs_codes, route_plan)
    chol_groups = gather_pieces(variational_chol, nz)

    code_ids = arrived[2:3].astype(jnp.int32)
    band_ids = code_ids % NB
    labels = code_ids // NB
    coupling = jnp.eye(NB, dtype=f32) + jnp.dot(band_mix, band_mix.T, precision=precise)
    kinds = jnp.arange(NB, dtype=jnp.int32)
    row_hot = (band_ids == kinds[:, None]).astype(f32)
    col_hot = (inducing_bands[:, None] == kinds[None, :]).astype(f32)
    self_cov = jnp.sum(row_hot * jnp.diagonal(coupling)[:, None], axis=0, keepdims=True)
    mixing = jnp.dot(jnp.dot(col_hot, coupling, precision=precise), row_hot, precision=precise)
    delta_t = (arrived[0][None, :] - inducing_coords[0][:, None]) / lengthscales[0]
    delta_w = (arrived[1][None, :] - inducing_coords[1][:, None]) / lengthscales[1]
    kt = (jnp.exp(-0.5 * (delta_t * delta_t + delta_w * delta_w)) * mixing).astype(bf16)

    whole = [
        pltpu.VMEM((width, width), bf16),
        pltpu.VMEM((width, width), bf16),
        pltpu.SemaphoreType.DMA((4, nz)),
    ]
    by_column = lambda height: pl.BlockSpec((height, COL), lambda i: (0, i))
    fixed = lambda shape: pl.BlockSpec(shape, lambda i: tuple(0 for _ in shape))
    big = pltpu.CompilerParams(vmem_limit_bytes=40 * 1024 * 1024)
    ab, part_stats = pl.pallas_call(
        functools.partial(whiten_kernel, nz),
        grid=(steps,),
        out_shape=(
            jax.ShapeDtypeStruct((width, ROWS_DEV), bf16),
            jax.ShapeDtypeStruct((2 * C, ROWS_DEV), f32),
        ),
        in_specs=[SMEM, by_column(width), ANY, ANY, ANY, ANY, fixed((C, width))],
        out_specs=(by_column(width), by_column(2 * C)),
        scratch_shapes=whole,
        compiler_params=big,
        cost_estimate=pl.CostEstimate(
            flops=2 * width * width * ROWS_DEV, bytes_accessed=10 * 1024 * 1024, transcendentals=0
        ),
        name="whiten",
    )(me, kt, *prior_groups, variational_mean)
    bt, sums = pl.pallas_call(
        functools.partial(covary_kernel, nz),
        grid=(steps,),
        out_shape=(
            jax.ShapeDtypeStruct((width, ROWS_DEV), bf16),
            jax.ShapeDtypeStruct((C, ROWS_DEV + COL // 2), f32),
        ),
        in_specs=[SMEM, by_column(width), by_column(2 * C), ANY, ANY, ANY, ANY],
        out_specs=(by_column(width), fixed((C, ROWS_DEV + COL // 2))),
        scratch_shapes=whole,
        compiler_params=big,
        cost_estimate=pl.CostEstimate(
            flops=width * width * ROWS_DEV, bytes_accessed=10 * 1024 * 1024, transcendentals=0
        ),
        name="covary",
    )(me, ab, part_stats, *chol_groups)

    other = swap(sums, "ind", 1)
    bit = 2
    while bit < lax.axis_size("ind"):
        sums = sums + other
        other = swap(sums, "ind", bit)
        bit *= 2

    by_row = pl.BlockSpec((block, ROWS_DEV), lambda i: (i, 0))
    chances, keep, send = pl.pallas_call(
        functools.partial(slope_kernel, nz),
        grid=(nz,),
        out_shape=(
            jax.ShapeDtypeStruct((C, ROWS_DEV), f32),
            jax.ShapeDtypeStruct((2, rows, packed), f32),
            jax.ShapeDtypeStruct((2, rows, packed), bf16),
        ),
        in_specs=[
            SMEM,
            fixed(sums.shape),
            fixed(sums.shape),
            fixed((C, 1)),
            fixed((1, ROWS_DEV)),
            fixed((1, ROWS_DEV)),
            by_row,
            by_row,
        ],
        out_specs=(fixed((C, ROWS_DEV)), fixed((2, rows, packed)), fixed((2, rows, packed))),
        scratch_shapes=[
            pltpu.VMEM((width, ROWS_DEV), bf16),
            pltpu.VMEM((C, ROWS_DEV), bf16),
            pltpu.VMEM((1, ROWS_DEV), f32),
        ],
        compiler_params=big,
        cost_estimate=pl.CostEstimate(
            flops=width * width * ROWS_DEV, bytes_accessed=10 * 1024 * 1024, transcendentals=0
        ),
        name="slopes",
    )(me, sums, other, class_scales[:, None], labels, self_cov, ab, bt)

    kept, send = pl.pallas_call(
        functools.partial(pair_kernel, body_width),
        out_shape=(
            jax.ShapeDtypeStruct((rows, packed), f32),
            jax.ShapeDtypeStruct((rows, packed), bf16),
        ),
        in_specs=[SMEM, VMEM, VMEM],
        out_specs=(VMEM, VMEM),
        compiler_params=big,
        name="add_pair",
    )(me, keep, swap(send, "obs", 1))
    piece = (rows, width + extra_width)
    mine, *sends = pl.pallas_call(
        functools.partial(chip_kernel, nz, body_width),
        out_shape=[jax.ShapeDtypeStruct(piece, f32)]
        + [jax.ShapeDtypeStruct(piece, bf16)] * (nz - 1),
        in_specs=[SMEM, VMEM, VMEM],
        out_specs=[VMEM] * nz,
        compiler_params=big,
        name="add_chip",
    )(me, kept, swap(send, "obs", 2))
    arrivals = [swap(value, "obs", 4 * (k + 1)) for k, value in enumerate(sends)]
    grad_chol, grad_mean = pl.pallas_call(
        functools.partial(finish_kernel, nz),
        out_shape=(
            jax.ShapeDtypeStruct((rows, width), f32),
            jax.ShapeDtypeStruct((C, width), f32),
        ),
        in_specs=[SMEM] + [VMEM] * (nz + 2),
        out_specs=(VMEM, VMEM),
        compiler_params=big,
        name="finish",
    )(me, mine, variational_chol, variational_mean, *arrivals)
    return (chances, grad_chol, grad_mean)


def solution(mesh):
    placed = (
        P(None, "obs"),
        P("obs"),
        P(),
        P(None, "ind"),
        P("ind"),
        P(),
        P(),
        P(),
        P(("ind", "obs"), None),
        P(("ind", "obs"), None),
        P(None, "ind"),
    )
    return jax.shard_map(
        body,
        mesh=mesh,
        in_specs=placed,
        out_specs=(P(None, "obs"), P(("ind", "obs"), None), P(None, "ind")),
        check_vma=False,
    )
```

time: 207 us -> 111 us (0.54)
  blocking collectives: 66 us -> 0 us
  local copies, waits for them, and re-layouts: 48.6 us -> 5.41 us
  matrix products: 43.9 us -> 9.47 us
  waiting for transfers between devices: 16.3 us -> 42.9 us
  Pallas kernels: 0 us -> 24.8 us
  starting transfers between devices: 7.69 us -> 24.7 us
  between operations: 14 us -> 0.86 us
  other arithmetic: 9.15 us -> 2.25 us
    psum x2 -> x0, blocking collectives: 66 us -> none  [the longest x1 61 us: body(): lax.psum(mean_term, 'obs') - variational_mean.astype(jnp.float32)]
    gather x49 -> x1, local copies, waits for them, and re-layouts: 43.2 us -> 0.64 us  [body(): jnp.diagonal(coupling)[:, None]]
    ppermute x0 -> x18, waiting for transfers between devices: none -> 40.4 us  [swap(): return lax.ppermute(value, axis, [(i, i ^ bit) for i in range(size)])]
    dot_general x7 -> x2, matrix products: 43.8 us -> 9.34 us  [the longest x1 8.2 us: body(): jnp.dot(jnp.dot(col_hot, coupling, precision=precise), row_hot, precision...]
    pallas_call x0 -> x6, Pallas kernels: none -> 24.8 us  [the longest x1 9.67 us: body(): pl.pallas_call(functools.partial(whiten_kernel, nz), grid=(steps,), out_s...]
    ppermute x0 -> x18, starting transfers between devices: none -> 21.2 us  [swap(): return lax.ppermute(value, axis, [(i, i ^ bit) for i in range(size)])]
    psum x1 -> x0, waiting for transfers between devices: 6.73 us -> none  [body(): mean_sum, var_sum = lax.psum((mean_part, var_part), 'ind')]
    all_gather x2 -> x0, waiting for transfers between devices: 5.67 us -> none  [the longest x1 5.67 us: body(): lax.all_gather(variational_chol, 'obs', axis=0, tiled=True)]
  transfers between devices with their start and end apart: 5 -> 19, of which waited for: 3 -> 9; matrix products, arithmetic and copies ran while one was open for 42% -> 16% of each run, Pallas kernels for 0% -> 9%
where the time goes in v1:
time: 111 us; the launch traced here: 110 us
  waiting for transfers between devices  42.9 us (39%)
  Pallas kernels  24.8 us (22%)
  starting transfers between devices  24.7 us (22%)
  matrix products  9.47 us (9%)
  local copies, waits for them, and re-layouts  5.41 us (5%)
  other arithmetic  2.25 us (2%)
    ppermute x18, waiting for transfers between devices, swap(): return lax.ppermute(value, axis, [(i, i ^ bit) for i in range(size)])  40.4 us
    ppermute x18, starting transfers between devices, swap(): return lax.ppermute(value, axis, [(i, i ^ bit) for i in range(size)])  21.2 us
    pallas_call x1, Pallas kernels, body(): pl.pallas_call(functools.partial(whiten_kernel, nz), grid=(steps,), out_s...  9.67 us
    dot_general x1, matrix products, body(): jnp.dot(jnp.dot(col_hot, coupling, precision=precise), row_hot, precision...  8.2 us
    pallas_call x1, Pallas kernels, body(): pl.pallas_call(functools.partial(covary_kernel, nz), grid=(steps,), out_s...  7.86 us
    pallas_call x1, Pallas kernels, body(): pl.pallas_call(functools.partial(slope_kernel, nz), grid=(nz,), out_shape...  6.02 us
    all_to_all x1, starting transfers between devices, route(): lax.all_to_all(stacked, 'obs', split_axis=1, concat_axis=1, tiled=True)  3.5 us
    all_to_all x1, waiting for transfers between devices, route(): lax.all_to_all(stacked, 'obs', split_axis=1, concat_axis=1, tiled=True)  2.48 us
  transfers between devices with their start and end apart: 19, of which 9 were waited for; matrix products, arithmetic and copies ran while one was open for 16% of the time, Pallas kernels for 9%

profile of v1, /device:TPU:0, one launch (start us, length us, event | category | flops | bytes accessed | tf_op | source)
XLA Modules:
  0.0 110.4 jit_solution(15634539029754557698)
XLA Ops:
  0.6 0.0 copy-start
  0.6 3.1 %collective-permute-start = (bf16[64,1024]{1,0:T(8,128)(2,1)}, bf16[64,1024]{1,0:T(8,128)(2,1)S(1)}, u32[]{:S(2)}, u32[]{:S(2)}) collective-permute-start(bf16[64,1024]{1,0:T(8,128)(2,1)} %param.18), channel_id=1, source_target_pairs={{0,8},{2,10},{4,12},{6,14},{8,0},{10,2},{12,4},{14,6},{16,24},{18,... | collective-permute-start | bytes 393224 | tf_op jit(solution)/shard_map/ppermute | solution.py:34
  3.7 2.6 %collective-permute-start.1 = (bf16[64,1024]{1,0:T(8,128)(2,1)}, bf16[64,1024]{1,0:T(8,128)(2,1)S(1)}, u32[]{:S(2)}, u32[]{:S(2)}) collective-permute-start(bf16[64,1024]{1,0:T(8,128)(2,1)} %param.18), channel_id=1, source_target_pairs={{0,16},{2,18},{4,20},{6,22},{8,24},{10,26},{12,28},{14,30},{16,0},... | collective-permute-start | bytes 393224 | tf_op jit(solution)/shard_map/ppermute | solution.py:34
  6.3 0.0 collective-permute-start.2
  6.3 0.9 collective-permute-start.6
  7.2 3.5 %collective-permute-start.7 = (bf16[64,1024]{1,0:T(8,128)(2,1)}, bf16[64,1024]{1,0:T(8,128)(2,1)S(1)}, u32[]{:S(2)}, u32[]{:S(2)}) collective-permute-start(bf16[64,1024]{1,0:T(8,128)(2,1)} %chol.1), channel_id=1, source_target_pairs={{0,16},{2,18},{4,20},{6,22},{8,24},{10,26},{12,28},{14,30},{16,0},... | collective-permute-start | bytes 393224 | tf_op jit(solution)/shard_map/ppermute | solution.py:34
  10.7 0.7 convert_element_type.24
  11.4 1.3 %pad_maximum_fusion = f32[3,16,128]{2,0,1:T(4,128)} fusion(f32[1,16,128]{2,0,1:T(1,128)S(1)} %bitcast.23, f32[2,16,128]{2,0,1:T(2,128)} %bitcast.25), kind=kLoop, calls=%fused_computation.8 | loop fusion | flops 6144 | bytes 49152 | tf_op jit(solution)/shard_map/concatenate | solution.py:235
  12.8 3.5 %all-to-all-start = ((f32[3,16,128]{2,0,1:T(4,128)}), f32[3,16,128]{2,0,1:T(4,128)S(1)}, u32[]{:S(2)}, u32[]{:S(2)}) async-start(f32[3,16,128]{2,0,1:T(4,128)} %pad_maximum_fusion), calls=%async_computation | async-start | bytes 65536 | tf_op jit(solution)/shard_map/all_to_all | solution.py:237
  16.3 0.9 constant_dynamic-update-slice_fusion.3
  17.2 0.9 constant_dynamic-update-slice_fusion.7
  18.1 0.0 copy-done
  18.1 0.1 convolution_add_fusion
  18.2 0.8 fusion.5
  19.0 1.3 %fusion.6 = (f32[1]{0:T(128)}, f32[1]{0:T(128)}) fusion(f32[2]{0:T(128)} %param.16), kind=kLoop, calls=%fused_computation.26 | loop fusion | bytes 16 | tf_op jit(solution)/shard_map/slice | solution.py:291
  20.3 1.1 %fusion = f32[1024,6]{0,1:T(8,128)S(1)} fusion(f32[6,6]{1,0:T(8,128)S(1)} %convolution_add_fusion, s32[1024]{0:T(1024)} %param.14), kind=kOutput, calls=%fused_computation.4 | convolution fusion | flops 448512 | bytes 28816 | tf_op jit(solution)/shard_map/dot_general | solution.py:290
  21.5 0.6 gather_fusion
  22.2 0.7 copy.16.scales
  22.9 2.5 %all-to-all-done = f32[3,16,128]{2,0,1:T(4,128)S(1)} async-done(((f32[3,16,128]{2,0,1:T(4,128)}), f32[3,16,128]{2,0,1:T(4,128)S(1)}, u32[]{:S(2)}, u32[]{:S(2)}) %all-to-all-start) | async-done | bytes 24608 | tf_op jit(solution)/shard_map/all_to_all | solution.py:237
  25.4 0.0 collective-permute-done
  25.5 2.6 %collective-permute-start.8 = (bf16[64,1024]{1,0:T(8,128)(2,1)}, bf16[64,1024]{1,0:T(8,128)(2,1)S(1)}, u32[]{:S(2)}, u32[]{:S(2)}) collective-permute-start(bf16[64,1024]{1,0:T(8,128)(2,1)} %chol.1), channel_id=1, source_target_pairs={{0,24},{2,26},{4,28},{6,30},{8,16},{10,18},{12,20},{14,22},{16,8},... | collective-permute-start | bytes 393224 | tf_op jit(solution)/shard_map/ppermute | solution.py:34
  28.0 0.0 collective-permute-done.1
  28.1 0.0 collective-permute-done.2
  28.1 0.7 collective-permute-start.3
  28.8 0.0 collective-permute-start.4
  28.8 0.0 collective-permute-done.6
  28.8 0.0 collective-permute-done.7
  28.8 4.3 %collective-permute-done.8 = bf16[64,1024]{1,0:T(8,128)(2,1)S(1)} collective-permute-done((bf16[64,1024]{1,0:T(8,128)(2,1)}, bf16[64,1024]{1,0:T(8,128)(2,1)S(1)}, u32[]{:S(2)}, u32[]{:S(2)}) %collective-permute-start.8) | collective-permute-done | bytes 131104 | tf_op jit(solution)/shard_map/ppermute | solution.py:34
  33.2 0.7 collective-permute-start.9
  33.8 9.2 %collective-permute-done.3.g1 = bf16[256,1024]{1,0:T(8,128)(2,1)S(1)} collective-permute-done((bf16[256,1024]{1,0:T(8,128)(2,1)S(1)}, bf16[256,1024]{1,0:T(8,128)(2,1)S(1)}, u32[]{:S(2)}, u32[]{:S(2)}) %collective-permute-start.3) | collective-permute-done | bytes 524320 | tf_op jit(solution)/shard_map/ppermute | solution.py:34
  43.0 0.0 collective-permute-start.5
  43.0 0.0 copy-start.2
  43.0 8.2 %multiply_convert_fusion.kt = bf16[1024,2048]{1,0:T(8,128)(2,1)S(1)} fusion(f32[1024,6]{0,1:T(8,128)S(1)} %fusion, f32[]{:T(128)} %bitcast.8, f32[1024]{0:T(1024)S(1)} %bitcast.29, f32[2048]{0:T(1024)S(1)} %bitcast.27, f32[]{:T(128)} %bitcast.5, f32[1024]{0:T(1024)S(1)} %bitcast.28, f32[2048]{0:T(1024)S(1)} %bitcast.26, s32[2048]{0:T(1024)S(1)} %add_select_fusion), kind=kOutput, calls=%fused_computation.1 | convolution fusion | flops 171978752 | bytes 4251656 | tf_op jit(solution)/shard_map/dot_general | solution.py:290
  51.2 0.6 collective-permute-start.10
  51.8 1.3 %collective-permute-done.9.g1 = bf16[256,1024]{1,0:T(8,128)(2,1)S(1)} collective-permute-done((bf16[256,1024]{1,0:T(8,128)(2,1)S(1)}, bf16[256,1024]{1,0:T(8,128)(2,1)S(1)}, u32[]{:S(2)}, u32[]{:S(2)}) %collective-permute-start.9) | collective-permute-done | bytes 524320 | tf_op jit(solution)/shard_map/ppermute | solution.py:34
  53.1 0.0 collective-permute-start.11
  53.1 0.1 bitcast_select_fusion.labels
  53.1 0.0 collective-permute-done.4.g2
  53.1 0.0 collective-permute-done.5.g3
  53.2 0.0 copy-done.2
  53.2 9.7 %whiten.1 = (bf16[1024,2048]{1,0:T(8,128)(2,1)S(1)}, f32[16,2048]{1,0:T(8,128)S(1)}) custom-call(s32[1]{0:T(128)} %bitcast.me, bf16[1024,2048]{1,0:T(8,128)(2,1)S(1)} %multiply_convert_fusion.kt, bf16[256,1024]{1,0:T(8,128)(2,1)S(1)} %constant_dynamic-update-slice_fusion.g0, bf16[256,1024]{1,0:T(8,128)(2,1)S(1)} %collective-permute-done.3.g1, ...), custom_call_target="tpu_custom_call" | custom-call | flops 4294967296 | bytes 10485760 | tf_op jit(solution)/shard_map/whiten/pallas_call | solution.py:303
  62.8 0.0 collective-permute-done.10.g2
  62.9 0.0 collective-permute-done.11.g3
  62.9 7.9 %covary.1 = (bf16[1024,2048]{1,0:T(8,128)(2,1)S(1)}, f32[8,2304]{1,0:T(8,128)S(1)}) custom-call(s32[1]{0:T(128)} %bitcast.me, bf16[1024,2048]{1,0:T(8,128)(2,1)S(1)} %get-tuple-element.18.ab, f32[16,2048]{1,0:T(8,128)S(1)} %get-tuple-element.19.stats, bf16[256,1024]{1,0:T(8,128)(2,1)S(1)} %constant_dynamic-update-slice_fusion.4.g0, ...), custom_call_target="tpu_custom_call" | custom-call | flops 2147483648 | bytes 10485760 | tf_op jit(solution)/shard_map/covary/pallas_call | solution.py:319
  70.7 1.6 %collective-permute-start.12 = (f32[8,2304]{1,0:T(8,128)S(1)}, f32[8,2304]{1,0:T(8,128)S(1)}, u32[]{:S(2)}, u32[]{:S(2)}) collective-permute-start(f32[8,2304]{1,0:T(8,128)S(1)} %get-tuple-element.20.own), channel_id=1, source_target_pairs={{0,1},{1,0},{2,3},{3,2},{4,5},{5,4},{6,7},{7,6},{8,9},{9,8},{10,11... | collective-permute-start | bytes 221192 | tf_op jit(solution)/shard_map/ppermute | solution.py:34
  72.3 0.1 select_reduce_fusion
  72.4 3.1 %collective-permute-done.12.other = f32[8,2304]{1,0:T(8,128)S(1)} collective-permute-done((f32[8,2304]{1,0:T(8,128)S(1)}, f32[8,2304]{1,0:T(8,128)S(1)}, u32[]{:S(2)}, u32[]{:S(2)}) %collective-permute-start.12) | collective-permute-done | bytes 73760 | tf_op jit(solution)/shard_map/ppermute | solution.py:34
  75.5 0.0 copy-start.1
  75.5 6.0 %slopes.1 = (f32[8,2048]{1,0:T(8,128)}, f32[2,64,2816]{2,1,0:T(8,128)S(1)}, bf16[2,64,2816]{2,1,0:T(8,128)(2,1)S(1)}) custom-call(s32[1]{0:T(128)} %bitcast.me, f32[8,2304]{1,0:T(8,128)S(1)} %get-tuple-element.20.own, f32[8,2304]{1,0:T(8,128)S(1)} %collective-permute-done.12.other, f32[8,1]{1,0:T(8,128)S(1)} %copy.16.scales, ...), custom_call_target="tpu_custom_call" | custom-call | flops 2147483648 | bytes 10485760 | tf_op jit(solution)/shard_map/slopes/pallas_call | solution.py:344
  81.5 0.0 collective-permute-start.13
  81.5 2.2 %collective-permute-done.13.arrived = bf16[2,64,2816]{2,1,0:T(8,128)(2,1)S(1)} collective-permute-done((bf16[2,64,2816]{2,1,0:T(8,128)(2,1)S(1)}, bf16[2,64,2816]{2,1,0:T(8,128)(2,1)S(1)}, u32[]{:S(2)}, u32[]{:S(2)}) %collective-permute-start.13) | collective-permute-done | bytes 720928 | tf_op jit(solution)/shard_map/ppermute | solution.py:34
  83.7 0.1 add_pair.1
  83.8 0.7 collective-permute-start.14
  84.5 9.9 %collective-permute-done.14.arrived = bf16[64,2816]{1,0:T(8,128)(2,1)S(1)} collective-permute-done((bf16[64,2816]{1,0:T(8,128)(2,1)S(1)}, bf16[64,2816]{1,0:T(8,128)(2,1)S(1)}, u32[]{:S(2)}, u32[]{:S(2)}) %collective-permute-start.14) | collective-permute-done | bytes 360480 | tf_op jit(solution)/shard_map/ppermute | solution.py:34
  94.4 0.1 add_chip.1
  94.5 0.1 collective-permute-start.15
  94.6 1.9 %collective-permute-start.16 = (bf16[64,1280]{1,0:T(8,128)(2,1)S(1)}, bf16[64,1280]{1,0:T(8,128)(2,1)S(1)}, u32[]{:S(2)}, u32[]{:S(2)}) collective-permute-start(bf16[64,1280]{1,0:T(8,128)(2,1)S(1)} %get-tuple-element.29), channel_id=1, source_target_pairs={{0,16},{2,18},{4,20},{6,22},{8,24},{10,26},{12,28},{14,30},{16,0},... | collective-permute-start | bytes 491528 | tf_op jit(solution)/shard_map/ppermute | solution.py:34
  96.4 2.5 %collective-permute-start.17 = (bf16[64,1280]{1,0:T(8,128)(2,1)S(1)}, bf16[64,1280]{1,0:T(8,128)(2,1)S(1)}, u32[]{:S(2)}, u32[]{:S(2)}) collective-permute-start(bf16[64,1280]{1,0:T(8,128)(2,1)S(1)} %get-tuple-element.30), channel_id=1, source_target_pairs={{0,24},{2,26},{4,28},{6,30},{8,16},{10,18},{12,20},{14,22},{16,8},... | collective-permute-start | bytes 491528 | tf_op jit(solution)/shard_map/ppermute | solution.py:34
  98.9 3.2 %collective-permute-done.15.rest_0_ = bf16[64,1280]{1,0:T(8,128)(2,1)S(1)} collective-permute-done((bf16[64,1280]{1,0:T(8,128)(2,1)S(1)}, bf16[64,1280]{1,0:T(8,128)(2,1)S(1)}, u32[]{:S(2)}, u32[]{:S(2)}) %collective-permute-start.15) | collective-permute-done | bytes 163872 | tf_op jit(solution)/shard_map/ppermute | solution.py:34
  102.1 7.3 %collective-permute-done.16.rest_1_ = bf16[64,1280]{1,0:T(8,128)(2,1)S(1)} collective-permute-done((bf16[64,1280]{1,0:T(8,128)(2,1)S(1)}, bf16[64,1280]{1,0:T(8,128)(2,1)S(1)}, u32[]{:S(2)}, u32[]{:S(2)}) %collective-permute-start.16) | collective-permute-done | bytes 163872 | tf_op jit(solution)/shard_map/ppermute | solution.py:34
  109.4 0.0 collective-permute-done.17.rest_2_
  109.4 0.0 copy-done.1
  109.4 0.9 finish.1
  (10 shorter events, 0.1 us)
Async XLA Ops:
  0.6 17.5 %copy-start = (f32[6,6]{1,0:T(8,128)S(1)}, f32[6,6]{1,0:T(8,128)}, u32[]{:S(2)}) copy-start(f32[6,6]{1,0:T(8,128)} %param.15) | copy-start | bytes 436
  0.6 24.8 %collective-permute-start = (bf16[64,1024]{1,0:T(8,128)(2,1)}, bf16[64,1024]{1,0:T(8,128)(2,1)S(1)}, u32[]{:S(2)}, u32[]{:S(2)}) collective-permute-start(bf16[64,1024]{1,0:T(8,128)(2,1)} %param.18), channel_id=1, source_target_pairs={{0,8},{2,10},{4,12},{6,14},{8,0},{10,2},{12,4},{14,6},{16,24},{18,... | collective-permute-start | bytes 393224 | tf_op jit(solution)/shard_map/ppermute | solution.py:34
  3.7 24.3 %collective-permute-start.1 = (bf16[64,1024]{1,0:T(8,128)(2,1)}, bf16[64,1024]{1,0:T(8,128)(2,1)S(1)}, u32[]{:S(2)}, u32[]{:S(2)}) collective-permute-start(bf16[64,1024]{1,0:T(8,128)(2,1)} %param.18), channel_id=1, source_target_pairs={{0,16},{2,18},{4,20},{6,22},{8,24},{10,26},{12,28},{14,30},{16,0},... | collective-permute-start | bytes 393224 | tf_op jit(solution)/shard_map/ppermute | solution.py:34
  6.3 21.8 %collective-permute-start.2 = (bf16[64,1024]{1,0:T(8,128)(2,1)}, bf16[64,1024]{1,0:T(8,128)(2,1)S(1)}, u32[]{:S(2)}, u32[]{:S(2)}) collective-permute-start(bf16[64,1024]{1,0:T(8,128)(2,1)} %param.18), channel_id=1, source_target_pairs={{0,24},{2,26},{4,28},{6,30},{8,16},{10,18},{12,20},{14,22},{16,8},... | collective-permute-start | bytes 393224 | tf_op jit(solution)/shard_map/ppermute | solution.py:34
  6.3 22.4 %collective-permute-start.6 = (bf16[64,1024]{1,0:T(8,128)(2,1)}, bf16[64,1024]{1,0:T(8,128)(2,1)S(1)}, u32[]{:S(2)}, u32[]{:S(2)}) collective-permute-start(bf16[64,1024]{1,0:T(8,128)(2,1)} %chol.1), channel_id=1, source_target_pairs={{0,8},{2,10},{4,12},{6,14},{8,0},{10,2},{12,4},{14,6},{16,24},{18,... | collective-permute-start | bytes 393224 | tf_op jit(solution)/shard_map/ppermute | solution.py:34
  7.2 21.6 %collective-permute-start.7 = (bf16[64,1024]{1,0:T(8,128)(2,1)}, bf16[64,1024]{1,0:T(8,128)(2,1)S(1)}, u32[]{:S(2)}, u32[]{:S(2)}) collective-permute-start(bf16[64,1024]{1,0:T(8,128)(2,1)} %chol.1), channel_id=1, source_target_pairs={{0,16},{2,18},{4,20},{6,22},{8,24},{10,26},{12,28},{14,30},{16,0},... | collective-permute-start | bytes 393224 | tf_op jit(solution)/shard_map/ppermute | solution.py:34
  12.8 12.6 %all-to-all-start = ((f32[3,16,128]{2,0,1:T(4,128)}), f32[3,16,128]{2,0,1:T(4,128)S(1)}, u32[]{:S(2)}, u32[]{:S(2)}) async-start(f32[3,16,128]{2,0,1:T(4,128)} %pad_maximum_fusion), calls=%async_computation | async-start | bytes 65536 | tf_op jit(solution)/shard_map/all_to_all | solution.py:237
  25.5 7.7 %collective-permute-start.8 = (bf16[64,1024]{1,0:T(8,128)(2,1)}, bf16[64,1024]{1,0:T(8,128)(2,1)S(1)}, u32[]{:S(2)}, u32[]{:S(2)}) collective-permute-start(bf16[64,1024]{1,0:T(8,128)(2,1)} %chol.1), channel_id=1, source_target_pairs={{0,24},{2,26},{4,28},{6,30},{8,16},{10,18},{12,20},{14,22},{16,8},... | collective-permute-start | bytes 393224 | tf_op jit(solution)/shard_map/ppermute | solution.py:34
  28.1 14.9 %collective-permute-start.3 = (bf16[256,1024]{1,0:T(8,128)(2,1)S(1)}, bf16[256,1024]{1,0:T(8,128)(2,1)S(1)}, u32[]{:S(2)}, u32[]{:S(2)}) collective-permute-start(bf16[256,1024]{1,0:T(8,128)(2,1)S(1)} %constant_dynamic-update-slice_fusion.g0), channel_id=1, source_target_pairs={{0,4},{2,6},{4,0},{6,2},{8,12},{10,14},{12,8},{14,10},{16,20},{18,... | collective-permute-start | bytes 1572872 | tf_op jit(solution)/shard_map/ppermute | solution.py:34
  28.8 24.4 %collective-permute-start.4 = (bf16[256,1024]{1,0:T(8,128)(2,1)S(1)}, bf16[256,1024]{1,0:T(8,128)(2,1)S(1)}, u32[]{:S(2)}, u32[]{:S(2)}) collective-permute-start(bf16[256,1024]{1,0:T(8,128)(2,1)S(1)} %constant_dynamic-update-slice_fusion.g0), channel_id=1, source_target_pairs={{0,2},{2,0},{4,6},{6,4},{8,10},{10,8},{12,14},{14,12},{16,18},{18,... | collective-permute-start | bytes 1572872 | tf_op jit(solution)/shard_map/ppermute | solution.py:34
  33.2 19.9 %collective-permute-start.9 = (bf16[256,1024]{1,0:T(8,128)(2,1)S(1)}, bf16[256,1024]{1,0:T(8,128)(2,1)S(1)}, u32[]{:S(2)}, u32[]{:S(2)}) collective-permute-start(bf16[256,1024]{1,0:T(8,128)(2,1)S(1)} %constant_dynamic-update-slice_fusion.4.g0), channel_id=1, source_target_pairs={{0,4},{2,6},{4,0},{6,2},{8,12},{10,14},{12,8},{14,10},{16,20},{18,... | collective-permute-start | bytes 1572872 | tf_op jit(solution)/shard_map/ppermute | solution.py:34
  43.0 10.2 %collective-permute-start.5 = (bf16[256,1024]{1,0:T(8,128)(2,1)S(1)}, bf16[256,1024]{1,0:T(8,128)(2,1)S(1)}, u32[]{:S(2)}, u32[]{:S(2)}) collective-permute-start(bf16[256,1024]{1,0:T(8,128)(2,1)S(1)} %collective-permute-done.3.g1), channel_id=1, source_target_pairs={{0,2},{2,0},{4,6},{6,4},{8,10},{10,8},{12,14},{14,12},{16,18},{18,... | collective-permute-start | bytes 1572872 | tf_op jit(solution)/shard_map/ppermute | solution.py:34
  43.0 10.2 %copy-start.2 = (bf16[8,1024]{1,0:T(8,128)(2,1)S(1)}, bf16[8,1024]{1,0:T(8,128)(2,1)}, u32[]{:S(2)}) copy-start(bf16[8,1024]{1,0:T(8,128)(2,1)} %means.3) | copy-start | bytes 49156
  51.2 11.6 %collective-permute-start.10 = (bf16[256,1024]{1,0:T(8,128)(2,1)S(1)}, bf16[256,1024]{1,0:T(8,128)(2,1)S(1)}, u32[]{:S(2)}, u32[]{:S(2)}) collective-permute-start(bf16[256,1024]{1,0:T(8,128)(2,1)S(1)} %constant_dynamic-update-slice_fusion.4.g0), channel_id=1, source_target_pairs={{0,2},{2,0},{4,6},{6,4},{8,10},{10,8},{12,14},{14,12},{16,18},{18,... | collective-permute-start | bytes 1572872 | tf_op jit(solution)/shard_map/ppermute | solution.py:34
  53.1 9.8 %collective-permute-start.11 = (bf16[256,1024]{1,0:T(8,128)(2,1)S(1)}, bf16[256,1024]{1,0:T(8,128)(2,1)S(1)}, u32[]{:S(2)}, u32[]{:S(2)}) collective-permute-start(bf16[256,1024]{1,0:T(8,128)(2,1)S(1)} %collective-permute-done.9.g1), channel_id=1, source_target_pairs={{0,2},{2,0},{4,6},{6,4},{8,10},{10,8},{12,14},{14,12},{16,18},{18,... | collective-permute-start | bytes 1572872 | tf_op jit(solution)/shard_map/ppermute | solution.py:34
  70.7 4.7 %collective-permute-start.12 = (f32[8,2304]{1,0:T(8,128)S(1)}, f32[8,2304]{1,0:T(8,128)S(1)}, u32[]{:S(2)}, u32[]{:S(2)}) collective-permute-start(f32[8,2304]{1,0:T(8,128)S(1)} %get-tuple-element.20.own), channel_id=1, source_target_pairs={{0,1},{1,0},{2,3},{3,2},{4,5},{5,4},{6,7},{7,6},{8,9},{9,8},{10,11... | collective-permute-start | bytes 221192 | tf_op jit(solution)/shard_map/ppermute | solution.py:34
  75.5 34.0 %copy-start.1 = (bf16[64,1024]{1,0:T(8,128)(2,1)S(1)}, bf16[64,1024]{1,0:T(8,128)(2,1)}, u32[]{:S(2)}) copy-start(bf16[64,1024]{1,0:T(8,128)(2,1)} %chol.1) | copy-start | bytes 393220
  81.5 2.2 %collective-permute-start.13 = (bf16[2,64,2816]{2,1,0:T(8,128)(2,1)S(1)}, bf16[2,64,2816]{2,1,0:T(8,128)(2,1)S(1)}, u32[]{:S(2)}, u32[]{:S(2)}) collective-permute-start(bf16[2,64,2816]{2,1,0:T(8,128)(2,1)S(1)} %get-tuple-element.24), channel_id=1, source_target_pairs={{0,2},{2,0},{4,6},{6,4},{8,10},{10,8},{12,14},{14,12},{16,18},{18,... | collective-permute-start | bytes 2162696 | tf_op jit(solution)/shard_map/ppermute | solution.py:34
  83.8 10.5 %collective-permute-start.14 = (bf16[64,2816]{1,0:T(8,128)(2,1)S(1)}, bf16[64,2816]{1,0:T(8,128)(2,1)S(1)}, u32[]{:S(2)}, u32[]{:S(2)}) collective-permute-start(bf16[64,2816]{1,0:T(8,128)(2,1)S(1)} %get-tuple-element.26), channel_id=1, source_target_pairs={{0,4},{2,6},{4,0},{6,2},{8,12},{10,14},{12,8},{14,10},{16,20},{18,... | collective-permute-start | bytes 1081352 | tf_op jit(solution)/shard_map/ppermute | solution.py:34
  94.5 7.6 %collective-permute-start.15 = (bf16[64,1280]{1,0:T(8,128)(2,1)S(1)}, bf16[64,1280]{1,0:T(8,128)(2,1)S(1)}, u32[]{:S(2)}, u32[]{:S(2)}) collective-permute-start(bf16[64,1280]{1,0:T(8,128)(2,1)S(1)} %get-tuple-element.28), channel_id=1, source_target_pairs={{0,8},{2,10},{4,12},{6,14},{8,0},{10,2},{12,4},{14,6},{16,24},{18,... | collective-permute-start | bytes 491528 | tf_op jit(solution)/shard_map/ppermute | solution.py:34
  94.6 14.9 %collective-permute-start.16 = (bf16[64,1280]{1,0:T(8,128)(2,1)S(1)}, bf16[64,1280]{1,0:T(8,128)(2,1)S(1)}, u32[]{:S(2)}, u32[]{:S(2)}) collective-permute-start(bf16[64,1280]{1,0:T(8,128)(2,1)S(1)} %get-tuple-element.29), channel_id=1, source_target_pairs={{0,16},{2,18},{4,20},{6,22},{8,24},{10,26},{12,28},{14,30},{16,0},... | collective-permute-start | bytes 491528 | tf_op jit(solution)/shard_map/ppermute | solution.py:34
  96.4 13.0 %collective-permute-start.17 = (bf16[64,1280]{1,0:T(8,128)(2,1)S(1)}, bf16[64,1280]{1,0:T(8,128)(2,1)S(1)}, u32[]{:S(2)}, u32[]{:S(2)}) collective-permute-start(bf16[64,1280]{1,0:T(8,128)(2,1)S(1)} %get-tuple-element.30), channel_id=1, source_target_pairs={{0,24},{2,26},{4,28},{6,30},{8,16},{10,18},{12,20},{14,22},{16,8},... | collective-permute-start | bytes 491528 | tf_op jit(solution)/shard_map/ppermute | solution.py:34

commit v2 on v1

v2 whole, which is shorter than its diff:
```python
import functools

import jax
import jax.numpy as jnp
from jax import lax
from jax.experimental import pallas as pl
from jax.experimental.pallas import tpu as pltpu
from jax.sharding import PartitionSpec as P

C = 8
NB = 6
ROWS_DEV = 2048
SLOT = 128
COL = 1024
SQRT_HALF_LOG2E = 0.8493218002880191

precise = lax.Precision.HIGHEST
f32 = jnp.float32
bf16 = jnp.bfloat16
SMEM = pl.BlockSpec(memory_space=pltpu.SMEM)
VMEM = pl.BlockSpec(memory_space=pltpu.VMEM)
HBM = pl.BlockSpec(memory_space=pltpu.HBM)
SMALL = pltpu.CompilerParams(vmem_limit_bytes=4 * 1024 * 1024)


def dot(a, b):
    return jnp.dot(a, b, preferred_element_type=f32)


def dot_nt(a, b):
    return lax.dot_general(a, b, (((1,), (1,)), ((), ())), preferred_element_type=f32)


def swap(value, axis, bit):
    size = lax.axis_size(axis)
    return lax.ppermute(value, axis, [(i, i ^ bit) for i in range(size)])


def after(value, *earlier):
    return lax.optimization_barrier((value,) + earlier)[0]


def join_kernel(*refs):
    out = refs[-1]
    top = 0
    for ref in refs[:-1]:
        out[top : top + ref.shape[0], :] = ref[...]
        top += ref.shape[0]


def join(*pieces):
    rows = sum(piece.shape[0] for piece in pieces)
    return pl.pallas_call(
        join_kernel,
        out_shape=jax.ShapeDtypeStruct((rows, pieces[0].shape[1]), pieces[0].dtype),
        in_specs=[VMEM] * len(pieces),
        out_specs=VMEM,
        compiler_params=SMALL,
        name="join",
    )(*pieces)


def phases_of(nz):
    offsets = range(2, 4 * nz, 2)
    most = max(offset.bit_count() for offset in offsets)
    return [[o for o in reversed(offsets) if o.bit_count() == p] for p in range(1, most + 1)]


def store_pieces(groups, whole, nz, at):
    me = lax.axis_index("obs")
    rows = whole.shape[0] // (4 * nz)
    phases = phases_of(nz)
    phases[0] = [0] + phases[0]
    for g, group in enumerate(groups):
        for s, offset in enumerate(phases[g // 2]):
            piece = me ^ offset ^ (g % 2)
            top = (2 * s + at) * rows
            whole[pl.ds(pl.multiple_of(rows * piece, rows), rows), :] = group[top : top + rows, :]


def stack_kernel(coords_in, codes_in, out, coords, codes, sems):
    fetch((coords_in, codes_in), (coords, codes), sems)
    out[0:2, :] = coords[...]
    out[2:3, :] = codes[...].astype(f32)


def fetch(sources, targets, sems):
    copies = [pltpu.make_async_copy(a, b, sems.at[i]) for i, (a, b) in enumerate(zip(sources, targets))]
    for copy in copies:
        copy.start()
    for copy in copies:
        copy.wait()


def kernel_rows_kernel(
    arrived, points_in, bands_in, mix_in, lengthscales, kt, labels, self_cov, points, point_bands, band_mix, sems
):
    fetch((points_in, bands_in, mix_in), (points, point_bands, band_mix), sems)
    codes = arrived[2:3, :]
    label = jnp.floor((codes + 0.5) * (1.0 / NB))
    labels[...] = label.astype(jnp.int32)
    bands = (codes - NB * label).astype(jnp.int32)
    kinds = lax.broadcasted_iota(jnp.int32, (C, ROWS_DEV), 0)
    hot = (kinds == bands).astype(f32)
    eye = lax.broadcasted_iota(jnp.int32, (C, C), 0) == lax.broadcasted_iota(jnp.int32, (C, C), 1)
    factor = jnp.concatenate([band_mix[...], jnp.zeros((NB, C - NB), f32)], axis=1)
    factor = jnp.concatenate([factor, jnp.zeros((C - NB, C), f32)], axis=0)
    mix = eye.astype(f32) + lax.dot_general(
        factor, factor, (((1,), (1,)), ((), ())), precision=precise, preferred_element_type=f32
    )
    scales = [SQRT_HALF_LOG2E / lengthscales[i] for i in range(2)]
    diagonal = jnp.sum(jnp.where(eye, mix, 0.0), axis=1, keepdims=True)
    self_cov[...] = jnp.sum(hot * diagonal, axis=0, keepdims=True)
    hots = jnp.concatenate([hot, hot, hot, jnp.zeros_like(hot)], axis=0).astype(bf16)
    times = arrived[0:1, :] * scales[0]
    waves = arrived[1:2, :] * scales[1]
    width = points.shape[1]
    columns = jnp.concatenate(
        [points[...], point_bands[...].astype(f32), jnp.zeros((C - 3, width), f32)], axis=0
    ).T
    step = 128
    for j in range(0, width, step):
        here = columns[j : j + step, :]
        picked = jnp.zeros((step, C), f32)
        for kind in range(NB):
            picked = jnp.where(here[:, 2:3] == float(kind), mix[kind : kind + 1, :], picked)
        high = picked.astype(bf16).astype(f32)
        middle = (picked - high).astype(bf16).astype(f32)
        low = picked - high - middle
        split = jnp.concatenate([high, middle, low, jnp.zeros_like(low)], axis=1).astype(bf16)
        mixing = dot(split, hots)
        delta_t = times - here[:, 0:1] * scales[0]
        delta_w = waves - here[:, 1:2] * scales[1]
        value = jnp.exp2(-(delta_t * delta_t + delta_w * delta_w)) * mixing
        kt[j : j + step, :] = value.astype(bf16)


def whiten_kernel(nz, kt, means, *rest):
    groups, (ab, stats, whole, turned) = rest[:-4], rest[-4:]
    width = whole.shape[0]
    store_pieces(groups, whole, nz, 0)
    for j in range(0, width, 256):
        turned[:, j : j + 256] = whole[j : j + 256, :].T

    @pl.loop(0, ROWS_DEV // COL)
    def _(step):
        columns = pl.ds(pl.multiple_of(step * COL, COL), COL)
        square = jnp.zeros((1, COL), f32)
        for k in range(0, width, 256):
            part = dot(turned[k : k + 256, :], kt[:, columns])
            square = square + jnp.sum(part * part, axis=0, keepdims=True)
            ab[k : k + 256, columns] = part.astype(bf16)
        stats[0:C, columns] = dot(means[...], ab[:, columns])
        stats[C : 2 * C, columns] = jnp.broadcast_to(-square, (C, COL))


def covary_kernel(nz, ab, stats, *rest):
    groups, (bt, sums, whole, turned) = rest[:-4], rest[-4:]
    width = whole.shape[0]
    store_pieces(groups, whole, nz, 1)
    for j in range(0, width, 256):
        turned[:, j : j + 256] = whole[j : j + 256, :].T

    @pl.loop(0, ROWS_DEV // COL)
    def _(step):
        columns = pl.ds(pl.multiple_of(step * COL, COL), COL)
        square = stats[C : C + 1, columns]
        for l in range(0, width, 256):
            part = dot(turned[l : l + 256, l:], ab[l:, columns])
            square = square + jnp.sum(part * part, axis=0, keepdims=True)
            bt[l : l + 256, columns] = part.astype(bf16)
        sums[:, columns] = stats[0:C, columns]
        piece = ROWS_DEV // C
        for i in range(COL // piece):
            sums[pl.ds((COL // piece) * step + i, 1), ROWS_DEV:] = square[:, piece * i : piece * (i + 1)]


def slope_kernel(nz, own, other, scales, labels, self_cov, ab, bt, chances_out, keep, send, heavy):
    core = lax.axis_index("obs") % 2
    block = ab.shape[0] // nz
    quarter = block // 4
    groups = quarter // 16
    total = own[...] + other[...]
    variance = jnp.concatenate([total[i : i + 1, ROWS_DEV:] for i in range(C)], axis=1) + self_cov[...]
    classes = lax.broadcasted_iota(jnp.int32, (C, 1), 0)
    scale = jnp.zeros((C, 1), f32)
    for i in range(C):
        scale = jnp.where(classes == i, scales[i], scale)
    logits = total[:, :ROWS_DEV] + 0.5 * scale * variance
    weights = jnp.exp(logits)
    chances = weights / jnp.sum(weights, axis=0, keepdims=True)
    chances_out[...] = chances
    twice = -jnp.sum(chances * scale, axis=0, keepdims=True)
    slope = ((labels[...] == classes).astype(f32) - chances).astype(bf16)
    extra = block * nz * (nz + 1) // 2
    for z in range(nz):
        rows = slice(block * z, block * (z + 1))
        heavy[rows, :] = (bt[rows, :].astype(f32) * twice).astype(bf16)
        wide = block * (z + 1)
        start = block * z * (z + 1) // 2
        term = dot_nt(ab[rows, :], heavy[:wide, :])
        for x in range(2):
            first = term[2 * quarter * x : 2 * quarter * x + quarter, :]
            second = term[2 * quarter * x + quarter : 2 * quarter * (x + 1), :]
            keep[x, :, start : start + wide] = jnp.where(core == 0, first, second)
            send[x, :, start : start + wide] = jnp.where(core == 0, second, first).astype(bf16)
        mean = dot_nt(slope, ab[rows, :])
        high = mean.astype(bf16).astype(f32)
        both = jnp.concatenate([high, mean - high], axis=0).astype(bf16)
        held = jnp.concatenate([mean, jnp.zeros_like(mean)], axis=0)
        top = 16 * (z % groups)
        left = extra + block * (z // groups)
        for x in range(2):
            keep[x, top : top + 16, left : left + block] = held
            send[x, top : top + 16, left : left + block] = both


def add_extra(kept, arrived, groups):
    parts = []
    for g in range(groups):
        top = kept[16 * g : 16 * g + 8] + arrived[16 * g : 16 * g + 8] + arrived[16 * g + 8 : 16 * g + 16]
        parts.append(top)
    return parts


def fold_extra(parts):
    held, sent = [], []
    for part in parts:
        high = part.astype(bf16).astype(f32)
        held += [part, jnp.zeros_like(part)]
        sent += [high, part - high]
    return jnp.concatenate(held, axis=0), jnp.concatenate(sent, axis=0).astype(bf16)


def pair_kernel(body_width, keep, arrived, kept, send):
    x = (lax.axis_index("obs") // 2) % 2
    groups = keep.shape[1] // 16
    send[:, :body_width] = (
        keep[1 - x, :, :body_width] + arrived[1 - x, :, :body_width].astype(f32)
    ).astype(bf16)
    kept[:, :body_width] = keep[x, :, :body_width] + arrived[x, :, :body_width].astype(f32)
    parts = add_extra(
        keep[0, :, body_width:], arrived[0, :, body_width:].astype(f32), groups
    )
    held, sent = fold_extra(parts)
    kept[:, body_width:] = held
    send[:, body_width:] = sent


def chip_kernel(nz, body_width, kept, arrived, mine, *sends):
    z = lax.axis_index("obs") // 4
    groups = kept.shape[0] // 16
    width = mine.shape[1] - (kept.shape[1] - body_width)
    block = width // nz
    parts = add_extra(kept[:, body_width:], arrived[:, body_width:].astype(f32), groups)
    held, sent = fold_extra(parts)
    for k in range(nz):
        target = z ^ k
        start = pl.multiple_of(block * (target * (target + 1) // 2), block)
        value = kept[:, pl.ds(start, width)] + arrived[:, pl.ds(start, width)].astype(f32)
        if k == 0:
            mine[:, :width] = value
            mine[:, width:] = held
        else:
            sends[k - 1][:, :width] = value.astype(bf16)
            sends[k - 1][:, width:] = sent


def finish_kernel(nz, mine, chol, means, *rest):
    arrived, grad_chol, grad_mean = rest[: nz - 1], rest[nz - 1], rest[nz]
    rows, width = chol.shape
    groups = rows // 16
    total = mine[:, :width]
    for piece in arrived:
        total = total + piece[:, :width].astype(f32)
    row_ids = lax.axis_index("obs") * rows + lax.broadcasted_iota(jnp.int32, (rows, width), 0)
    column_ids = lax.broadcasted_iota(jnp.int32, (rows, width), 1)
    own = chol[...].astype(f32)
    on_diag = column_ids == row_ids
    diagonal = jnp.sum(jnp.where(on_diag, own, 0.0), axis=1, keepdims=True)
    grad_chol[...] = (
        jnp.where(column_ids <= row_ids, total, 0.0) - own + jnp.where(on_diag, 1.0 / diagonal, 0.0)
    )
    extra = mine[:, width:]
    parts = [extra[16 * g : 16 * g + 8] for g in range(groups)]
    for piece in arrived:
        values = piece[:, width:].astype(f32)
        parts = [
            part + values[16 * g : 16 * g + 8] + values[16 * g + 8 : 16 * g + 16]
            for g, part in enumerate(parts)
        ]
    block = width // nz
    for z in range(nz):
        part = parts[z % groups][:, block * (z // groups) : block * (z // groups + 1)]
        here = slice(block * z, block * (z + 1))
        grad_mean[:, here] = part - means[:, here].astype(f32)


def route(obs_coords, obs_codes, route_plan):
    devices = lax.axis_size("obs")
    stacked = pl.pallas_call(
        stack_kernel,
        out_shape=jax.ShapeDtypeStruct((3, obs_coords.shape[1]), f32),
        in_specs=[HBM, HBM],
        out_specs=VMEM,
        scratch_shapes=[
            pltpu.VMEM(obs_coords.shape, f32),
            pltpu.VMEM((1, obs_coords.shape[1]), jnp.int32),
            pltpu.SemaphoreType.DMA((2,)),
        ],
        compiler_params=SMALL,
        name="stack",
    )(obs_coords, obs_codes[None, :])
    if devices * SLOT == ROWS_DEV:
        return lax.all_to_all(stacked, "obs", split_axis=1, concat_axis=1, tiled=True)
    me = lax.axis_index("obs")
    blocks = route_plan * SLOT
    send_start = jnp.cumsum(blocks, axis=1) - blocks
    recv_start = jnp.cumsum(blocks, axis=0) - blocks
    my_sends = lax.dynamic_index_in_dim(send_start, me, 0, keepdims=False)
    my_recvs = lax.dynamic_index_in_dim(recv_start, me, 1, keepdims=False)
    padded = jnp.concatenate([stacked, jnp.zeros((3, SLOT), f32)], axis=1)
    outgoing = jax.vmap(lambda offset: lax.dynamic_slice_in_dim(padded, offset, SLOT, 1))(my_sends)
    incoming = lax.all_to_all(outgoing, "obs", split_axis=0, concat_axis=0, tiled=True)
    position = jnp.arange(ROWS_DEV, dtype=jnp.int32)
    sources = jnp.arange(devices, dtype=jnp.int32)
    source = jnp.sum((my_recvs[None, :] <= position[:, None]).astype(jnp.int32), axis=1) - 1
    pick = (source[:, None] == sources[None, :]).astype(jnp.int32)
    begin_row = jnp.sum(pick * my_recvs[None, :], axis=1)
    return incoming[source, :, position - begin_row].T


def body(
    obs_coords,
    obs_codes,
    route_plan,
    inducing_coords,
    inducing_bands,
    band_mix,
    lengthscales,
    class_scales,
    prior_factor,
    variational_chol,
    variational_mean,
):
    n = lax.axis_size("obs")
    nz = n // 4
    rows, width = variational_chol.shape
    body_width = width // nz * (nz * (nz + 1) // 2)
    extra_width = 16 * width // rows
    packed = body_width + extra_width

    phases = phases_of(nz)
    pieces = {0: join(prior_factor, variational_chol)}
    pieces.update({offset: swap(pieces[0], "obs", offset) for offset in phases[0]})
    arrived = route(obs_coords, obs_codes, route_plan)
    pieces, arrived = lax.optimization_barrier((pieces, arrived))
    own_side = join(*[pieces[offset] for offset in [0] + phases[0]])
    groups = [own_side, swap(own_side, "obs", 1)]

    big = pltpu.CompilerParams(vmem_limit_bytes=16 * 1024 * 1024)
    kt, labels, self_cov = pl.pallas_call(
        kernel_rows_kernel,
        out_shape=(
            jax.ShapeDtypeStruct((width, ROWS_DEV), bf16),
            jax.ShapeDtypeStruct((1, ROWS_DEV), jnp.int32),
            jax.ShapeDtypeStruct((1, ROWS_DEV), f32),
        ),
        in_specs=[VMEM, HBM, HBM, HBM, SMEM],
        out_specs=(VMEM, VMEM, VMEM),
        scratch_shapes=[
            pltpu.VMEM((2, width), f32),
            pltpu.VMEM((1, width), jnp.int32),
            pltpu.VMEM((NB, NB), f32),
            pltpu.SemaphoreType.DMA((3,)),
        ],
        compiler_params=big,
        cost_estimate=pl.CostEstimate(
            flops=20 * width * ROWS_DEV, bytes_accessed=4 * 1024 * 1024, transcendentals=width * ROWS_DEV
        ),
        name="kernel_rows",
    )(after(arrived, own_side), inducing_coords, inducing_bands[None, :], band_mix, lengthscales)

    for phase in phases[1:]:
        for offset in phase:
            low = offset & -offset
            pieces[offset] = swap(pieces[offset ^ low], "obs", low)
        if phase is phases[1]:
            pieces, kt = lax.optimization_barrier((pieces, kt))
        group = join(*[pieces[offset] for offset in phase]) if len(phase) > 1 else pieces[phase[0]]
        groups += [group, swap(group, "obs", 1)]

    whole = [pltpu.VMEM((width, width), bf16), pltpu.VMEM((width, width), bf16)]
    ab, part_stats = pl.pallas_call(
        functools.partial(whiten_kernel, nz),
        out_shape=(
            jax.ShapeDtypeStruct((width, ROWS_DEV), bf16),
            jax.ShapeDtypeStruct((2 * C, ROWS_DEV), f32),
        ),
        in_specs=[VMEM] * (2 + len(groups)),
        out_specs=(VMEM, VMEM),
        scratch_shapes=whole,
        compiler_params=big,
        cost_estimate=pl.CostEstimate(
            flops=2 * width * width * ROWS_DEV, bytes_accessed=10 * 1024 * 1024, transcendentals=0
        ),
        name="whiten",
    )(kt, variational_mean, *groups)
    bt, sums = pl.pallas_call(
        functools.partial(covary_kernel, nz),
        out_shape=(
            jax.ShapeDtypeStruct((width, ROWS_DEV), bf16),
            jax.ShapeDtypeStruct((C, ROWS_DEV + ROWS_DEV // C), f32),
        ),
        in_specs=[VMEM] * (2 + len(groups)),
        out_specs=(VMEM, VMEM),
        scratch_shapes=whole,
        compiler_params=big,
        cost_estimate=pl.CostEstimate(
            flops=width * width * ROWS_DEV, bytes_accessed=10 * 1024 * 1024, transcendentals=0
        ),
        name="covary",
    )(ab, part_stats, *groups)

    other = swap(sums, "ind", 1)
    bit = 2
    while bit < lax.axis_size("ind"):
        sums = sums + other
        other = swap(sums, "ind", bit)
        bit *= 2

    chances, keep, send = pl.pallas_call(
        functools.partial(slope_kernel, nz),
        out_shape=(
            jax.ShapeDtypeStruct((C, ROWS_DEV), f32),
            jax.ShapeDtypeStruct((2, rows, packed), f32),
            jax.ShapeDtypeStruct((2, rows, packed), bf16),
        ),
        in_specs=[VMEM, VMEM, SMEM] + [VMEM] * 4,
        out_specs=(VMEM, VMEM, VMEM),
        scratch_shapes=[pltpu.VMEM((width, ROWS_DEV), bf16)],
        compiler_params=big,
        cost_estimate=pl.CostEstimate(
            flops=width * width * ROWS_DEV, bytes_accessed=10 * 1024 * 1024, transcendentals=0
        ),
        name="slopes",
    )(sums, other, class_scales, labels, self_cov, ab, bt)

    kept, send = pl.pallas_call(
        functools.partial(pair_kernel, body_width),
        out_shape=(
            jax.ShapeDtypeStruct((rows, packed), f32),
            jax.ShapeDtypeStruct((rows, packed), bf16),
        ),
        in_specs=[VMEM, VMEM],
        out_specs=(VMEM, VMEM),
        compiler_params=big,
        name="add_pair",
    )(keep, swap(send, "obs", 1))
    piece = (rows, width + extra_width)
    mine, *sends = pl.pallas_call(
        functools.partial(chip_kernel, nz, body_width),
        out_shape=[jax.ShapeDtypeStruct(piece, f32)]
        + [jax.ShapeDtypeStruct(piece, bf16)] * (nz - 1),
        in_specs=[VMEM, VMEM],
        out_specs=[VMEM] * nz,
        compiler_params=big,
        name="add_chip",
    )(kept, swap(send, "obs", 2))
    arrivals = [swap(value, "obs", 4 * (k + 1)) for k, value in enumerate(sends)]
    grad_chol, grad_mean = pl.pallas_call(
        functools.partial(finish_kernel, nz),
        out_shape=(
            jax.ShapeDtypeStruct((rows, width), f32),
            jax.ShapeDtypeStruct((C, width), f32),
        ),
        in_specs=[VMEM] * (nz + 2),
        out_specs=(VMEM, VMEM),
        compiler_params=big,
        name="finish",
    )(mine, variational_chol, variational_mean, *arrivals)
    return (chances, grad_chol, grad_mean)


def solution(mesh):
    placed = (
        P(None, "obs"),
        P("obs"),
        P(),
        P(None, "ind"),
        P("ind"),
        P(),
        P(),
        P(),
        P(("ind", "obs"), None),
        P(("ind", "obs"), None),
        P(None, "ind"),
    )
    return jax.shard_map(
        body,
        mesh=mesh,
        in_specs=placed,
        out_specs=(P(None, "obs"), P(("ind", "obs"), None), P(None, "ind")),
        check_vma=False,
    )
```

time: 111 us -> 94.5 us (0.85)
  blocking collectives: 0 us -> 9.96 us
  matrix products: 9.47 us -> 0 us
  starting transfers between devices: 24.7 us -> 17.8 us
  waiting for transfers between devices: 42.9 us -> 38.6 us
  Pallas kernels: 24.8 us -> 21 us
  other arithmetic: 2.25 us -> 0 us
    all_to_all x0 -> x1, blocking collectives: none -> 9.96 us  [route(): lax.all_to_all(stacked, 'obs', split_axis=1, concat_axis=1, tiled=True)]
    dot_general x3 -> x0, matrix products: 9.47 us -> none  [the longest x1 8.2 us: body(): jnp.dot(jnp.dot(col_hot, coupling, precision=precise), row_hot, precision...]
    unnamed x12 -> x22, local copies, waits for them, and re-layouts: 1.89 us -> 5.95 us
    pallas_call x3 -> x8, Pallas kernels: 23.6 us -> 19.8 us  [the longest x1 6.14 us: body(): pl.pallas_call(functools.partial(whiten_kernel, nz), out_shape=(jax.Shape...]
    all_to_all x1 -> x0, starting transfers between devices: 3.5 us -> none  [route(): lax.all_to_all(stacked, 'obs', split_axis=1, concat_axis=1, tiled=True)]
    ppermute x18 -> x16, starting transfers between devices: 21.2 us -> 17.8 us  [swap(): return lax.ppermute(value, axis, [(i, i ^ bit) for i in range(size)])]
    all_to_all x1 -> x0, waiting for transfers between devices: 2.48 us -> none  [route(): lax.all_to_all(stacked, 'obs', split_axis=1, concat_axis=1, tiled=True)]
    slice x3 -> x0, local copies, waits for them, and re-layouts: 2.12 us -> none  [the longest x1 1.31 us: body(): lengthscales[0]]
  transfers between devices with their start and end apart: 19 -> 16, of which waited for: 9 -> 8; matrix products, arithmetic and copies ran while one was open for 16% -> 0% of each run, Pallas kernels for 9% -> 5%
where the time goes in v2:
time: 94.5 us; the launch traced here: 94 us
  waiting for transfers between devices  38.6 us (41%)
  Pallas kernels  21 us (22%)
  starting transfers between devices  17.8 us (19%)
  blocking collectives  9.96 us (11%)
  local copies, waits for them, and re-layouts  5.95 us (6%)
    ppermute x16, waiting for transfers between devices, swap(): return lax.ppermute(value, axis, [(i, i ^ bit) for i in range(size)])  38.6 us
    ppermute x16, starting transfers between devices, swap(): return lax.ppermute(value, axis, [(i, i ^ bit) for i in range(size)])  17.8 us
    all_to_all x1, blocking collectives, route(): lax.all_to_all(stacked, 'obs', split_axis=1, concat_axis=1, tiled=True)  9.96 us
    pallas_call x1, Pallas kernels, body(): pl.pallas_call(functools.partial(whiten_kernel, nz), out_shape=(jax.Shape...  6.14 us
    unnamed x22, local copies, waits for them, and re-layouts  5.95 us
    pallas_call x1, Pallas kernels, body(): pl.pallas_call(kernel_rows_kernel, out_shape=(jax.ShapeDtypeStruct((width...  4.76 us
    pallas_call x1, Pallas kernels, body(): pl.pallas_call(functools.partial(slope_kernel, nz), out_shape=(jax.ShapeD...  4.59 us
    pallas_call x1, Pallas kernels, body(): pl.pallas_call(functools.partial(covary_kernel, nz), out_shape=(jax.Shape...  4.11 us
  transfers between devices with their start and end apart: 16, of which 8 were waited for; matrix products, arithmetic and copies ran while one was open for 0% of the time, Pallas kernels for 5%

profile of v2, /device:TPU:0, one launch (start us, length us, event | category | flops | bytes accessed | tf_op | source)
XLA Modules:
  0.0 94.0 jit_solution(14548134184393794775)
XLA Ops:
  0.6 0.0 copy-start
  0.6 0.9 copy-done
  1.5 0.0 copy-start.2
  1.5 0.9 copy-done.2
  2.4 0.0 copy-start.3
  2.5 4.1 %collective-permute-start.2 = (bf16[128,1024]{1,0:T(8,128)(2,1)S(1)}, bf16[128,1024]{1,0:T(8,128)(2,1)S(1)}, u32[]{:S(2)}, u32[]{:S(2)}) collective-permute-start(bf16[128,1024]{1,0:T(8,128)(2,1)S(1)} %join.3.refs_0_), channel_id=1, source_target_pairs={{0,16},{2,18},{4,20},{6,22},{8,24},{10,26},{12,28},{14,30},{16,0},... | collective-permute-start | bytes 786440 | tf_op jit(solution)/shard_map/ppermute | solution.py:36
  6.6 1.6 %collective-permute-start.1 = (bf16[128,1024]{1,0:T(8,128)(2,1)S(1)}, bf16[128,1024]{1,0:T(8,128)(2,1)S(1)}, u32[]{:S(2)}, u32[]{:S(2)}) collective-permute-start(bf16[128,1024]{1,0:T(8,128)(2,1)S(1)} %join.3.refs_0_), channel_id=1, source_target_pairs={{0,8},{2,10},{4,12},{6,14},{8,0},{10,2},{12,4},{14,6},{16,24},{18,... | collective-permute-start | bytes 786440 | tf_op jit(solution)/shard_map/ppermute | solution.py:36
  8.1 1.5 %collective-permute-start = (bf16[128,1024]{1,0:T(8,128)(2,1)S(1)}, bf16[128,1024]{1,0:T(8,128)(2,1)S(1)}, u32[]{:S(2)}, u32[]{:S(2)}) collective-permute-start(bf16[128,1024]{1,0:T(8,128)(2,1)S(1)} %join.3.refs_0_), channel_id=1, source_target_pairs={{0,4},{2,6},{4,0},{6,2},{8,12},{10,14},{12,8},{14,10},{16,20},{18,... | collective-permute-start | bytes 786440 | tf_op jit(solution)/shard_map/ppermute | solution.py:36
  9.6 0.0 copy-start.4
  9.6 0.7 copy-done.4
  10.4 0.0 copy-start.5
  10.4 0.7 copy-done.5
  11.1 10.0 %all_to_all.12 = f32[3,16,128]{2,0,1:T(4,128)S(1)} all-to-all(f32[3,16,128]{2,0,1:T(4,128)S(1)} %bitcast.4), channel_id=1, replica_groups=mesh['obs'=16,'ind'=2] {'obs'}, dimensions={1} | all-to-all | bytes 49152 | tf_op jit(solution)/shard_map/all_to_all | solution.py:315
  21.1 0.0 collective-permute-done.2.refs_1_
  21.1 0.0 collective-permute-done.1.refs_2_
  21.1 0.0 collective-permute-done.refs_3_
  21.1 0.4 collective-permute-start.3
  21.5 0.7 collective-permute-start.5
  22.1 1.7 %collective-permute-start.4 = (bf16[128,1024]{1,0:T(8,128)(2,1)S(1)}, bf16[128,1024]{1,0:T(8,128)(2,1)S(1)}, u32[]{:S(2)}, u32[]{:S(2)}) collective-permute-start(bf16[128,1024]{1,0:T(8,128)(2,1)S(1)} %collective-permute-done.2.refs_1_), channel_id=1, source_target_pairs={{0,4},{2,6},{4,0},{6,2},{8,12},{10,14},{12,8},{14,10},{16,20},{18,... | collective-permute-start | bytes 786440 | tf_op jit(solution)/shard_map/ppermute | solution.py:36
  23.8 0.1 join.4.rest_0_
  23.9 0.1 collective-permute-start.6
  24.0 0.0 copy-start.7
  24.0 0.7 copy-done.7
  24.7 0.0 copy-start.8
  24.7 0.7 copy-done.8
  25.4 0.0 copy-start.9
  25.4 0.7 copy-done.9
  26.1 0.0 copy-start.10
  26.1 0.7 copy-done.10
  26.7 4.8 %kernel_rows.1 = (bf16[1024,2048]{1,0:T(8,128)(2,1)S(1)}, s32[1,2048]{1,0:T(1,128)S(1)}, f32[1,2048]{1,0:T(1,128)S(1)}) custom-call(f32[3,2048]{1,0:T(4,128)S(1)} %bitcast.5, f32[2,1024]{1,0:T(2,128)S(1)} %copy-done.7, s32[1,1024]{1,0:T(1,128)S(1)} %bitcast.7, f32[6,6]{1,0:T(8,128)S(1)} %copy-done.9, f32[2]{0:T(128)S(1)} %copy-done.10), custom_call_target="tpu_custom_call" | custom-call | flops 41943040 | bytes 4194304 | tf_op jit(solution)/shard_map/kernel_rows/pallas_call | solution.py:362
  31.5 0.0 collective-permute-done.3.refs_2_
  31.5 0.0 collective-permute-done.5.refs_0_
  31.5 3.1 %collective-permute-done.4.refs_1_ = bf16[128,1024]{1,0:T(8,128)(2,1)S(1)} collective-permute-done((bf16[128,1024]{1,0:T(8,128)(2,1)S(1)}, bf16[128,1024]{1,0:T(8,128)(2,1)S(1)}, u32[]{:S(2)}, u32[]{:S(2)}) %collective-permute-start.4) | collective-permute-done | bytes 262176 | tf_op jit(solution)/shard_map/ppermute | solution.py:36
  34.6 0.1 join.5.rest_2_
  34.7 0.1 collective-permute-start.7
  34.8 0.8 collective-permute-start.8
  35.6 7.9 %collective-permute-done.8.rest_4_ = bf16[128,1024]{1,0:T(8,128)(2,1)S(1)} collective-permute-done((bf16[128,1024]{1,0:T(8,128)(2,1)S(1)}, bf16[128,1024]{1,0:T(8,128)(2,1)S(1)}, u32[]{:S(2)}, u32[]{:S(2)}) %collective-permute-start.8) | collective-permute-done | bytes 262176 | tf_op jit(solution)/shard_map/ppermute | solution.py:36
  43.5 0.0 collective-permute-start.9
  43.5 1.5 %collective-permute-done.9.rest_5_ = bf16[128,1024]{1,0:T(8,128)(2,1)S(1)} collective-permute-done((bf16[128,1024]{1,0:T(8,128)(2,1)S(1)}, bf16[128,1024]{1,0:T(8,128)(2,1)S(1)}, u32[]{:S(2)}, u32[]{:S(2)}) %collective-permute-start.9) | collective-permute-done | bytes 262176 | tf_op jit(solution)/shard_map/ppermute | solution.py:36
  45.0 0.0 collective-permute-done.6.rest_1_
  45.0 0.0 collective-permute-done.7.rest_3_
  45.0 0.0 copy-done.3
  45.1 6.1 %whiten.1 = (bf16[1024,2048]{1,0:T(8,128)(2,1)S(1)}, f32[16,2048]{1,0:T(8,128)S(1)}) custom-call(bf16[1024,2048]{1,0:T(8,128)(2,1)S(1)} %get-tuple-element.38.kt, bf16[8,1024]{1,0:T(8,128)(2,1)S(1)} %copy-done.3, bf16[512,1024]{1,0:T(8,128)(2,1)S(1)} %join.4.rest_0_, bf16[512,1024]{1,0:T(8,128)(2,1)S(1)} %collective-permute-done.6.rest_1_, ...), custom_call_target="tpu_custom_call" | custom-call | flops 4294967296 | bytes 10485760 | tf_op jit(solution)/shard_map/whiten/pallas_call | solution.py:394
  51.2 0.0 copy-start.6
  51.2 4.1 %covary.1 = (bf16[1024,2048]{1,0:T(8,128)(2,1)S(1)}, f32[8,2304]{1,0:T(8,128)S(1)}) custom-call(bf16[1024,2048]{1,0:T(8,128)(2,1)S(1)} %get-tuple-element.42.ab, f32[16,2048]{1,0:T(8,128)S(1)} %get-tuple-element.43.stats, bf16[512,1024]{1,0:T(8,128)(2,1)S(1)} %join.4.rest_0_, bf16[512,1024]{1,0:T(8,128)(2,1)S(1)} %collective-permute-done.6.rest_1_, ...), custom_call_target="tpu_custom_call" | custom-call | flops 2147483648 | bytes 10485760 | tf_op jit(solution)/shard_map/covary/pallas_call | solution.py:409
  55.3 1.6 %collective-permute-start.10 = (f32[8,2304]{1,0:T(8,128)S(1)}, f32[8,2304]{1,0:T(8,128)S(1)}, u32[]{:S(2)}, u32[]{:S(2)}) collective-permute-start(f32[8,2304]{1,0:T(8,128)S(1)} %get-tuple-element.44.own), channel_id=1, source_target_pairs={{0,1},{1,0},{2,3},{3,2},{4,5},{5,4},{6,7},{7,6},{8,9},{9,8},{10,11... | collective-permute-start | bytes 221192 | tf_op jit(solution)/shard_map/ppermute | solution.py:36
  56.9 2.8 %collective-permute-done.10.other = f32[8,2304]{1,0:T(8,128)S(1)} collective-permute-done((f32[8,2304]{1,0:T(8,128)S(1)}, f32[8,2304]{1,0:T(8,128)S(1)}, u32[]{:S(2)}, u32[]{:S(2)}) %collective-permute-start.10) | collective-permute-done | bytes 73760 | tf_op jit(solution)/shard_map/ppermute | solution.py:36
  59.7 0.0 copy-done.6
  59.7 0.0 copy-start.1
  59.7 4.6 %slopes.1 = (f32[8,2048]{1,0:T(8,128)}, f32[2,64,2816]{2,1,0:T(8,128)S(1)}, bf16[2,64,2816]{2,1,0:T(8,128)(2,1)S(1)}) custom-call(f32[8,2304]{1,0:T(8,128)S(1)} %get-tuple-element.44.own, f32[8,2304]{1,0:T(8,128)S(1)} %collective-permute-done.10.other, f32[8]{0:T(128)S(1)} %copy-done.6, s32[1,2048]{1,0:T(1,128)S(1)} %get-tuple-element.45.labels, ...), custom_call_target="tpu_custom_call" | custom-call | flops 2147483648 | bytes 10485760 | tf_op jit(solution)/shard_map/slopes/pallas_call | solution.py:432
  64.3 0.1 collective-permute-start.11
  64.4 2.2 %collective-permute-done.11.arrived = bf16[2,64,2816]{2,1,0:T(8,128)(2,1)S(1)} collective-permute-done((bf16[2,64,2816]{2,1,0:T(8,128)(2,1)S(1)}, bf16[2,64,2816]{2,1,0:T(8,128)(2,1)S(1)}, u32[]{:S(2)}, u32[]{:S(2)}) %collective-permute-start.11) | collective-permute-done | bytes 720928 | tf_op jit(solution)/shard_map/ppermute | solution.py:36
  66.6 0.1 add_pair.1
  66.7 0.8 collective-permute-start.12
  67.6 9.7 %collective-permute-done.12.arrived = bf16[64,2816]{1,0:T(8,128)(2,1)S(1)} collective-permute-done((bf16[64,2816]{1,0:T(8,128)(2,1)S(1)}, bf16[64,2816]{1,0:T(8,128)(2,1)S(1)}, u32[]{:S(2)}, u32[]{:S(2)}) %collective-permute-start.12) | collective-permute-done | bytes 360480 | tf_op jit(solution)/shard_map/ppermute | solution.py:36
  77.3 0.1 add_chip.1
  77.4 0.9 collective-permute-start.13
  78.3 2.5 %collective-permute-start.14 = (bf16[64,1280]{1,0:T(8,128)(2,1)S(1)}, bf16[64,1280]{1,0:T(8,128)(2,1)S(1)}, u32[]{:S(2)}, u32[]{:S(2)}) collective-permute-start(bf16[64,1280]{1,0:T(8,128)(2,1)S(1)} %get-tuple-element.55), channel_id=1, source_target_pairs={{0,16},{2,18},{4,20},{6,22},{8,24},{10,26},{12,28},{14,30},{16,0},... | collective-permute-start | bytes 491528 | tf_op jit(solution)/shard_map/ppermute | solution.py:36
  80.8 1.1 %collective-permute-start.15 = (bf16[64,1280]{1,0:T(8,128)(2,1)S(1)}, bf16[64,1280]{1,0:T(8,128)(2,1)S(1)}, u32[]{:S(2)}, u32[]{:S(2)}) collective-permute-start(bf16[64,1280]{1,0:T(8,128)(2,1)S(1)} %get-tuple-element.56), channel_id=1, source_target_pairs={{0,24},{2,26},{4,28},{6,30},{8,16},{10,18},{12,20},{14,22},{16,8},... | collective-permute-start | bytes 491528 | tf_op jit(solution)/shard_map/ppermute | solution.py:36
  81.9 3.4 %collective-permute-done.13.rest_0_ = bf16[64,1280]{1,0:T(8,128)(2,1)S(1)} collective-permute-done((bf16[64,1280]{1,0:T(8,128)(2,1)S(1)}, bf16[64,1280]{1,0:T(8,128)(2,1)S(1)}, u32[]{:S(2)}, u32[]{:S(2)}) %collective-permute-start.13) | collective-permute-done | bytes 163872 | tf_op jit(solution)/shard_map/ppermute | solution.py:36
  85.2 7.9 %collective-permute-done.14.rest_1_ = bf16[64,1280]{1,0:T(8,128)(2,1)S(1)} collective-permute-done((bf16[64,1280]{1,0:T(8,128)(2,1)S(1)}, bf16[64,1280]{1,0:T(8,128)(2,1)S(1)}, u32[]{:S(2)}, u32[]{:S(2)}) %collective-permute-start.14) | collective-permute-done | bytes 163872 | tf_op jit(solution)/shard_map/ppermute | solution.py:36
  93.1 0.0 collective-permute-done.15.rest_2_
  93.1 0.0 copy-done.1
  93.1 0.9 finish.1
  (2 shorter events, 0.1 us)
Async XLA Ops:
  0.6 0.9 copy-start
  1.5 0.9 copy-start.2
  2.4 42.6 %copy-start.3 = (bf16[8,1024]{1,0:T(8,128)(2,1)S(1)}, bf16[8,1024]{1,0:T(8,128)(2,1)}, u32[]{:S(2)}) copy-start(bf16[8,1024]{1,0:T(8,128)(2,1)} %means.3) | copy-start | bytes 49156
  2.5 18.6 %collective-permute-start.2 = (bf16[128,1024]{1,0:T(8,128)(2,1)S(1)}, bf16[128,1024]{1,0:T(8,128)(2,1)S(1)}, u32[]{:S(2)}, u32[]{:S(2)}) collective-permute-start(bf16[128,1024]{1,0:T(8,128)(2,1)S(1)} %join.3.refs_0_), channel_id=1, source_target_pairs={{0,16},{2,18},{4,20},{6,22},{8,24},{10,26},{12,28},{14,30},{16,0},... | collective-permute-start | bytes 786440 | tf_op jit(solution)/shard_map/ppermute | solution.py:36
  6.6 14.5 %collective-permute-start.1 = (bf16[128,1024]{1,0:T(8,128)(2,1)S(1)}, bf16[128,1024]{1,0:T(8,128)(2,1)S(1)}, u32[]{:S(2)}, u32[]{:S(2)}) collective-permute-start(bf16[128,1024]{1,0:T(8,128)(2,1)S(1)} %join.3.refs_0_), channel_id=1, source_target_pairs={{0,8},{2,10},{4,12},{6,14},{8,0},{10,2},{12,4},{14,6},{16,24},{18,... | collective-permute-start | bytes 786440 | tf_op jit(solution)/shard_map/ppermute | solution.py:36
  8.1 12.9 %collective-permute-start = (bf16[128,1024]{1,0:T(8,128)(2,1)S(1)}, bf16[128,1024]{1,0:T(8,128)(2,1)S(1)}, u32[]{:S(2)}, u32[]{:S(2)}) collective-permute-start(bf16[128,1024]{1,0:T(8,128)(2,1)S(1)} %join.3.refs_0_), channel_id=1, source_target_pairs={{0,4},{2,6},{4,0},{6,2},{8,12},{10,14},{12,8},{14,10},{16,20},{18,... | collective-permute-start | bytes 786440 | tf_op jit(solution)/shard_map/ppermute | solution.py:36
  9.6 0.7 copy-start.4
  10.4 0.7 copy-start.5
  21.1 10.4 %collective-permute-start.3 = (bf16[128,1024]{1,0:T(8,128)(2,1)S(1)}, bf16[128,1024]{1,0:T(8,128)(2,1)S(1)}, u32[]{:S(2)}, u32[]{:S(2)}) collective-permute-start(bf16[128,1024]{1,0:T(8,128)(2,1)S(1)} %collective-permute-done.1.refs_2_), channel_id=1, source_target_pairs={{0,4},{2,6},{4,0},{6,2},{8,12},{10,14},{12,8},{14,10},{16,20},{18,... | collective-permute-start | bytes 786440 | tf_op jit(solution)/shard_map/ppermute | solution.py:36
  21.5 10.0 %collective-permute-start.5 = (bf16[128,1024]{1,0:T(8,128)(2,1)S(1)}, bf16[128,1024]{1,0:T(8,128)(2,1)S(1)}, u32[]{:S(2)}, u32[]{:S(2)}) collective-permute-start(bf16[128,1024]{1,0:T(8,128)(2,1)S(1)} %collective-permute-done.2.refs_1_), channel_id=1, source_target_pairs={{0,8},{2,10},{4,12},{6,14},{8,0},{10,2},{12,4},{14,6},{16,24},{18,... | collective-permute-start | bytes 786440 | tf_op jit(solution)/shard_map/ppermute | solution.py:36
  22.1 12.5 %collective-permute-start.4 = (bf16[128,1024]{1,0:T(8,128)(2,1)S(1)}, bf16[128,1024]{1,0:T(8,128)(2,1)S(1)}, u32[]{:S(2)}, u32[]{:S(2)}) collective-permute-start(bf16[128,1024]{1,0:T(8,128)(2,1)S(1)} %collective-permute-done.2.refs_1_), channel_id=1, source_target_pairs={{0,4},{2,6},{4,0},{6,2},{8,12},{10,14},{12,8},{14,10},{16,20},{18,... | collective-permute-start | bytes 786440 | tf_op jit(solution)/shard_map/ppermute | solution.py:36
  23.9 21.1 %collective-permute-start.6 = (bf16[512,1024]{1,0:T(8,128)(2,1)S(1)}, bf16[512,1024]{1,0:T(8,128)(2,1)S(1)}, u32[]{:S(2)}, u32[]{:S(2)}) collective-permute-start(bf16[512,1024]{1,0:T(8,128)(2,1)S(1)} %join.4.rest_0_), channel_id=1, source_target_pairs={{0,2},{2,0},{4,6},{6,4},{8,10},{10,8},{12,14},{14,12},{16,18},{18,... | collective-permute-start | bytes 3145736 | tf_op jit(solution)/shard_map/ppermute | solution.py:36
  24.0 0.7 copy-start.7
  24.7 0.7 copy-start.8
  25.4 0.7 copy-start.9
  26.1 0.7 copy-start.10
  34.7 10.3 %collective-permute-start.7 = (bf16[384,1024]{1,0:T(8,128)(2,1)S(1)}, bf16[384,1024]{1,0:T(8,128)(2,1)S(1)}, u32[]{:S(2)}, u32[]{:S(2)}) collective-permute-start(bf16[384,1024]{1,0:T(8,128)(2,1)S(1)} %join.5.rest_2_), channel_id=1, source_target_pairs={{0,2},{2,0},{4,6},{6,4},{8,10},{10,8},{12,14},{14,12},{16,18},{18,... | collective-permute-start | bytes 2359304 | tf_op jit(solution)/shard_map/ppermute | solution.py:36
  34.8 8.7 %collective-permute-start.8 = (bf16[128,1024]{1,0:T(8,128)(2,1)S(1)}, bf16[128,1024]{1,0:T(8,128)(2,1)S(1)}, u32[]{:S(2)}, u32[]{:S(2)}) collective-permute-start(bf16[128,1024]{1,0:T(8,128)(2,1)S(1)} %collective-permute-done.5.refs_0_), channel_id=1, source_target_pairs={{0,4},{2,6},{4,0},{6,2},{8,12},{10,14},{12,8},{14,10},{16,20},{18,... | collective-permute-start | bytes 786440 | tf_op jit(solution)/shard_map/ppermute | solution.py:36
  43.5 1.5 %collective-permute-start.9 = (bf16[128,1024]{1,0:T(8,128)(2,1)S(1)}, bf16[128,1024]{1,0:T(8,128)(2,1)S(1)}, u32[]{:S(2)}, u32[]{:S(2)}) collective-permute-start(bf16[128,1024]{1,0:T(8,128)(2,1)S(1)} %collective-permute-done.8.rest_4_), channel_id=1, source_target_pairs={{0,2},{2,0},{4,6},{6,4},{8,10},{10,8},{12,14},{14,12},{16,18},{18,... | collective-permute-start | bytes 786440 | tf_op jit(solution)/shard_map/ppermute | solution.py:36
  51.2 8.5 %copy-start.6 = (f32[8]{0:T(128)S(1)}, f32[8]{0:T(128)}, u32[]{:S(2)}) copy-start(f32[8]{0:T(128)} %scales.1) | copy-start | bytes 100
  55.3 4.4 %collective-permute-start.10 = (f32[8,2304]{1,0:T(8,128)S(1)}, f32[8,2304]{1,0:T(8,128)S(1)}, u32[]{:S(2)}, u32[]{:S(2)}) collective-permute-start(f32[8,2304]{1,0:T(8,128)S(1)} %get-tuple-element.44.own), channel_id=1, source_target_pairs={{0,1},{1,0},{2,3},{3,2},{4,5},{5,4},{6,7},{7,6},{8,9},{9,8},{10,11... | collective-permute-start | bytes 221192 | tf_op jit(solution)/shard_map/ppermute | solution.py:36
  59.7 33.4 %copy-start.1 = (bf16[64,1024]{1,0:T(8,128)(2,1)S(1)}, bf16[64,1024]{1,0:T(8,128)(2,1)}, u32[]{:S(2)}) copy-start(bf16[64,1024]{1,0:T(8,128)(2,1)} %chol.1) | copy-start | bytes 393220
  64.3 2.3 %collective-permute-start.11 = (bf16[2,64,2816]{2,1,0:T(8,128)(2,1)S(1)}, bf16[2,64,2816]{2,1,0:T(8,128)(2,1)S(1)}, u32[]{:S(2)}, u32[]{:S(2)}) collective-permute-start(bf16[2,64,2816]{2,1,0:T(8,128)(2,1)S(1)} %get-tuple-element.50), channel_id=1, source_target_pairs={{0,2},{2,0},{4,6},{6,4},{8,10},{10,8},{12,14},{14,12},{16,18},{18,... | collective-permute-start | bytes 2162696 | tf_op jit(solution)/shard_map/ppermute | solution.py:36
  66.7 10.5 %collective-permute-start.12 = (bf16[64,2816]{1,0:T(8,128)(2,1)S(1)}, bf16[64,2816]{1,0:T(8,128)(2,1)S(1)}, u32[]{:S(2)}, u32[]{:S(2)}) collective-permute-start(bf16[64,2816]{1,0:T(8,128)(2,1)S(1)} %get-tuple-element.52), channel_id=1, source_target_pairs={{0,4},{2,6},{4,0},{6,2},{8,12},{10,14},{12,8},{14,10},{16,20},{18,... | collective-permute-start | bytes 1081352 | tf_op jit(solution)/shard_map/ppermute | solution.py:36
  77.4 7.8 %collective-permute-start.13 = (bf16[64,1280]{1,0:T(8,128)(2,1)S(1)}, bf16[64,1280]{1,0:T(8,128)(2,1)S(1)}, u32[]{:S(2)}, u32[]{:S(2)}) collective-permute-start(bf16[64,1280]{1,0:T(8,128)(2,1)S(1)} %get-tuple-element.54), channel_id=1, source_target_pairs={{0,8},{2,10},{4,12},{6,14},{8,0},{10,2},{12,4},{14,6},{16,24},{18,... | collective-permute-start | bytes 491528 | tf_op jit(solution)/shard_map/ppermute | solution.py:36
  78.3 14.9 %collective-permute-start.14 = (bf16[64,1280]{1,0:T(8,128)(2,1)S(1)}, bf16[64,1280]{1,0:T(8,128)(2,1)S(1)}, u32[]{:S(2)}, u32[]{:S(2)}) collective-permute-start(bf16[64,1280]{1,0:T(8,128)(2,1)S(1)} %get-tuple-element.55), channel_id=1, source_target_pairs={{0,16},{2,18},{4,20},{6,22},{8,24},{10,26},{12,28},{14,30},{16,0},... | collective-permute-start | bytes 491528 | tf_op jit(solution)/shard_map/ppermute | solution.py:36
  80.8 12.3 %collective-permute-start.15 = (bf16[64,1280]{1,0:T(8,128)(2,1)S(1)}, bf16[64,1280]{1,0:T(8,128)(2,1)S(1)}, u32[]{:S(2)}, u32[]{:S(2)}) collective-permute-start(bf16[64,1280]{1,0:T(8,128)(2,1)S(1)} %get-tuple-element.56), channel_id=1, source_target_pairs={{0,24},{2,26},{4,28},{6,30},{8,16},{10,18},{12,20},{14,22},{16,8},... | collective-permute-start | bytes 491528 | tf_op jit(solution)/shard_map/ppermute | solution.py:36

commit v3 on v2

v3 whole, which is shorter than its diff:
```python
import functools

import jax
import jax.numpy as jnp
from jax import lax
from jax.experimental import pallas as pl
from jax.experimental.pallas import tpu as pltpu
from jax.sharding import PartitionSpec as P

C = 8
NB = 6
ROWS_DEV = 2048
SLOT = 128
COL = 1024
SQRT_HALF_LOG2E = 0.8493218002880191

precise = lax.Precision.HIGHEST
f32 = jnp.float32
bf16 = jnp.bfloat16
SMEM = pl.BlockSpec(memory_space=pltpu.SMEM)
VMEM = pl.BlockSpec(memory_space=pltpu.VMEM)
HBM = pl.BlockSpec(memory_space=pltpu.HBM)
SMALL = pltpu.CompilerParams(vmem_limit_bytes=4 * 1024 * 1024)


def dot(a, b):
    return jnp.dot(a, b, preferred_element_type=f32)


def dot_nt(a, b):
    return lax.dot_general(a, b, (((1,), (1,)), ((), ())), preferred_element_type=f32)


def swap(value, axis, bit):
    size = lax.axis_size(axis)
    return lax.ppermute(value, axis, [(i, i ^ bit) for i in range(size)])


def after(value, *earlier):
    return lax.optimization_barrier((value,) + earlier)[0]


def join_kernel(places, rows, *refs):
    out = refs[-1]
    for i, (source, slot) in enumerate(places):
        out[rows * i : rows * (i + 1), :] = refs[source][rows * slot : rows * (slot + 1), :]


def join(parts, rows):
    first = parts[0][0]
    if first.shape[0] == rows * len(parts) and parts == [(first, slot) for slot in range(len(parts))]:
        return first
    arrays = list({id(array): array for array, _ in parts}.values())
    places = [([array is other for other in arrays].index(True), slot) for array, slot in parts]
    return pl.pallas_call(
        functools.partial(join_kernel, places, rows),
        out_shape=jax.ShapeDtypeStruct((rows * len(parts), parts[0][0].shape[1]), parts[0][0].dtype),
        in_specs=[VMEM] * len(arrays),
        out_specs=VMEM,
        compiler_params=SMALL,
        name="join",
    )(*arrays)


def phases_of(nz):
    offsets = range(2, 4 * nz, 2)
    most = max(offset.bit_count() for offset in offsets)
    return [[o for o in reversed(offsets) if o.bit_count() == p] for p in range(1, most + 1)]


class Gather:
    def __init__(self, factors, nz):
        self.rows = factors[0].shape[0]
        own = join([(factor, 0) for factor in factors], self.rows)
        self.pieces = {(m, 0): (own, m) for m in range(2)}
        self.phases = phases_of(nz)
        self.groups = []

    def phase(self, number, beside=None):
        wanted = {}
        for offset in self.phases[number]:
            for m in range(2):
                bit = 4 if m == 1 and offset & 4 else offset & -offset
                wanted.setdefault(bit, []).append((m, offset))
        arrivals = {}
        for bit, keys in sorted(wanted.items(), reverse=True):
            sent = join([self.pieces[m, offset ^ bit] for m, offset in keys], self.rows)
            arrivals[bit] = swap(sent, "obs", bit)
        if beside is not None:
            arrivals, beside = lax.optimization_barrier((arrivals, beside()))
        new = [(0, 0), (1, 0)] if number == 0 else []
        for bit, keys in sorted(wanted.items()):
            self.pieces.update({key: (arrivals[bit], slot) for slot, key in enumerate(keys)})
            new += keys
        last = number == len(self.phases) - 1
        for part in [[key] for key in new] if last else [new]:
            group = join([self.pieces[key] for key in part], self.rows)
            self.groups.append((part, group, swap(group, "obs", 1)))
        return beside

    def of(self, m):
        arrays, places = [], []
        for new, *pair in self.groups:
            slots = [(slot, offset) for slot, (owner, offset) in enumerate(new) if owner == m]
            for core, array in enumerate(pair):
                places += [(len(arrays), slot, offset ^ core) for slot, offset in slots]
                arrays += [array] if slots else []
        return arrays, places


def store_pieces(groups, places, whole):
    me = lax.axis_index("obs")
    rows = whole.shape[0] // len(places)
    for source, slot, offset in places:
        target = pl.ds(pl.multiple_of(rows * (me ^ offset), rows), rows)
        whole[target, :] = groups[source][rows * slot : rows * (slot + 1), :]


def stack_kernel(coords_in, codes_in, out, coords, codes, sems):
    fetch((coords_in, codes_in), (coords, codes), sems)
    out[0:2, :] = coords[...]
    out[2:3, :] = codes[...].astype(f32)


def fetch(sources, targets, sems):
    copies = [pltpu.make_async_copy(a, b, sems.at[i]) for i, (a, b) in enumerate(zip(sources, targets))]
    for copy in copies:
        copy.start()
    for copy in copies:
        copy.wait()


def kernel_rows_kernel(
    arrived, points_in, bands_in, mix_in, lengthscales, kt, labels, self_cov, points, point_bands, band_mix, sems
):
    fetch((points_in, bands_in, mix_in), (points, point_bands, band_mix), sems)
    codes = arrived[2:3, :]
    label = jnp.floor((codes + 0.5) * (1.0 / NB))
    labels[...] = label.astype(jnp.int32)
    bands = (codes - NB * label).astype(jnp.int32)
    kinds = lax.broadcasted_iota(jnp.int32, (C, ROWS_DEV), 0)
    hot = (kinds == bands).astype(f32)
    eye = lax.broadcasted_iota(jnp.int32, (C, C), 0) == lax.broadcasted_iota(jnp.int32, (C, C), 1)
    factor = jnp.concatenate([band_mix[...], jnp.zeros((NB, C - NB), f32)], axis=1)
    factor = jnp.concatenate([factor, jnp.zeros((C - NB, C), f32)], axis=0)
    mix = eye.astype(f32) + lax.dot_general(
        factor, factor, (((1,), (1,)), ((), ())), precision=precise, preferred_element_type=f32
    )
    scales = [SQRT_HALF_LOG2E / lengthscales[i] for i in range(2)]
    diagonal = jnp.sum(jnp.where(eye, mix, 0.0), axis=1, keepdims=True)
    self_cov[...] = jnp.sum(hot * diagonal, axis=0, keepdims=True)
    hots = jnp.concatenate([hot, hot, hot, jnp.zeros_like(hot)], axis=0).astype(bf16)
    times = arrived[0:1, :] * scales[0]
    waves = arrived[1:2, :] * scales[1]
    width = points.shape[1]
    columns = jnp.concatenate(
        [points[...], point_bands[...].astype(f32), jnp.zeros((C - 3, width), f32)], axis=0
    ).T
    step = 128
    for j in range(0, width, step):
        here = columns[j : j + step, :]
        picked = jnp.zeros((step, C), f32)
        for kind in range(NB):
            picked = jnp.where(here[:, 2:3] == float(kind), mix[kind : kind + 1, :], picked)
        high = picked.astype(bf16).astype(f32)
        middle = (picked - high).astype(bf16).astype(f32)
        low = picked - high - middle
        split = jnp.concatenate([high, middle, low, jnp.zeros_like(low)], axis=1).astype(bf16)
        mixing = dot(split, hots)
        delta_t = times - here[:, 0:1] * scales[0]
        delta_w = waves - here[:, 1:2] * scales[1]
        value = jnp.exp2(-(delta_t * delta_t + delta_w * delta_w)) * mixing
        kt[j : j + step, :] = value.astype(bf16)


def whiten_kernel(places, kt, means, *rest):
    groups, (ab, stats, whole, turned) = rest[:-4], rest[-4:]
    width = whole.shape[0]
    store_pieces(groups, places, whole)
    for j in range(0, width, 256):
        turned[:, j : j + 256] = whole[j : j + 256, :].T

    @pl.loop(0, ROWS_DEV // COL)
    def _(step):
        columns = pl.ds(pl.multiple_of(step * COL, COL), COL)
        square = jnp.zeros((1, COL), f32)
        for k in range(0, width, 256):
            part = dot(turned[k : k + 256, :], kt[:, columns])
            square = square + jnp.sum(part * part, axis=0, keepdims=True)
            ab[k : k + 256, columns] = part.astype(bf16)
        stats[0:C, columns] = dot(means[...], ab[:, columns])
        stats[C : 2 * C, columns] = jnp.broadcast_to(-square, (C, COL))


def covary_kernel(places, ab, stats, *rest):
    groups, (bt, sums, whole, turned) = rest[:-4], rest[-4:]
    width = whole.shape[0]
    store_pieces(groups, places, whole)
    for j in range(0, width, 256):
        turned[:, j : j + 256] = whole[j : j + 256, :].T

    @pl.loop(0, ROWS_DEV // COL)
    def _(step):
        columns = pl.ds(pl.multiple_of(step * COL, COL), COL)
        square = stats[C : C + 1, columns]
        for l in range(0, width, 256):
            part = dot(turned[l : l + 256, l:], ab[l:, columns])
            square = square + jnp.sum(part * part, axis=0, keepdims=True)
            bt[l : l + 256, columns] = part.astype(bf16)
        sums[:, columns] = stats[0:C, columns]
        piece = ROWS_DEV // C
        for i in range(COL // piece):
            sums[pl.ds((COL // piece) * step + i, 1), ROWS_DEV:] = square[:, piece * i : piece * (i + 1)]


def slope_kernel(nz, own, other, scales, labels, self_cov, ab, bt, chances_out, mean, keep, send, heavy):
    total = own[...] + other[...]
    variance = jnp.concatenate([total[i : i + 1, ROWS_DEV:] for i in range(C)], axis=1) + self_cov[...]
    classes = lax.broadcasted_iota(jnp.int32, (C, 1), 0)
    scale = jnp.zeros((C, 1), f32)
    for i in range(C):
        scale = jnp.where(classes == i, scales[i], scale)
    logits = total[:, :ROWS_DEV] + 0.5 * scale * variance
    weights = jnp.exp(logits)
    chances = weights / jnp.sum(weights, axis=0, keepdims=True)
    chances_out[...] = chances
    twice = -jnp.sum(chances * scale, axis=0, keepdims=True)
    slope = ((labels[...] == classes).astype(f32) - chances).astype(bf16)
    core = lax.axis_index("obs") % 2
    block = ab.shape[0] // nz
    quarter = block // 4
    for z in range(nz):
        rows = slice(block * z, block * (z + 1))
        heavy[rows, :] = (bt[rows, :].astype(f32) * twice).astype(bf16)
        wide = block * (z + 1)
        start = block * z * (z + 1) // 2
        here = slice(start, start + wide)
        term = dot_nt(ab[rows, :], heavy[:wide, :])
        for x in range(2):
            even = term[2 * quarter * x : 2 * quarter * x + quarter, :]
            odd = term[2 * quarter * x + quarter : 2 * quarter * (x + 1), :]
            keep[quarter * x : quarter * (x + 1), here] = jnp.where(core == 0, even, odd)
            send[quarter * x : quarter * (x + 1), here] = jnp.where(core == 0, odd, even).astype(bf16)
    value = dot_nt(slope, ab[...])
    mean[...] = value
    send[2 * quarter :, : ab.shape[0]] = halves(value)


def halves(value):
    high = value.astype(bf16).astype(f32)
    return jnp.concatenate([high, value - high], axis=0).astype(bf16)


def joined(pair):
    return pair[:C].astype(f32) + pair[C:].astype(f32)


def pair_kernel(mean, keep, arrived, mean_out, total):
    rows, width = keep.shape[0], mean.shape[1]
    total[...] = keep[...] + arrived[:rows, :].astype(f32)
    mean_out[...] = mean[...] + joined(arrived[rows:, :width])


def part_of(nz, total, width, offset):
    target = lax.axis_index("obs") ^ offset
    rows = total.shape[0] // 2
    x, z = (target // 2) % 2, target // 4
    start = pl.multiple_of(width // nz * (z * (z + 1) // 2), width // nz)
    return total[pl.ds(pl.multiple_of(rows * x, rows), rows), pl.ds(start, width)]


def with_children(nz, total, width, offset, children, refs):
    rows = total.shape[0] // 2
    value = part_of(nz, total, width, offset)
    for source, slot in children:
        value = value + refs[source][rows * slot : rows * (slot + 1), :].astype(f32)
    return value


def level_kernel(nz, plan, mean_from, mean, total, *refs):
    outs = refs[len(refs) - len(plan) - 1 :]
    rows, width = total.shape[0] // 2, mean.shape[1]
    value = mean[...]
    if mean_from is not None:
        value = value + joined(refs[mean_from][refs[mean_from].shape[0] - 2 * C :, :])
    outs[0][...] = value
    for out, (pieces, with_mean) in zip(outs[1:], plan):
        for i, (offset, children) in enumerate(pieces):
            out[rows * i : rows * (i + 1), :] = with_children(nz, total, width, offset, children, refs).astype(bf16)
        if with_mean:
            out[rows * len(pieces) :, :] = halves(value)


class Scatter:
    def __init__(self, nz, mean, total):
        self.nz, self.mean, self.total = nz, mean, total
        self.arrived = {}
        self.mean_from = None

    def children(self, offset, arrays):
        found = []
        for child, (array, slot) in self.arrived.items():
            if child ^ (child & -child) == offset:
                if not any(array is other for other in arrays):
                    arrays.append(array)
                found.append(([array is other for other in arrays].index(True), slot))
        return found

    def level(self, sends, mean_bit):
        arrays = []
        plan = [([(o, self.children(o, arrays)) for o in offsets], offsets[0] & -offsets[0] == mean_bit and i == 0)
                for i, offsets in enumerate(sends)]
        mean_from = None
        if self.mean_from is not None:
            if not any(self.mean_from is other for other in arrays):
                arrays.append(self.mean_from)
            mean_from = [self.mean_from is other for other in arrays].index(True)
        rows, width = self.total.shape[0] // 2, self.mean.shape[1]
        self.mean, *outs = pl.pallas_call(
            functools.partial(level_kernel, self.nz, plan, mean_from),
            out_shape=[jax.ShapeDtypeStruct(self.mean.shape, f32)]
            + [jax.ShapeDtypeStruct((rows * len(pieces) + 2 * C * m, width), bf16) for pieces, m in plan],
            in_specs=[VMEM] * (2 + len(arrays)),
            out_specs=[VMEM] * (1 + len(plan)),
            compiler_params=SMALL,
            name="add_level",
        )(self.mean, self.total, *arrays)
        for i, (offsets, out) in enumerate(zip(sends, outs)):
            out = swap(out, "obs", offsets[0] & -offsets[0])
            self.arrived.update({offset: (out, slot) for slot, offset in enumerate(offsets)})
            if i == 0:
                self.mean_from = out


def finish_kernel(nz, children, mean_from, mean, total, chol, means, *refs):
    grad_chol, grad_mean = refs[-2:]
    rows, width = chol.shape
    value = with_children(nz, total, width, 0, children, refs)
    row_ids = lax.axis_index("obs") * rows + lax.broadcasted_iota(jnp.int32, (rows, width), 0)
    column_ids = lax.broadcasted_iota(jnp.int32, (rows, width), 1)
    own = chol[...].astype(f32)
    on_diag = column_ids == row_ids
    inverse = 1.0 / jnp.where(on_diag, own, 1.0)
    grad_chol[...] = jnp.where(column_ids <= row_ids, value, 0.0) - own + jnp.where(on_diag, inverse, 0.0)
    summed = mean[...] + joined(refs[mean_from][rows:, :])
    grad_mean[...] = summed - means[...].astype(f32)


def route(obs_coords, obs_codes, route_plan):
    devices = lax.axis_size("obs")
    stacked = pl.pallas_call(
        stack_kernel,
        out_shape=jax.ShapeDtypeStruct((3, obs_coords.shape[1]), f32),
        in_specs=[HBM, HBM],
        out_specs=VMEM,
        scratch_shapes=[
            pltpu.VMEM(obs_coords.shape, f32),
            pltpu.VMEM((1, obs_coords.shape[1]), jnp.int32),
            pltpu.SemaphoreType.DMA((2,)),
        ],
        compiler_params=SMALL,
        name="stack",
    )(obs_coords, obs_codes[None, :])
    if devices * SLOT == ROWS_DEV:
        return lax.all_to_all(stacked, "obs", split_axis=1, concat_axis=1, tiled=True)
    me = lax.axis_index("obs")
    blocks = route_plan * SLOT
    send_start = jnp.cumsum(blocks, axis=1) - blocks
    recv_start = jnp.cumsum(blocks, axis=0) - blocks
    my_sends = lax.dynamic_index_in_dim(send_start, me, 0, keepdims=False)
    my_recvs = lax.dynamic_index_in_dim(recv_start, me, 1, keepdims=False)
    padded = jnp.concatenate([stacked, jnp.zeros((3, SLOT), f32)], axis=1)
    outgoing = jax.vmap(lambda offset: lax.dynamic_slice_in_dim(padded, offset, SLOT, 1))(my_sends)
    incoming = lax.all_to_all(outgoing, "obs", split_axis=0, concat_axis=0, tiled=True)
    position = jnp.arange(ROWS_DEV, dtype=jnp.int32)
    sources = jnp.arange(devices, dtype=jnp.int32)
    source = jnp.sum((my_recvs[None, :] <= position[:, None]).astype(jnp.int32), axis=1) - 1
    pick = (source[:, None] == sources[None, :]).astype(jnp.int32)
    begin_row = jnp.sum(pick * my_recvs[None, :], axis=1)
    return incoming[source, :, position - begin_row].T


def body(
    obs_coords,
    obs_codes,
    route_plan,
    inducing_coords,
    inducing_bands,
    band_mix,
    lengthscales,
    class_scales,
    prior_factor,
    variational_chol,
    variational_mean,
):
    n = lax.axis_size("obs")
    nz = n // 4
    rows, width = variational_chol.shape
    gather = Gather((prior_factor, variational_chol), nz)
    arrived = gather.phase(0, lambda: route(obs_coords, obs_codes, route_plan))
    big = pltpu.CompilerParams(vmem_limit_bytes=16 * 1024 * 1024)
    cover = lambda: pl.pallas_call(
        kernel_rows_kernel,
        out_shape=(
            jax.ShapeDtypeStruct((width, ROWS_DEV), bf16),
            jax.ShapeDtypeStruct((1, ROWS_DEV), jnp.int32),
            jax.ShapeDtypeStruct((1, ROWS_DEV), f32),
        ),
        in_specs=[VMEM, HBM, HBM, HBM, SMEM],
        out_specs=(VMEM, VMEM, VMEM),
        scratch_shapes=[
            pltpu.VMEM((2, width), f32),
            pltpu.VMEM((1, width), jnp.int32),
            pltpu.VMEM((NB, NB), f32),
            pltpu.SemaphoreType.DMA((3,)),
        ],
        compiler_params=big,
        cost_estimate=pl.CostEstimate(
            flops=20 * width * ROWS_DEV, bytes_accessed=4 * 1024 * 1024, transcendentals=width * ROWS_DEV
        ),
        name="kernel_rows",
    )(arrived, inducing_coords, inducing_bands[None, :], band_mix, lengthscales)
    kt, labels, self_cov = gather.phase(1, cover)
    for number in range(2, len(gather.phases)):
        gather.phase(number)
    prior_arrays, prior_places = gather.of(0)
    chol_arrays, chol_places = gather.of(1)
    whole = [pltpu.VMEM((width, width), bf16), pltpu.VMEM((width, width), bf16)]
    ab, part_stats = pl.pallas_call(
        functools.partial(whiten_kernel, prior_places),
        out_shape=(
            jax.ShapeDtypeStruct((width, ROWS_DEV), bf16),
            jax.ShapeDtypeStruct((2 * C, ROWS_DEV), f32),
        ),
        in_specs=[VMEM] * (2 + len(prior_arrays)),
        out_specs=(VMEM, VMEM),
        scratch_shapes=whole,
        compiler_params=big,
        cost_estimate=pl.CostEstimate(
            flops=2 * width * width * ROWS_DEV, bytes_accessed=10 * 1024 * 1024, transcendentals=0
        ),
        name="whiten",
    )(kt, variational_mean, *prior_arrays)
    bt, sums = pl.pallas_call(
        functools.partial(covary_kernel, chol_places),
        out_shape=(
            jax.ShapeDtypeStruct((width, ROWS_DEV), bf16),
            jax.ShapeDtypeStruct((C, ROWS_DEV + ROWS_DEV // C), f32),
        ),
        in_specs=[VMEM] * (2 + len(chol_arrays)),
        out_specs=(VMEM, VMEM),
        scratch_shapes=whole,
        compiler_params=big,
        cost_estimate=pl.CostEstimate(
            flops=width * width * ROWS_DEV, bytes_accessed=10 * 1024 * 1024, transcendentals=0
        ),
        name="covary",
    )(ab, part_stats, *chol_arrays)

    other = swap(sums, "ind", 1)
    bit = 2
    while bit < lax.axis_size("ind"):
        sums = sums + other
        other = swap(sums, "ind", bit)
        bit *= 2

    packed = width // nz * (nz * (nz + 1) // 2)
    chances, mean, keep, send = pl.pallas_call(
        functools.partial(slope_kernel, nz),
        out_shape=[
            jax.ShapeDtypeStruct((C, ROWS_DEV), f32),
            jax.ShapeDtypeStruct((C, width), f32),
            jax.ShapeDtypeStruct((2 * rows, packed), f32),
            jax.ShapeDtypeStruct((2 * rows + 2 * C, packed), bf16),
        ],
        in_specs=[VMEM, VMEM, SMEM] + [VMEM] * 4,
        out_specs=[VMEM] * 4,
        scratch_shapes=[pltpu.VMEM((width, ROWS_DEV), bf16)],
        compiler_params=big,
        name="slopes",
    )(sums, other, class_scales, labels, self_cov, ab, bt)
    mean, total = pl.pallas_call(
        pair_kernel,
        out_shape=[jax.ShapeDtypeStruct(mean.shape, f32), jax.ShapeDtypeStruct(keep.shape, f32)],
        in_specs=[VMEM] * 3,
        out_specs=[VMEM] * 2,
        compiler_params=SMALL,
        name="add_pair",
    )(mean, keep, swap(send, "obs", 1))
    scatter = Scatter(nz, mean, total)
    along_x = [o for phase in reversed(gather.phases) for o in phase if o & 2]
    scatter.level([along_x[:1], along_x[1:-1], along_x[-1:]], 2)
    along_z = [[o for o in phase if not o & 2] for phase in gather.phases]
    along_z = [phase for phase in along_z if phase]
    for i, phase in enumerate(reversed(along_z)):
        bits = sorted({o & -o for o in phase}, reverse=True)
        scatter.level([[o for o in phase if o & -o == bit] for bit in bits], 4 << i)
    arrays = []
    children = scatter.children(0, arrays)
    mean_from = [scatter.mean_from is array for array in arrays].index(True)
    grad_chol, grad_mean = pl.pallas_call(
        functools.partial(finish_kernel, nz, children, mean_from),
        out_shape=(
            jax.ShapeDtypeStruct((rows, width), f32),
            jax.ShapeDtypeStruct((C, width), f32),
        ),
        in_specs=[VMEM] * (4 + len(arrays)),
        out_specs=(VMEM, VMEM),
        compiler_params=SMALL,
        name="finish",
    )(scatter.mean, total, variational_chol, variational_mean, *arrays)
    return (chances, grad_chol, grad_mean)


def solution(mesh):
    placed = (
        P(None, "obs"),
        P("obs"),
        P(),
        P(None, "ind"),
        P("ind"),
        P(),
        P(),
        P(),
        P(("ind", "obs"), None),
        P(("ind", "obs"), None),
        P(None, "ind"),
    )
    return jax.shard_map(
        body,
        mesh=mesh,
        in_specs=placed,
        out_specs=(P(None, "obs"), P(("ind", "obs"), None), P(None, "ind")),
        check_vma=False,
    )
```

time: 94.5 us -> 85.3 us (0.903)
  waiting for transfers between devices: 38.6 us -> 30.3 us
  local copies, waits for them, and re-layouts: 5.95 us -> 3.24 us
  starting transfers between devices: 17.8 us -> 19.6 us
    ppermute x16 -> x19, waiting for transfers between devices: 38.6 us -> 30.3 us  [swap(): return lax.ppermute(value, axis, [(i, i ^ bit) for i in range(size)])]
    unnamed x22, local copies, waits for them, and re-layouts: 5.95 us -> 3.24 us
    ppermute x16 -> x19, starting transfers between devices: 17.8 us -> 19.6 us  [swap(): return lax.ppermute(value, axis, [(i, i ^ bit) for i in range(size)])]
    pallas_call x9 -> x15, Pallas kernels: 16.2 us -> 16.3 us  [the longest x1 6.14 us: body(): pl.pallas_call(functools.partial(whiten_kernel, prior_places), out_shape=...]
  transfers between devices with their start and end apart: 16 -> 19, of which waited for: 8 -> 12; matrix products, arithmetic and copies ran while one was open for 0% -> 0% of each run, Pallas kernels for 5% -> 13%
where the time goes in v3:
time: 85.3 us; the launch traced here: 85 us
  waiting for transfers between devices  30.3 us (36%)
  Pallas kernels  21.1 us (25%)
  starting transfers between devices  19.6 us (23%)
  blocking collectives  9.96 us (12%)
  local copies, waits for them, and re-layouts  3.24 us (4%)
    ppermute x19, waiting for transfers between devices, swap(): return lax.ppermute(value, axis, [(i, i ^ bit) for i in range(size)])  30.3 us
    ppermute x19, starting transfers between devices, swap(): return lax.ppermute(value, axis, [(i, i ^ bit) for i in range(size)])  19.6 us
    all_to_all x1, blocking collectives, route(): lax.all_to_all(stacked, 'obs', split_axis=1, concat_axis=1, tiled=True)  9.96 us
    pallas_call x1, Pallas kernels, body(): pl.pallas_call(functools.partial(whiten_kernel, prior_places), out_shape=...  6.14 us
    pallas_call x1, Pallas kernels, body(): pl.pallas_call(kernel_rows_kernel, out_shape=(jax.ShapeDtypeStruct((width...  4.75 us
    pallas_call x1, Pallas kernels, body(): pl.pallas_call(functools.partial(slope_kernel, nz), out_shape=[jax.ShapeD...  4.54 us
    pallas_call x1, Pallas kernels, body(): pl.pallas_call(functools.partial(covary_kernel, chol_places), out_shape=(...  4.11 us
    unnamed x22, local copies, waits for them, and re-layouts  3.24 us
  transfers between devices with their start and end apart: 19, of which 12 were waited for; matrix products, arithmetic and copies ran while one was open for 0% of the time, Pallas kernels for 13%

profile of v3, /device:TPU:0, one launch (start us, length us, event | category | flops | bytes accessed | tf_op | source)
XLA Modules:
  0.0 85.0 jit_solution(9741993697427035947)
XLA Ops:
  0.6 0.0 copy-start
  0.6 0.9 %copy-done = bf16[64,1024]{1,0:T(8,128)(2,1)S(1)} copy-done((bf16[64,1024]{1,0:T(8,128)(2,1)S(1)}, bf16[64,1024]{1,0:T(8,128)(2,1)}, u32[]{:S(2)}) %copy-start) | copy-done | bytes 131096
  1.5 0.0 copy-start.2
  1.5 0.9 %copy-done.2 = bf16[64,1024]{1,0:T(8,128)(2,1)S(1)} copy-done((bf16[64,1024]{1,0:T(8,128)(2,1)S(1)}, bf16[64,1024]{1,0:T(8,128)(2,1)}, u32[]{:S(2)}) %copy-start.2) | copy-done | bytes 131096
  2.4 0.0 copy-start.7
  2.5 4.1 %collective-permute-start.2 = (bf16[128,1024]{1,0:T(8,128)(2,1)S(1)}, bf16[128,1024]{1,0:T(8,128)(2,1)S(1)}, u32[]{:S(2)}, u32[]{:S(2)}) collective-permute-start(bf16[128,1024]{1,0:T(8,128)(2,1)S(1)} %join.7.refs_0_), channel_id=1, source_target_pairs={{0,16},{2,18},{4,20},{6,22},{8,24},{10,26},{12,28},{14,30},{16,0},... | collective-permute-start | bytes 786440 | tf_op jit(solution)/shard_map/ppermute | solution.py:36
  6.6 1.6 %collective-permute-start.1 = (bf16[128,1024]{1,0:T(8,128)(2,1)S(1)}, bf16[128,1024]{1,0:T(8,128)(2,1)S(1)}, u32[]{:S(2)}, u32[]{:S(2)}) collective-permute-start(bf16[128,1024]{1,0:T(8,128)(2,1)S(1)} %join.7.refs_0_), channel_id=1, source_target_pairs={{0,8},{2,10},{4,12},{6,14},{8,0},{10,2},{12,4},{14,6},{16,24},{18,... | collective-permute-start | bytes 786440 | tf_op jit(solution)/shard_map/ppermute | solution.py:36
  8.2 1.5 %collective-permute-start = (bf16[128,1024]{1,0:T(8,128)(2,1)S(1)}, bf16[128,1024]{1,0:T(8,128)(2,1)S(1)}, u32[]{:S(2)}, u32[]{:S(2)}) collective-permute-start(bf16[128,1024]{1,0:T(8,128)(2,1)S(1)} %join.7.refs_0_), channel_id=1, source_target_pairs={{0,4},{2,6},{4,0},{6,2},{8,12},{10,14},{12,8},{14,10},{16,20},{18,... | collective-permute-start | bytes 786440 | tf_op jit(solution)/shard_map/ppermute | solution.py:36
  9.7 0.7 copy-done.4
  10.4 0.7 copy-done.5
  11.1 10.0 %all_to_all.12 = f32[3,16,128]{2,0,1:T(4,128)S(1)} all-to-all(f32[3,16,128]{2,0,1:T(4,128)S(1)} %bitcast.4), channel_id=1, replica_groups=mesh['obs'=16,'ind'=2] {'obs'}, dimensions={1} | all-to-all | bytes 49152 | tf_op jit(solution)/shard_map/all_to_all | solution.py:365
  21.1 0.0 collective-permute-done.2.refs_0_.refs_3_
  21.1 0.0 collective-permute-done.1.refs_1_.refs_2_
  21.1 0.0 collective-permute-done.refs_1_
  21.2 0.0 copy-start.3
  21.2 0.7 collective-permute-start.4
  21.9 0.3 collective-permute-start.3
  22.2 0.1 join.10.rest_0_
  22.3 0.1 collective-permute-start.5
  22.4 0.0 copy-done.7
  22.4 0.0 copy-done.8
  22.4 0.0 copy-done.9
  22.4 0.0 copy-done.10
  22.4 4.7 %kernel_rows.1 = (bf16[1024,2048]{1,0:T(8,128)(2,1)S(1)}, s32[1,2048]{1,0:T(1,128)S(1)}, f32[1,2048]{1,0:T(1,128)S(1)}) custom-call(f32[3,2048]{1,0:T(4,128)S(1)} %bitcast.5, f32[2,1024]{1,0:T(2,128)S(1)} %copy-done.7, s32[1,1024]{1,0:T(1,128)S(1)} %bitcast.7, f32[6,6]{1,0:T(8,128)S(1)} %copy-done.9, f32[2]{0:T(128)S(1)} %copy-done.10), custom_call_target="tpu_custom_call" | custom-call | flops 41943040 | bytes 4194304 | tf_op jit(solution)/shard_map/kernel_rows/pallas_call | solution.py:402
  27.2 4.8 %collective-permute-done.4.refs_1_.refs_0_ = bf16[192,1024]{1,0:T(8,128)(2,1)S(1)} collective-permute-done((bf16[192,1024]{1,0:T(8,128)(2,1)S(1)}, bf16[192,1024]{1,0:T(8,128)(2,1)S(1)}, u32[]{:S(2)}, u32[]{:S(2)}) %collective-permute-start.4) | collective-permute-done | bytes 393248 | tf_op jit(solution)/shard_map/ppermute | solution.py:36
  31.9 0.5 collective-permute-done.3.refs_0_
  32.4 0.1 join.11.rest_2_
  32.5 0.1 collective-permute-start.6
  32.6 0.7 collective-permute-start.7
  33.3 1.4 %collective-permute-start.9 = (bf16[64,1024]{1,0:T(8,128)(2,1)S(1)}, bf16[64,1024]{1,0:T(8,128)(2,1)S(1)}, u32[]{:S(2)}, u32[]{:S(2)}) collective-permute-start(bf16[64,1024]{1,0:T(8,128)(2,1)S(1)} %join.13), channel_id=1, source_target_pairs={{0,8},{2,10},{4,12},{6,14},{8,0},{10,2},{12,4},{14,6},{16,24},{18,... | collective-permute-start | bytes 393224 | tf_op jit(solution)/shard_map/ppermute | solution.py:36
  34.7 3.8 %collective-permute-done.7.rest_4_ = bf16[64,1024]{1,0:T(8,128)(2,1)S(1)} collective-permute-done((bf16[64,1024]{1,0:T(8,128)(2,1)S(1)}, bf16[64,1024]{1,0:T(8,128)(2,1)S(1)}, u32[]{:S(2)}, u32[]{:S(2)}) %collective-permute-start.7) | collective-permute-done | bytes 131104 | tf_op jit(solution)/shard_map/ppermute | solution.py:36
  38.5 0.0 collective-permute-start.8
  38.5 0.4 collective-permute-done.9.rest_4_
  39.0 0.1 collective-permute-start.10
  39.1 0.8 collective-permute-done.8.rest_5_
  39.9 0.0 collective-permute-done.5.rest_1_
  39.9 0.0 collective-permute-done.6.rest_3_
  39.9 0.0 copy-done.3
  39.9 6.1 %whiten.1 = (bf16[1024,2048]{1,0:T(8,128)(2,1)S(1)}, f32[16,2048]{1,0:T(8,128)S(1)}) custom-call(bf16[1024,2048]{1,0:T(8,128)(2,1)S(1)} %get-tuple-element.43.kt, bf16[8,1024]{1,0:T(8,128)(2,1)S(1)} %copy-done.3, bf16[512,1024]{1,0:T(8,128)(2,1)S(1)} %join.10.rest_0_, bf16[512,1024]{1,0:T(8,128)(2,1)S(1)} %collective-permute-done.5.rest_1_, ...), custom_call_target="tpu_custom_call" | custom-call | flops 4294967296 | bytes 10485760 | tf_op jit(solution)/shard_map/whiten/pallas_call | solution.py:429
  46.0 0.0 collective-permute-done.10.rest_5_
  46.1 4.1 %covary.1 = (bf16[1024,2048]{1,0:T(8,128)(2,1)S(1)}, f32[8,2304]{1,0:T(8,128)S(1)}) custom-call(bf16[1024,2048]{1,0:T(8,128)(2,1)S(1)} %get-tuple-element.46.ab, f32[16,2048]{1,0:T(8,128)S(1)} %get-tuple-element.47.stats, bf16[512,1024]{1,0:T(8,128)(2,1)S(1)} %join.10.rest_0_, bf16[512,1024]{1,0:T(8,128)(2,1)S(1)} %collective-permute-done.5.rest_1_, ...), custom_call_target="tpu_custom_call" | custom-call | flops 2147483648 | bytes 10485760 | tf_op jit(solution)/shard_map/covary/pallas_call | solution.py:444
  50.2 1.6 %collective-permute-start.11 = (f32[8,2304]{1,0:T(8,128)S(1)}, f32[8,2304]{1,0:T(8,128)S(1)}, u32[]{:S(2)}, u32[]{:S(2)}) collective-permute-start(f32[8,2304]{1,0:T(8,128)S(1)} %get-tuple-element.48.own), channel_id=1, source_target_pairs={{0,1},{1,0},{2,3},{3,2},{4,5},{5,4},{6,7},{7,6},{8,9},{9,8},{10,11... | collective-permute-start | bytes 221192 | tf_op jit(solution)/shard_map/ppermute | solution.py:36
  51.8 2.8 %collective-permute-done.11.other = f32[8,2304]{1,0:T(8,128)S(1)} collective-permute-done((f32[8,2304]{1,0:T(8,128)S(1)}, f32[8,2304]{1,0:T(8,128)S(1)}, u32[]{:S(2)}, u32[]{:S(2)}) %collective-permute-start.11) | collective-permute-done | bytes 73760 | tf_op jit(solution)/shard_map/ppermute | solution.py:36
  54.6 0.0 copy-done.6
  54.6 4.5 %slopes.1 = (f32[8,2048]{1,0:T(8,128)}, f32[8,1024]{1,0:T(8,128)S(1)}, f32[128,2560]{1,0:T(8,128)S(1)}, bf16[144,2560]{1,0:T(8,128)(2,1)S(1)}) custom-call(f32[8,2304]{1,0:T(8,128)S(1)} %get-tuple-element.48.own, f32[8,2304]{1,0:T(8,128)S(1)} %collective-permute-done.11.other, f32[8]{0:T(128)S(1)} %copy-done.6, s32[1,2048]{1,0:T(1,128)S(1)} %get-tuple-element.49.labels, ...), custom_call_target="tpu_custom_call" | custom-call | tf_op jit(solution)/shard_map/slopes/pallas_call | solution.py:468
  59.1 0.1 collective-permute-start.12
  59.2 2.2 %collective-permute-done.12.arrived = bf16[144,2560]{1,0:T(8,128)(2,1)S(1)} collective-permute-done((bf16[144,2560]{1,0:T(8,128)(2,1)S(1)}, bf16[144,2560]{1,0:T(8,128)(2,1)S(1)}, u32[]{:S(2)}, u32[]{:S(2)}) %collective-permute-start.12) | collective-permute-done | bytes 737312 | tf_op jit(solution)/shard_map/ppermute | solution.py:36
  61.4 0.2 add_pair.1
  61.6 0.1 add_level.3
  61.7 0.9 %collective-permute-start.13 = (bf16[80,1024]{1,0:T(8,128)(2,1)S(1)}, bf16[80,1024]{1,0:T(8,128)(2,1)S(1)}, u32[]{:S(2)}, u32[]{:S(2)}) collective-permute-start(bf16[80,1024]{1,0:T(8,128)(2,1)S(1)} %get-tuple-element.59), channel_id=1, source_target_pairs={{0,4},{2,6},{4,0},{6,2},{8,12},{10,14},{12,8},{14,10},{16,20},{18,... | collective-permute-start | bytes 491528 | tf_op jit(solution)/shard_map/ppermute | solution.py:36
  62.6 1.2 %collective-permute-start.14 = (bf16[128,1024]{1,0:T(8,128)(2,1)S(1)}, bf16[128,1024]{1,0:T(8,128)(2,1)S(1)}, u32[]{:S(2)}, u32[]{:S(2)}) collective-permute-start(bf16[128,1024]{1,0:T(8,128)(2,1)S(1)} %get-tuple-element.61), channel_id=1, source_target_pairs={{0,4},{2,6},{4,0},{6,2},{8,12},{10,14},{12,8},{14,10},{16,20},{18,... | collective-permute-start | bytes 786440 | tf_op jit(solution)/shard_map/ppermute | solution.py:36
  63.8 5.0 %collective-permute-done.13.refs_0_ = bf16[80,1024]{1,0:T(8,128)(2,1)S(1)} collective-permute-done((bf16[80,1024]{1,0:T(8,128)(2,1)S(1)}, bf16[80,1024]{1,0:T(8,128)(2,1)S(1)}, u32[]{:S(2)}, u32[]{:S(2)}) %collective-permute-start.13) | collective-permute-done | bytes 163872 | tf_op jit(solution)/shard_map/ppermute | solution.py:36
  68.8 1.3 %collective-permute-start.15 = (bf16[80,1024]{1,0:T(8,128)(2,1)S(1)}, bf16[80,1024]{1,0:T(8,128)(2,1)S(1)}, u32[]{:S(2)}, u32[]{:S(2)}) collective-permute-start(bf16[80,1024]{1,0:T(8,128)(2,1)S(1)} %get-tuple-element.62), channel_id=1, source_target_pairs={{0,8},{2,10},{4,12},{6,14},{8,0},{10,2},{12,4},{14,6},{16,24},{18,... | collective-permute-start | bytes 491528 | tf_op jit(solution)/shard_map/ppermute | solution.py:36
  70.2 3.4 %collective-permute-done.14.refs_0_ = bf16[128,1024]{1,0:T(8,128)(2,1)S(1)} collective-permute-done((bf16[128,1024]{1,0:T(8,128)(2,1)S(1)}, bf16[128,1024]{1,0:T(8,128)(2,1)S(1)}, u32[]{:S(2)}, u32[]{:S(2)}) %collective-permute-start.14) | collective-permute-done | bytes 262176 | tf_op jit(solution)/shard_map/ppermute | solution.py:36
  73.6 0.6 collective-permute-done.15.refs_1_
  74.2 0.1 add_level.5
  74.3 2.6 %collective-permute-start.17 = (bf16[80,1024]{1,0:T(8,128)(2,1)S(1)}, bf16[80,1024]{1,0:T(8,128)(2,1)S(1)}, u32[]{:S(2)}, u32[]{:S(2)}) collective-permute-start(bf16[80,1024]{1,0:T(8,128)(2,1)S(1)} %get-tuple-element.65), channel_id=1, source_target_pairs={{0,16},{2,18},{4,20},{6,22},{8,24},{10,26},{12,28},{14,30},{16,0},... | collective-permute-start | bytes 491528 | tf_op jit(solution)/shard_map/ppermute | solution.py:36
  76.9 0.8 collective-permute-start.16
  77.7 0.5 collective-permute-start.18
  78.3 3.6 %collective-permute-done.16.refs_0_ = bf16[64,1024]{1,0:T(8,128)(2,1)S(1)} collective-permute-done((bf16[64,1024]{1,0:T(8,128)(2,1)S(1)}, bf16[64,1024]{1,0:T(8,128)(2,1)S(1)}, u32[]{:S(2)}, u32[]{:S(2)}) %collective-permute-start.16) | collective-permute-done | bytes 131104 | tf_op jit(solution)/shard_map/ppermute | solution.py:36
  81.9 2.2 %collective-permute-done.18.refs_2_ = bf16[64,1024]{1,0:T(8,128)(2,1)S(1)} collective-permute-done((bf16[64,1024]{1,0:T(8,128)(2,1)S(1)}, bf16[64,1024]{1,0:T(8,128)(2,1)S(1)}, u32[]{:S(2)}, u32[]{:S(2)}) %collective-permute-start.18) | collective-permute-done | bytes 131104 | tf_op jit(solution)/shard_map/ppermute | solution.py:36
  84.1 0.0 collective-permute-done.17.refs_1_
  84.1 0.0 copy-done.1
  84.1 0.9 %finish.1 = (f32[64,1024]{1,0:T(8,128)}, f32[8,1024]{1,0:T(8,128)}) custom-call(f32[8,1024]{1,0:T(8,128)S(1)} %get-tuple-element.63.mean, f32[128,2560]{1,0:T(8,128)S(1)} %get-tuple-element.57.total, bf16[64,1024]{1,0:T(8,128)(2,1)S(1)} %copy-done.1, bf16[8,1024]{1,0:T(8,128)(2,1)S(1)} %copy-done.3, bf16[64,1024]{1,0:T(8,128)(2,1)S(1)} %collective-permute-done.16.refs_0_, ...), custom_call_target="tpu_custom_call" | custom-call | tf_op jit(solution)/shard_map/finish/pallas_call | solution.py:501
  (14 shorter events, 0.2 us)
Async XLA Ops:
  0.6 0.9 %copy-start = (bf16[64,1024]{1,0:T(8,128)(2,1)S(1)}, bf16[64,1024]{1,0:T(8,128)(2,1)}, u32[]{:S(2)}) copy-start(bf16[64,1024]{1,0:T(8,128)(2,1)} %chol.1) | copy-start | bytes 393220
  1.5 0.9 %copy-start.2 = (bf16[64,1024]{1,0:T(8,128)(2,1)S(1)}, bf16[64,1024]{1,0:T(8,128)(2,1)}, u32[]{:S(2)}) copy-start(bf16[64,1024]{1,0:T(8,128)(2,1)} %refs_0_.1) | copy-start | bytes 393220
  2.4 19.9 %copy-start.7 = (f32[2,1024]{1,0:T(2,128)S(1)}, f32[2,1024]{1,0:T(2,128)}, u32[]{:S(2)}) copy-start(f32[2,1024]{1,0:T(2,128)} %points_in.1) | copy-start | bytes 24580
  2.4 19.9 %copy-start.8 = (s32[1024]{0:T(1024)S(1)}, s32[1024]{0:T(1024)}, u32[]{:S(2)}) copy-start(s32[1024]{0:T(1024)} %param.14) | copy-start | bytes 12292
  2.4 20.0 %copy-start.9 = (f32[6,6]{1,0:T(8,128)S(1)}, f32[6,6]{1,0:T(8,128)}, u32[]{:S(2)}) copy-start(f32[6,6]{1,0:T(8,128)} %mix_in.1) | copy-start | bytes 436
  2.5 20.0 %copy-start.10 = (f32[2]{0:T(128)S(1)}, f32[2]{0:T(128)}, u32[]{:S(2)}) copy-start(f32[2]{0:T(128)} %lengthscales.1) | copy-start | bytes 28
  2.5 18.6 %collective-permute-start.2 = (bf16[128,1024]{1,0:T(8,128)(2,1)S(1)}, bf16[128,1024]{1,0:T(8,128)(2,1)S(1)}, u32[]{:S(2)}, u32[]{:S(2)}) collective-permute-start(bf16[128,1024]{1,0:T(8,128)(2,1)S(1)} %join.7.refs_0_), channel_id=1, source_target_pairs={{0,16},{2,18},{4,20},{6,22},{8,24},{10,26},{12,28},{14,30},{16,0},... | collective-permute-start | bytes 786440 | tf_op jit(solution)/shard_map/ppermute | solution.py:36
  6.6 14.5 %collective-permute-start.1 = (bf16[128,1024]{1,0:T(8,128)(2,1)S(1)}, bf16[128,1024]{1,0:T(8,128)(2,1)S(1)}, u32[]{:S(2)}, u32[]{:S(2)}) collective-permute-start(bf16[128,1024]{1,0:T(8,128)(2,1)S(1)} %join.7.refs_0_), channel_id=1, source_target_pairs={{0,8},{2,10},{4,12},{6,14},{8,0},{10,2},{12,4},{14,6},{16,24},{18,... | collective-permute-start | bytes 786440 | tf_op jit(solution)/shard_map/ppermute | solution.py:36
  8.2 12.9 %collective-permute-start = (bf16[128,1024]{1,0:T(8,128)(2,1)S(1)}, bf16[128,1024]{1,0:T(8,128)(2,1)S(1)}, u32[]{:S(2)}, u32[]{:S(2)}) collective-permute-start(bf16[128,1024]{1,0:T(8,128)(2,1)S(1)} %join.7.refs_0_), channel_id=1, source_target_pairs={{0,4},{2,6},{4,0},{6,2},{8,12},{10,14},{12,8},{14,10},{16,20},{18,... | collective-permute-start | bytes 786440 | tf_op jit(solution)/shard_map/ppermute | solution.py:36
  9.7 0.7 copy-start.4
  10.4 0.7 copy-start.5
  21.2 18.7 %copy-start.3 = (bf16[8,1024]{1,0:T(8,128)(2,1)S(1)}, bf16[8,1024]{1,0:T(8,128)(2,1)}, u32[]{:S(2)}) copy-start(bf16[8,1024]{1,0:T(8,128)(2,1)} %means.3) | copy-start | bytes 49156
  21.2 10.8 %collective-permute-start.4 = (bf16[192,1024]{1,0:T(8,128)(2,1)S(1)}, bf16[192,1024]{1,0:T(8,128)(2,1)S(1)}, u32[]{:S(2)}, u32[]{:S(2)}) collective-permute-start(bf16[192,1024]{1,0:T(8,128)(2,1)S(1)} %join.9), channel_id=1, source_target_pairs={{0,8},{2,10},{4,12},{6,14},{8,0},{10,2},{12,4},{14,6},{16,24},{18,... | collective-permute-start | bytes 1179656 | tf_op jit(solution)/shard_map/ppermute | solution.py:36
  21.9 10.5 %collective-permute-start.3 = (bf16[192,1024]{1,0:T(8,128)(2,1)S(1)}, bf16[192,1024]{1,0:T(8,128)(2,1)S(1)}, u32[]{:S(2)}, u32[]{:S(2)}) collective-permute-start(bf16[192,1024]{1,0:T(8,128)(2,1)S(1)} %join.8), channel_id=1, source_target_pairs={{0,4},{2,6},{4,0},{6,2},{8,12},{10,14},{12,8},{14,10},{16,20},{18,... | collective-permute-start | bytes 1179656 | tf_op jit(solution)/shard_map/ppermute | solution.py:36
  22.3 17.6 %collective-permute-start.5 = (bf16[512,1024]{1,0:T(8,128)(2,1)S(1)}, bf16[512,1024]{1,0:T(8,128)(2,1)S(1)}, u32[]{:S(2)}, u32[]{:S(2)}) collective-permute-start(bf16[512,1024]{1,0:T(8,128)(2,1)S(1)} %join.10.rest_0_), channel_id=1, source_target_pairs={{0,2},{2,0},{4,6},{6,4},{8,10},{10,8},{12,14},{14,12},{16,18},{18,... | collective-permute-start | bytes 3145736 | tf_op jit(solution)/shard_map/ppermute | solution.py:36
  32.5 7.4 %collective-permute-start.6 = (bf16[384,1024]{1,0:T(8,128)(2,1)S(1)}, bf16[384,1024]{1,0:T(8,128)(2,1)S(1)}, u32[]{:S(2)}, u32[]{:S(2)}) collective-permute-start(bf16[384,1024]{1,0:T(8,128)(2,1)S(1)} %join.11.rest_2_), channel_id=1, source_target_pairs={{0,2},{2,0},{4,6},{6,4},{8,10},{10,8},{12,14},{14,12},{16,18},{18,... | collective-permute-start | bytes 2359304 | tf_op jit(solution)/shard_map/ppermute | solution.py:36
  32.6 6.0 %collective-permute-start.7 = (bf16[64,1024]{1,0:T(8,128)(2,1)S(1)}, bf16[64,1024]{1,0:T(8,128)(2,1)S(1)}, u32[]{:S(2)}, u32[]{:S(2)}) collective-permute-start(bf16[64,1024]{1,0:T(8,128)(2,1)S(1)} %join.12), channel_id=1, source_target_pairs={{0,4},{2,6},{4,0},{6,2},{8,12},{10,14},{12,8},{14,10},{16,20},{18,... | collective-permute-start | bytes 393224 | tf_op jit(solution)/shard_map/ppermute | solution.py:36
  33.3 5.7 %collective-permute-start.9 = (bf16[64,1024]{1,0:T(8,128)(2,1)S(1)}, bf16[64,1024]{1,0:T(8,128)(2,1)S(1)}, u32[]{:S(2)}, u32[]{:S(2)}) collective-permute-start(bf16[64,1024]{1,0:T(8,128)(2,1)S(1)} %join.13), channel_id=1, source_target_pairs={{0,8},{2,10},{4,12},{6,14},{8,0},{10,2},{12,4},{14,6},{16,24},{18,... | collective-permute-start | bytes 393224 | tf_op jit(solution)/shard_map/ppermute | solution.py:36
  38.5 1.3 %collective-permute-start.8 = (bf16[64,1024]{1,0:T(8,128)(2,1)S(1)}, bf16[64,1024]{1,0:T(8,128)(2,1)S(1)}, u32[]{:S(2)}, u32[]{:S(2)}) collective-permute-start(bf16[64,1024]{1,0:T(8,128)(2,1)S(1)} %collective-permute-done.7.rest_4_), channel_id=1, source_target_pairs={{0,2},{2,0},{4,6},{6,4},{8,10},{10,8},{12,14},{14,12},{16,18},{18,... | collective-permute-start | bytes 393224 | tf_op jit(solution)/shard_map/ppermute | solution.py:36
  39.0 7.1 %collective-permute-start.10 = (bf16[64,1024]{1,0:T(8,128)(2,1)S(1)}, bf16[64,1024]{1,0:T(8,128)(2,1)S(1)}, u32[]{:S(2)}, u32[]{:S(2)}) collective-permute-start(bf16[64,1024]{1,0:T(8,128)(2,1)S(1)} %collective-permute-done.9.rest_4_), channel_id=1, source_target_pairs={{0,2},{2,0},{4,6},{6,4},{8,10},{10,8},{12,14},{14,12},{16,18},{18,... | collective-permute-start | bytes 393224 | tf_op jit(solution)/shard_map/ppermute | solution.py:36
  46.0 8.5 %copy-start.6 = (f32[8]{0:T(128)S(1)}, f32[8]{0:T(128)}, u32[]{:S(2)}) copy-start(f32[8]{0:T(128)} %scales.1) | copy-start | bytes 100
  50.2 4.4 %collective-permute-start.11 = (f32[8,2304]{1,0:T(8,128)S(1)}, f32[8,2304]{1,0:T(8,128)S(1)}, u32[]{:S(2)}, u32[]{:S(2)}) collective-permute-start(f32[8,2304]{1,0:T(8,128)S(1)} %get-tuple-element.48.own), channel_id=1, source_target_pairs={{0,1},{1,0},{2,3},{3,2},{4,5},{5,4},{6,7},{7,6},{8,9},{9,8},{10,11... | collective-permute-start | bytes 221192 | tf_op jit(solution)/shard_map/ppermute | solution.py:36
  59.1 25.0 %copy-start.1 = (bf16[64,1024]{1,0:T(8,128)(2,1)S(1)}, bf16[64,1024]{1,0:T(8,128)(2,1)}, u32[]{:S(2)}) copy-start(bf16[64,1024]{1,0:T(8,128)(2,1)} %chol.1) | copy-start | bytes 393220
  59.1 2.3 %collective-permute-start.12 = (bf16[144,2560]{1,0:T(8,128)(2,1)S(1)}, bf16[144,2560]{1,0:T(8,128)(2,1)S(1)}, u32[]{:S(2)}, u32[]{:S(2)}) collective-permute-start(bf16[144,2560]{1,0:T(8,128)(2,1)S(1)} %get-tuple-element.55), channel_id=1, source_target_pairs={{0,2},{2,0},{4,6},{6,4},{8,10},{10,8},{12,14},{14,12},{16,18},{18,... | collective-permute-start | bytes 2211848 | tf_op jit(solution)/shard_map/ppermute | solution.py:36
  61.7 7.1 %collective-permute-start.13 = (bf16[80,1024]{1,0:T(8,128)(2,1)S(1)}, bf16[80,1024]{1,0:T(8,128)(2,1)S(1)}, u32[]{:S(2)}, u32[]{:S(2)}) collective-permute-start(bf16[80,1024]{1,0:T(8,128)(2,1)S(1)} %get-tuple-element.59), channel_id=1, source_target_pairs={{0,4},{2,6},{4,0},{6,2},{8,12},{10,14},{12,8},{14,10},{16,20},{18,... | collective-permute-start | bytes 491528 | tf_op jit(solution)/shard_map/ppermute | solution.py:36
  62.6 11.1 %collective-permute-start.14 = (bf16[128,1024]{1,0:T(8,128)(2,1)S(1)}, bf16[128,1024]{1,0:T(8,128)(2,1)S(1)}, u32[]{:S(2)}, u32[]{:S(2)}) collective-permute-start(bf16[128,1024]{1,0:T(8,128)(2,1)S(1)} %get-tuple-element.61), channel_id=1, source_target_pairs={{0,4},{2,6},{4,0},{6,2},{8,12},{10,14},{12,8},{14,10},{16,20},{18,... | collective-permute-start | bytes 786440 | tf_op jit(solution)/shard_map/ppermute | solution.py:36
  68.8 5.4 %collective-permute-start.15 = (bf16[80,1024]{1,0:T(8,128)(2,1)S(1)}, bf16[80,1024]{1,0:T(8,128)(2,1)S(1)}, u32[]{:S(2)}, u32[]{:S(2)}) collective-permute-start(bf16[80,1024]{1,0:T(8,128)(2,1)S(1)} %get-tuple-element.62), channel_id=1, source_target_pairs={{0,8},{2,10},{4,12},{6,14},{8,0},{10,2},{12,4},{14,6},{16,24},{18,... | collective-permute-start | bytes 491528 | tf_op jit(solution)/shard_map/ppermute | solution.py:36
  74.3 9.8 %collective-permute-start.17 = (bf16[80,1024]{1,0:T(8,128)(2,1)S(1)}, bf16[80,1024]{1,0:T(8,128)(2,1)S(1)}, u32[]{:S(2)}, u32[]{:S(2)}) collective-permute-start(bf16[80,1024]{1,0:T(8,128)(2,1)S(1)} %get-tuple-element.65), channel_id=1, source_target_pairs={{0,16},{2,18},{4,20},{6,22},{8,24},{10,26},{12,28},{14,30},{16,0},... | collective-permute-start | bytes 491528 | tf_op jit(solution)/shard_map/ppermute | solution.py:36
  76.9 5.0 %collective-permute-start.16 = (bf16[64,1024]{1,0:T(8,128)(2,1)S(1)}, bf16[64,1024]{1,0:T(8,128)(2,1)S(1)}, u32[]{:S(2)}, u32[]{:S(2)}) collective-permute-start(bf16[64,1024]{1,0:T(8,128)(2,1)S(1)} %get-tuple-element.64), channel_id=1, source_target_pairs={{0,4},{2,6},{4,0},{6,2},{8,12},{10,14},{12,8},{14,10},{16,20},{18,... | collective-permute-start | bytes 393224 | tf_op jit(solution)/shard_map/ppermute | solution.py:36
  77.7 6.4 %collective-permute-start.18 = (bf16[64,1024]{1,0:T(8,128)(2,1)S(1)}, bf16[64,1024]{1,0:T(8,128)(2,1)S(1)}, u32[]{:S(2)}, u32[]{:S(2)}) collective-permute-start(bf16[64,1024]{1,0:T(8,128)(2,1)S(1)} %get-tuple-element.66), channel_id=1, source_target_pairs={{0,8},{2,10},{4,12},{6,14},{8,0},{10,2},{12,4},{14,6},{16,24},{18,... | collective-permute-start | bytes 393224 | tf_op jit(solution)/shard_map/ppermute | solution.py:36

commit v4 on v3

--- a/solution.py
+++ b/solution.py
@@ -95,12 +95,14 @@
         last = number == len(self.phases) - 1
         for part in [[key] for key in new] if last else [new]:
             group = join([self.pieces[key] for key in part], self.rows)
-            self.groups.append((part, group, swap(group, "obs", 1)))
+            self.groups.append((number, part, group, swap(group, "obs", 1)))
         return beside
 
-    def of(self, m):
+    def of(self, m, number=None):
         arrays, places = [], []
-        for new, *pair in self.groups:
+        for at, new, *pair in self.groups:
+            if number not in (None, at):
+                continue
             slots = [(slot, offset) for slot, (owner, offset) in enumerate(new) if owner == m]
             for core, array in enumerate(pair):
                 places += [(len(arrays), slot, offset ^ core) for slot, offset in slots]
@@ -173,9 +175,46 @@
         kt[j : j + step, :] = value.astype(bf16)
 
 
-def whiten_kernel(places, kt, means, *rest):
-    groups, (ab, stats, whole, turned) = rest[:-4], rest[-4:]
+def join_pairs(nz, number, places, groups, kt, factor, rows_of):
+    me = lax.axis_index("obs")
+    offsets = pair_offsets(nz, number)
+    size = factor.shape[0] // len(offsets) // 2
+    for source, slot, offset in places:
+        base = 2 * size * offsets.index(offset & -2)
+        target = pl.multiple_of(base + size * ((me ^ offset) & 1), size)
+        factor[pl.ds(target, size), :] = groups[source][size * slot : size * (slot + 1), :]
+    for i, offset in enumerate(offsets):
+        here = pl.ds(pl.multiple_of(2 * size * ((me ^ offset) // 2), 2 * size), 2 * size)
+        rows_of[2 * size * i : 2 * size * (i + 1), :] = kt[here, :]
+
+
+def pair_offsets(nz, number):
+    return ([0] if number == 0 else []) + phases_of(nz)[number]
+
+
+def whiten_kernel(nz, number, places, kt, *refs):
+    start = refs[:-4][0] if number > 0 else None
+    groups, (total, factor, turned, met) = refs[(number > 0) : -4], refs[-4:]
+    join_pairs(nz, number, places, groups, kt, factor, met)
+    turned[...] = factor[...].T
+
+    @pl.loop(0, ROWS_DEV // COL)
+    def _(step):
+        columns = pl.ds(pl.multiple_of(step * COL, COL), COL)
+        for k in range(0, turned.shape[0], 256):
+            part = dot(turned[k : k + 256, :], met[:, columns])
+            if number > 0:
+                part = part + start[k : k + 256, columns]
+            total[k : k + 256, columns] = part
+
+
+def covary_kernel(nz, last, last_places, places, kt, start, means, *refs):
+    ab, bt, sums, factor, last_turned, met, whole, turned = refs[-8:]
+    count = 1 + max(source for source, _, _ in last_places)
+    last_groups, groups = refs[:count], refs[count:-8]
     width = whole.shape[0]
+    join_pairs(nz, last, last_places, last_groups, kt, factor, met)
+    last_turned[...] = factor[...].T
     store_pieces(groups, places, whole)
     for j in range(0, width, 256):
         turned[:, j : j + 256] = whole[j : j + 256, :].T
@@ -185,35 +224,37 @@
         columns = pl.ds(pl.multiple_of(step * COL, COL), COL)
         square = jnp.zeros((1, COL), f32)
         for k in range(0, width, 256):
-            part = dot(turned[k : k + 256, :], kt[:, columns])
-            square = square + jnp.sum(part * part, axis=0, keepdims=True)
+            part = start[k : k + 256, columns] + dot(last_turned[k : k + 256, :], met[:, columns])
+            square = square - jnp.sum(part * part, axis=0, keepdims=True)
             ab[k : k + 256, columns] = part.astype(bf16)
-        stats[0:C, columns] = dot(means[...], ab[:, columns])
-        stats[C : 2 * C, columns] = jnp.broadcast_to(-square, (C, COL))
-
-
-def covary_kernel(places, ab, stats, *rest):
-    groups, (bt, sums, whole, turned) = rest[:-4], rest[-4:]
-    width = whole.shape[0]
-    store_pieces(groups, places, whole)
-    for j in range(0, width, 256):
-        turned[:, j : j + 256] = whole[j : j + 256, :].T
-
-    @pl.loop(0, ROWS_DEV // COL)
-    def _(step):
-        columns = pl.ds(pl.multiple_of(step * COL, COL), COL)
-        square = stats[C : C + 1, columns]
+        sums[:, columns] = dot(means[...], ab[:, columns])
         for l in range(0, width, 256):
             part = dot(turned[l : l + 256, l:], ab[l:, columns])
             square = square + jnp.sum(part * part, axis=0, keepdims=True)
             bt[l : l + 256, columns] = part.astype(bf16)
-        sums[:, columns] = stats[0:C, columns]
         piece = ROWS_DEV // C
         for i in range(COL // piece):
             sums[pl.ds((COL // piece) * step + i, 1), ROWS_DEV:] = square[:, piece * i : piece * (i + 1)]
 
 
-def slope_kernel(nz, own, other, scales, labels, self_cov, ab, bt, chances_out, mean, keep, send, heavy):
+def outer_rows(nz, x, ab, heavy, picked, keep, send):
+    core = lax.axis_index("obs") % 2
+    block = ab.shape[0] // nz
+    pair = block // 2
+    for z in range(nz):
+        picked[pair * z : pair * (z + 1), :] = ab[pl.ds(pl.multiple_of(block * z + pair * x, pair), pair), :]
+    for chunk in range(nz):
+        term = dot_nt(picked[pair * chunk :, :], heavy[block * chunk : block * (chunk + 1), :])
+        for z in range(chunk, nz):
+            left = block * (z * (z + 1) // 2 + chunk)
+            top = pair * (z - chunk)
+            even = term[top : top + pair // 2, :]
+            odd = term[top + pair // 2 : top + pair, :]
+            keep[:, left : left + block] = jnp.where(core == 0, even, odd)
+            send[: pair // 2, left : left + block] = jnp.where(core == 0, odd, even).astype(bf16)
+
+
+def slope_kernel(nz, own, other, scales, labels, self_cov, ab, bt, chances_out, mean, heavy, keep, send, picked):
     total = own[...] + other[...]
     variance = jnp.concatenate([total[i : i + 1, ROWS_DEV:] for i in range(C)], axis=1) + self_cov[...]
     classes = lax.broadcasted_iota(jnp.int32, (C, 1), 0)
@@ -226,24 +267,15 @@
     chances_out[...] = chances
     twice = -jnp.sum(chances * scale, axis=0, keepdims=True)
     slope = ((labels[...] == classes).astype(f32) - chances).astype(bf16)
-    core = lax.axis_index("obs") % 2
-    block = ab.shape[0] // nz
-    quarter = block // 4
-    for z in range(nz):
-        rows = slice(block * z, block * (z + 1))
-        heavy[rows, :] = (bt[rows, :].astype(f32) * twice).astype(bf16)
-        wide = block * (z + 1)
-        start = block * z * (z + 1) // 2
-        here = slice(start, start + wide)
-        term = dot_nt(ab[rows, :], heavy[:wide, :])
-        for x in range(2):
-            even = term[2 * quarter * x : 2 * quarter * x + quarter, :]
-            odd = term[2 * quarter * x + quarter : 2 * quarter * (x + 1), :]
-            keep[quarter * x : quarter * (x + 1), here] = jnp.where(core == 0, even, odd)
-            send[quarter * x : quarter * (x + 1), here] = jnp.where(core == 0, odd, even).astype(bf16)
+    heavy[...] = (bt[...].astype(f32) * twice).astype(bf16)
     value = dot_nt(slope, ab[...])
     mean[...] = value
-    send[2 * quarter :, : ab.shape[0]] = halves(value)
+    send[keep.shape[0] :, : ab.shape[0]] = halves(value)
+    outer_rows(nz, 1 - (lax.axis_index("obs") // 2) % 2, ab, heavy, picked, keep, send)
+
+
+def near_kernel(nz, ab, heavy, keep, send, picked):
+    outer_rows(nz, (lax.axis_index("obs") // 2) % 2, ab, heavy, picked, keep, send)
 
 
 def halves(value):
@@ -261,89 +293,100 @@
     mean_out[...] = mean[...] + joined(arrived[rows:, :width])
 
 
-def part_of(nz, total, width, offset):
-    target = lax.axis_index("obs") ^ offset
-    rows = total.shape[0] // 2
-    x, z = (target // 2) % 2, target // 4
+def near_pair_kernel(keep, arrived, total):
+    total[...] = keep[...] + arrived[...].astype(f32)
+
+
+def with_children(nz, totals, width, offset, children, refs):
+    total = totals[(offset // 2) % 2]
+    rows = total.shape[0]
+    z = (lax.axis_index("obs") ^ offset) // 4
     start = pl.multiple_of(width // nz * (z * (z + 1) // 2), width // nz)
-    return total[pl.ds(pl.multiple_of(rows * x, rows), rows), pl.ds(start, width)]
-
-
-def with_children(nz, total, width, offset, children, refs):
-    rows = total.shape[0] // 2
-    value = part_of(nz, total, width, offset)
+    value = total[:, pl.ds(start, width)]
     for source, slot in children:
         value = value + refs[source][rows * slot : rows * (slot + 1), :].astype(f32)
     return value
 
 
-def level_kernel(nz, plan, mean_from, mean, total, *refs):
+def mean_of(mean, refs, mean_from):
+    if mean_from is None:
+        return mean[...]
+    arrived = refs[mean_from]
+    if arrived.dtype == f32:
+        return mean[...] + arrived[...]
+    return mean[...] + joined(arrived[arrived.shape[0] - 2 * C :, :])
+
+
+def level_kernel(nz, plan, mean_from, mean, near, far, *refs):
     outs = refs[len(refs) - len(plan) - 1 :]
-    rows, width = total.shape[0] // 2, mean.shape[1]
-    value = mean[...]
-    if mean_from is not None:
-        value = value + joined(refs[mean_from][refs[mean_from].shape[0] - 2 * C :, :])
+    rows, width = far.shape[0], mean.shape[1]
+    value = mean_of(mean, refs, mean_from)
     outs[0][...] = value
     for out, (pieces, with_mean) in zip(outs[1:], plan):
         for i, (offset, children) in enumerate(pieces):
-            out[rows * i : rows * (i + 1), :] = with_children(nz, total, width, offset, children, refs).astype(bf16)
+            part = with_children(nz, (near, far), width, offset, children, refs)
+            out[rows * i : rows * (i + 1), :] = part.astype(bf16)
         if with_mean:
             out[rows * len(pieces) :, :] = halves(value)
 
 
+def index_in(arrays, array):
+    for i, other in enumerate(arrays):
+        if other is array:
+            return i
+    arrays.append(array)
+    return len(arrays) - 1
+
+
 class Scatter:
-    def __init__(self, nz, mean, total):
-        self.nz, self.mean, self.total = nz, mean, total
+    def __init__(self, nz, mean):
+        self.nz, self.mean = nz, mean
         self.arrived = {}
         self.mean_from = None
 
     def children(self, offset, arrays):
-        found = []
-        for child, (array, slot) in self.arrived.items():
-            if child ^ (child & -child) == offset:
-                if not any(array is other for other in arrays):
-                    arrays.append(array)
-                found.append(([array is other for other in arrays].index(True), slot))
-        return found
-
-    def level(self, sends, mean_bit):
+        return [
+            (index_in(arrays, array), slot)
+            for child, (array, slot) in self.arrived.items()
+            if child ^ (child & -child) == offset
+        ]
+
+    def level(self, near, far, sends, mean_bit):
         arrays = []
-        plan = [([(o, self.children(o, arrays)) for o in offsets], offsets[0] & -offsets[0] == mean_bit and i == 0)
-                for i, offsets in enumerate(sends)]
-        mean_from = None
-        if self.mean_from is not None:
-            if not any(self.mean_from is other for other in arrays):
-                arrays.append(self.mean_from)
-            mean_from = [self.mean_from is other for other in arrays].index(True)
-        rows, width = self.total.shape[0] // 2, self.mean.shape[1]
+        plan = [
+            ([(o, self.children(o, arrays)) for o in offsets], offsets[0] & -offsets[0] == mean_bit)
+            for offsets in sends
+        ]
+        mean_from = None if self.mean_from is None else index_in(arrays, self.mean_from)
+        rows, width = far.shape[0], self.mean.shape[1]
         self.mean, *outs = pl.pallas_call(
             functools.partial(level_kernel, self.nz, plan, mean_from),
             out_shape=[jax.ShapeDtypeStruct(self.mean.shape, f32)]
             + [jax.ShapeDtypeStruct((rows * len(pieces) + 2 * C * m, width), bf16) for pieces, m in plan],
-            in_specs=[VMEM] * (2 + len(arrays)),
+            in_specs=[VMEM] * (3 + len(arrays)),
             out_specs=[VMEM] * (1 + len(plan)),
             compiler_params=SMALL,
             name="add_level",
-        )(self.mean, self.total, *arrays)
-        for i, (offsets, out) in enumerate(zip(sends, outs)):
+        )(self.mean, near, far, *arrays)
+        for (pieces, with_mean), out in zip(plan, outs):
+            offsets = [offset for offset, _ in pieces]
             out = swap(out, "obs", offsets[0] & -offsets[0])
             self.arrived.update({offset: (out, slot) for slot, offset in enumerate(offsets)})
-            if i == 0:
+            if with_mean:
                 self.mean_from = out
 
 
-def finish_kernel(nz, children, mean_from, mean, total, chol, means, *refs):
+def finish_kernel(nz, children, mean_from, mean, near, chol, means, *refs):
     grad_chol, grad_mean = refs[-2:]
     rows, width = chol.shape
-    value = with_children(nz, total, width, 0, children, refs)
+    value = with_children(nz, (near, near), width, 0, children, refs)
     row_ids = lax.axis_index("obs") * rows + lax.broadcasted_iota(jnp.int32, (rows, width), 0)
     column_ids = lax.broadcasted_iota(jnp.int32, (rows, width), 1)
     own = chol[...].astype(f32)
     on_diag = column_ids == row_ids
     inverse = 1.0 / jnp.where(on_diag, own, 1.0)
     grad_chol[...] = jnp.where(column_ids <= row_ids, value, 0.0) - own + jnp.where(on_diag, inverse, 0.0)
-    summed = mean[...] + joined(refs[mean_from][rows:, :])
-    grad_mean[...] = summed - means[...].astype(f32)
+    grad_mean[...] = mean_of(mean, refs, mean_from) - means[...].astype(f32)
 
 
 def route(obs_coords, obs_codes, route_plan):
@@ -420,42 +463,60 @@
         ),
         name="kernel_rows",
     )(arrived, inducing_coords, inducing_bands[None, :], band_mix, lengthscales)
-    kt, labels, self_cov = gather.phase(1, cover)
-    for number in range(2, len(gather.phases)):
-        gather.phase(number)
-    prior_arrays, prior_places = gather.of(0)
+
+    def whiten(number, kt, *start):
+        arrays, places = gather.of(0, number)
+        inner = 2 * rows * len(pair_offsets(nz, number))
+        return pl.pallas_call(
+            functools.partial(whiten_kernel, nz, number, places),
+            out_shape=jax.ShapeDtypeStruct((width, ROWS_DEV), f32),
+            in_specs=[VMEM] * (1 + len(start) + len(arrays)),
+            out_specs=VMEM,
+            scratch_shapes=[
+                pltpu.VMEM((inner, width), bf16),
+                pltpu.VMEM((width, inner), bf16),
+                pltpu.VMEM((inner, ROWS_DEV), bf16),
+            ],
+            input_output_aliases={1: 0} if start else {},
+            compiler_params=big,
+            cost_estimate=pl.CostEstimate(
+                flops=2 * width * inner * ROWS_DEV, bytes_accessed=10 * 1024 * 1024, transcendentals=0
+            ),
+            name="whiten",
+        )(kt, *start, *arrays)
+
+    def cover_and_whiten():
+        kt, labels, self_cov = cover()
+        return kt, labels, self_cov, whiten(0, kt)
+
+    kt, labels, self_cov, whitened = gather.phase(1, cover_and_whiten)
+    last = len(gather.phases) - 1
+    for number in range(2, last + 1):
+        whitened = gather.phase(number, lambda: whiten(number - 1, kt, whitened))
+    last_arrays, last_places = gather.of(0, last)
     chol_arrays, chol_places = gather.of(1)
-    whole = [pltpu.VMEM((width, width), bf16), pltpu.VMEM((width, width), bf16)]
-    ab, part_stats = pl.pallas_call(
-        functools.partial(whiten_kernel, prior_places),
+    ab, bt, sums = pl.pallas_call(
+        functools.partial(covary_kernel, nz, last, last_places, chol_places),
         out_shape=(
             jax.ShapeDtypeStruct((width, ROWS_DEV), bf16),
-            jax.ShapeDtypeStruct((2 * C, ROWS_DEV), f32),
-        ),
-        in_specs=[VMEM] * (2 + len(prior_arrays)),
-        out_specs=(VMEM, VMEM),
-        scratch_shapes=whole,
-        compiler_params=big,
-        cost_estimate=pl.CostEstimate(
-            flops=2 * width * width * ROWS_DEV, bytes_accessed=10 * 1024 * 1024, transcendentals=0
-        ),
-        name="whiten",
-    )(kt, variational_mean, *prior_arrays)
-    bt, sums = pl.pallas_call(
-        functools.partial(covary_kernel, chol_places),
-        out_shape=(
             jax.ShapeDtypeStruct((width, ROWS_DEV), bf16),
             jax.ShapeDtypeStruct((C, ROWS_DEV + ROWS_DEV // C), f32),
         ),
-        in_specs=[VMEM] * (2 + len(chol_arrays)),
-        out_specs=(VMEM, VMEM),
-        scratch_shapes=whole,
+        in_specs=[VMEM] * (3 + len(last_arrays) + len(chol_arrays)),
+        out_specs=(VMEM, VMEM, VMEM),
+        scratch_shapes=[
+            pltpu.VMEM((2 * rows, width), bf16),
+            pltpu.VMEM((width, 2 * rows), bf16),
+            pltpu.VMEM((2 * rows, ROWS_DEV), bf16),
+            pltpu.VMEM((width, width), bf16),
+            pltpu.VMEM((width, width), bf16),
+        ],
         compiler_params=big,
         cost_estimate=pl.CostEstimate(
             flops=width * width * ROWS_DEV, bytes_accessed=10 * 1024 * 1024, transcendentals=0
         ),
         name="covary",
-    )(ab, part_stats, *chol_arrays)
+    )(kt, whitened, variational_mean, *last_arrays, *chol_arrays)
 
     other = swap(sums, "ind", 1)
     bit = 2
@@ -465,39 +526,61 @@
         bit *= 2
 
     packed = width // nz * (nz * (nz + 1) // 2)
-    chances, mean, keep, send = pl.pallas_call(
+    kept = jax.ShapeDtypeStruct((rows, packed), f32)
+    chances, mean, heavy, keep, send = pl.pallas_call(
         functools.partial(slope_kernel, nz),
         out_shape=[
             jax.ShapeDtypeStruct((C, ROWS_DEV), f32),
             jax.ShapeDtypeStruct((C, width), f32),
-            jax.ShapeDtypeStruct((2 * rows, packed), f32),
-            jax.ShapeDtypeStruct((2 * rows + 2 * C, packed), bf16),
+            jax.ShapeDtypeStruct((width, ROWS_DEV), bf16),
+            kept,
+            jax.ShapeDtypeStruct((rows + 2 * C, packed), bf16),
         ],
         in_specs=[VMEM, VMEM, SMEM] + [VMEM] * 4,
-        out_specs=[VMEM] * 4,
-        scratch_shapes=[pltpu.VMEM((width, ROWS_DEV), bf16)],
+        out_specs=[VMEM] * 5,
+        scratch_shapes=[pltpu.VMEM((width // 2, ROWS_DEV), bf16)],
         compiler_params=big,
         name="slopes",
     )(sums, other, class_scales, labels, self_cov, ab, bt)
-    mean, total = pl.pallas_call(
+    near_keep, near_send = pl.pallas_call(
+        functools.partial(near_kernel, nz),
+        out_shape=[kept, jax.ShapeDtypeStruct((rows, packed), bf16)],
+        in_specs=[VMEM] * 2,
+        out_specs=[VMEM] * 2,
+        scratch_shapes=[pltpu.VMEM((width // 2, ROWS_DEV), bf16)],
+        compiler_params=big,
+        name="near_outer",
+    )(ab, heavy)
+    mean, far = pl.pallas_call(
         pair_kernel,
-        out_shape=[jax.ShapeDtypeStruct(mean.shape, f32), jax.ShapeDtypeStruct(keep.shape, f32)],
+        out_shape=[jax.ShapeDtypeStruct(mean.shape, f32), kept],
         in_specs=[VMEM] * 3,
         out_specs=[VMEM] * 2,
         compiler_params=SMALL,
         name="add_pair",
     )(mean, keep, swap(send, "obs", 1))
-    scatter = Scatter(nz, mean, total)
+    near = pl.pallas_call(
+        near_pair_kernel,
+        out_shape=kept,
+        in_specs=[VMEM] * 2,
+        out_specs=VMEM,
+        compiler_params=SMALL,
+        name="add_near_pair",
+    )(near_keep, swap(near_send, "obs", 1))
+    scatter = Scatter(nz, mean)
     along_x = [o for phase in reversed(gather.phases) for o in phase if o & 2]
-    scatter.level([along_x[:1], along_x[1:-1], along_x[-1:]], 2)
+    scatter.level(far, far, [along_x[:1], along_x[1:-1]], None)
+    scatter.mean_from = swap(scatter.mean, "obs", 2 * nz)
     along_z = [[o for o in phase if not o & 2] for phase in gather.phases]
     along_z = [phase for phase in along_z if phase]
     for i, phase in enumerate(reversed(along_z)):
         bits = sorted({o & -o for o in phase}, reverse=True)
-        scatter.level([[o for o in phase if o & -o == bit] for bit in bits], 4 << i)
+        sends = [[o for o in phase if o & -o == bit] for bit in bits]
+        last_step = i == len(along_z) - 1
+        scatter.level(near, far, sends + [along_x[-1:]] * last_step, 2 if last_step else 4 << i)
     arrays = []
     children = scatter.children(0, arrays)
-    mean_from = [scatter.mean_from is array for array in arrays].index(True)
+    mean_from = index_in(arrays, scatter.mean_from)
     grad_chol, grad_mean = pl.pallas_call(
         functools.partial(finish_kernel, nz, children, mean_from),
         out_shape=(
@@ -508,7 +591,7 @@
         out_specs=(VMEM, VMEM),
         compiler_params=SMALL,
         name="finish",
-    )(scatter.mean, total, variational_chol, variational_mean, *arrays)
+    )(scatter.mean, near, variational_chol, variational_mean, *arrays)
     return (chances, grad_chol, grad_mean)
 
 

time: 85.3 us -> 81 us (0.950)
  waiting for transfers between devices: 30.3 us -> 22.1 us
  Pallas kernels: 21.1 us -> 23.6 us
  starting transfers between devices: 19.6 us -> 20.8 us
    ppermute x19 -> x21, waiting for transfers between devices: 30.3 us -> 22.1 us  [swap(): return lax.ppermute(value, axis, [(i, i ^ bit) for i in range(size)])]
    pallas_call x2 -> x5, Pallas kernels: 10.3 us -> 13.7 us  [the longest x1 5.99 us: body(): pl.pallas_call(functools.partial(covary_kernel, nz, last, last_places, ch...]
    ppermute x19 -> x21, starting transfers between devices: 19.6 us -> 20.8 us  [swap(): return lax.ppermute(value, axis, [(i, i ^ bit) for i in range(size)])]
  transfers between devices with their start and end apart: 19 -> 21, of which waited for: 12 -> 13; matrix products, arithmetic and copies ran while one was open for 0% -> 0% of each run, Pallas kernels for 13% -> 16%
where the time goes in v4:
time: 81 us; the launch traced here: 80.7 us
  Pallas kernels  23.6 us (29%)
  waiting for transfers between devices  22.1 us (27%)
  starting transfers between devices  20.8 us (26%)
  blocking collectives  9.96 us (12%)
  local copies, waits for them, and re-layouts  3.25 us (4%)
  between operations  0.85 us (1%)
    ppermute x21, waiting for transfers between devices, swap(): return lax.ppermute(value, axis, [(i, i ^ bit) for i in range(size)])  22.1 us
    ppermute x21, starting transfers between devices, swap(): return lax.ppermute(value, axis, [(i, i ^ bit) for i in range(size)])  20.8 us
    all_to_all x1, blocking collectives, route(): lax.all_to_all(stacked, 'obs', split_axis=1, concat_axis=1, tiled=True)  9.96 us
    pallas_call x1, Pallas kernels, body(): pl.pallas_call(functools.partial(covary_kernel, nz, last, last_places, ch...  5.99 us
    pallas_call x2, Pallas kernels, whiten(): pl.pallas_call(functools.partial(whiten_kernel, nz, number, places), out_...  5.92 us
    pallas_call x1, Pallas kernels, body(): pl.pallas_call(kernel_rows_kernel, out_shape=(jax.ShapeDtypeStruct((width...  4.75 us
    pallas_call x1, Pallas kernels, body(): pl.pallas_call(functools.partial(slope_kernel, nz), out_shape=[jax.ShapeD...  3.83 us
    unnamed x22, local copies, waits for them, and re-layouts  3.25 us
  transfers between devices with their start and end apart: 21, of which 13 were waited for; matrix products, arithmetic and copies ran while one was open for 0% of the time, Pallas kernels for 16%

profile of v4, /device:TPU:0, one launch (start us, length us, event | category | flops | bytes accessed | tf_op | source)
XLA Modules:
  0.0 80.7 jit_solution(14054464602005244121)
XLA Ops:
  0.6 0.0 copy-start
  0.6 0.9 %copy-done = bf16[64,1024]{1,0:T(8,128)(2,1)S(1)} copy-done((bf16[64,1024]{1,0:T(8,128)(2,1)S(1)}, bf16[64,1024]{1,0:T(8,128)(2,1)}, u32[]{:S(2)}) %copy-start) | copy-done | bytes 131096
  1.5 0.9 %copy-done.2 = bf16[64,1024]{1,0:T(8,128)(2,1)S(1)} copy-done((bf16[64,1024]{1,0:T(8,128)(2,1)S(1)}, bf16[64,1024]{1,0:T(8,128)(2,1)}, u32[]{:S(2)}) %copy-start.2) | copy-done | bytes 131096
  2.5 4.1 %collective-permute-start.2 = (bf16[128,1024]{1,0:T(8,128)(2,1)S(1)}, bf16[128,1024]{1,0:T(8,128)(2,1)S(1)}, u32[]{:S(2)}, u32[]{:S(2)}) collective-permute-start(bf16[128,1024]{1,0:T(8,128)(2,1)S(1)} %join.7.refs_0_), channel_id=1, source_target_pairs={{0,16},{2,18},{4,20},{6,22},{8,24},{10,26},{12,28},{14,30},{16,0},... | collective-permute-start | bytes 786440 | tf_op jit(solution)/shard_map/ppermute | solution.py:36
  6.6 1.6 %collective-permute-start.1 = (bf16[128,1024]{1,0:T(8,128)(2,1)S(1)}, bf16[128,1024]{1,0:T(8,128)(2,1)S(1)}, u32[]{:S(2)}, u32[]{:S(2)}) collective-permute-start(bf16[128,1024]{1,0:T(8,128)(2,1)S(1)} %join.7.refs_0_), channel_id=1, source_target_pairs={{0,8},{2,10},{4,12},{6,14},{8,0},{10,2},{12,4},{14,6},{16,24},{18,... | collective-permute-start | bytes 786440 | tf_op jit(solution)/shard_map/ppermute | solution.py:36
  8.2 1.5 %collective-permute-start = (bf16[128,1024]{1,0:T(8,128)(2,1)S(1)}, bf16[128,1024]{1,0:T(8,128)(2,1)S(1)}, u32[]{:S(2)}, u32[]{:S(2)}) collective-permute-start(bf16[128,1024]{1,0:T(8,128)(2,1)S(1)} %join.7.refs_0_), channel_id=1, source_target_pairs={{0,4},{2,6},{4,0},{6,2},{8,12},{10,14},{12,8},{14,10},{16,20},{18,... | collective-permute-start | bytes 786440 | tf_op jit(solution)/shard_map/ppermute | solution.py:36
  9.7 0.7 copy-done.4
  10.4 0.7 copy-done.5
  11.1 10.0 %all_to_all.12 = f32[3,16,128]{2,0,1:T(4,128)S(1)} all-to-all(f32[3,16,128]{2,0,1:T(4,128)S(1)} %bitcast.4), channel_id=1, replica_groups=mesh['obs'=16,'ind'=2] {'obs'}, dimensions={1} | all-to-all | bytes 49152 | tf_op jit(solution)/shard_map/all_to_all | solution.py:408
  21.1 0.0 collective-permute-done.2.refs_0_.refs_3_
  21.1 0.0 collective-permute-done.1.refs_1_.refs_2_
  21.1 0.0 collective-permute-done.refs_1_
  21.1 0.1 join.10.refs_0_.refs_2_
  21.2 0.1 collective-permute-start.5
  21.3 0.7 collective-permute-start.4
  22.1 0.5 collective-permute-start.3
  22.5 4.7 %kernel_rows.1 = (bf16[1024,2048]{1,0:T(8,128)(2,1)S(1)}, s32[1,2048]{1,0:T(1,128)S(1)}, f32[1,2048]{1,0:T(1,128)S(1)}) custom-call(f32[3,2048]{1,0:T(4,128)S(1)} %bitcast.5, f32[2,1024]{1,0:T(2,128)S(1)} %copy-done.7, s32[1,1024]{1,0:T(1,128)S(1)} %bitcast.7, f32[6,6]{1,0:T(8,128)S(1)} %copy-done.9, f32[2]{0:T(128)S(1)} %copy-done.10), custom_call_target="tpu_custom_call" | custom-call | flops 41943040 | bytes 4194304 | tf_op jit(solution)/shard_map/kernel_rows/pallas_call | solution.py:445
  27.3 0.0 collective-permute-done.5.refs_1_.refs_3_
  27.3 3.0 %whiten.2.refs_0_ = f32[1024,2048]{1,0:T(8,128)S(1)} custom-call(bf16[1024,2048]{1,0:T(8,128)(2,1)S(1)} %get-tuple-element.49.kt, bf16[512,1024]{1,0:T(8,128)(2,1)S(1)} %join.10.refs_0_.refs_2_, bf16[512,1024]{1,0:T(8,128)(2,1)S(1)} %collective-permute-done.5.refs_1_.refs_3_), custom_call_target="tpu_custom_call" | custom-call | flops 2147483648 | bytes 10485760 | tf_op jit(solution)/shard_map/whiten/pallas_call | solution.py:470
  30.3 2.6 %collective-permute-done.4.refs_0_.refs_1_ = bf16[192,1024]{1,0:T(8,128)(2,1)S(1)} collective-permute-done((bf16[192,1024]{1,0:T(8,128)(2,1)S(1)}, bf16[192,1024]{1,0:T(8,128)(2,1)S(1)}, u32[]{:S(2)}, u32[]{:S(2)}) %collective-permute-start.4) | collective-permute-done | bytes 393248 | tf_op jit(solution)/shard_map/ppermute | solution.py:36
  32.9 0.4 collective-permute-done.3.refs_0_
  33.3 0.1 join.13.refs_1_.refs_4_
  33.3 0.1 collective-permute-start.8
  33.5 0.0 copy-start.3
  33.5 1.4 %collective-permute-start.7 = (bf16[64,1024]{1,0:T(8,128)(2,1)S(1)}, bf16[64,1024]{1,0:T(8,128)(2,1)S(1)}, u32[]{:S(2)}, u32[]{:S(2)}) collective-permute-start(bf16[64,1024]{1,0:T(8,128)(2,1)S(1)} %join.12), channel_id=1, source_target_pairs={{0,8},{2,10},{4,12},{6,14},{8,0},{10,2},{12,4},{14,6},{16,24},{18,... | collective-permute-start | bytes 393224 | tf_op jit(solution)/shard_map/ppermute | solution.py:36
  34.9 0.3 collective-permute-start.6
  35.2 0.5 collective-permute-done.8.refs_2_.refs_5_
  35.7 2.9 %whiten.3.start = f32[1024,2048]{1,0:T(8,128)S(1)} custom-call(bf16[1024,2048]{1,0:T(8,128)(2,1)S(1)} %get-tuple-element.49.kt, f32[1024,2048]{1,0:T(8,128)S(1)} %whiten.2.refs_0_, bf16[384,1024]{1,0:T(8,128)(2,1)S(1)} %join.13.refs_1_.refs_4_, bf16[384,1024]{1,0:T(8,128)(2,1)S(1)} %collective-permute-done.8.refs_2_.refs_5_), custom_call_target="tpu_custom_call", output_to_operand_aliasing={{}: (1, {})} | custom-call | flops 1610612736 | bytes 10485760 | tf_op jit(solution)/shard_map/whiten/pallas_call | solution.py:470
  38.6 0.0 copy-start.6
  38.6 0.8 collective-permute-done.7.refs_6_
  39.4 1.1 %collective-permute-done.6.refs_0_ = bf16[64,1024]{1,0:T(8,128)(2,1)S(1)} collective-permute-done((bf16[64,1024]{1,0:T(8,128)(2,1)S(1)}, bf16[64,1024]{1,0:T(8,128)(2,1)S(1)}, u32[]{:S(2)}, u32[]{:S(2)}) %collective-permute-start.6) | collective-permute-done | bytes 131104 | tf_op jit(solution)/shard_map/ppermute | solution.py:36
  40.5 0.0 collective-permute-start.9
  40.5 0.5 collective-permute-start.10
  41.0 0.8 %collective-permute-done.9.refs_1_ = bf16[64,1024]{1,0:T(8,128)(2,1)S(1)} collective-permute-done((bf16[64,1024]{1,0:T(8,128)(2,1)S(1)}, bf16[64,1024]{1,0:T(8,128)(2,1)S(1)}, u32[]{:S(2)}, u32[]{:S(2)}) %collective-permute-start.9) | collective-permute-done | bytes 131104 | tf_op jit(solution)/shard_map/ppermute | solution.py:36
  41.8 0.2 collective-permute-done.10.refs_7_
  42.0 6.0 %covary.1 = (bf16[1024,2048]{1,0:T(8,128)(2,1)S(1)}, bf16[1024,2048]{1,0:T(8,128)(2,1)S(1)}, f32[8,2304]{1,0:T(8,128)S(1)}) custom-call(bf16[1024,2048]{1,0:T(8,128)(2,1)S(1)} %get-tuple-element.49.kt, f32[1024,2048]{1,0:T(8,128)S(1)} %whiten.3.start, bf16[8,1024]{1,0:T(8,128)(2,1)S(1)} %copy-done.3, bf16[64,1024]{1,0:T(8,128)(2,1)S(1)} %collective-permute-done.6.refs_0_, ...), custom_call_target="tpu_custom_call" | custom-call | flops 2147483648 | bytes 10485760 | tf_op jit(solution)/shard_map/covary/pallas_call | solution.py:498
  48.0 1.6 %collective-permute-start.11 = (f32[8,2304]{1,0:T(8,128)S(1)}, f32[8,2304]{1,0:T(8,128)S(1)}, u32[]{:S(2)}, u32[]{:S(2)}) collective-permute-start(f32[8,2304]{1,0:T(8,128)S(1)} %get-tuple-element.56.own), channel_id=1, source_target_pairs={{0,1},{1,0},{2,3},{3,2},{4,5},{5,4},{6,7},{7,6},{8,9},{9,8},{10,11... | collective-permute-start | bytes 221192 | tf_op jit(solution)/shard_map/ppermute | solution.py:36
  49.6 3.0 %collective-permute-done.11.other = f32[8,2304]{1,0:T(8,128)S(1)} collective-permute-done((f32[8,2304]{1,0:T(8,128)S(1)}, f32[8,2304]{1,0:T(8,128)S(1)}, u32[]{:S(2)}, u32[]{:S(2)}) %collective-permute-start.11) | collective-permute-done | bytes 73760 | tf_op jit(solution)/shard_map/ppermute | solution.py:36
  52.6 3.8 %slopes.1 = (f32[8,2048]{1,0:T(8,128)}, f32[8,1024]{1,0:T(8,128)S(1)}, bf16[1024,2048]{1,0:T(8,128)(2,1)S(1)}, f32[64,2560]{1,0:T(8,128)S(1)}, bf16[80,2560]{1,0:T(8,128)(2,1)S(1)}) custom-call(f32[8,2304]{1,0:T(8,128)S(1)} %get-tuple-element.56.own, f32[8,2304]{1,0:T(8,128)S(1)} %collective-permute-done.11.other, f32[8]{0:T(128)S(1)} %copy-done.6, ...), custom_call_target="tpu_custom_call" | custom-call | tf_op jit(solution)/shard_map/slopes/pallas_call | solution.py:530
  56.4 0.0 collective-permute-start.12
  56.4 1.7 %near_outer.1 = (f32[64,2560]{1,0:T(8,128)S(1)}, bf16[64,2560]{1,0:T(8,128)(2,1)S(1)}) custom-call(bf16[1024,2048]{1,0:T(8,128)(2,1)S(1)} %get-tuple-element.59.ab, bf16[1024,2048]{1,0:T(8,128)(2,1)S(1)} %get-tuple-element.68.heavy), custom_call_target="tpu_custom_call" | custom-call | tf_op jit(solution)/shard_map/near_outer/pallas_call | solution.py:545
  58.1 0.0 copy-start.1
  58.2 0.6 collective-permute-start.13
  58.7 0.0 collective-permute-done.12.arrived
  58.7 0.1 add_pair.1
  58.8 0.1 add_level.3
  58.9 0.4 collective-permute-start.14
  59.3 1.7 %collective-permute-start.16 = (bf16[128,1024]{1,0:T(8,128)(2,1)S(1)}, bf16[128,1024]{1,0:T(8,128)(2,1)S(1)}, u32[]{:S(2)}, u32[]{:S(2)}) collective-permute-start(bf16[128,1024]{1,0:T(8,128)(2,1)S(1)} %get-tuple-element.73), channel_id=1, source_target_pairs={{0,4},{2,6},{4,0},{6,2},{8,12},{10,14},{12,8},{14,10},{16,20},{18,... | collective-permute-start | bytes 786440 | tf_op jit(solution)/shard_map/ppermute | solution.py:36
  61.0 1.7 %collective-permute-start.15 = (f32[8,1024]{1,0:T(8,128)S(1)}, f32[8,1024]{1,0:T(8,128)S(1)}, u32[]{:S(2)}, u32[]{:S(2)}) collective-permute-start(f32[8,1024]{1,0:T(8,128)S(1)} %get-tuple-element.67.mean), channel_id=1, source_target_pairs={{0,16},{2,18},{4,20},{6,22},{8,24},{10,26},{12,28},{14,30},{16,0},... | collective-permute-start | bytes 98312 | tf_op jit(solution)/shard_map/ppermute | solution.py:36
  62.7 0.0 collective-permute-done.13.arrived
  62.7 0.1 add_near_pair.1.near
  62.8 3.4 %collective-permute-done.15.refs_1_ = f32[8,1024]{1,0:T(8,128)S(1)} collective-permute-done((f32[8,1024]{1,0:T(8,128)S(1)}, f32[8,1024]{1,0:T(8,128)S(1)}, u32[]{:S(2)}, u32[]{:S(2)}) %collective-permute-start.15) | collective-permute-done | bytes 32800 | tf_op jit(solution)/shard_map/ppermute | solution.py:36
  66.1 0.0 collective-permute-done.14.refs_0_
  66.2 0.5 collective-permute-start.17
  66.7 3.3 %collective-permute-done.16.refs_0_ = bf16[128,1024]{1,0:T(8,128)(2,1)S(1)} collective-permute-done((bf16[128,1024]{1,0:T(8,128)(2,1)S(1)}, bf16[128,1024]{1,0:T(8,128)(2,1)S(1)}, u32[]{:S(2)}, u32[]{:S(2)}) %collective-permute-start.16) | collective-permute-done | bytes 262176 | tf_op jit(solution)/shard_map/ppermute | solution.py:36
  70.0 1.6 %collective-permute-done.17.refs_1_ = bf16[80,1024]{1,0:T(8,128)(2,1)S(1)} collective-permute-done((bf16[80,1024]{1,0:T(8,128)(2,1)S(1)}, bf16[80,1024]{1,0:T(8,128)(2,1)S(1)}, u32[]{:S(2)}, u32[]{:S(2)}) %collective-permute-start.17) | collective-permute-done | bytes 163872 | tf_op jit(solution)/shard_map/ppermute | solution.py:36
  71.6 0.1 add_level.5
  71.7 0.4 collective-permute-start.20
  72.1 1.4 %collective-permute-start.18 = (bf16[64,1024]{1,0:T(8,128)(2,1)S(1)}, bf16[64,1024]{1,0:T(8,128)(2,1)S(1)}, u32[]{:S(2)}, u32[]{:S(2)}) collective-permute-start(bf16[64,1024]{1,0:T(8,128)(2,1)S(1)} %get-tuple-element.76), channel_id=1, source_target_pairs={{0,16},{2,18},{4,20},{6,22},{8,24},{10,26},{12,28},{14,30},{16,0},... | collective-permute-start | bytes 393224 | tf_op jit(solution)/shard_map/ppermute | solution.py:36
  73.4 1.8 %collective-permute-start.19 = (bf16[64,1024]{1,0:T(8,128)(2,1)S(1)}, bf16[64,1024]{1,0:T(8,128)(2,1)S(1)}, u32[]{:S(2)}, u32[]{:S(2)}) collective-permute-start(bf16[64,1024]{1,0:T(8,128)(2,1)S(1)} %get-tuple-element.77), channel_id=1, source_target_pairs={{0,8},{2,10},{4,12},{6,14},{8,0},{10,2},{12,4},{14,6},{16,24},{18,... | collective-permute-start | bytes 393224 | tf_op jit(solution)/shard_map/ppermute | solution.py:36
  75.2 4.1 %collective-permute-done.18.refs_0_ = bf16[64,1024]{1,0:T(8,128)(2,1)S(1)} collective-permute-done((bf16[64,1024]{1,0:T(8,128)(2,1)S(1)}, bf16[64,1024]{1,0:T(8,128)(2,1)S(1)}, u32[]{:S(2)}, u32[]{:S(2)}) %collective-permute-start.18) | collective-permute-done | bytes 131104 | tf_op jit(solution)/shard_map/ppermute | solution.py:36
  79.3 0.5 collective-permute-done.19.refs_1_
  79.8 0.0 collective-permute-done.20.refs_2_
  79.8 0.9 %finish.1 = (f32[64,1024]{1,0:T(8,128)}, f32[8,1024]{1,0:T(8,128)}) custom-call(f32[8,1024]{1,0:T(8,128)S(1)} %get-tuple-element.75.mean, f32[64,2560]{1,0:T(8,128)S(1)} %add_near_pair.1.near, bf16[64,1024]{1,0:T(8,128)(2,1)S(1)} %copy-done.1, bf16[8,1024]{1,0:T(8,128)(2,1)S(1)} %copy-done.3, bf16[64,1024]{1,0:T(8,128)(2,1)S(1)} %collective-permute-done.18.refs_0_, ...), custom_call_target="tpu_custom_call" | custom-call | tf_op jit(solution)/shard_map/finish/pallas_call | solution.py:584
  (21 shorter events, 0.2 us)
Async XLA Ops:
  0.6 0.9 %copy-start = (bf16[64,1024]{1,0:T(8,128)(2,1)S(1)}, bf16[64,1024]{1,0:T(8,128)(2,1)}, u32[]{:S(2)}) copy-start(bf16[64,1024]{1,0:T(8,128)(2,1)} %chol.1) | copy-start | bytes 393220
  1.5 0.9 %copy-start.2 = (bf16[64,1024]{1,0:T(8,128)(2,1)S(1)}, bf16[64,1024]{1,0:T(8,128)(2,1)}, u32[]{:S(2)}) copy-start(bf16[64,1024]{1,0:T(8,128)(2,1)} %refs_0_.1) | copy-start | bytes 393220
  2.4 20.1 %copy-start.7 = (f32[2,1024]{1,0:T(2,128)S(1)}, f32[2,1024]{1,0:T(2,128)}, u32[]{:S(2)}) copy-start(f32[2,1024]{1,0:T(2,128)} %points_in.1) | copy-start | bytes 24580
  2.4 20.1 %copy-start.8 = (s32[1024]{0:T(1024)S(1)}, s32[1024]{0:T(1024)}, u32[]{:S(2)}) copy-start(s32[1024]{0:T(1024)} %param.14) | copy-start | bytes 12292
  2.4 20.1 %copy-start.9 = (f32[6,6]{1,0:T(8,128)S(1)}, f32[6,6]{1,0:T(8,128)}, u32[]{:S(2)}) copy-start(f32[6,6]{1,0:T(8,128)} %mix_in.1) | copy-start | bytes 436
  2.5 20.1 %copy-start.10 = (f32[2]{0:T(128)S(1)}, f32[2]{0:T(128)}, u32[]{:S(2)}) copy-start(f32[2]{0:T(128)} %lengthscales.1) | copy-start | bytes 28
  2.5 18.6 %collective-permute-start.2 = (bf16[128,1024]{1,0:T(8,128)(2,1)S(1)}, bf16[128,1024]{1,0:T(8,128)(2,1)S(1)}, u32[]{:S(2)}, u32[]{:S(2)}) collective-permute-start(bf16[128,1024]{1,0:T(8,128)(2,1)S(1)} %join.7.refs_0_), channel_id=1, source_target_pairs={{0,16},{2,18},{4,20},{6,22},{8,24},{10,26},{12,28},{14,30},{16,0},... | collective-permute-start | bytes 786440 | tf_op jit(solution)/shard_map/ppermute | solution.py:36
  6.6 14.5 %collective-permute-start.1 = (bf16[128,1024]{1,0:T(8,128)(2,1)S(1)}, bf16[128,1024]{1,0:T(8,128)(2,1)S(1)}, u32[]{:S(2)}, u32[]{:S(2)}) collective-permute-start(bf16[128,1024]{1,0:T(8,128)(2,1)S(1)} %join.7.refs_0_), channel_id=1, source_target_pairs={{0,8},{2,10},{4,12},{6,14},{8,0},{10,2},{12,4},{14,6},{16,24},{18,... | collective-permute-start | bytes 786440 | tf_op jit(solution)/shard_map/ppermute | solution.py:36
  8.2 12.9 %collective-permute-start = (bf16[128,1024]{1,0:T(8,128)(2,1)S(1)}, bf16[128,1024]{1,0:T(8,128)(2,1)S(1)}, u32[]{:S(2)}, u32[]{:S(2)}) collective-permute-start(bf16[128,1024]{1,0:T(8,128)(2,1)S(1)} %join.7.refs_0_), channel_id=1, source_target_pairs={{0,4},{2,6},{4,0},{6,2},{8,12},{10,14},{12,8},{14,10},{16,20},{18,... | collective-permute-start | bytes 786440 | tf_op jit(solution)/shard_map/ppermute | solution.py:36
  9.7 0.7 copy-start.4
  10.4 0.7 copy-start.5
  21.2 6.1 %collective-permute-start.5 = (bf16[512,1024]{1,0:T(8,128)(2,1)S(1)}, bf16[512,1024]{1,0:T(8,128)(2,1)S(1)}, u32[]{:S(2)}, u32[]{:S(2)}) collective-permute-start(bf16[512,1024]{1,0:T(8,128)(2,1)S(1)} %join.10.refs_0_.refs_2_), channel_id=1, source_target_pairs={{0,2},{2,0},{4,6},{6,4},{8,10},{10,8},{12,14},{14,12},{16,18},{18,... | collective-permute-start | bytes 3145736 | tf_op jit(solution)/shard_map/ppermute | solution.py:36
  21.3 11.6 %collective-permute-start.4 = (bf16[192,1024]{1,0:T(8,128)(2,1)S(1)}, bf16[192,1024]{1,0:T(8,128)(2,1)S(1)}, u32[]{:S(2)}, u32[]{:S(2)}) collective-permute-start(bf16[192,1024]{1,0:T(8,128)(2,1)S(1)} %join.9), channel_id=1, source_target_pairs={{0,8},{2,10},{4,12},{6,14},{8,0},{10,2},{12,4},{14,6},{16,24},{18,... | collective-permute-start | bytes 1179656 | tf_op jit(solution)/shard_map/ppermute | solution.py:36
  22.1 11.2 %collective-permute-start.3 = (bf16[192,1024]{1,0:T(8,128)(2,1)S(1)}, bf16[192,1024]{1,0:T(8,128)(2,1)S(1)}, u32[]{:S(2)}, u32[]{:S(2)}) collective-permute-start(bf16[192,1024]{1,0:T(8,128)(2,1)S(1)} %join.8), channel_id=1, source_target_pairs={{0,4},{2,6},{4,0},{6,2},{8,12},{10,14},{12,8},{14,10},{16,20},{18,... | collective-permute-start | bytes 1179656 | tf_op jit(solution)/shard_map/ppermute | solution.py:36
  33.3 2.4 %collective-permute-start.8 = (bf16[384,1024]{1,0:T(8,128)(2,1)S(1)}, bf16[384,1024]{1,0:T(8,128)(2,1)S(1)}, u32[]{:S(2)}, u32[]{:S(2)}) collective-permute-start(bf16[384,1024]{1,0:T(8,128)(2,1)S(1)} %join.13.refs_1_.refs_4_), channel_id=1, source_target_pairs={{0,2},{2,0},{4,6},{6,4},{8,10},{10,8},{12,14},{14,12},{16,18},{18,... | collective-permute-start | bytes 2359304 | tf_op jit(solution)/shard_map/ppermute | solution.py:36
  33.5 8.6 %copy-start.3 = (bf16[8,1024]{1,0:T(8,128)(2,1)S(1)}, bf16[8,1024]{1,0:T(8,128)(2,1)}, u32[]{:S(2)}) copy-start(bf16[8,1024]{1,0:T(8,128)(2,1)} %means.3) | copy-start | bytes 49156
  33.5 6.0 %collective-permute-start.7 = (bf16[64,1024]{1,0:T(8,128)(2,1)S(1)}, bf16[64,1024]{1,0:T(8,128)(2,1)S(1)}, u32[]{:S(2)}, u32[]{:S(2)}) collective-permute-start(bf16[64,1024]{1,0:T(8,128)(2,1)S(1)} %join.12), channel_id=1, source_target_pairs={{0,8},{2,10},{4,12},{6,14},{8,0},{10,2},{12,4},{14,6},{16,24},{18,... | collective-permute-start | bytes 393224 | tf_op jit(solution)/shard_map/ppermute | solution.py:36
  34.9 5.6 %collective-permute-start.6 = (bf16[64,1024]{1,0:T(8,128)(2,1)S(1)}, bf16[64,1024]{1,0:T(8,128)(2,1)S(1)}, u32[]{:S(2)}, u32[]{:S(2)}) collective-permute-start(bf16[64,1024]{1,0:T(8,128)(2,1)S(1)} %join.11), channel_id=1, source_target_pairs={{0,4},{2,6},{4,0},{6,2},{8,12},{10,14},{12,8},{14,10},{16,20},{18,... | collective-permute-start | bytes 393224 | tf_op jit(solution)/shard_map/ppermute | solution.py:36
  38.6 14.0 %copy-start.6 = (f32[8]{0:T(128)S(1)}, f32[8]{0:T(128)}, u32[]{:S(2)}) copy-start(f32[8]{0:T(128)} %scales.1) | copy-start | bytes 100
  40.5 1.3 %collective-permute-start.9 = (bf16[64,1024]{1,0:T(8,128)(2,1)S(1)}, bf16[64,1024]{1,0:T(8,128)(2,1)S(1)}, u32[]{:S(2)}, u32[]{:S(2)}) collective-permute-start(bf16[64,1024]{1,0:T(8,128)(2,1)S(1)} %collective-permute-done.6.refs_0_), channel_id=1, source_target_pairs={{0,2},{2,0},{4,6},{6,4},{8,10},{10,8},{12,14},{14,12},{16,18},{18,... | collective-permute-start | bytes 393224 | tf_op jit(solution)/shard_map/ppermute | solution.py:36
  40.5 1.5 %collective-permute-start.10 = (bf16[64,1024]{1,0:T(8,128)(2,1)S(1)}, bf16[64,1024]{1,0:T(8,128)(2,1)S(1)}, u32[]{:S(2)}, u32[]{:S(2)}) collective-permute-start(bf16[64,1024]{1,0:T(8,128)(2,1)S(1)} %collective-permute-done.7.refs_6_), channel_id=1, source_target_pairs={{0,2},{2,0},{4,6},{6,4},{8,10},{10,8},{12,14},{14,12},{16,18},{18,... | collective-permute-start | bytes 393224 | tf_op jit(solution)/shard_map/ppermute | solution.py:36
  48.0 4.6 %collective-permute-start.11 = (f32[8,2304]{1,0:T(8,128)S(1)}, f32[8,2304]{1,0:T(8,128)S(1)}, u32[]{:S(2)}, u32[]{:S(2)}) collective-permute-start(f32[8,2304]{1,0:T(8,128)S(1)} %get-tuple-element.56.own), channel_id=1, source_target_pairs={{0,1},{1,0},{2,3},{3,2},{4,5},{5,4},{6,7},{7,6},{8,9},{9,8},{10,11... | collective-permute-start | bytes 221192 | tf_op jit(solution)/shard_map/ppermute | solution.py:36
  56.4 2.3 %collective-permute-start.12 = (bf16[80,2560]{1,0:T(8,128)(2,1)S(1)}, bf16[80,2560]{1,0:T(8,128)(2,1)S(1)}, u32[]{:S(2)}, u32[]{:S(2)}) collective-permute-start(bf16[80,2560]{1,0:T(8,128)(2,1)S(1)} %get-tuple-element.64), channel_id=1, source_target_pairs={{0,2},{2,0},{4,6},{6,4},{8,10},{10,8},{12,14},{14,12},{16,18},{18,... | collective-permute-start | bytes 1228808 | tf_op jit(solution)/shard_map/ppermute | solution.py:36
  58.1 21.6 %copy-start.1 = (bf16[64,1024]{1,0:T(8,128)(2,1)S(1)}, bf16[64,1024]{1,0:T(8,128)(2,1)}, u32[]{:S(2)}) copy-start(bf16[64,1024]{1,0:T(8,128)(2,1)} %chol.1) | copy-start | bytes 393220
  58.2 4.6 %collective-permute-start.13 = (bf16[64,2560]{1,0:T(8,128)(2,1)S(1)}, bf16[64,2560]{1,0:T(8,128)(2,1)S(1)}, u32[]{:S(2)}, u32[]{:S(2)}) collective-permute-start(bf16[64,2560]{1,0:T(8,128)(2,1)S(1)} %get-tuple-element.70), channel_id=1, source_target_pairs={{0,2},{2,0},{4,6},{6,4},{8,10},{10,8},{12,14},{14,12},{16,18},{18,... | collective-permute-start | bytes 983048 | tf_op jit(solution)/shard_map/ppermute | solution.py:36
  58.9 7.3 %collective-permute-start.14 = (bf16[64,1024]{1,0:T(8,128)(2,1)S(1)}, bf16[64,1024]{1,0:T(8,128)(2,1)S(1)}, u32[]{:S(2)}, u32[]{:S(2)}) collective-permute-start(bf16[64,1024]{1,0:T(8,128)(2,1)S(1)} %get-tuple-element.71), channel_id=1, source_target_pairs={{0,4},{2,6},{4,0},{6,2},{8,12},{10,14},{12,8},{14,10},{16,20},{18,... | collective-permute-start | bytes 393224 | tf_op jit(solution)/shard_map/ppermute | solution.py:36
  59.3 10.7 %collective-permute-start.16 = (bf16[128,1024]{1,0:T(8,128)(2,1)S(1)}, bf16[128,1024]{1,0:T(8,128)(2,1)S(1)}, u32[]{:S(2)}, u32[]{:S(2)}) collective-permute-start(bf16[128,1024]{1,0:T(8,128)(2,1)S(1)} %get-tuple-element.73), channel_id=1, source_target_pairs={{0,4},{2,6},{4,0},{6,2},{8,12},{10,14},{12,8},{14,10},{16,20},{18,... | collective-permute-start | bytes 786440 | tf_op jit(solution)/shard_map/ppermute | solution.py:36
  61.0 5.2 %collective-permute-start.15 = (f32[8,1024]{1,0:T(8,128)S(1)}, f32[8,1024]{1,0:T(8,128)S(1)}, u32[]{:S(2)}, u32[]{:S(2)}) collective-permute-start(f32[8,1024]{1,0:T(8,128)S(1)} %get-tuple-element.67.mean), channel_id=1, source_target_pairs={{0,16},{2,18},{4,20},{6,22},{8,24},{10,26},{12,28},{14,30},{16,0},... | collective-permute-start | bytes 98312 | tf_op jit(solution)/shard_map/ppermute | solution.py:36
  66.2 5.4 %collective-permute-start.17 = (bf16[80,1024]{1,0:T(8,128)(2,1)S(1)}, bf16[80,1024]{1,0:T(8,128)(2,1)S(1)}, u32[]{:S(2)}, u32[]{:S(2)}) collective-permute-start(bf16[80,1024]{1,0:T(8,128)(2,1)S(1)} %get-tuple-element.74), channel_id=1, source_target_pairs={{0,8},{2,10},{4,12},{6,14},{8,0},{10,2},{12,4},{14,6},{16,24},{18,... | collective-permute-start | bytes 491528 | tf_op jit(solution)/shard_map/ppermute | solution.py:36
  71.7 8.1 %collective-permute-start.20 = (bf16[80,1024]{1,0:T(8,128)(2,1)S(1)}, bf16[80,1024]{1,0:T(8,128)(2,1)S(1)}, u32[]{:S(2)}, u32[]{:S(2)}) collective-permute-start(bf16[80,1024]{1,0:T(8,128)(2,1)S(1)} %get-tuple-element.78), channel_id=1, source_target_pairs={{0,4},{2,6},{4,0},{6,2},{8,12},{10,14},{12,8},{14,10},{16,20},{18,... | collective-permute-start | bytes 491528 | tf_op jit(solution)/shard_map/ppermute | solution.py:36
  72.1 7.2 %collective-permute-start.18 = (bf16[64,1024]{1,0:T(8,128)(2,1)S(1)}, bf16[64,1024]{1,0:T(8,128)(2,1)S(1)}, u32[]{:S(2)}, u32[]{:S(2)}) collective-permute-start(bf16[64,1024]{1,0:T(8,128)(2,1)S(1)} %get-tuple-element.76), channel_id=1, source_target_pairs={{0,16},{2,18},{4,20},{6,22},{8,24},{10,26},{12,28},{14,30},{16,0},... | collective-permute-start | bytes 393224 | tf_op jit(solution)/shard_map/ppermute | solution.py:36
  73.4 6.3 %collective-permute-start.19 = (bf16[64,1024]{1,0:T(8,128)(2,1)S(1)}, bf16[64,1024]{1,0:T(8,128)(2,1)S(1)}, u32[]{:S(2)}, u32[]{:S(2)}) collective-permute-start(bf16[64,1024]{1,0:T(8,128)(2,1)S(1)} %get-tuple-element.77), channel_id=1, source_target_pairs={{0,8},{2,10},{4,12},{6,14},{8,0},{10,2},{12,4},{14,6},{16,24},{18,... | collective-permute-start | bytes 393224 | tf_op jit(solution)/shard_map/ppermute | solution.py:36

commit v5 on v4

--- a/solution.py
+++ b/solution.py
@@ -11,7 +11,7 @@
 NB = 6
 ROWS_DEV = 2048
 SLOT = 128
-COL = 1024
+COL = 2048
 SQRT_HALF_LOG2E = 0.8493218002880191
 
 precise = lax.Precision.HIGHEST
@@ -83,7 +83,7 @@
                 bit = 4 if m == 1 and offset & 4 else offset & -offset
                 wanted.setdefault(bit, []).append((m, offset))
         arrivals = {}
-        for bit, keys in sorted(wanted.items(), reverse=True):
+        for bit, keys in sorted(wanted.items()):
             sent = join([self.pieces[m, offset ^ bit] for m, offset in keys], self.rows)
             arrivals[bit] = swap(sent, "obs", bit)
         if beside is not None:
@@ -132,35 +132,15 @@
         copy.wait()
 
 
-def kernel_rows_kernel(
-    arrived, points_in, bands_in, mix_in, lengthscales, kt, labels, self_cov, points, point_bands, band_mix, sems
-):
-    fetch((points_in, bands_in, mix_in), (points, point_bands, band_mix), sems)
-    codes = arrived[2:3, :]
-    label = jnp.floor((codes + 0.5) * (1.0 / NB))
-    labels[...] = label.astype(jnp.int32)
-    bands = (codes - NB * label).astype(jnp.int32)
-    kinds = lax.broadcasted_iota(jnp.int32, (C, ROWS_DEV), 0)
-    hot = (kinds == bands).astype(f32)
-    eye = lax.broadcasted_iota(jnp.int32, (C, C), 0) == lax.broadcasted_iota(jnp.int32, (C, C), 1)
-    factor = jnp.concatenate([band_mix[...], jnp.zeros((NB, C - NB), f32)], axis=1)
-    factor = jnp.concatenate([factor, jnp.zeros((C - NB, C), f32)], axis=0)
-    mix = eye.astype(f32) + lax.dot_general(
-        factor, factor, (((1,), (1,)), ((), ())), precision=precise, preferred_element_type=f32
-    )
-    scales = [SQRT_HALF_LOG2E / lengthscales[i] for i in range(2)]
-    diagonal = jnp.sum(jnp.where(eye, mix, 0.0), axis=1, keepdims=True)
-    self_cov[...] = jnp.sum(hot * diagonal, axis=0, keepdims=True)
+def cover_rows(nz, number, columns, table, mix, kt):
+    me = lax.axis_index("obs")
+    times, waves, bands = table[0:1, :], table[1:2, :], table[2:3, :]
+    hot = (lax.broadcasted_iota(jnp.int32, (C, ROWS_DEV), 0).astype(f32) == bands).astype(f32)
     hots = jnp.concatenate([hot, hot, hot, jnp.zeros_like(hot)], axis=0).astype(bf16)
-    times = arrived[0:1, :] * scales[0]
-    waves = arrived[1:2, :] * scales[1]
-    width = points.shape[1]
-    columns = jnp.concatenate(
-        [points[...], point_bands[...].astype(f32), jnp.zeros((C - 3, width), f32)], axis=0
-    ).T
-    step = 128
-    for j in range(0, width, step):
-        here = columns[j : j + step, :]
+    offsets = pair_offsets(nz, number)
+    step = kt.shape[0] // len(offsets)
+    for i, offset in enumerate(offsets):
+        here = columns[pl.ds(pl.multiple_of(step * ((me ^ offset) // 2), step), step), :]
         picked = jnp.zeros((step, C), f32)
         for kind in range(NB):
             picked = jnp.where(here[:, 2:3] == float(kind), mix[kind : kind + 1, :], picked)
@@ -169,13 +149,49 @@
         low = picked - high - middle
         split = jnp.concatenate([high, middle, low, jnp.zeros_like(low)], axis=1).astype(bf16)
         mixing = dot(split, hots)
-        delta_t = times - here[:, 0:1] * scales[0]
-        delta_w = waves - here[:, 1:2] * scales[1]
+        delta_t = times - here[:, 0:1]
+        delta_w = waves - here[:, 1:2]
         value = jnp.exp2(-(delta_t * delta_t + delta_w * delta_w)) * mixing
-        kt[j : j + step, :] = value.astype(bf16)
-
-
-def join_pairs(nz, number, places, groups, kt, factor, rows_of):
+        kt[step * i : step * (i + 1), :] = value.astype(bf16)
+
+
+def first_rows_kernel(
+    nz, arrived, points_in, bands_in, mix_in, lengthscales,
+    kt, labels, self_cov, columns, table, mix, points, point_bands, band_mix, sems,
+):
+    fetch((points_in, bands_in, mix_in), (points, point_bands, band_mix), sems)
+    codes = arrived[2:3, :]
+    label = jnp.floor((codes + 0.5) * (1.0 / NB))
+    labels[...] = label.astype(jnp.int32)
+    bands = codes - NB * label
+    hot = (lax.broadcasted_iota(jnp.int32, (C, ROWS_DEV), 0).astype(f32) == bands).astype(f32)
+    eye = lax.broadcasted_iota(jnp.int32, (C, C), 0) == lax.broadcasted_iota(jnp.int32, (C, C), 1)
+    factor = jnp.concatenate([band_mix[...], jnp.zeros((NB, C - NB), f32)], axis=1)
+    factor = jnp.concatenate([factor, jnp.zeros((C - NB, C), f32)], axis=0)
+    coupling = eye.astype(f32) + lax.dot_general(
+        factor, factor, (((1,), (1,)), ((), ())), precision=precise, preferred_element_type=f32
+    )
+    mix[...] = coupling
+    diagonal = jnp.sum(jnp.where(eye, coupling, 0.0), axis=1, keepdims=True)
+    self_cov[...] = jnp.sum(hot * diagonal, axis=0, keepdims=True)
+    scales = [SQRT_HALF_LOG2E / lengthscales[i] for i in range(2)]
+    table[0:1, :] = arrived[0:1, :] * scales[0]
+    table[1:2, :] = arrived[1:2, :] * scales[1]
+    table[2:3, :] = bands
+    width = points.shape[1]
+    columns[...] = jnp.concatenate(
+        [points[0:1, :] * scales[0], points[1:2, :] * scales[1], point_bands[...].astype(f32), jnp.zeros((C - 3, width), f32)],
+        axis=0,
+    ).T
+    cover_rows(nz, 0, columns, table, mix, kt)
+
+
+def more_rows_kernel(nz, columns, table, mix, *kts):
+    for number, kt in enumerate(kts):
+        cover_rows(nz, number + 1, columns, table, mix, kt)
+
+
+def join_pairs(nz, number, places, groups, factor):
     me = lax.axis_index("obs")
     offsets = pair_offsets(nz, number)
     size = factor.shape[0] // len(offsets) // 2
@@ -183,9 +199,6 @@
         base = 2 * size * offsets.index(offset & -2)
         target = pl.multiple_of(base + size * ((me ^ offset) & 1), size)
         factor[pl.ds(target, size), :] = groups[source][size * slot : size * (slot + 1), :]
-    for i, offset in enumerate(offsets):
-        here = pl.ds(pl.multiple_of(2 * size * ((me ^ offset) // 2), 2 * size), 2 * size)
-        rows_of[2 * size * i : 2 * size * (i + 1), :] = kt[here, :]
 
 
 def pair_offsets(nz, number):
@@ -193,27 +206,27 @@
 
 
 def whiten_kernel(nz, number, places, kt, *refs):
-    start = refs[:-4][0] if number > 0 else None
-    groups, (total, factor, turned, met) = refs[(number > 0) : -4], refs[-4:]
-    join_pairs(nz, number, places, groups, kt, factor, met)
+    start = refs[0] if number > 0 else None
+    groups, (total, factor, turned) = refs[(number > 0) : -3], refs[-3:]
+    join_pairs(nz, number, places, groups, factor)
     turned[...] = factor[...].T
 
     @pl.loop(0, ROWS_DEV // COL)
     def _(step):
         columns = pl.ds(pl.multiple_of(step * COL, COL), COL)
         for k in range(0, turned.shape[0], 256):
-            part = dot(turned[k : k + 256, :], met[:, columns])
+            part = dot(turned[k : k + 256, :], kt[:, columns])
             if number > 0:
                 part = part + start[k : k + 256, columns]
             total[k : k + 256, columns] = part
 
 
 def covary_kernel(nz, last, last_places, places, kt, start, means, *refs):
-    ab, bt, sums, factor, last_turned, met, whole, turned = refs[-8:]
+    ab, bt, sums, factor, last_turned, whole, turned = refs[-7:]
     count = 1 + max(source for source, _, _ in last_places)
-    last_groups, groups = refs[:count], refs[count:-8]
+    last_groups, groups = refs[:count], refs[count:-7]
     width = whole.shape[0]
-    join_pairs(nz, last, last_places, last_groups, kt, factor, met)
+    join_pairs(nz, last, last_places, last_groups, factor)
     last_turned[...] = factor[...].T
     store_pieces(groups, places, whole)
     for j in range(0, width, 256):
@@ -224,7 +237,7 @@
         columns = pl.ds(pl.multiple_of(step * COL, COL), COL)
         square = jnp.zeros((1, COL), f32)
         for k in range(0, width, 256):
-            part = start[k : k + 256, columns] + dot(last_turned[k : k + 256, :], met[:, columns])
+            part = start[k : k + 256, columns] + dot(last_turned[k : k + 256, :], kt[:, columns])
             square = square - jnp.sum(part * part, axis=0, keepdims=True)
             ab[k : k + 256, columns] = part.astype(bf16)
         sums[:, columns] = dot(means[...], ab[:, columns])
@@ -254,7 +267,31 @@
             send[: pair // 2, left : left + block] = jnp.where(core == 0, odd, even).astype(bf16)
 
 
-def slope_kernel(nz, own, other, scales, labels, self_cov, ab, bt, chances_out, mean, heavy, keep, send, picked):
+def blocks_at(values, bit, wanted):
+    blocks = [i for i in range(values.shape[1] // SLOT) if bool(i & bit) == wanted]
+    return {i: values[:, SLOT * i : SLOT * (i + 1)] for i in blocks}
+
+
+def outgoing(state, width, bit):
+    values = state[...]
+    rows = [values[:, :width]]
+    if values.shape[1] > width:
+        rows.append(jnp.concatenate(list(blocks_at(values[:, width:], bit, True).values()), axis=1))
+    return jnp.concatenate(rows, axis=0)
+
+
+def absorbed(state, width, bit, arrived):
+    values = state[...]
+    mean = values[:, :width] + arrived[:C]
+    if values.shape[1] == width:
+        return mean
+    blocks = blocks_at(values[:, width:], bit, False)
+    came = blocks_at(values[:, width:], bit, True)
+    blocks.update({i: arrived[C:, SLOT * at : SLOT * (at + 1)] for at, i in enumerate(came)})
+    return jnp.concatenate([mean] + [blocks[i] for i in sorted(blocks)], axis=1)
+
+
+def slope_kernel(nz, own, other, scales, labels, self_cov, ab, bt, chances_out, state, heavy, keep, send, picked):
     total = own[...] + other[...]
     variance = jnp.concatenate([total[i : i + 1, ROWS_DEV:] for i in range(C)], axis=1) + self_cov[...]
     classes = lax.broadcasted_iota(jnp.int32, (C, 1), 0)
@@ -268,9 +305,13 @@
     twice = -jnp.sum(chances * scale, axis=0, keepdims=True)
     slope = ((labels[...] == classes).astype(f32) - chances).astype(bf16)
     heavy[...] = (bt[...].astype(f32) * twice).astype(bf16)
-    value = dot_nt(slope, ab[...])
-    mean[...] = value
-    send[keep.shape[0] :, : ab.shape[0]] = halves(value)
+    width = ab.shape[0]
+    state[:, :width] = dot_nt(slope, ab[...])
+    if state.shape[1] > width:
+        for i in range(ROWS_DEV // SLOT):
+            there = pl.ds(pl.multiple_of(SLOT * (lax.axis_index("obs") ^ i), SLOT), SLOT)
+            state[:, width + SLOT * i : width + SLOT * (i + 1)] = chances_out[:, there]
+    send[keep.shape[0] :, :width] = halves(outgoing(state, width, 1))
     outer_rows(nz, 1 - (lax.axis_index("obs") // 2) % 2, ab, heavy, picked, keep, send)
 
 
@@ -284,13 +325,15 @@
 
 
 def joined(pair):
-    return pair[:C].astype(f32) + pair[C:].astype(f32)
-
-
-def pair_kernel(mean, keep, arrived, mean_out, total):
-    rows, width = keep.shape[0], mean.shape[1]
+    rows = pair.shape[0] // 2
+    return pair[:rows].astype(f32) + pair[rows:].astype(f32)
+
+
+def pair_kernel(width, bit, state, keep, arrived, state_out, ahead, total):
+    rows = keep.shape[0]
     total[...] = keep[...] + arrived[:rows, :].astype(f32)
-    mean_out[...] = mean[...] + joined(arrived[rows:, :width])
+    state_out[...] = absorbed(state, width, 1, joined(arrived[rows:, :width]))
+    ahead[...] = outgoing(state_out, width, bit)
 
 
 def near_pair_kernel(keep, arrived, total):
@@ -308,26 +351,28 @@
     return value
 
 
-def mean_of(mean, refs, mean_from):
-    if mean_from is None:
-        return mean[...]
-    arrived = refs[mean_from]
+def state_of(state, refs, came, width):
+    if came is None:
+        return state[...]
+    source, bit = came
+    arrived = refs[source]
     if arrived.dtype == f32:
-        return mean[...] + arrived[...]
-    return mean[...] + joined(arrived[arrived.shape[0] - 2 * C :, :])
-
-
-def level_kernel(nz, plan, mean_from, mean, near, far, *refs):
+        return absorbed(state, width, bit, arrived[...])
+    extra = 2 * C * (2 if state.shape[1] > width else 1)
+    return absorbed(state, width, bit, joined(arrived[arrived.shape[0] - extra :, :]))
+
+
+def level_kernel(nz, plan, came, bit, state, near, far, *refs):
     outs = refs[len(refs) - len(plan) - 1 :]
-    rows, width = far.shape[0], mean.shape[1]
-    value = mean_of(mean, refs, mean_from)
-    outs[0][...] = value
-    for out, (pieces, with_mean) in zip(outs[1:], plan):
+    rows = far.shape[0]
+    width = outs[1].shape[1]
+    outs[0][...] = state_of(state, refs, came, width)
+    for out, (pieces, with_state) in zip(outs[1:], plan):
         for i, (offset, children) in enumerate(pieces):
             part = with_children(nz, (near, far), width, offset, children, refs)
             out[rows * i : rows * (i + 1), :] = part.astype(bf16)
-        if with_mean:
-            out[rows * len(pieces) :, :] = halves(value)
+        if with_state:
+            out[rows * len(pieces) :, :] = halves(outgoing(outs[0], width, bit))
 
 
 def index_in(arrays, array):
@@ -339,10 +384,10 @@
 
 
 class Scatter:
-    def __init__(self, nz, mean):
-        self.nz, self.mean = nz, mean
+    def __init__(self, nz, width, state):
+        self.nz, self.width, self.state = nz, width, state
         self.arrived = {}
-        self.mean_from = None
+        self.came = None
 
     def children(self, offset, arrays):
         return [
@@ -351,33 +396,38 @@
             if child ^ (child & -child) == offset
         ]
 
-    def level(self, near, far, sends, mean_bit):
+    def came_in(self, arrays):
+        return None if self.came is None else (index_in(arrays, self.came[0]), self.came[1])
+
+    def level(self, near, far, sends, bit):
         arrays = []
         plan = [
-            ([(o, self.children(o, arrays)) for o in offsets], offsets[0] & -offsets[0] == mean_bit)
+            ([(o, self.children(o, arrays)) for o in offsets], offsets[0] & -offsets[0] == bit)
             for offsets in sends
         ]
-        mean_from = None if self.mean_from is None else index_in(arrays, self.mean_from)
-        rows, width = far.shape[0], self.mean.shape[1]
-        self.mean, *outs = pl.pallas_call(
-            functools.partial(level_kernel, self.nz, plan, mean_from),
-            out_shape=[jax.ShapeDtypeStruct(self.mean.shape, f32)]
-            + [jax.ShapeDtypeStruct((rows * len(pieces) + 2 * C * m, width), bf16) for pieces, m in plan],
+        came = self.came_in(arrays)
+        rows = far.shape[0]
+        extra = 2 * C * (2 if self.state.shape[1] > self.width else 1)
+        self.state, *outs = pl.pallas_call(
+            functools.partial(level_kernel, self.nz, plan, came, bit),
+            out_shape=[jax.ShapeDtypeStruct(self.state.shape, f32)]
+            + [jax.ShapeDtypeStruct((rows * len(pieces) + extra * m, self.width), bf16) for pieces, m in plan],
             in_specs=[VMEM] * (3 + len(arrays)),
             out_specs=[VMEM] * (1 + len(plan)),
             compiler_params=SMALL,
             name="add_level",
-        )(self.mean, near, far, *arrays)
-        for (pieces, with_mean), out in zip(plan, outs):
+        )(self.state, near, far, *arrays)
+        for (pieces, with_state), out in zip(plan, outs):
             offsets = [offset for offset, _ in pieces]
             out = swap(out, "obs", offsets[0] & -offsets[0])
             self.arrived.update({offset: (out, slot) for slot, offset in enumerate(offsets)})
-            if with_mean:
-                self.mean_from = out
-
-
-def finish_kernel(nz, children, mean_from, mean, near, chol, means, *refs):
-    grad_chol, grad_mean = refs[-2:]
+            if with_state:
+                self.came = (out, bit)
+
+
+def finish_kernel(nz, children, came, state, near, chol, means, *refs):
+    outs = refs[-3:] if state.shape[1] > chol.shape[1] else refs[-2:]
+    grad_chol, grad_mean = outs[:2]
     rows, width = chol.shape
     value = with_children(nz, (near, near), width, 0, children, refs)
     row_ids = lax.axis_index("obs") * rows + lax.broadcasted_iota(jnp.int32, (rows, width), 0)
@@ -386,7 +436,11 @@
     on_diag = column_ids == row_ids
     inverse = 1.0 / jnp.where(on_diag, own, 1.0)
     grad_chol[...] = jnp.where(column_ids <= row_ids, value, 0.0) - own + jnp.where(on_diag, inverse, 0.0)
-    grad_mean[...] = mean_of(mean, refs, mean_from) - means[...].astype(f32)
+    values = state_of(state, refs, came, width)
+    grad_mean[...] = values[:, :width] - means[...].astype(f32)
+    for i in range((values.shape[1] - width) // SLOT):
+        there = pl.ds(pl.multiple_of(SLOT * (lax.axis_index("obs") ^ i), SLOT), SLOT)
+        outs[2][:, there] = values[:, width + SLOT * i : width + SLOT * (i + 1)]
 
 
 def route(obs_coords, obs_codes, route_plan):
@@ -405,7 +459,7 @@
         name="stack",
     )(obs_coords, obs_codes[None, :])
     if devices * SLOT == ROWS_DEV:
-        return lax.all_to_all(stacked, "obs", split_axis=1, concat_axis=1, tiled=True)
+        return stacked
     me = lax.axis_index("obs")
     blocks = route_plan * SLOT
     send_start = jnp.cumsum(blocks, axis=1) - blocks
@@ -440,17 +494,24 @@
     nz = n // 4
     rows, width = variational_chol.shape
     gather = Gather((prior_factor, variational_chol), nz)
-    arrived = gather.phase(0, lambda: route(obs_coords, obs_codes, route_plan))
+    arrived = route(obs_coords, obs_codes, route_plan)
     big = pltpu.CompilerParams(vmem_limit_bytes=16 * 1024 * 1024)
+    phases = range(len(gather.phases))
+    covered = [
+        jax.ShapeDtypeStruct((2 * rows * len(pair_offsets(nz, number)), ROWS_DEV), bf16) for number in phases
+    ]
     cover = lambda: pl.pallas_call(
-        kernel_rows_kernel,
-        out_shape=(
-            jax.ShapeDtypeStruct((width, ROWS_DEV), bf16),
+        functools.partial(first_rows_kernel, nz),
+        out_shape=[
+            covered[0],
             jax.ShapeDtypeStruct((1, ROWS_DEV), jnp.int32),
             jax.ShapeDtypeStruct((1, ROWS_DEV), f32),
-        ),
+            jax.ShapeDtypeStruct((width, C), f32),
+            jax.ShapeDtypeStruct((C, ROWS_DEV), f32),
+            jax.ShapeDtypeStruct((C, C), f32),
+        ],
         in_specs=[VMEM, HBM, HBM, HBM, SMEM],
-        out_specs=(VMEM, VMEM, VMEM),
+        out_specs=[VMEM] * 6,
         scratch_shapes=[
             pltpu.VMEM((2, width), f32),
             pltpu.VMEM((1, width), jnp.int32),
@@ -459,10 +520,21 @@
         ],
         compiler_params=big,
         cost_estimate=pl.CostEstimate(
-            flops=20 * width * ROWS_DEV, bytes_accessed=4 * 1024 * 1024, transcendentals=width * ROWS_DEV
+            flops=10 * width * ROWS_DEV, bytes_accessed=2 * 1024 * 1024, transcendentals=width * ROWS_DEV // 2
         ),
-        name="kernel_rows",
+        name="first_rows",
     )(arrived, inducing_coords, inducing_bands[None, :], band_mix, lengthscales)
+    cover_more = lambda *given: pl.pallas_call(
+        functools.partial(more_rows_kernel, nz),
+        out_shape=covered[1:],
+        in_specs=[VMEM] * 3,
+        out_specs=[VMEM] * (len(covered) - 1),
+        compiler_params=big,
+        cost_estimate=pl.CostEstimate(
+            flops=10 * width * ROWS_DEV, bytes_accessed=2 * 1024 * 1024, transcendentals=width * ROWS_DEV // 2
+        ),
+        name="more_rows",
+    )(*given)
 
     def whiten(number, kt, *start):
         arrays, places = gather.of(0, number)
@@ -475,7 +547,6 @@
             scratch_shapes=[
                 pltpu.VMEM((inner, width), bf16),
                 pltpu.VMEM((width, inner), bf16),
-                pltpu.VMEM((inner, ROWS_DEV), bf16),
             ],
             input_output_aliases={1: 0} if start else {},
             compiler_params=big,
@@ -485,14 +556,11 @@
             name="whiten",
         )(kt, *start, *arrays)
 
-    def cover_and_whiten():
-        kt, labels, self_cov = cover()
-        return kt, labels, self_cov, whiten(0, kt)
-
-    kt, labels, self_cov, whitened = gather.phase(1, cover_and_whiten)
+    kt, labels, self_cov, *given = gather.phase(0, cover)
     last = len(gather.phases) - 1
+    whitened, kts = gather.phase(1, lambda: (whiten(0, kt), cover_more(*given)))
     for number in range(2, last + 1):
-        whitened = gather.phase(number, lambda: whiten(number - 1, kt, whitened))
+        whitened = gather.phase(number, lambda: whiten(number - 1, kts[number - 2], whitened))
     last_arrays, last_places = gather.of(0, last)
     chol_arrays, chol_places = gather.of(1)
     ab, bt, sums = pl.pallas_call(
@@ -507,7 +575,6 @@
         scratch_shapes=[
             pltpu.VMEM((2 * rows, width), bf16),
             pltpu.VMEM((width, 2 * rows), bf16),
-            pltpu.VMEM((2 * rows, ROWS_DEV), bf16),
             pltpu.VMEM((width, width), bf16),
             pltpu.VMEM((width, width), bf16),
         ],
@@ -516,7 +583,7 @@
             flops=width * width * ROWS_DEV, bytes_accessed=10 * 1024 * 1024, transcendentals=0
         ),
         name="covary",
-    )(kt, whitened, variational_mean, *last_arrays, *chol_arrays)
+    )(kts[-1], whitened, variational_mean, *last_arrays, *chol_arrays)
 
     other = swap(sums, "ind", 1)
     bit = 2
@@ -527,14 +594,17 @@
 
     packed = width // nz * (nz * (nz + 1) // 2)
     kept = jax.ShapeDtypeStruct((rows, packed), f32)
-    chances, mean, heavy, keep, send = pl.pallas_call(
+    moving = n * SLOT == ROWS_DEV
+    held = jax.ShapeDtypeStruct((C, width + ROWS_DEV * moving), f32)
+    extra = C * (2 if moving else 1)
+    chances, state, heavy, keep, send = pl.pallas_call(
         functools.partial(slope_kernel, nz),
         out_shape=[
             jax.ShapeDtypeStruct((C, ROWS_DEV), f32),
-            jax.ShapeDtypeStruct((C, width), f32),
+            held,
             jax.ShapeDtypeStruct((width, ROWS_DEV), bf16),
             kept,
-            jax.ShapeDtypeStruct((rows + 2 * C, packed), bf16),
+            jax.ShapeDtypeStruct((rows + 2 * extra, packed), bf16),
         ],
         in_specs=[VMEM, VMEM, SMEM] + [VMEM] * 4,
         out_specs=[VMEM] * 5,
@@ -551,14 +621,14 @@
         compiler_params=big,
         name="near_outer",
     )(ab, heavy)
-    mean, far = pl.pallas_call(
-        pair_kernel,
-        out_shape=[jax.ShapeDtypeStruct(mean.shape, f32), kept],
+    state, ahead, far = pl.pallas_call(
+        functools.partial(pair_kernel, width, 2 * nz),
+        out_shape=[held, jax.ShapeDtypeStruct((extra, width), f32), kept],
         in_specs=[VMEM] * 3,
-        out_specs=[VMEM] * 2,
+        out_specs=[VMEM] * 3,
         compiler_params=SMALL,
         name="add_pair",
-    )(mean, keep, swap(send, "obs", 1))
+    )(state, keep, swap(send, "obs", 1))
     near = pl.pallas_call(
         near_pair_kernel,
         out_shape=kept,
@@ -567,10 +637,11 @@
         compiler_params=SMALL,
         name="add_near_pair",
     )(near_keep, swap(near_send, "obs", 1))
-    scatter = Scatter(nz, mean)
+    scatter = Scatter(nz, width, state)
+    ahead = swap(ahead, "obs", 2 * nz)
     along_x = [o for phase in reversed(gather.phases) for o in phase if o & 2]
     scatter.level(far, far, [along_x[:1], along_x[1:-1]], None)
-    scatter.mean_from = swap(scatter.mean, "obs", 2 * nz)
+    scatter.came = (ahead, 2 * nz)
     along_z = [[o for o in phase if not o & 2] for phase in gather.phases]
     along_z = [phase for phase in along_z if phase]
     for i, phase in enumerate(reversed(along_z)):
@@ -580,18 +651,19 @@
         scatter.level(near, far, sends + [along_x[-1:]] * last_step, 2 if last_step else 4 << i)
     arrays = []
     children = scatter.children(0, arrays)
-    mean_from = index_in(arrays, scatter.mean_from)
-    grad_chol, grad_mean = pl.pallas_call(
-        functools.partial(finish_kernel, nz, children, mean_from),
-        out_shape=(
-            jax.ShapeDtypeStruct((rows, width), f32),
-            jax.ShapeDtypeStruct((C, width), f32),
-        ),
+    came = scatter.came_in(arrays)
+    shapes = [jax.ShapeDtypeStruct((rows, width), f32), jax.ShapeDtypeStruct((C, width), f32)]
+    if moving:
+        shapes.append(jax.ShapeDtypeStruct((C, ROWS_DEV), f32))
+    grad_chol, grad_mean, *moved = pl.pallas_call(
+        functools.partial(finish_kernel, nz, children, came),
+        out_shape=shapes,
         in_specs=[VMEM] * (4 + len(arrays)),
-        out_specs=(VMEM, VMEM),
+        out_specs=[VMEM] * len(shapes),
         compiler_params=SMALL,
         name="finish",
-    )(scatter.mean, near, variational_chol, variational_mean, *arrays)
+    )(scatter.state, near, variational_chol, variational_mean, *arrays)
+    chances = moved[0] if moving else chances
     return (chances, grad_chol, grad_mean)
 
 

time: 81 us -> 79.3 us (0.979)
  blocking collectives: 9.96 us -> 0 us
  starting transfers between devices: 20.8 us -> 24.6 us
  local copies, waits for them, and re-layouts: 3.25 us -> 5.95 us
  waiting for transfers between devices: 22.1 us -> 24.7 us
    all_to_all x1 -> x0, blocking collectives: 9.96 us -> none  [route(): lax.all_to_all(stacked, 'obs', split_axis=1, concat_axis=1, tiled=True)]
    ppermute x21, starting transfers between devices: 20.8 us -> 24.6 us  [swap(): return lax.ppermute(value, axis, [(i, i ^ bit) for i in range(size)])]
    unnamed x22, local copies, waits for them, and re-layouts: 3.25 us -> 5.95 us
    ppermute x21, waiting for transfers between devices: 22.1 us -> 24.7 us  [swap(): return lax.ppermute(value, axis, [(i, i ^ bit) for i in range(size)])]
    pallas_call x6 -> x7, Pallas kernels: 5.9 us -> 6.18 us  [the longest x1 2.93 us: body(): pl.pallas_call(functools.partial(first_rows_kernel, nz), out_shape=[cover...]
  transfers between devices with their start and end apart: 21 -> 21, of which waited for: 13 -> 15; matrix products, arithmetic and copies ran while one was open for 0% -> 0% of each run, Pallas kernels for 16% -> 16%
where the time goes in v5:
time: 79.3 us; the launch traced here: 78.8 us
  waiting for transfers between devices  24.7 us (31%)
  starting transfers between devices  24.6 us (31%)
  Pallas kernels  22.8 us (29%)
  local copies, waits for them, and re-layouts  5.95 us (8%)
  between operations  0.85 us (1%)
    ppermute x21, waiting for transfers between devices, swap(): return lax.ppermute(value, axis, [(i, i ^ bit) for i in range(size)])  24.7 us
    ppermute x21, starting transfers between devices, swap(): return lax.ppermute(value, axis, [(i, i ^ bit) for i in range(size)])  24.6 us
    unnamed x22, local copies, waits for them, and re-layouts  5.95 us
    pallas_call x2, Pallas kernels, whiten(): pl.pallas_call(functools.partial(whiten_kernel, nz, number, places), out_...  5.39 us
    pallas_call x1, Pallas kernels, body(): pl.pallas_call(functools.partial(covary_kernel, nz, last, last_places, ch...  5.31 us
    pallas_call x1, Pallas kernels, body(): pl.pallas_call(functools.partial(slope_kernel, nz), out_shape=[jax.ShapeD...  3.86 us
    pallas_call x1, Pallas kernels, body(): pl.pallas_call(functools.partial(first_rows_kernel, nz), out_shape=[cover...  2.93 us
    pallas_call x1, Pallas kernels, body(): pl.pallas_call(functools.partial(more_rows_kernel, nz), out_shape=covered...  2.04 us
  transfers between devices with their start and end apart: 21, of which 15 were waited for; matrix products, arithmetic and copies ran while one was open for 0% of the time, Pallas kernels for 16%

profile of v5, /device:TPU:0, one launch (start us, length us, event | category | flops | bytes accessed | tf_op | source)
XLA Modules:
  0.0 78.8 jit_solution(3047909672251628588)
XLA Ops:
  0.6 0.0 copy-start
  0.6 0.9 %copy-done = bf16[64,1024]{1,0:T(8,128)(2,1)S(1)} copy-done((bf16[64,1024]{1,0:T(8,128)(2,1)S(1)}, bf16[64,1024]{1,0:T(8,128)(2,1)}, u32[]{:S(2)}) %copy-start) | copy-done | bytes 131096
  1.5 0.9 %copy-done.2 = bf16[64,1024]{1,0:T(8,128)(2,1)S(1)} copy-done((bf16[64,1024]{1,0:T(8,128)(2,1)S(1)}, bf16[64,1024]{1,0:T(8,128)(2,1)}, u32[]{:S(2)}) %copy-start.2) | copy-done | bytes 131096
  2.5 4.1 %collective-permute-start.2 = (bf16[128,1024]{1,0:T(8,128)(2,1)S(1)}, bf16[128,1024]{1,0:T(8,128)(2,1)S(1)}, u32[]{:S(2)}, u32[]{:S(2)}) collective-permute-start(bf16[128,1024]{1,0:T(8,128)(2,1)S(1)} %join.7.refs_0_), channel_id=1, source_target_pairs={{0,16},{2,18},{4,20},{6,22},{8,24},{10,26},{12,28},{14,30},{16,0},... | collective-permute-start | bytes 786440 | tf_op jit(solution)/shard_map/ppermute | solution.py:36
  6.6 1.6 %collective-permute-start.1 = (bf16[128,1024]{1,0:T(8,128)(2,1)S(1)}, bf16[128,1024]{1,0:T(8,128)(2,1)S(1)}, u32[]{:S(2)}, u32[]{:S(2)}) collective-permute-start(bf16[128,1024]{1,0:T(8,128)(2,1)S(1)} %join.7.refs_0_), channel_id=1, source_target_pairs={{0,8},{2,10},{4,12},{6,14},{8,0},{10,2},{12,4},{14,6},{16,24},{18,... | collective-permute-start | bytes 786440 | tf_op jit(solution)/shard_map/ppermute | solution.py:36
  8.1 1.5 %collective-permute-start = (bf16[128,1024]{1,0:T(8,128)(2,1)S(1)}, bf16[128,1024]{1,0:T(8,128)(2,1)S(1)}, u32[]{:S(2)}, u32[]{:S(2)}) collective-permute-start(bf16[128,1024]{1,0:T(8,128)(2,1)S(1)} %join.7.refs_0_), channel_id=1, source_target_pairs={{0,4},{2,6},{4,0},{6,2},{8,12},{10,14},{12,8},{14,10},{16,20},{18,... | collective-permute-start | bytes 786440 | tf_op jit(solution)/shard_map/ppermute | solution.py:36
  9.6 0.7 copy-done.4
  10.4 0.7 copy-done.5
  11.1 0.0 copy-start.7
  11.1 0.7 copy-done.7
  11.8 0.7 copy-done.8
  12.5 0.7 copy-done.9
  13.2 0.7 copy-done.10
  13.8 2.9 %first_rows.1 = (bf16[512,2048]{1,0:T(8,128)(2,1)S(1)}, s32[1,2048]{1,0:T(1,128)S(1)}, f32[1,2048]{1,0:T(1,128)S(1)}, f32[1024,8]{1,0:T(8,128)S(1)}, f32[8,2048]{1,0:T(8,128)S(1)}, /*index=5*/f32[8,8]{1,0:T(8,128)S(1)}) custom-call(f32[3,2048]{1,0:T(4,128)S(1)} %stack.1.arrived, f32[2,1024]{1,0:T(2,128)S(1)} %copy-done.7, s32[1,1024]{1,0:T(1,128)S(1)} %bitcast.3, ...), custom_call_target="tpu_custom_call" | custom-call | flops 20971520 | bytes 2097152 | tf_op jit(solution)/shard_map/first_rows/pallas_call | solution.py:503
  16.8 1.8 %collective-permute-done.2.refs_0_.refs_3_ = bf16[128,1024]{1,0:T(8,128)(2,1)S(1)} collective-permute-done((bf16[128,1024]{1,0:T(8,128)(2,1)S(1)}, bf16[128,1024]{1,0:T(8,128)(2,1)S(1)}, u32[]{:S(2)}, u32[]{:S(2)}) %collective-permute-start.2) | collective-permute-done | bytes 262176 | tf_op jit(solution)/shard_map/ppermute | solution.py:36
  18.6 0.2 collective-permute-done.1.refs_1_.refs_2_
  18.8 0.1 join.10.refs_0_.refs_2_
  18.9 0.1 collective-permute-start.5
  19.0 1.6 %collective-permute-start.4 = (bf16[192,1024]{1,0:T(8,128)(2,1)S(1)}, bf16[192,1024]{1,0:T(8,128)(2,1)S(1)}, u32[]{:S(2)}, u32[]{:S(2)}) collective-permute-start(bf16[192,1024]{1,0:T(8,128)(2,1)S(1)} %join.9), channel_id=1, source_target_pairs={{0,8},{2,10},{4,12},{6,14},{8,0},{10,2},{12,4},{14,6},{16,24},{18,... | collective-permute-start | bytes 1179656 | tf_op jit(solution)/shard_map/ppermute | solution.py:36
  20.6 1.5 %collective-permute-start.3 = (bf16[192,1024]{1,0:T(8,128)(2,1)S(1)}, bf16[192,1024]{1,0:T(8,128)(2,1)S(1)}, u32[]{:S(2)}, u32[]{:S(2)}) collective-permute-start(bf16[192,1024]{1,0:T(8,128)(2,1)S(1)} %join.8), channel_id=1, source_target_pairs={{0,4},{2,6},{4,0},{6,2},{8,12},{10,14},{12,8},{14,10},{16,20},{18,... | collective-permute-start | bytes 1179656 | tf_op jit(solution)/shard_map/ppermute | solution.py:36
  22.1 2.0 %more_rows.1 = (bf16[384,2048]{1,0:T(8,128)(2,1)S(1)}, bf16[128,2048]{1,0:T(8,128)(2,1)S(1)}) custom-call(f32[1024,8]{1,0:T(8,128)S(1)} %get-tuple-element.62.columns, f32[8,2048]{1,0:T(8,128)S(1)} %get-tuple-element.63.table, f32[8,8]{1,0:T(8,128)S(1)} %get-tuple-element.64.mix), custom_call_target="tpu_custom_call" | custom-call | flops 20971520 | bytes 2097152 | tf_op jit(solution)/shard_map/more_rows/pallas_call | solution.py:527
  24.1 2.5 %whiten.2.refs_0_ = f32[1024,2048]{1,0:T(8,128)S(1)} custom-call(bf16[512,2048]{1,0:T(8,128)(2,1)S(1)} %get-tuple-element.61.kt, bf16[512,1024]{1,0:T(8,128)(2,1)S(1)} %join.10.refs_0_.refs_2_, bf16[512,1024]{1,0:T(8,128)(2,1)S(1)} %collective-permute-done.5.refs_1_.refs_3_), custom_call_target="tpu_custom_call" | custom-call | flops 2147483648 | bytes 10485760 | tf_op jit(solution)/shard_map/whiten/pallas_call | solution.py:542
  26.6 4.0 %collective-permute-done.4.refs_0_.refs_1_ = bf16[192,1024]{1,0:T(8,128)(2,1)S(1)} collective-permute-done((bf16[192,1024]{1,0:T(8,128)(2,1)S(1)}, bf16[192,1024]{1,0:T(8,128)(2,1)S(1)}, u32[]{:S(2)}, u32[]{:S(2)}) %collective-permute-start.4) | collective-permute-done | bytes 393248 | tf_op jit(solution)/shard_map/ppermute | solution.py:36
  30.6 1.2 %collective-permute-done.3.refs_0_ = bf16[192,1024]{1,0:T(8,128)(2,1)S(1)} collective-permute-done((bf16[192,1024]{1,0:T(8,128)(2,1)S(1)}, bf16[192,1024]{1,0:T(8,128)(2,1)S(1)}, u32[]{:S(2)}, u32[]{:S(2)}) %collective-permute-start.3) | collective-permute-done | bytes 393248 | tf_op jit(solution)/shard_map/ppermute | solution.py:36
  31.8 0.1 join.13.refs_1_.refs_4_
  31.9 0.1 collective-permute-start.8
  32.0 0.0 copy-start.3
  32.0 0.6 collective-permute-start.7
  32.6 1.5 %collective-permute-start.6 = (bf16[64,1024]{1,0:T(8,128)(2,1)S(1)}, bf16[64,1024]{1,0:T(8,128)(2,1)S(1)}, u32[]{:S(2)}, u32[]{:S(2)}) collective-permute-start(bf16[64,1024]{1,0:T(8,128)(2,1)S(1)} %join.11), channel_id=1, source_target_pairs={{0,4},{2,6},{4,0},{6,2},{8,12},{10,14},{12,8},{14,10},{16,20},{18,... | collective-permute-start | bytes 393224 | tf_op jit(solution)/shard_map/ppermute | solution.py:36
  34.1 0.1 collective-permute-done.8.refs_2_.refs_5_
  34.2 2.9 %whiten.3.start = f32[1024,2048]{1,0:T(8,128)S(1)} custom-call(bf16[384,2048]{1,0:T(8,128)(2,1)S(1)} %get-tuple-element.70.kt, f32[1024,2048]{1,0:T(8,128)S(1)} %whiten.2.refs_0_, bf16[384,1024]{1,0:T(8,128)(2,1)S(1)} %join.13.refs_1_.refs_4_, bf16[384,1024]{1,0:T(8,128)(2,1)S(1)} %collective-permute-done.8.refs_2_.refs_5_), custom_call_target="tpu_custom_call", output_to_operand_aliasing={{}: (1, {})} | custom-call | flops 1610612736 | bytes 10485760 | tf_op jit(solution)/shard_map/whiten/pallas_call | solution.py:542
  37.1 0.0 copy-start.6
  37.1 0.8 %collective-permute-done.7.refs_6_ = bf16[64,1024]{1,0:T(8,128)(2,1)S(1)} collective-permute-done((bf16[64,1024]{1,0:T(8,128)(2,1)S(1)}, bf16[64,1024]{1,0:T(8,128)(2,1)S(1)}, u32[]{:S(2)}, u32[]{:S(2)}) %collective-permute-start.7) | collective-permute-done | bytes 131104 | tf_op jit(solution)/shard_map/ppermute | solution.py:36
  37.9 0.3 collective-permute-done.6.refs_0_
  38.2 0.5 collective-permute-start.10
  38.7 0.8 %collective-permute-done.9.refs_1_ = bf16[64,1024]{1,0:T(8,128)(2,1)S(1)} collective-permute-done((bf16[64,1024]{1,0:T(8,128)(2,1)S(1)}, bf16[64,1024]{1,0:T(8,128)(2,1)S(1)}, u32[]{:S(2)}, u32[]{:S(2)}) %collective-permute-start.9) | collective-permute-done | bytes 131104 | tf_op jit(solution)/shard_map/ppermute | solution.py:36
  39.5 0.2 collective-permute-done.10.refs_7_
  39.7 5.3 %covary.1 = (bf16[1024,2048]{1,0:T(8,128)(2,1)S(1)}, bf16[1024,2048]{1,0:T(8,128)(2,1)S(1)}, f32[8,2304]{1,0:T(8,128)S(1)}) custom-call(bf16[128,2048]{1,0:T(8,128)(2,1)S(1)} %get-tuple-element.67.kt, f32[1024,2048]{1,0:T(8,128)S(1)} %whiten.3.start, bf16[8,1024]{1,0:T(8,128)(2,1)S(1)} %copy-done.3, bf16[64,1024]{1,0:T(8,128)(2,1)S(1)} %collective-permute-done.6.refs_0_, ...), custom_call_target="tpu_custom_call" | custom-call | flops 2147483648 | bytes 10485760 | tf_op jit(solution)/shard_map/covary/pallas_call | solution.py:566
  45.1 1.6 %collective-permute-start.11 = (f32[8,2304]{1,0:T(8,128)S(1)}, f32[8,2304]{1,0:T(8,128)S(1)}, u32[]{:S(2)}, u32[]{:S(2)}) collective-permute-start(f32[8,2304]{1,0:T(8,128)S(1)} %get-tuple-element.75.own), channel_id=1, source_target_pairs={{0,1},{1,0},{2,3},{3,2},{4,5},{5,4},{6,7},{7,6},{8,9},{9,8},{10,11... | collective-permute-start | bytes 221192 | tf_op jit(solution)/shard_map/ppermute | solution.py:36
  46.7 2.9 %collective-permute-done.11.other = f32[8,2304]{1,0:T(8,128)S(1)} collective-permute-done((f32[8,2304]{1,0:T(8,128)S(1)}, f32[8,2304]{1,0:T(8,128)S(1)}, u32[]{:S(2)}, u32[]{:S(2)}) %collective-permute-start.11) | collective-permute-done | bytes 73760 | tf_op jit(solution)/shard_map/ppermute | solution.py:36
  49.6 3.9 %slopes.1 = (f32[8,2048]{1,0:T(8,128)}, f32[8,3072]{1,0:T(8,128)S(1)}, bf16[1024,2048]{1,0:T(8,128)(2,1)S(1)}, f32[64,2560]{1,0:T(8,128)S(1)}, bf16[96,2560]{1,0:T(8,128)(2,1)S(1)}) custom-call(f32[8,2304]{1,0:T(8,128)S(1)} %get-tuple-element.75.own, f32[8,2304]{1,0:T(8,128)S(1)} %collective-permute-done.11.other, f32[8]{0:T(128)S(1)} %copy-done.6, ...), custom_call_target="tpu_custom_call" | custom-call | tf_op jit(solution)/shard_map/slopes/pallas_call | solution.py:600
  53.5 1.7 %near_outer.1 = (f32[64,2560]{1,0:T(8,128)S(1)}, bf16[64,2560]{1,0:T(8,128)(2,1)S(1)}) custom-call(bf16[1024,2048]{1,0:T(8,128)(2,1)S(1)} %get-tuple-element.78.ab, bf16[1024,2048]{1,0:T(8,128)(2,1)S(1)} %get-tuple-element.86.heavy), custom_call_target="tpu_custom_call" | custom-call | tf_op jit(solution)/shard_map/near_outer/pallas_call | solution.py:615
  55.2 0.0 copy-start.1
  55.2 0.6 collective-permute-start.13
  55.8 0.0 collective-permute-done.12.arrived
  55.8 0.1 add_pair.1
  55.9 0.1 add_level.3
  56.0 1.6 %collective-permute-start.14 = (bf16[64,1024]{1,0:T(8,128)(2,1)S(1)}, bf16[64,1024]{1,0:T(8,128)(2,1)S(1)}, u32[]{:S(2)}, u32[]{:S(2)}) collective-permute-start(bf16[64,1024]{1,0:T(8,128)(2,1)S(1)} %get-tuple-element.89), channel_id=1, source_target_pairs={{0,4},{2,6},{4,0},{6,2},{8,12},{10,14},{12,8},{14,10},{16,20},{18,... | collective-permute-start | bytes 393224 | tf_op jit(solution)/shard_map/ppermute | solution.py:36
  57.6 2.1 %collective-permute-start.15 = (f32[16,1024]{1,0:T(8,128)S(1)}, f32[16,1024]{1,0:T(8,128)S(1)}, u32[]{:S(2)}, u32[]{:S(2)}) collective-permute-start(f32[16,1024]{1,0:T(8,128)S(1)} %get-tuple-element.90), channel_id=1, source_target_pairs={{0,16},{2,18},{4,20},{6,22},{8,24},{10,26},{12,28},{14,30},{16,0},... | collective-permute-start | bytes 196616 | tf_op jit(solution)/shard_map/ppermute | solution.py:36
  59.7 0.5 collective-permute-start.16
  60.2 0.0 collective-permute-done.13.arrived
  60.2 0.1 add_near_pair.1.near
  60.3 3.5 %collective-permute-done.15.refs_1_ = f32[16,1024]{1,0:T(8,128)S(1)} collective-permute-done((f32[16,1024]{1,0:T(8,128)S(1)}, f32[16,1024]{1,0:T(8,128)S(1)}, u32[]{:S(2)}, u32[]{:S(2)}) %collective-permute-start.15) | collective-permute-done | bytes 65568 | tf_op jit(solution)/shard_map/ppermute | solution.py:36
  63.8 0.0 collective-permute-done.14.refs_0_
  63.8 0.6 collective-permute-start.17
  64.4 2.9 %collective-permute-done.16.refs_0_ = bf16[128,1024]{1,0:T(8,128)(2,1)S(1)} collective-permute-done((bf16[128,1024]{1,0:T(8,128)(2,1)S(1)}, bf16[128,1024]{1,0:T(8,128)(2,1)S(1)}, u32[]{:S(2)}, u32[]{:S(2)}) %collective-permute-start.16) | collective-permute-done | bytes 262176 | tf_op jit(solution)/shard_map/ppermute | solution.py:36
  67.3 2.2 %collective-permute-done.17.refs_1_ = bf16[96,1024]{1,0:T(8,128)(2,1)S(1)} collective-permute-done((bf16[96,1024]{1,0:T(8,128)(2,1)S(1)}, bf16[96,1024]{1,0:T(8,128)(2,1)S(1)}, u32[]{:S(2)}, u32[]{:S(2)}) %collective-permute-start.17) | collective-permute-done | bytes 196640 | tf_op jit(solution)/shard_map/ppermute | solution.py:36
  69.6 0.1 add_level.5
  69.7 0.6 collective-permute-start.20
  70.3 2.2 %collective-permute-start.18 = (bf16[64,1024]{1,0:T(8,128)(2,1)S(1)}, bf16[64,1024]{1,0:T(8,128)(2,1)S(1)}, u32[]{:S(2)}, u32[]{:S(2)}) collective-permute-start(bf16[64,1024]{1,0:T(8,128)(2,1)S(1)} %get-tuple-element.95), channel_id=1, source_target_pairs={{0,16},{2,18},{4,20},{6,22},{8,24},{10,26},{12,28},{14,30},{16,0},... | collective-permute-start | bytes 393224 | tf_op jit(solution)/shard_map/ppermute | solution.py:36
  72.6 1.7 %collective-permute-start.19 = (bf16[64,1024]{1,0:T(8,128)(2,1)S(1)}, bf16[64,1024]{1,0:T(8,128)(2,1)S(1)}, u32[]{:S(2)}, u32[]{:S(2)}) collective-permute-start(bf16[64,1024]{1,0:T(8,128)(2,1)S(1)} %get-tuple-element.96), channel_id=1, source_target_pairs={{0,8},{2,10},{4,12},{6,14},{8,0},{10,2},{12,4},{14,6},{16,24},{18,... | collective-permute-start | bytes 393224 | tf_op jit(solution)/shard_map/ppermute | solution.py:36
  74.3 3.4 %collective-permute-done.18.refs_0_ = bf16[64,1024]{1,0:T(8,128)(2,1)S(1)} collective-permute-done((bf16[64,1024]{1,0:T(8,128)(2,1)S(1)}, bf16[64,1024]{1,0:T(8,128)(2,1)S(1)}, u32[]{:S(2)}, u32[]{:S(2)}) %collective-permute-start.18) | collective-permute-done | bytes 131104 | tf_op jit(solution)/shard_map/ppermute | solution.py:36
  77.7 0.3 collective-permute-done.19.refs_1_
  78.0 0.9 %finish.1 = (f32[64,1024]{1,0:T(8,128)}, f32[8,1024]{1,0:T(8,128)}, f32[8,2048]{1,0:T(8,128)}) custom-call(f32[8,3072]{1,0:T(8,128)S(1)} %get-tuple-element.94.state, f32[64,2560]{1,0:T(8,128)S(1)} %add_near_pair.1.near, bf16[64,1024]{1,0:T(8,128)(2,1)S(1)} %copy-done.1, bf16[8,1024]{1,0:T(8,128)(2,1)S(1)} %copy-done.3, ...), custom_call_target="tpu_custom_call" | custom-call | tf_op jit(solution)/shard_map/finish/pallas_call | solution.py:658
  (21 shorter events, 0.2 us)
Async XLA Ops:
  0.6 0.9 %copy-start = (bf16[64,1024]{1,0:T(8,128)(2,1)S(1)}, bf16[64,1024]{1,0:T(8,128)(2,1)}, u32[]{:S(2)}) copy-start(bf16[64,1024]{1,0:T(8,128)(2,1)} %chol.1) | copy-start | bytes 393220
  1.5 0.9 %copy-start.2 = (bf16[64,1024]{1,0:T(8,128)(2,1)S(1)}, bf16[64,1024]{1,0:T(8,128)(2,1)}, u32[]{:S(2)}) copy-start(bf16[64,1024]{1,0:T(8,128)(2,1)} %refs_0_.1) | copy-start | bytes 393220
  2.5 16.1 %collective-permute-start.2 = (bf16[128,1024]{1,0:T(8,128)(2,1)S(1)}, bf16[128,1024]{1,0:T(8,128)(2,1)S(1)}, u32[]{:S(2)}, u32[]{:S(2)}) collective-permute-start(bf16[128,1024]{1,0:T(8,128)(2,1)S(1)} %join.7.refs_0_), channel_id=1, source_target_pairs={{0,16},{2,18},{4,20},{6,22},{8,24},{10,26},{12,28},{14,30},{16,0},... | collective-permute-start | bytes 786440 | tf_op jit(solution)/shard_map/ppermute | solution.py:36
  6.6 12.2 %collective-permute-start.1 = (bf16[128,1024]{1,0:T(8,128)(2,1)S(1)}, bf16[128,1024]{1,0:T(8,128)(2,1)S(1)}, u32[]{:S(2)}, u32[]{:S(2)}) collective-permute-start(bf16[128,1024]{1,0:T(8,128)(2,1)S(1)} %join.7.refs_0_), channel_id=1, source_target_pairs={{0,8},{2,10},{4,12},{6,14},{8,0},{10,2},{12,4},{14,6},{16,24},{18,... | collective-permute-start | bytes 786440 | tf_op jit(solution)/shard_map/ppermute | solution.py:36
  8.1 10.6 %collective-permute-start = (bf16[128,1024]{1,0:T(8,128)(2,1)S(1)}, bf16[128,1024]{1,0:T(8,128)(2,1)S(1)}, u32[]{:S(2)}, u32[]{:S(2)}) collective-permute-start(bf16[128,1024]{1,0:T(8,128)(2,1)S(1)} %join.7.refs_0_), channel_id=1, source_target_pairs={{0,4},{2,6},{4,0},{6,2},{8,12},{10,14},{12,8},{14,10},{16,20},{18,... | collective-permute-start | bytes 786440 | tf_op jit(solution)/shard_map/ppermute | solution.py:36
  9.6 0.7 copy-start.4
  10.4 0.7 copy-start.5
  11.1 0.7 copy-start.7
  11.8 0.7 copy-start.8
  12.5 0.7 copy-start.9
  13.2 0.7 copy-start.10
  18.9 5.2 %collective-permute-start.5 = (bf16[512,1024]{1,0:T(8,128)(2,1)S(1)}, bf16[512,1024]{1,0:T(8,128)(2,1)S(1)}, u32[]{:S(2)}, u32[]{:S(2)}) collective-permute-start(bf16[512,1024]{1,0:T(8,128)(2,1)S(1)} %join.10.refs_0_.refs_2_), channel_id=1, source_target_pairs={{0,2},{2,0},{4,6},{6,4},{8,10},{10,8},{12,14},{14,12},{16,18},{18,... | collective-permute-start | bytes 3145736 | tf_op jit(solution)/shard_map/ppermute | solution.py:36
  19.0 11.6 %collective-permute-start.4 = (bf16[192,1024]{1,0:T(8,128)(2,1)S(1)}, bf16[192,1024]{1,0:T(8,128)(2,1)S(1)}, u32[]{:S(2)}, u32[]{:S(2)}) collective-permute-start(bf16[192,1024]{1,0:T(8,128)(2,1)S(1)} %join.9), channel_id=1, source_target_pairs={{0,8},{2,10},{4,12},{6,14},{8,0},{10,2},{12,4},{14,6},{16,24},{18,... | collective-permute-start | bytes 1179656 | tf_op jit(solution)/shard_map/ppermute | solution.py:36
  20.6 11.2 %collective-permute-start.3 = (bf16[192,1024]{1,0:T(8,128)(2,1)S(1)}, bf16[192,1024]{1,0:T(8,128)(2,1)S(1)}, u32[]{:S(2)}, u32[]{:S(2)}) collective-permute-start(bf16[192,1024]{1,0:T(8,128)(2,1)S(1)} %join.8), channel_id=1, source_target_pairs={{0,4},{2,6},{4,0},{6,2},{8,12},{10,14},{12,8},{14,10},{16,20},{18,... | collective-permute-start | bytes 1179656 | tf_op jit(solution)/shard_map/ppermute | solution.py:36
  31.9 2.4 %collective-permute-start.8 = (bf16[384,1024]{1,0:T(8,128)(2,1)S(1)}, bf16[384,1024]{1,0:T(8,128)(2,1)S(1)}, u32[]{:S(2)}, u32[]{:S(2)}) collective-permute-start(bf16[384,1024]{1,0:T(8,128)(2,1)S(1)} %join.13.refs_1_.refs_4_), channel_id=1, source_target_pairs={{0,2},{2,0},{4,6},{6,4},{8,10},{10,8},{12,14},{14,12},{16,18},{18,... | collective-permute-start | bytes 2359304 | tf_op jit(solution)/shard_map/ppermute | solution.py:36
  32.0 7.8 %copy-start.3 = (bf16[8,1024]{1,0:T(8,128)(2,1)S(1)}, bf16[8,1024]{1,0:T(8,128)(2,1)}, u32[]{:S(2)}) copy-start(bf16[8,1024]{1,0:T(8,128)(2,1)} %means.3) | copy-start | bytes 49156
  32.0 6.0 %collective-permute-start.7 = (bf16[64,1024]{1,0:T(8,128)(2,1)S(1)}, bf16[64,1024]{1,0:T(8,128)(2,1)S(1)}, u32[]{:S(2)}, u32[]{:S(2)}) collective-permute-start(bf16[64,1024]{1,0:T(8,128)(2,1)S(1)} %join.12), channel_id=1, source_target_pairs={{0,8},{2,10},{4,12},{6,14},{8,0},{10,2},{12,4},{14,6},{16,24},{18,... | collective-permute-start | bytes 393224 | tf_op jit(solution)/shard_map/ppermute | solution.py:36
  32.6 5.6 %collective-permute-start.6 = (bf16[64,1024]{1,0:T(8,128)(2,1)S(1)}, bf16[64,1024]{1,0:T(8,128)(2,1)S(1)}, u32[]{:S(2)}, u32[]{:S(2)}) collective-permute-start(bf16[64,1024]{1,0:T(8,128)(2,1)S(1)} %join.11), channel_id=1, source_target_pairs={{0,4},{2,6},{4,0},{6,2},{8,12},{10,14},{12,8},{14,10},{16,20},{18,... | collective-permute-start | bytes 393224 | tf_op jit(solution)/shard_map/ppermute | solution.py:36
  37.1 12.5 %copy-start.6 = (f32[8]{0:T(128)S(1)}, f32[8]{0:T(128)}, u32[]{:S(2)}) copy-start(f32[8]{0:T(128)} %scales.1) | copy-start | bytes 100
  38.2 1.3 %collective-permute-start.9 = (bf16[64,1024]{1,0:T(8,128)(2,1)S(1)}, bf16[64,1024]{1,0:T(8,128)(2,1)S(1)}, u32[]{:S(2)}, u32[]{:S(2)}) collective-permute-start(bf16[64,1024]{1,0:T(8,128)(2,1)S(1)} %collective-permute-done.6.refs_0_), channel_id=1, source_target_pairs={{0,2},{2,0},{4,6},{6,4},{8,10},{10,8},{12,14},{14,12},{16,18},{18,... | collective-permute-start | bytes 393224 | tf_op jit(solution)/shard_map/ppermute | solution.py:36
  38.2 1.5 %collective-permute-start.10 = (bf16[64,1024]{1,0:T(8,128)(2,1)S(1)}, bf16[64,1024]{1,0:T(8,128)(2,1)S(1)}, u32[]{:S(2)}, u32[]{:S(2)}) collective-permute-start(bf16[64,1024]{1,0:T(8,128)(2,1)S(1)} %collective-permute-done.7.refs_6_), channel_id=1, source_target_pairs={{0,2},{2,0},{4,6},{6,4},{8,10},{10,8},{12,14},{14,12},{16,18},{18,... | collective-permute-start | bytes 393224 | tf_op jit(solution)/shard_map/ppermute | solution.py:36
  45.1 4.6 %collective-permute-start.11 = (f32[8,2304]{1,0:T(8,128)S(1)}, f32[8,2304]{1,0:T(8,128)S(1)}, u32[]{:S(2)}, u32[]{:S(2)}) collective-permute-start(f32[8,2304]{1,0:T(8,128)S(1)} %get-tuple-element.75.own), channel_id=1, source_target_pairs={{0,1},{1,0},{2,3},{3,2},{4,5},{5,4},{6,7},{7,6},{8,9},{9,8},{10,11... | collective-permute-start | bytes 221192 | tf_op jit(solution)/shard_map/ppermute | solution.py:36
  53.5 2.3 %collective-permute-start.12 = (bf16[96,2560]{1,0:T(8,128)(2,1)S(1)}, bf16[96,2560]{1,0:T(8,128)(2,1)S(1)}, u32[]{:S(2)}, u32[]{:S(2)}) collective-permute-start(bf16[96,2560]{1,0:T(8,128)(2,1)S(1)} %get-tuple-element.82), channel_id=1, source_target_pairs={{0,2},{2,0},{4,6},{6,4},{8,10},{10,8},{12,14},{14,12},{16,18},{18,... | collective-permute-start | bytes 1474568 | tf_op jit(solution)/shard_map/ppermute | solution.py:36
  55.2 22.7 %copy-start.1 = (bf16[64,1024]{1,0:T(8,128)(2,1)S(1)}, bf16[64,1024]{1,0:T(8,128)(2,1)}, u32[]{:S(2)}) copy-start(bf16[64,1024]{1,0:T(8,128)(2,1)} %chol.1) | copy-start | bytes 393220
  55.2 5.0 %collective-permute-start.13 = (bf16[64,2560]{1,0:T(8,128)(2,1)S(1)}, bf16[64,2560]{1,0:T(8,128)(2,1)S(1)}, u32[]{:S(2)}, u32[]{:S(2)}) collective-permute-start(bf16[64,2560]{1,0:T(8,128)(2,1)S(1)} %get-tuple-element.88), channel_id=1, source_target_pairs={{0,2},{2,0},{4,6},{6,4},{8,10},{10,8},{12,14},{14,12},{16,18},{18,... | collective-permute-start | bytes 983048 | tf_op jit(solution)/shard_map/ppermute | solution.py:36
  56.0 7.8 %collective-permute-start.14 = (bf16[64,1024]{1,0:T(8,128)(2,1)S(1)}, bf16[64,1024]{1,0:T(8,128)(2,1)S(1)}, u32[]{:S(2)}, u32[]{:S(2)}) collective-permute-start(bf16[64,1024]{1,0:T(8,128)(2,1)S(1)} %get-tuple-element.89), channel_id=1, source_target_pairs={{0,4},{2,6},{4,0},{6,2},{8,12},{10,14},{12,8},{14,10},{16,20},{18,... | collective-permute-start | bytes 393224 | tf_op jit(solution)/shard_map/ppermute | solution.py:36
  57.6 6.2 %collective-permute-start.15 = (f32[16,1024]{1,0:T(8,128)S(1)}, f32[16,1024]{1,0:T(8,128)S(1)}, u32[]{:S(2)}, u32[]{:S(2)}) collective-permute-start(f32[16,1024]{1,0:T(8,128)S(1)} %get-tuple-element.90), channel_id=1, source_target_pairs={{0,16},{2,18},{4,20},{6,22},{8,24},{10,26},{12,28},{14,30},{16,0},... | collective-permute-start | bytes 196616 | tf_op jit(solution)/shard_map/ppermute | solution.py:36
  59.7 7.7 %collective-permute-start.16 = (bf16[128,1024]{1,0:T(8,128)(2,1)S(1)}, bf16[128,1024]{1,0:T(8,128)(2,1)S(1)}, u32[]{:S(2)}, u32[]{:S(2)}) collective-permute-start(bf16[128,1024]{1,0:T(8,128)(2,1)S(1)} %get-tuple-element.92), channel_id=1, source_target_pairs={{0,4},{2,6},{4,0},{6,2},{8,12},{10,14},{12,8},{14,10},{16,20},{18,... | collective-permute-start | bytes 786440 | tf_op jit(solution)/shard_map/ppermute | solution.py:36
  63.8 5.7 %collective-permute-start.17 = (bf16[96,1024]{1,0:T(8,128)(2,1)S(1)}, bf16[96,1024]{1,0:T(8,128)(2,1)S(1)}, u32[]{:S(2)}, u32[]{:S(2)}) collective-permute-start(bf16[96,1024]{1,0:T(8,128)(2,1)S(1)} %get-tuple-element.93), channel_id=1, source_target_pairs={{0,8},{2,10},{4,12},{6,14},{8,0},{10,2},{12,4},{14,6},{16,24},{18,... | collective-permute-start | bytes 589832 | tf_op jit(solution)/shard_map/ppermute | solution.py:36
  69.7 8.2 %collective-permute-start.20 = (bf16[96,1024]{1,0:T(8,128)(2,1)S(1)}, bf16[96,1024]{1,0:T(8,128)(2,1)S(1)}, u32[]{:S(2)}, u32[]{:S(2)}) collective-permute-start(bf16[96,1024]{1,0:T(8,128)(2,1)S(1)} %get-tuple-element.97), channel_id=1, source_target_pairs={{0,4},{2,6},{4,0},{6,2},{8,12},{10,14},{12,8},{14,10},{16,20},{18,... | collective-permute-start | bytes 589832 | tf_op jit(solution)/shard_map/ppermute | solution.py:36
  70.3 7.4 %collective-permute-start.18 = (bf16[64,1024]{1,0:T(8,128)(2,1)S(1)}, bf16[64,1024]{1,0:T(8,128)(2,1)S(1)}, u32[]{:S(2)}, u32[]{:S(2)}) collective-permute-start(bf16[64,1024]{1,0:T(8,128)(2,1)S(1)} %get-tuple-element.95), channel_id=1, source_target_pairs={{0,16},{2,18},{4,20},{6,22},{8,24},{10,26},{12,28},{14,30},{16,0},... | collective-permute-start | bytes 393224 | tf_op jit(solution)/shard_map/ppermute | solution.py:36
  72.6 5.4 %collective-permute-start.19 = (bf16[64,1024]{1,0:T(8,128)(2,1)S(1)}, bf16[64,1024]{1,0:T(8,128)(2,1)S(1)}, u32[]{:S(2)}, u32[]{:S(2)}) collective-permute-start(bf16[64,1024]{1,0:T(8,128)(2,1)S(1)} %get-tuple-element.96), channel_id=1, source_target_pairs={{0,8},{2,10},{4,12},{6,14},{8,0},{10,2},{12,4},{14,6},{16,24},{18,... | collective-permute-start | bytes 393224 | tf_op jit(solution)/shard_map/ppermute | solution.py:36

commit v6 on v5

--- a/solution.py
+++ b/solution.py
@@ -240,9 +240,14 @@
             part = start[k : k + 256, columns] + dot(last_turned[k : k + 256, :], kt[:, columns])
             square = square - jnp.sum(part * part, axis=0, keepdims=True)
             ab[k : k + 256, columns] = part.astype(bf16)
-        sums[:, columns] = dot(means[...], ab[:, columns])
         for l in range(0, width, 256):
-            part = dot(turned[l : l + 256, l:], ab[l:, columns])
+            rows = turned[l : l + 256, l:]
+            if l == 0:
+                rows = jnp.concatenate([rows, means[...], jnp.zeros_like(means)], axis=0)
+            part = dot(rows, ab[l:, columns])
+            if l == 0:
+                sums[:, columns] = part[256 : 256 + C, :]
+                part = part[:256, :]
             square = square + jnp.sum(part * part, axis=0, keepdims=True)
             bt[l : l + 256, columns] = part.astype(bf16)
         piece = ROWS_DEV // C

time: 79.3 us -> 78.9 us (level)
  no operation moved by 1% of the time
where the time goes in v6:
time: 78.9 us; the launch traced here: 78.4 us
  waiting for transfers between devices  24.7 us (31%)
  starting transfers between devices  24.6 us (31%)
  Pallas kernels  22.3 us (28%)
  local copies, waits for them, and re-layouts  5.95 us (8%)
  between operations  0.85 us (1%)
    ppermute x21, waiting for transfers between devices, swap(): return lax.ppermute(value, axis, [(i, i ^ bit) for i in range(size)])  24.7 us
    ppermute x21, starting transfers between devices, swap(): return lax.ppermute(value, axis, [(i, i ^ bit) for i in range(size)])  24.6 us
    unnamed x22, local copies, waits for them, and re-layouts  5.95 us
    pallas_call x2, Pallas kernels, whiten(): pl.pallas_call(functools.partial(whiten_kernel, nz, number, places), out_...  5.39 us
    pallas_call x1, Pallas kernels, body(): pl.pallas_call(functools.partial(covary_kernel, nz, last, last_places, ch...  4.87 us
    pallas_call x1, Pallas kernels, body(): pl.pallas_call(functools.partial(slope_kernel, nz), out_shape=[jax.ShapeD...  3.86 us
    pallas_call x1, Pallas kernels, body(): pl.pallas_call(functools.partial(first_rows_kernel, nz), out_shape=[cover...  2.93 us
    pallas_call x1, Pallas kernels, body(): pl.pallas_call(functools.partial(more_rows_kernel, nz), out_shape=covered...  2.04 us
  transfers between devices with their start and end apart: 21, of which 15 were waited for; matrix products, arithmetic and copies ran while one was open for 0% of the time, Pallas kernels for 16%

profile of v6, /device:TPU:0, one launch (start us, length us, event | category | flops | bytes accessed | tf_op | source)
XLA Modules:
  0.0 78.4 jit_solution(7672837440590648164)
XLA Ops:
  0.6 0.0 copy-start
  0.6 0.9 %copy-done = bf16[64,1024]{1,0:T(8,128)(2,1)S(1)} copy-done((bf16[64,1024]{1,0:T(8,128)(2,1)S(1)}, bf16[64,1024]{1,0:T(8,128)(2,1)}, u32[]{:S(2)}) %copy-start) | copy-done | bytes 131096
  1.5 0.9 %copy-done.2 = bf16[64,1024]{1,0:T(8,128)(2,1)S(1)} copy-done((bf16[64,1024]{1,0:T(8,128)(2,1)S(1)}, bf16[64,1024]{1,0:T(8,128)(2,1)}, u32[]{:S(2)}) %copy-start.2) | copy-done | bytes 131096
  2.5 4.1 %collective-permute-start.2 = (bf16[128,1024]{1,0:T(8,128)(2,1)S(1)}, bf16[128,1024]{1,0:T(8,128)(2,1)S(1)}, u32[]{:S(2)}, u32[]{:S(2)}) collective-permute-start(bf16[128,1024]{1,0:T(8,128)(2,1)S(1)} %join.7.refs_0_), channel_id=1, source_target_pairs={{0,16},{2,18},{4,20},{6,22},{8,24},{10,26},{12,28},{14,30},{16,0},... | collective-permute-start | bytes 786440 | tf_op jit(solution)/shard_map/ppermute | solution.py:36
  6.6 1.6 %collective-permute-start.1 = (bf16[128,1024]{1,0:T(8,128)(2,1)S(1)}, bf16[128,1024]{1,0:T(8,128)(2,1)S(1)}, u32[]{:S(2)}, u32[]{:S(2)}) collective-permute-start(bf16[128,1024]{1,0:T(8,128)(2,1)S(1)} %join.7.refs_0_), channel_id=1, source_target_pairs={{0,8},{2,10},{4,12},{6,14},{8,0},{10,2},{12,4},{14,6},{16,24},{18,... | collective-permute-start | bytes 786440 | tf_op jit(solution)/shard_map/ppermute | solution.py:36
  8.1 1.5 %collective-permute-start = (bf16[128,1024]{1,0:T(8,128)(2,1)S(1)}, bf16[128,1024]{1,0:T(8,128)(2,1)S(1)}, u32[]{:S(2)}, u32[]{:S(2)}) collective-permute-start(bf16[128,1024]{1,0:T(8,128)(2,1)S(1)} %join.7.refs_0_), channel_id=1, source_target_pairs={{0,4},{2,6},{4,0},{6,2},{8,12},{10,14},{12,8},{14,10},{16,20},{18,... | collective-permute-start | bytes 786440 | tf_op jit(solution)/shard_map/ppermute | solution.py:36
  9.6 0.7 copy-done.4
  10.4 0.7 copy-done.5
  11.1 0.0 copy-start.7
  11.1 0.7 copy-done.7
  11.8 0.7 copy-done.8
  12.5 0.7 copy-done.9
  13.2 0.7 copy-done.10
  13.8 2.9 %first_rows.1 = (bf16[512,2048]{1,0:T(8,128)(2,1)S(1)}, s32[1,2048]{1,0:T(1,128)S(1)}, f32[1,2048]{1,0:T(1,128)S(1)}, f32[1024,8]{1,0:T(8,128)S(1)}, f32[8,2048]{1,0:T(8,128)S(1)}, /*index=5*/f32[8,8]{1,0:T(8,128)S(1)}) custom-call(f32[3,2048]{1,0:T(4,128)S(1)} %stack.1.arrived, f32[2,1024]{1,0:T(2,128)S(1)} %copy-done.7, s32[1,1024]{1,0:T(1,128)S(1)} %bitcast.3, ...), custom_call_target="tpu_custom_call" | custom-call | flops 20971520 | bytes 2097152 | tf_op jit(solution)/shard_map/first_rows/pallas_call | solution.py:508
  16.8 1.8 %collective-permute-done.2.refs_0_.refs_3_ = bf16[128,1024]{1,0:T(8,128)(2,1)S(1)} collective-permute-done((bf16[128,1024]{1,0:T(8,128)(2,1)S(1)}, bf16[128,1024]{1,0:T(8,128)(2,1)S(1)}, u32[]{:S(2)}, u32[]{:S(2)}) %collective-permute-start.2) | collective-permute-done | bytes 262176 | tf_op jit(solution)/shard_map/ppermute | solution.py:36
  18.6 0.2 collective-permute-done.1.refs_1_.refs_2_
  18.8 0.0 collective-permute-done.refs_1_
  18.8 0.1 join.10.refs_0_.refs_2_
  18.9 0.1 collective-permute-start.5
  19.0 1.6 %collective-permute-start.4 = (bf16[192,1024]{1,0:T(8,128)(2,1)S(1)}, bf16[192,1024]{1,0:T(8,128)(2,1)S(1)}, u32[]{:S(2)}, u32[]{:S(2)}) collective-permute-start(bf16[192,1024]{1,0:T(8,128)(2,1)S(1)} %join.9), channel_id=1, source_target_pairs={{0,8},{2,10},{4,12},{6,14},{8,0},{10,2},{12,4},{14,6},{16,24},{18,... | collective-permute-start | bytes 1179656 | tf_op jit(solution)/shard_map/ppermute | solution.py:36
  20.6 1.5 %collective-permute-start.3 = (bf16[192,1024]{1,0:T(8,128)(2,1)S(1)}, bf16[192,1024]{1,0:T(8,128)(2,1)S(1)}, u32[]{:S(2)}, u32[]{:S(2)}) collective-permute-start(bf16[192,1024]{1,0:T(8,128)(2,1)S(1)} %join.8), channel_id=1, source_target_pairs={{0,4},{2,6},{4,0},{6,2},{8,12},{10,14},{12,8},{14,10},{16,20},{18,... | collective-permute-start | bytes 1179656 | tf_op jit(solution)/shard_map/ppermute | solution.py:36
  22.1 2.0 %more_rows.1 = (bf16[384,2048]{1,0:T(8,128)(2,1)S(1)}, bf16[128,2048]{1,0:T(8,128)(2,1)S(1)}) custom-call(f32[1024,8]{1,0:T(8,128)S(1)} %get-tuple-element.62.columns, f32[8,2048]{1,0:T(8,128)S(1)} %get-tuple-element.63.table, f32[8,8]{1,0:T(8,128)S(1)} %get-tuple-element.64.mix), custom_call_target="tpu_custom_call" | custom-call | flops 20971520 | bytes 2097152 | tf_op jit(solution)/shard_map/more_rows/pallas_call | solution.py:532
  24.1 0.0 collective-permute-done.5.refs_1_.refs_3_
  24.1 2.5 %whiten.2.refs_0_ = f32[1024,2048]{1,0:T(8,128)S(1)} custom-call(bf16[512,2048]{1,0:T(8,128)(2,1)S(1)} %get-tuple-element.61.kt, bf16[512,1024]{1,0:T(8,128)(2,1)S(1)} %join.10.refs_0_.refs_2_, bf16[512,1024]{1,0:T(8,128)(2,1)S(1)} %collective-permute-done.5.refs_1_.refs_3_), custom_call_target="tpu_custom_call" | custom-call | flops 2147483648 | bytes 10485760 | tf_op jit(solution)/shard_map/whiten/pallas_call | solution.py:547
  26.6 4.0 %collective-permute-done.4.refs_0_.refs_1_ = bf16[192,1024]{1,0:T(8,128)(2,1)S(1)} collective-permute-done((bf16[192,1024]{1,0:T(8,128)(2,1)S(1)}, bf16[192,1024]{1,0:T(8,128)(2,1)S(1)}, u32[]{:S(2)}, u32[]{:S(2)}) %collective-permute-start.4) | collective-permute-done | bytes 393248 | tf_op jit(solution)/shard_map/ppermute | solution.py:36
  30.6 1.2 %collective-permute-done.3.refs_0_ = bf16[192,1024]{1,0:T(8,128)(2,1)S(1)} collective-permute-done((bf16[192,1024]{1,0:T(8,128)(2,1)S(1)}, bf16[192,1024]{1,0:T(8,128)(2,1)S(1)}, u32[]{:S(2)}, u32[]{:S(2)}) %collective-permute-start.3) | collective-permute-done | bytes 393248 | tf_op jit(solution)/shard_map/ppermute | solution.py:36
  31.8 0.1 join.13.refs_1_.refs_4_
  31.9 0.1 collective-permute-start.8
  32.0 0.0 copy-start.3
  32.0 0.6 collective-permute-start.7
  32.6 1.5 %collective-permute-start.6 = (bf16[64,1024]{1,0:T(8,128)(2,1)S(1)}, bf16[64,1024]{1,0:T(8,128)(2,1)S(1)}, u32[]{:S(2)}, u32[]{:S(2)}) collective-permute-start(bf16[64,1024]{1,0:T(8,128)(2,1)S(1)} %join.11), channel_id=1, source_target_pairs={{0,4},{2,6},{4,0},{6,2},{8,12},{10,14},{12,8},{14,10},{16,20},{18,... | collective-permute-start | bytes 393224 | tf_op jit(solution)/shard_map/ppermute | solution.py:36
  34.1 0.1 collective-permute-done.8.refs_2_.refs_5_
  34.2 2.9 %whiten.3.start = f32[1024,2048]{1,0:T(8,128)S(1)} custom-call(bf16[384,2048]{1,0:T(8,128)(2,1)S(1)} %get-tuple-element.70.kt, f32[1024,2048]{1,0:T(8,128)S(1)} %whiten.2.refs_0_, bf16[384,1024]{1,0:T(8,128)(2,1)S(1)} %join.13.refs_1_.refs_4_, bf16[384,1024]{1,0:T(8,128)(2,1)S(1)} %collective-permute-done.8.refs_2_.refs_5_), custom_call_target="tpu_custom_call", output_to_operand_aliasing={{}: (1, {})} | custom-call | flops 1610612736 | bytes 10485760 | tf_op jit(solution)/shard_map/whiten/pallas_call | solution.py:547
  37.1 0.0 copy-start.6
  37.1 0.8 %collective-permute-done.7.refs_6_ = bf16[64,1024]{1,0:T(8,128)(2,1)S(1)} collective-permute-done((bf16[64,1024]{1,0:T(8,128)(2,1)S(1)}, bf16[64,1024]{1,0:T(8,128)(2,1)S(1)}, u32[]{:S(2)}, u32[]{:S(2)}) %collective-permute-start.7) | collective-permute-done | bytes 131104 | tf_op jit(solution)/shard_map/ppermute | solution.py:36
  37.9 0.3 collective-permute-done.6.refs_0_
  38.2 0.0 collective-permute-start.9
  38.2 0.5 collective-permute-start.10
  38.7 0.8 %collective-permute-done.9.refs_1_ = bf16[64,1024]{1,0:T(8,128)(2,1)S(1)} collective-permute-done((bf16[64,1024]{1,0:T(8,128)(2,1)S(1)}, bf16[64,1024]{1,0:T(8,128)(2,1)S(1)}, u32[]{:S(2)}, u32[]{:S(2)}) %collective-permute-start.9) | collective-permute-done | bytes 131104 | tf_op jit(solution)/shard_map/ppermute | solution.py:36
  39.5 0.2 collective-permute-done.10.refs_7_
  39.7 4.9 %covary.1 = (bf16[1024,2048]{1,0:T(8,128)(2,1)S(1)}, bf16[1024,2048]{1,0:T(8,128)(2,1)S(1)}, f32[8,2304]{1,0:T(8,128)S(1)}) custom-call(bf16[128,2048]{1,0:T(8,128)(2,1)S(1)} %get-tuple-element.67.kt, f32[1024,2048]{1,0:T(8,128)S(1)} %whiten.3.start, bf16[8,1024]{1,0:T(8,128)(2,1)S(1)} %copy-done.3, bf16[64,1024]{1,0:T(8,128)(2,1)S(1)} %collective-permute-done.6.refs_0_, ...), custom_call_target="tpu_custom_call" | custom-call | flops 2147483648 | bytes 10485760 | tf_op jit(solution)/shard_map/covary/pallas_call | solution.py:571
  44.6 1.6 %collective-permute-start.11 = (f32[8,2304]{1,0:T(8,128)S(1)}, f32[8,2304]{1,0:T(8,128)S(1)}, u32[]{:S(2)}, u32[]{:S(2)}) collective-permute-start(f32[8,2304]{1,0:T(8,128)S(1)} %get-tuple-element.75.own), channel_id=1, source_target_pairs={{0,1},{1,0},{2,3},{3,2},{4,5},{5,4},{6,7},{7,6},{8,9},{9,8},{10,11... | collective-permute-start | bytes 221192 | tf_op jit(solution)/shard_map/ppermute | solution.py:36
  46.2 2.9 %collective-permute-done.11.other = f32[8,2304]{1,0:T(8,128)S(1)} collective-permute-done((f32[8,2304]{1,0:T(8,128)S(1)}, f32[8,2304]{1,0:T(8,128)S(1)}, u32[]{:S(2)}, u32[]{:S(2)}) %collective-permute-start.11) | collective-permute-done | bytes 73760 | tf_op jit(solution)/shard_map/ppermute | solution.py:36
  49.2 3.9 %slopes.1 = (f32[8,2048]{1,0:T(8,128)}, f32[8,3072]{1,0:T(8,128)S(1)}, bf16[1024,2048]{1,0:T(8,128)(2,1)S(1)}, f32[64,2560]{1,0:T(8,128)S(1)}, bf16[96,2560]{1,0:T(8,128)(2,1)S(1)}) custom-call(f32[8,2304]{1,0:T(8,128)S(1)} %get-tuple-element.75.own, f32[8,2304]{1,0:T(8,128)S(1)} %collective-permute-done.11.other, f32[8]{0:T(128)S(1)} %copy-done.6, ...), custom_call_target="tpu_custom_call" | custom-call | tf_op jit(solution)/shard_map/slopes/pallas_call | solution.py:605
  53.0 1.7 %near_outer.1 = (f32[64,2560]{1,0:T(8,128)S(1)}, bf16[64,2560]{1,0:T(8,128)(2,1)S(1)}) custom-call(bf16[1024,2048]{1,0:T(8,128)(2,1)S(1)} %get-tuple-element.78.ab, bf16[1024,2048]{1,0:T(8,128)(2,1)S(1)} %get-tuple-element.86.heavy), custom_call_target="tpu_custom_call" | custom-call | tf_op jit(solution)/shard_map/near_outer/pallas_call | solution.py:620
  54.8 0.0 copy-start.1
  54.8 0.6 collective-permute-start.13
  55.3 0.1 add_pair.1
  55.4 0.1 add_level.3
  55.5 1.6 %collective-permute-start.14 = (bf16[64,1024]{1,0:T(8,128)(2,1)S(1)}, bf16[64,1024]{1,0:T(8,128)(2,1)S(1)}, u32[]{:S(2)}, u32[]{:S(2)}) collective-permute-start(bf16[64,1024]{1,0:T(8,128)(2,1)S(1)} %get-tuple-element.89), channel_id=1, source_target_pairs={{0,4},{2,6},{4,0},{6,2},{8,12},{10,14},{12,8},{14,10},{16,20},{18,... | collective-permute-start | bytes 393224 | tf_op jit(solution)/shard_map/ppermute | solution.py:36
  57.1 2.1 %collective-permute-start.15 = (f32[16,1024]{1,0:T(8,128)S(1)}, f32[16,1024]{1,0:T(8,128)S(1)}, u32[]{:S(2)}, u32[]{:S(2)}) collective-permute-start(f32[16,1024]{1,0:T(8,128)S(1)} %get-tuple-element.90), channel_id=1, source_target_pairs={{0,16},{2,18},{4,20},{6,22},{8,24},{10,26},{12,28},{14,30},{16,0},... | collective-permute-start | bytes 196616 | tf_op jit(solution)/shard_map/ppermute | solution.py:36
  59.2 0.5 collective-permute-start.16
  59.8 0.1 add_near_pair.1.near
  59.8 3.5 %collective-permute-done.15.refs_1_ = f32[16,1024]{1,0:T(8,128)S(1)} collective-permute-done((f32[16,1024]{1,0:T(8,128)S(1)}, f32[16,1024]{1,0:T(8,128)S(1)}, u32[]{:S(2)}, u32[]{:S(2)}) %collective-permute-start.15) | collective-permute-done | bytes 65568 | tf_op jit(solution)/shard_map/ppermute | solution.py:36
  63.4 0.6 collective-permute-start.17
  64.0 3.0 %collective-permute-done.16.refs_0_ = bf16[128,1024]{1,0:T(8,128)(2,1)S(1)} collective-permute-done((bf16[128,1024]{1,0:T(8,128)(2,1)S(1)}, bf16[128,1024]{1,0:T(8,128)(2,1)S(1)}, u32[]{:S(2)}, u32[]{:S(2)}) %collective-permute-start.16) | collective-permute-done | bytes 262176 | tf_op jit(solution)/shard_map/ppermute | solution.py:36
  66.9 2.2 %collective-permute-done.17.refs_1_ = bf16[96,1024]{1,0:T(8,128)(2,1)S(1)} collective-permute-done((bf16[96,1024]{1,0:T(8,128)(2,1)S(1)}, bf16[96,1024]{1,0:T(8,128)(2,1)S(1)}, u32[]{:S(2)}, u32[]{:S(2)}) %collective-permute-start.17) | collective-permute-done | bytes 196640 | tf_op jit(solution)/shard_map/ppermute | solution.py:36
  69.1 0.1 add_level.5
  69.3 0.6 collective-permute-start.20
  69.9 2.2 %collective-permute-start.18 = (bf16[64,1024]{1,0:T(8,128)(2,1)S(1)}, bf16[64,1024]{1,0:T(8,128)(2,1)S(1)}, u32[]{:S(2)}, u32[]{:S(2)}) collective-permute-start(bf16[64,1024]{1,0:T(8,128)(2,1)S(1)} %get-tuple-element.95), channel_id=1, source_target_pairs={{0,16},{2,18},{4,20},{6,22},{8,24},{10,26},{12,28},{14,30},{16,0},... | collective-permute-start | bytes 393224 | tf_op jit(solution)/shard_map/ppermute | solution.py:36
  72.1 1.7 %collective-permute-start.19 = (bf16[64,1024]{1,0:T(8,128)(2,1)S(1)}, bf16[64,1024]{1,0:T(8,128)(2,1)S(1)}, u32[]{:S(2)}, u32[]{:S(2)}) collective-permute-start(bf16[64,1024]{1,0:T(8,128)(2,1)S(1)} %get-tuple-element.96), channel_id=1, source_target_pairs={{0,8},{2,10},{4,12},{6,14},{8,0},{10,2},{12,4},{14,6},{16,24},{18,... | collective-permute-start | bytes 393224 | tf_op jit(solution)/shard_map/ppermute | solution.py:36
  73.8 3.4 %collective-permute-done.18.refs_0_ = bf16[64,1024]{1,0:T(8,128)(2,1)S(1)} collective-permute-done((bf16[64,1024]{1,0:T(8,128)(2,1)S(1)}, bf16[64,1024]{1,0:T(8,128)(2,1)S(1)}, u32[]{:S(2)}, u32[]{:S(2)}) %collective-permute-start.18) | collective-permute-done | bytes 131104 | tf_op jit(solution)/shard_map/ppermute | solution.py:36
  77.2 0.3 collective-permute-done.19.refs_1_
  77.5 0.9 %finish.1 = (f32[64,1024]{1,0:T(8,128)}, f32[8,1024]{1,0:T(8,128)}, f32[8,2048]{1,0:T(8,128)}) custom-call(f32[8,3072]{1,0:T(8,128)S(1)} %get-tuple-element.94.state, f32[64,2560]{1,0:T(8,128)S(1)} %add_near_pair.1.near, bf16[64,1024]{1,0:T(8,128)(2,1)S(1)} %copy-done.1, bf16[8,1024]{1,0:T(8,128)(2,1)S(1)} %copy-done.3, ...), custom_call_target="tpu_custom_call" | custom-call | tf_op jit(solution)/shard_map/finish/pallas_call | solution.py:663
  (21 shorter events, 0.2 us)
Async XLA Ops:
  0.6 0.9 %copy-start = (bf16[64,1024]{1,0:T(8,128)(2,1)S(1)}, bf16[64,1024]{1,0:T(8,128)(2,1)}, u32[]{:S(2)}) copy-start(bf16[64,1024]{1,0:T(8,128)(2,1)} %chol.1) | copy-start | bytes 393220
  1.5 0.9 %copy-start.2 = (bf16[64,1024]{1,0:T(8,128)(2,1)S(1)}, bf16[64,1024]{1,0:T(8,128)(2,1)}, u32[]{:S(2)}) copy-start(bf16[64,1024]{1,0:T(8,128)(2,1)} %refs_0_.1) | copy-start | bytes 393220
  2.5 16.1 %collective-permute-start.2 = (bf16[128,1024]{1,0:T(8,128)(2,1)S(1)}, bf16[128,1024]{1,0:T(8,128)(2,1)S(1)}, u32[]{:S(2)}, u32[]{:S(2)}) collective-permute-start(bf16[128,1024]{1,0:T(8,128)(2,1)S(1)} %join.7.refs_0_), channel_id=1, source_target_pairs={{0,16},{2,18},{4,20},{6,22},{8,24},{10,26},{12,28},{14,30},{16,0},... | collective-permute-start | bytes 786440 | tf_op jit(solution)/shard_map/ppermute | solution.py:36
  6.6 12.2 %collective-permute-start.1 = (bf16[128,1024]{1,0:T(8,128)(2,1)S(1)}, bf16[128,1024]{1,0:T(8,128)(2,1)S(1)}, u32[]{:S(2)}, u32[]{:S(2)}) collective-permute-start(bf16[128,1024]{1,0:T(8,128)(2,1)S(1)} %join.7.refs_0_), channel_id=1, source_target_pairs={{0,8},{2,10},{4,12},{6,14},{8,0},{10,2},{12,4},{14,6},{16,24},{18,... | collective-permute-start | bytes 786440 | tf_op jit(solution)/shard_map/ppermute | solution.py:36
  8.1 10.6 %collective-permute-start = (bf16[128,1024]{1,0:T(8,128)(2,1)S(1)}, bf16[128,1024]{1,0:T(8,128)(2,1)S(1)}, u32[]{:S(2)}, u32[]{:S(2)}) collective-permute-start(bf16[128,1024]{1,0:T(8,128)(2,1)S(1)} %join.7.refs_0_), channel_id=1, source_target_pairs={{0,4},{2,6},{4,0},{6,2},{8,12},{10,14},{12,8},{14,10},{16,20},{18,... | collective-permute-start | bytes 786440 | tf_op jit(solution)/shard_map/ppermute | solution.py:36
  9.6 0.7 copy-start.4
  10.4 0.7 copy-start.5
  11.1 0.7 copy-start.7
  11.8 0.7 copy-start.8
  12.5 0.7 copy-start.9
  13.2 0.7 copy-start.10
  18.9 5.2 %collective-permute-start.5 = (bf16[512,1024]{1,0:T(8,128)(2,1)S(1)}, bf16[512,1024]{1,0:T(8,128)(2,1)S(1)}, u32[]{:S(2)}, u32[]{:S(2)}) collective-permute-start(bf16[512,1024]{1,0:T(8,128)(2,1)S(1)} %join.10.refs_0_.refs_2_), channel_id=1, source_target_pairs={{0,2},{2,0},{4,6},{6,4},{8,10},{10,8},{12,14},{14,12},{16,18},{18,... | collective-permute-start | bytes 3145736 | tf_op jit(solution)/shard_map/ppermute | solution.py:36
  19.0 11.6 %collective-permute-start.4 = (bf16[192,1024]{1,0:T(8,128)(2,1)S(1)}, bf16[192,1024]{1,0:T(8,128)(2,1)S(1)}, u32[]{:S(2)}, u32[]{:S(2)}) collective-permute-start(bf16[192,1024]{1,0:T(8,128)(2,1)S(1)} %join.9), channel_id=1, source_target_pairs={{0,8},{2,10},{4,12},{6,14},{8,0},{10,2},{12,4},{14,6},{16,24},{18,... | collective-permute-start | bytes 1179656 | tf_op jit(solution)/shard_map/ppermute | solution.py:36
  20.6 11.2 %collective-permute-start.3 = (bf16[192,1024]{1,0:T(8,128)(2,1)S(1)}, bf16[192,1024]{1,0:T(8,128)(2,1)S(1)}, u32[]{:S(2)}, u32[]{:S(2)}) collective-permute-start(bf16[192,1024]{1,0:T(8,128)(2,1)S(1)} %join.8), channel_id=1, source_target_pairs={{0,4},{2,6},{4,0},{6,2},{8,12},{10,14},{12,8},{14,10},{16,20},{18,... | collective-permute-start | bytes 1179656 | tf_op jit(solution)/shard_map/ppermute | solution.py:36
  31.9 2.4 %collective-permute-start.8 = (bf16[384,1024]{1,0:T(8,128)(2,1)S(1)}, bf16[384,1024]{1,0:T(8,128)(2,1)S(1)}, u32[]{:S(2)}, u32[]{:S(2)}) collective-permute-start(bf16[384,1024]{1,0:T(8,128)(2,1)S(1)} %join.13.refs_1_.refs_4_), channel_id=1, source_target_pairs={{0,2},{2,0},{4,6},{6,4},{8,10},{10,8},{12,14},{14,12},{16,18},{18,... | collective-permute-start | bytes 2359304 | tf_op jit(solution)/shard_map/ppermute | solution.py:36
  32.0 7.8 %copy-start.3 = (bf16[8,1024]{1,0:T(8,128)(2,1)S(1)}, bf16[8,1024]{1,0:T(8,128)(2,1)}, u32[]{:S(2)}) copy-start(bf16[8,1024]{1,0:T(8,128)(2,1)} %means.3) | copy-start | bytes 49156
  32.0 6.0 %collective-permute-start.7 = (bf16[64,1024]{1,0:T(8,128)(2,1)S(1)}, bf16[64,1024]{1,0:T(8,128)(2,1)S(1)}, u32[]{:S(2)}, u32[]{:S(2)}) collective-permute-start(bf16[64,1024]{1,0:T(8,128)(2,1)S(1)} %join.12), channel_id=1, source_target_pairs={{0,8},{2,10},{4,12},{6,14},{8,0},{10,2},{12,4},{14,6},{16,24},{18,... | collective-permute-start | bytes 393224 | tf_op jit(solution)/shard_map/ppermute | solution.py:36
  32.6 5.6 %collective-permute-start.6 = (bf16[64,1024]{1,0:T(8,128)(2,1)S(1)}, bf16[64,1024]{1,0:T(8,128)(2,1)S(1)}, u32[]{:S(2)}, u32[]{:S(2)}) collective-permute-start(bf16[64,1024]{1,0:T(8,128)(2,1)S(1)} %join.11), channel_id=1, source_target_pairs={{0,4},{2,6},{4,0},{6,2},{8,12},{10,14},{12,8},{14,10},{16,20},{18,... | collective-permute-start | bytes 393224 | tf_op jit(solution)/shard_map/ppermute | solution.py:36
  37.1 12.1 %copy-start.6 = (f32[8]{0:T(128)S(1)}, f32[8]{0:T(128)}, u32[]{:S(2)}) copy-start(f32[8]{0:T(128)} %scales.1) | copy-start | bytes 100
  38.2 1.3 %collective-permute-start.9 = (bf16[64,1024]{1,0:T(8,128)(2,1)S(1)}, bf16[64,1024]{1,0:T(8,128)(2,1)S(1)}, u32[]{:S(2)}, u32[]{:S(2)}) collective-permute-start(bf16[64,1024]{1,0:T(8,128)(2,1)S(1)} %collective-permute-done.6.refs_0_), channel_id=1, source_target_pairs={{0,2},{2,0},{4,6},{6,4},{8,10},{10,8},{12,14},{14,12},{16,18},{18,... | collective-permute-start | bytes 393224 | tf_op jit(solution)/shard_map/ppermute | solution.py:36
  38.2 1.5 %collective-permute-start.10 = (bf16[64,1024]{1,0:T(8,128)(2,1)S(1)}, bf16[64,1024]{1,0:T(8,128)(2,1)S(1)}, u32[]{:S(2)}, u32[]{:S(2)}) collective-permute-start(bf16[64,1024]{1,0:T(8,128)(2,1)S(1)} %collective-permute-done.7.refs_6_), channel_id=1, source_target_pairs={{0,2},{2,0},{4,6},{6,4},{8,10},{10,8},{12,14},{14,12},{16,18},{18,... | collective-permute-start | bytes 393224 | tf_op jit(solution)/shard_map/ppermute | solution.py:36
  44.6 4.6 %collective-permute-start.11 = (f32[8,2304]{1,0:T(8,128)S(1)}, f32[8,2304]{1,0:T(8,128)S(1)}, u32[]{:S(2)}, u32[]{:S(2)}) collective-permute-start(f32[8,2304]{1,0:T(8,128)S(1)} %get-tuple-element.75.own), channel_id=1, source_target_pairs={{0,1},{1,0},{2,3},{3,2},{4,5},{5,4},{6,7},{7,6},{8,9},{9,8},{10,11... | collective-permute-start | bytes 221192 | tf_op jit(solution)/shard_map/ppermute | solution.py:36
  53.0 2.3 %collective-permute-start.12 = (bf16[96,2560]{1,0:T(8,128)(2,1)S(1)}, bf16[96,2560]{1,0:T(8,128)(2,1)S(1)}, u32[]{:S(2)}, u32[]{:S(2)}) collective-permute-start(bf16[96,2560]{1,0:T(8,128)(2,1)S(1)} %get-tuple-element.82), channel_id=1, source_target_pairs={{0,2},{2,0},{4,6},{6,4},{8,10},{10,8},{12,14},{14,12},{16,18},{18,... | collective-permute-start | bytes 1474568 | tf_op jit(solution)/shard_map/ppermute | solution.py:36
  54.8 22.8 %copy-start.1 = (bf16[64,1024]{1,0:T(8,128)(2,1)S(1)}, bf16[64,1024]{1,0:T(8,128)(2,1)}, u32[]{:S(2)}) copy-start(bf16[64,1024]{1,0:T(8,128)(2,1)} %chol.1) | copy-start | bytes 393220
  54.8 5.0 %collective-permute-start.13 = (bf16[64,2560]{1,0:T(8,128)(2,1)S(1)}, bf16[64,2560]{1,0:T(8,128)(2,1)S(1)}, u32[]{:S(2)}, u32[]{:S(2)}) collective-permute-start(bf16[64,2560]{1,0:T(8,128)(2,1)S(1)} %get-tuple-element.88), channel_id=1, source_target_pairs={{0,2},{2,0},{4,6},{6,4},{8,10},{10,8},{12,14},{14,12},{16,18},{18,... | collective-permute-start | bytes 983048 | tf_op jit(solution)/shard_map/ppermute | solution.py:36
  55.5 7.8 %collective-permute-start.14 = (bf16[64,1024]{1,0:T(8,128)(2,1)S(1)}, bf16[64,1024]{1,0:T(8,128)(2,1)S(1)}, u32[]{:S(2)}, u32[]{:S(2)}) collective-permute-start(bf16[64,1024]{1,0:T(8,128)(2,1)S(1)} %get-tuple-element.89), channel_id=1, source_target_pairs={{0,4},{2,6},{4,0},{6,2},{8,12},{10,14},{12,8},{14,10},{16,20},{18,... | collective-permute-start | bytes 393224 | tf_op jit(solution)/shard_map/ppermute | solution.py:36
  57.1 6.2 %collective-permute-start.15 = (f32[16,1024]{1,0:T(8,128)S(1)}, f32[16,1024]{1,0:T(8,128)S(1)}, u32[]{:S(2)}, u32[]{:S(2)}) collective-permute-start(f32[16,1024]{1,0:T(8,128)S(1)} %get-tuple-element.90), channel_id=1, source_target_pairs={{0,16},{2,18},{4,20},{6,22},{8,24},{10,26},{12,28},{14,30},{16,0},... | collective-permute-start | bytes 196616 | tf_op jit(solution)/shard_map/ppermute | solution.py:36
  59.2 7.7 %collective-permute-start.16 = (bf16[128,1024]{1,0:T(8,128)(2,1)S(1)}, bf16[128,1024]{1,0:T(8,128)(2,1)S(1)}, u32[]{:S(2)}, u32[]{:S(2)}) collective-permute-start(bf16[128,1024]{1,0:T(8,128)(2,1)S(1)} %get-tuple-element.92), channel_id=1, source_target_pairs={{0,4},{2,6},{4,0},{6,2},{8,12},{10,14},{12,8},{14,10},{16,20},{18,... | collective-permute-start | bytes 786440 | tf_op jit(solution)/shard_map/ppermute | solution.py:36
  63.4 5.7 %collective-permute-start.17 = (bf16[96,1024]{1,0:T(8,128)(2,1)S(1)}, bf16[96,1024]{1,0:T(8,128)(2,1)S(1)}, u32[]{:S(2)}, u32[]{:S(2)}) collective-permute-start(bf16[96,1024]{1,0:T(8,128)(2,1)S(1)} %get-tuple-element.93), channel_id=1, source_target_pairs={{0,8},{2,10},{4,12},{6,14},{8,0},{10,2},{12,4},{14,6},{16,24},{18,... | collective-permute-start | bytes 589832 | tf_op jit(solution)/shard_map/ppermute | solution.py:36
  69.3 8.2 %collective-permute-start.20 = (bf16[96,1024]{1,0:T(8,128)(2,1)S(1)}, bf16[96,1024]{1,0:T(8,128)(2,1)S(1)}, u32[]{:S(2)}, u32[]{:S(2)}) collective-permute-start(bf16[96,1024]{1,0:T(8,128)(2,1)S(1)} %get-tuple-element.97), channel_id=1, source_target_pairs={{0,4},{2,6},{4,0},{6,2},{8,12},{10,14},{12,8},{14,10},{16,20},{18,... | collective-permute-start | bytes 589832 | tf_op jit(solution)/shard_map/ppermute | solution.py:36
  69.9 7.4 %collective-permute-start.18 = (bf16[64,1024]{1,0:T(8,128)(2,1)S(1)}, bf16[64,1024]{1,0:T(8,128)(2,1)S(1)}, u32[]{:S(2)}, u32[]{:S(2)}) collective-permute-start(bf16[64,1024]{1,0:T(8,128)(2,1)S(1)} %get-tuple-element.95), channel_id=1, source_target_pairs={{0,16},{2,18},{4,20},{6,22},{8,24},{10,26},{12,28},{14,30},{16,0},... | collective-permute-start | bytes 393224 | tf_op jit(solution)/shard_map/ppermute | solution.py:36
  72.1 5.4 %collective-permute-start.19 = (bf16[64,1024]{1,0:T(8,128)(2,1)S(1)}, bf16[64,1024]{1,0:T(8,128)(2,1)S(1)}, u32[]{:S(2)}, u32[]{:S(2)}) collective-permute-start(bf16[64,1024]{1,0:T(8,128)(2,1)S(1)} %get-tuple-element.96), channel_id=1, source_target_pairs={{0,8},{2,10},{4,12},{6,14},{8,0},{10,2},{12,4},{14,6},{16,24},{18,... | collective-permute-start | bytes 393224 | tf_op jit(solution)/shard_map/ppermute | solution.py:36

commit v7 on v6

--- a/solution.py
+++ b/solution.py
@@ -236,10 +236,10 @@
     def _(step):
         columns = pl.ds(pl.multiple_of(step * COL, COL), COL)
         square = jnp.zeros((1, COL), f32)
-        for k in range(0, width, 256):
-            part = start[k : k + 256, columns] + dot(last_turned[k : k + 256, :], kt[:, columns])
+        for k in range(0, width, 512):
+            part = start[k : k + 512, columns] + dot(last_turned[k : k + 512, :], kt[:, columns])
             square = square - jnp.sum(part * part, axis=0, keepdims=True)
-            ab[k : k + 256, columns] = part.astype(bf16)
+            ab[k : k + 512, columns] = part.astype(bf16)
         for l in range(0, width, 256):
             rows = turned[l : l + 256, l:]
             if l == 0:
@@ -311,7 +311,7 @@
     slope = ((labels[...] == classes).astype(f32) - chances).astype(bf16)
     heavy[...] = (bt[...].astype(f32) * twice).astype(bf16)
     width = ab.shape[0]
-    state[:, :width] = dot_nt(slope, ab[...])
+    state[:, :width] = dot_nt(ab[...], slope).T
     if state.shape[1] > width:
         for i in range(ROWS_DEV // SLOT):
             there = pl.ds(pl.multiple_of(SLOT * (lax.axis_index("obs") ^ i), SLOT), SLOT)

time: 78.9 us -> 78.3 us (level)
  no operation moved by 1% of the time
where the time goes in v7:
time: 78.3 us; the launch traced here: 77.9 us
  starting transfers between devices  24.7 us (32%)
  waiting for transfers between devices  24.7 us (32%)
  Pallas kernels  21.7 us (28%)
  local copies, waits for them, and re-layouts  5.95 us (8%)
  between operations  0.86 us (1%)
    ppermute x21, waiting for transfers between devices, swap(): return lax.ppermute(value, axis, [(i, i ^ bit) for i in range(size)])  24.7 us
    ppermute x21, starting transfers between devices, swap(): return lax.ppermute(value, axis, [(i, i ^ bit) for i in range(size)])  24.7 us
    unnamed x22, local copies, waits for them, and re-layouts  5.95 us
    pallas_call x2, Pallas kernels, whiten(): pl.pallas_call(functools.partial(whiten_kernel, nz, number, places), out_...  5.39 us
    pallas_call x1, Pallas kernels, body(): pl.pallas_call(functools.partial(covary_kernel, nz, last, last_places, ch...  4.73 us
    pallas_call x1, Pallas kernels, body(): pl.pallas_call(functools.partial(slope_kernel, nz), out_shape=[jax.ShapeD...  3.38 us
    pallas_call x1, Pallas kernels, body(): pl.pallas_call(functools.partial(first_rows_kernel, nz), out_shape=[cover...  2.93 us
    pallas_call x1, Pallas kernels, body(): pl.pallas_call(functools.partial(more_rows_kernel, nz), out_shape=covered...  2.04 us
  transfers between devices with their start and end apart: 21, of which 15 were waited for; matrix products, arithmetic and copies ran while one was open for 0% of the time, Pallas kernels for 16%

profile of v7, /device:TPU:0, one launch (start us, length us, event | category | flops | bytes accessed | tf_op | source)
XLA Modules:
  0.0 77.9 jit_solution(12065825379094423189)
XLA Ops:
  0.6 0.0 copy-start
  0.6 0.9 %copy-done = bf16[64,1024]{1,0:T(8,128)(2,1)S(1)} copy-done((bf16[64,1024]{1,0:T(8,128)(2,1)S(1)}, bf16[64,1024]{1,0:T(8,128)(2,1)}, u32[]{:S(2)}) %copy-start) | copy-done | bytes 131096
  1.5 0.9 %copy-done.2 = bf16[64,1024]{1,0:T(8,128)(2,1)S(1)} copy-done((bf16[64,1024]{1,0:T(8,128)(2,1)S(1)}, bf16[64,1024]{1,0:T(8,128)(2,1)}, u32[]{:S(2)}) %copy-start.2) | copy-done | bytes 131096
  2.5 4.1 %collective-permute-start.2 = (bf16[128,1024]{1,0:T(8,128)(2,1)S(1)}, bf16[128,1024]{1,0:T(8,128)(2,1)S(1)}, u32[]{:S(2)}, u32[]{:S(2)}) collective-permute-start(bf16[128,1024]{1,0:T(8,128)(2,1)S(1)} %join.7.refs_0_), channel_id=1, source_target_pairs={{0,16},{2,18},{4,20},{6,22},{8,24},{10,26},{12,28},{14,30},{16,0},... | collective-permute-start | bytes 786440 | tf_op jit(solution)/shard_map/ppermute | solution.py:36
  6.6 1.6 %collective-permute-start.1 = (bf16[128,1024]{1,0:T(8,128)(2,1)S(1)}, bf16[128,1024]{1,0:T(8,128)(2,1)S(1)}, u32[]{:S(2)}, u32[]{:S(2)}) collective-permute-start(bf16[128,1024]{1,0:T(8,128)(2,1)S(1)} %join.7.refs_0_), channel_id=1, source_target_pairs={{0,8},{2,10},{4,12},{6,14},{8,0},{10,2},{12,4},{14,6},{16,24},{18,... | collective-permute-start | bytes 786440 | tf_op jit(solution)/shard_map/ppermute | solution.py:36
  8.1 1.5 %collective-permute-start = (bf16[128,1024]{1,0:T(8,128)(2,1)S(1)}, bf16[128,1024]{1,0:T(8,128)(2,1)S(1)}, u32[]{:S(2)}, u32[]{:S(2)}) collective-permute-start(bf16[128,1024]{1,0:T(8,128)(2,1)S(1)} %join.7.refs_0_), channel_id=1, source_target_pairs={{0,4},{2,6},{4,0},{6,2},{8,12},{10,14},{12,8},{14,10},{16,20},{18,... | collective-permute-start | bytes 786440 | tf_op jit(solution)/shard_map/ppermute | solution.py:36
  9.6 0.7 copy-done.4
  10.4 0.7 copy-done.5
  11.1 0.0 copy-start.7
  11.1 0.7 copy-done.7
  11.8 0.7 copy-done.8
  12.5 0.7 copy-done.9
  13.2 0.7 copy-done.10
  13.8 2.9 %first_rows.1 = (bf16[512,2048]{1,0:T(8,128)(2,1)S(1)}, s32[1,2048]{1,0:T(1,128)S(1)}, f32[1,2048]{1,0:T(1,128)S(1)}, f32[1024,8]{1,0:T(8,128)S(1)}, f32[8,2048]{1,0:T(8,128)S(1)}, /*index=5*/f32[8,8]{1,0:T(8,128)S(1)}) custom-call(f32[3,2048]{1,0:T(4,128)S(1)} %stack.1.arrived, f32[2,1024]{1,0:T(2,128)S(1)} %copy-done.7, s32[1,1024]{1,0:T(1,128)S(1)} %bitcast.3, ...), custom_call_target="tpu_custom_call" | custom-call | flops 20971520 | bytes 2097152 | tf_op jit(solution)/shard_map/first_rows/pallas_call | solution.py:508
  16.8 1.8 %collective-permute-done.2.refs_0_.refs_3_ = bf16[128,1024]{1,0:T(8,128)(2,1)S(1)} collective-permute-done((bf16[128,1024]{1,0:T(8,128)(2,1)S(1)}, bf16[128,1024]{1,0:T(8,128)(2,1)S(1)}, u32[]{:S(2)}, u32[]{:S(2)}) %collective-permute-start.2) | collective-permute-done | bytes 262176 | tf_op jit(solution)/shard_map/ppermute | solution.py:36
  18.6 0.2 collective-permute-done.1.refs_1_.refs_2_
  18.8 0.0 collective-permute-done.refs_1_
  18.8 0.1 join.10.refs_0_.refs_2_
  18.9 0.1 collective-permute-start.5
  19.0 1.6 %collective-permute-start.4 = (bf16[192,1024]{1,0:T(8,128)(2,1)S(1)}, bf16[192,1024]{1,0:T(8,128)(2,1)S(1)}, u32[]{:S(2)}, u32[]{:S(2)}) collective-permute-start(bf16[192,1024]{1,0:T(8,128)(2,1)S(1)} %join.9), channel_id=1, source_target_pairs={{0,8},{2,10},{4,12},{6,14},{8,0},{10,2},{12,4},{14,6},{16,24},{18,... | collective-permute-start | bytes 1179656 | tf_op jit(solution)/shard_map/ppermute | solution.py:36
  20.6 1.5 %collective-permute-start.3 = (bf16[192,1024]{1,0:T(8,128)(2,1)S(1)}, bf16[192,1024]{1,0:T(8,128)(2,1)S(1)}, u32[]{:S(2)}, u32[]{:S(2)}) collective-permute-start(bf16[192,1024]{1,0:T(8,128)(2,1)S(1)} %join.8), channel_id=1, source_target_pairs={{0,4},{2,6},{4,0},{6,2},{8,12},{10,14},{12,8},{14,10},{16,20},{18,... | collective-permute-start | bytes 1179656 | tf_op jit(solution)/shard_map/ppermute | solution.py:36
  22.1 2.0 %more_rows.1 = (bf16[384,2048]{1,0:T(8,128)(2,1)S(1)}, bf16[128,2048]{1,0:T(8,128)(2,1)S(1)}) custom-call(f32[1024,8]{1,0:T(8,128)S(1)} %get-tuple-element.62.columns, f32[8,2048]{1,0:T(8,128)S(1)} %get-tuple-element.63.table, f32[8,8]{1,0:T(8,128)S(1)} %get-tuple-element.64.mix), custom_call_target="tpu_custom_call" | custom-call | flops 20971520 | bytes 2097152 | tf_op jit(solution)/shard_map/more_rows/pallas_call | solution.py:532
  24.1 0.0 collective-permute-done.5.refs_1_.refs_3_
  24.1 2.5 %whiten.2.refs_0_ = f32[1024,2048]{1,0:T(8,128)S(1)} custom-call(bf16[512,2048]{1,0:T(8,128)(2,1)S(1)} %get-tuple-element.61.kt, bf16[512,1024]{1,0:T(8,128)(2,1)S(1)} %join.10.refs_0_.refs_2_, bf16[512,1024]{1,0:T(8,128)(2,1)S(1)} %collective-permute-done.5.refs_1_.refs_3_), custom_call_target="tpu_custom_call" | custom-call | flops 2147483648 | bytes 10485760 | tf_op jit(solution)/shard_map/whiten/pallas_call | solution.py:547
  26.6 4.0 %collective-permute-done.4.refs_0_.refs_1_ = bf16[192,1024]{1,0:T(8,128)(2,1)S(1)} collective-permute-done((bf16[192,1024]{1,0:T(8,128)(2,1)S(1)}, bf16[192,1024]{1,0:T(8,128)(2,1)S(1)}, u32[]{:S(2)}, u32[]{:S(2)}) %collective-permute-start.4) | collective-permute-done | bytes 393248 | tf_op jit(solution)/shard_map/ppermute | solution.py:36
  30.6 1.2 %collective-permute-done.3.refs_0_ = bf16[192,1024]{1,0:T(8,128)(2,1)S(1)} collective-permute-done((bf16[192,1024]{1,0:T(8,128)(2,1)S(1)}, bf16[192,1024]{1,0:T(8,128)(2,1)S(1)}, u32[]{:S(2)}, u32[]{:S(2)}) %collective-permute-start.3) | collective-permute-done | bytes 393248 | tf_op jit(solution)/shard_map/ppermute | solution.py:36
  31.8 0.1 join.13.refs_1_.refs_4_
  31.9 0.1 collective-permute-start.8
  32.0 0.0 copy-start.3
  32.0 0.6 collective-permute-start.7
  32.6 1.5 %collective-permute-start.6 = (bf16[64,1024]{1,0:T(8,128)(2,1)S(1)}, bf16[64,1024]{1,0:T(8,128)(2,1)S(1)}, u32[]{:S(2)}, u32[]{:S(2)}) collective-permute-start(bf16[64,1024]{1,0:T(8,128)(2,1)S(1)} %join.11), channel_id=1, source_target_pairs={{0,4},{2,6},{4,0},{6,2},{8,12},{10,14},{12,8},{14,10},{16,20},{18,... | collective-permute-start | bytes 393224 | tf_op jit(solution)/shard_map/ppermute | solution.py:36
  34.1 0.1 collective-permute-done.8.refs_2_.refs_5_
  34.2 2.9 %whiten.3.start = f32[1024,2048]{1,0:T(8,128)S(1)} custom-call(bf16[384,2048]{1,0:T(8,128)(2,1)S(1)} %get-tuple-element.70.kt, f32[1024,2048]{1,0:T(8,128)S(1)} %whiten.2.refs_0_, bf16[384,1024]{1,0:T(8,128)(2,1)S(1)} %join.13.refs_1_.refs_4_, bf16[384,1024]{1,0:T(8,128)(2,1)S(1)} %collective-permute-done.8.refs_2_.refs_5_), custom_call_target="tpu_custom_call", output_to_operand_aliasing={{}: (1, {})} | custom-call | flops 1610612736 | bytes 10485760 | tf_op jit(solution)/shard_map/whiten/pallas_call | solution.py:547
  37.1 0.0 copy-start.6
  37.1 0.8 %collective-permute-done.7.refs_6_ = bf16[64,1024]{1,0:T(8,128)(2,1)S(1)} collective-permute-done((bf16[64,1024]{1,0:T(8,128)(2,1)S(1)}, bf16[64,1024]{1,0:T(8,128)(2,1)S(1)}, u32[]{:S(2)}, u32[]{:S(2)}) %collective-permute-start.7) | collective-permute-done | bytes 131104 | tf_op jit(solution)/shard_map/ppermute | solution.py:36
  37.9 0.3 collective-permute-done.6.refs_0_
  38.2 0.5 collective-permute-start.10
  38.7 0.8 %collective-permute-done.9.refs_1_ = bf16[64,1024]{1,0:T(8,128)(2,1)S(1)} collective-permute-done((bf16[64,1024]{1,0:T(8,128)(2,1)S(1)}, bf16[64,1024]{1,0:T(8,128)(2,1)S(1)}, u32[]{:S(2)}, u32[]{:S(2)}) %collective-permute-start.9) | collective-permute-done | bytes 131104 | tf_op jit(solution)/shard_map/ppermute | solution.py:36
  39.5 0.2 collective-permute-done.10.refs_7_
  39.7 4.7 %covary.1 = (bf16[1024,2048]{1,0:T(8,128)(2,1)S(1)}, bf16[1024,2048]{1,0:T(8,128)(2,1)S(1)}, f32[8,2304]{1,0:T(8,128)S(1)}) custom-call(bf16[128,2048]{1,0:T(8,128)(2,1)S(1)} %get-tuple-element.67.kt, f32[1024,2048]{1,0:T(8,128)S(1)} %whiten.3.start, bf16[8,1024]{1,0:T(8,128)(2,1)S(1)} %copy-done.3, bf16[64,1024]{1,0:T(8,128)(2,1)S(1)} %collective-permute-done.6.refs_0_, ...), custom_call_target="tpu_custom_call" | custom-call | flops 2147483648 | bytes 10485760 | tf_op jit(solution)/shard_map/covary/pallas_call | solution.py:571
  44.5 1.6 %collective-permute-start.11 = (f32[8,2304]{1,0:T(8,128)S(1)}, f32[8,2304]{1,0:T(8,128)S(1)}, u32[]{:S(2)}, u32[]{:S(2)}) collective-permute-start(f32[8,2304]{1,0:T(8,128)S(1)} %get-tuple-element.75.own), channel_id=1, source_target_pairs={{0,1},{1,0},{2,3},{3,2},{4,5},{5,4},{6,7},{7,6},{8,9},{9,8},{10,11... | collective-permute-start | bytes 221192 | tf_op jit(solution)/shard_map/ppermute | solution.py:36
  46.1 2.9 %collective-permute-done.11.other = f32[8,2304]{1,0:T(8,128)S(1)} collective-permute-done((f32[8,2304]{1,0:T(8,128)S(1)}, f32[8,2304]{1,0:T(8,128)S(1)}, u32[]{:S(2)}, u32[]{:S(2)}) %collective-permute-start.11) | collective-permute-done | bytes 73760 | tf_op jit(solution)/shard_map/ppermute | solution.py:36
  49.0 3.4 %slopes.1 = (f32[8,2048]{1,0:T(8,128)}, f32[8,3072]{1,0:T(8,128)S(1)}, bf16[1024,2048]{1,0:T(8,128)(2,1)S(1)}, f32[64,2560]{1,0:T(8,128)S(1)}, bf16[96,2560]{1,0:T(8,128)(2,1)S(1)}) custom-call(f32[8,2304]{1,0:T(8,128)S(1)} %get-tuple-element.75.own, f32[8,2304]{1,0:T(8,128)S(1)} %collective-permute-done.11.other, f32[8]{0:T(128)S(1)} %copy-done.6, ...), custom_call_target="tpu_custom_call" | custom-call | tf_op jit(solution)/shard_map/slopes/pallas_call | solution.py:605
  52.4 0.1 collective-permute-start.12
  52.5 1.7 %near_outer.1 = (f32[64,2560]{1,0:T(8,128)S(1)}, bf16[64,2560]{1,0:T(8,128)(2,1)S(1)}) custom-call(bf16[1024,2048]{1,0:T(8,128)(2,1)S(1)} %get-tuple-element.78.ab, bf16[1024,2048]{1,0:T(8,128)(2,1)S(1)} %get-tuple-element.86.heavy), custom_call_target="tpu_custom_call" | custom-call | tf_op jit(solution)/shard_map/near_outer/pallas_call | solution.py:620
  54.2 0.0 copy-start.1
  54.2 0.6 collective-permute-start.13
  54.8 0.1 add_pair.1
  54.9 0.1 add_level.3
  55.0 1.6 %collective-permute-start.14 = (bf16[64,1024]{1,0:T(8,128)(2,1)S(1)}, bf16[64,1024]{1,0:T(8,128)(2,1)S(1)}, u32[]{:S(2)}, u32[]{:S(2)}) collective-permute-start(bf16[64,1024]{1,0:T(8,128)(2,1)S(1)} %get-tuple-element.89), channel_id=1, source_target_pairs={{0,4},{2,6},{4,0},{6,2},{8,12},{10,14},{12,8},{14,10},{16,20},{18,... | collective-permute-start | bytes 393224 | tf_op jit(solution)/shard_map/ppermute | solution.py:36
  56.6 2.1 %collective-permute-start.15 = (f32[16,1024]{1,0:T(8,128)S(1)}, f32[16,1024]{1,0:T(8,128)S(1)}, u32[]{:S(2)}, u32[]{:S(2)}) collective-permute-start(f32[16,1024]{1,0:T(8,128)S(1)} %get-tuple-element.90), channel_id=1, source_target_pairs={{0,16},{2,18},{4,20},{6,22},{8,24},{10,26},{12,28},{14,30},{16,0},... | collective-permute-start | bytes 196616 | tf_op jit(solution)/shard_map/ppermute | solution.py:36
  58.7 0.5 collective-permute-start.16
  59.2 0.1 add_near_pair.1.near
  59.3 3.5 %collective-permute-done.15.refs_1_ = f32[16,1024]{1,0:T(8,128)S(1)} collective-permute-done((f32[16,1024]{1,0:T(8,128)S(1)}, f32[16,1024]{1,0:T(8,128)S(1)}, u32[]{:S(2)}, u32[]{:S(2)}) %collective-permute-start.15) | collective-permute-done | bytes 65568 | tf_op jit(solution)/shard_map/ppermute | solution.py:36
  62.9 0.6 collective-permute-start.17
  63.4 3.0 %collective-permute-done.16.refs_0_ = bf16[128,1024]{1,0:T(8,128)(2,1)S(1)} collective-permute-done((bf16[128,1024]{1,0:T(8,128)(2,1)S(1)}, bf16[128,1024]{1,0:T(8,128)(2,1)S(1)}, u32[]{:S(2)}, u32[]{:S(2)}) %collective-permute-start.16) | collective-permute-done | bytes 262176 | tf_op jit(solution)/shard_map/ppermute | solution.py:36
  66.4 2.2 %collective-permute-done.17.refs_1_ = bf16[96,1024]{1,0:T(8,128)(2,1)S(1)} collective-permute-done((bf16[96,1024]{1,0:T(8,128)(2,1)S(1)}, bf16[96,1024]{1,0:T(8,128)(2,1)S(1)}, u32[]{:S(2)}, u32[]{:S(2)}) %collective-permute-start.17) | collective-permute-done | bytes 196640 | tf_op jit(solution)/shard_map/ppermute | solution.py:36
  68.6 0.1 add_level.5
  68.7 0.6 collective-permute-start.20
  69.3 2.3 %collective-permute-start.18 = (bf16[64,1024]{1,0:T(8,128)(2,1)S(1)}, bf16[64,1024]{1,0:T(8,128)(2,1)S(1)}, u32[]{:S(2)}, u32[]{:S(2)}) collective-permute-start(bf16[64,1024]{1,0:T(8,128)(2,1)S(1)} %get-tuple-element.95), channel_id=1, source_target_pairs={{0,16},{2,18},{4,20},{6,22},{8,24},{10,26},{12,28},{14,30},{16,0},... | collective-permute-start | bytes 393224 | tf_op jit(solution)/shard_map/ppermute | solution.py:36
  71.6 1.7 %collective-permute-start.19 = (bf16[64,1024]{1,0:T(8,128)(2,1)S(1)}, bf16[64,1024]{1,0:T(8,128)(2,1)S(1)}, u32[]{:S(2)}, u32[]{:S(2)}) collective-permute-start(bf16[64,1024]{1,0:T(8,128)(2,1)S(1)} %get-tuple-element.96), channel_id=1, source_target_pairs={{0,8},{2,10},{4,12},{6,14},{8,0},{10,2},{12,4},{14,6},{16,24},{18,... | collective-permute-start | bytes 393224 | tf_op jit(solution)/shard_map/ppermute | solution.py:36
  73.3 3.4 %collective-permute-done.18.refs_0_ = bf16[64,1024]{1,0:T(8,128)(2,1)S(1)} collective-permute-done((bf16[64,1024]{1,0:T(8,128)(2,1)S(1)}, bf16[64,1024]{1,0:T(8,128)(2,1)S(1)}, u32[]{:S(2)}, u32[]{:S(2)}) %collective-permute-start.18) | collective-permute-done | bytes 131104 | tf_op jit(solution)/shard_map/ppermute | solution.py:36
  76.7 0.3 collective-permute-done.19.refs_1_
  77.0 0.9 %finish.1 = (f32[64,1024]{1,0:T(8,128)}, f32[8,1024]{1,0:T(8,128)}, f32[8,2048]{1,0:T(8,128)}) custom-call(f32[8,3072]{1,0:T(8,128)S(1)} %get-tuple-element.94.state, f32[64,2560]{1,0:T(8,128)S(1)} %add_near_pair.1.near, bf16[64,1024]{1,0:T(8,128)(2,1)S(1)} %copy-done.1, bf16[8,1024]{1,0:T(8,128)(2,1)S(1)} %copy-done.3, ...), custom_call_target="tpu_custom_call" | custom-call | tf_op jit(solution)/shard_map/finish/pallas_call | solution.py:663
  (21 shorter events, 0.2 us)
Async XLA Ops:
  0.6 0.9 %copy-start = (bf16[64,1024]{1,0:T(8,128)(2,1)S(1)}, bf16[64,1024]{1,0:T(8,128)(2,1)}, u32[]{:S(2)}) copy-start(bf16[64,1024]{1,0:T(8,128)(2,1)} %chol.1) | copy-start | bytes 393220
  1.5 0.9 %copy-start.2 = (bf16[64,1024]{1,0:T(8,128)(2,1)S(1)}, bf16[64,1024]{1,0:T(8,128)(2,1)}, u32[]{:S(2)}) copy-start(bf16[64,1024]{1,0:T(8,128)(2,1)} %refs_0_.1) | copy-start | bytes 393220
  2.5 16.1 %collective-permute-start.2 = (bf16[128,1024]{1,0:T(8,128)(2,1)S(1)}, bf16[128,1024]{1,0:T(8,128)(2,1)S(1)}, u32[]{:S(2)}, u32[]{:S(2)}) collective-permute-start(bf16[128,1024]{1,0:T(8,128)(2,1)S(1)} %join.7.refs_0_), channel_id=1, source_target_pairs={{0,16},{2,18},{4,20},{6,22},{8,24},{10,26},{12,28},{14,30},{16,0},... | collective-permute-start | bytes 786440 | tf_op jit(solution)/shard_map/ppermute | solution.py:36
  6.6 12.2 %collective-permute-start.1 = (bf16[128,1024]{1,0:T(8,128)(2,1)S(1)}, bf16[128,1024]{1,0:T(8,128)(2,1)S(1)}, u32[]{:S(2)}, u32[]{:S(2)}) collective-permute-start(bf16[128,1024]{1,0:T(8,128)(2,1)S(1)} %join.7.refs_0_), channel_id=1, source_target_pairs={{0,8},{2,10},{4,12},{6,14},{8,0},{10,2},{12,4},{14,6},{16,24},{18,... | collective-permute-start | bytes 786440 | tf_op jit(solution)/shard_map/ppermute | solution.py:36
  8.1 10.6 %collective-permute-start = (bf16[128,1024]{1,0:T(8,128)(2,1)S(1)}, bf16[128,1024]{1,0:T(8,128)(2,1)S(1)}, u32[]{:S(2)}, u32[]{:S(2)}) collective-permute-start(bf16[128,1024]{1,0:T(8,128)(2,1)S(1)} %join.7.refs_0_), channel_id=1, source_target_pairs={{0,4},{2,6},{4,0},{6,2},{8,12},{10,14},{12,8},{14,10},{16,20},{18,... | collective-permute-start | bytes 786440 | tf_op jit(solution)/shard_map/ppermute | solution.py:36
  9.6 0.7 copy-start.4
  10.4 0.7 copy-start.5
  11.1 0.7 copy-start.7
  11.8 0.7 copy-start.8
  12.5 0.7 copy-start.9
  13.2 0.7 copy-start.10
  18.9 5.2 %collective-permute-start.5 = (bf16[512,1024]{1,0:T(8,128)(2,1)S(1)}, bf16[512,1024]{1,0:T(8,128)(2,1)S(1)}, u32[]{:S(2)}, u32[]{:S(2)}) collective-permute-start(bf16[512,1024]{1,0:T(8,128)(2,1)S(1)} %join.10.refs_0_.refs_2_), channel_id=1, source_target_pairs={{0,2},{2,0},{4,6},{6,4},{8,10},{10,8},{12,14},{14,12},{16,18},{18,... | collective-permute-start | bytes 3145736 | tf_op jit(solution)/shard_map/ppermute | solution.py:36
  19.0 11.6 %collective-permute-start.4 = (bf16[192,1024]{1,0:T(8,128)(2,1)S(1)}, bf16[192,1024]{1,0:T(8,128)(2,1)S(1)}, u32[]{:S(2)}, u32[]{:S(2)}) collective-permute-start(bf16[192,1024]{1,0:T(8,128)(2,1)S(1)} %join.9), channel_id=1, source_target_pairs={{0,8},{2,10},{4,12},{6,14},{8,0},{10,2},{12,4},{14,6},{16,24},{18,... | collective-permute-start | bytes 1179656 | tf_op jit(solution)/shard_map/ppermute | solution.py:36
  20.6 11.2 %collective-permute-start.3 = (bf16[192,1024]{1,0:T(8,128)(2,1)S(1)}, bf16[192,1024]{1,0:T(8,128)(2,1)S(1)}, u32[]{:S(2)}, u32[]{:S(2)}) collective-permute-start(bf16[192,1024]{1,0:T(8,128)(2,1)S(1)} %join.8), channel_id=1, source_target_pairs={{0,4},{2,6},{4,0},{6,2},{8,12},{10,14},{12,8},{14,10},{16,20},{18,... | collective-permute-start | bytes 1179656 | tf_op jit(solution)/shard_map/ppermute | solution.py:36
  31.9 2.4 %collective-permute-start.8 = (bf16[384,1024]{1,0:T(8,128)(2,1)S(1)}, bf16[384,1024]{1,0:T(8,128)(2,1)S(1)}, u32[]{:S(2)}, u32[]{:S(2)}) collective-permute-start(bf16[384,1024]{1,0:T(8,128)(2,1)S(1)} %join.13.refs_1_.refs_4_), channel_id=1, source_target_pairs={{0,2},{2,0},{4,6},{6,4},{8,10},{10,8},{12,14},{14,12},{16,18},{18,... | collective-permute-start | bytes 2359304 | tf_op jit(solution)/shard_map/ppermute | solution.py:36
  32.0 7.8 %copy-start.3 = (bf16[8,1024]{1,0:T(8,128)(2,1)S(1)}, bf16[8,1024]{1,0:T(8,128)(2,1)}, u32[]{:S(2)}) copy-start(bf16[8,1024]{1,0:T(8,128)(2,1)} %means.3) | copy-start | bytes 49156
  32.0 6.0 %collective-permute-start.7 = (bf16[64,1024]{1,0:T(8,128)(2,1)S(1)}, bf16[64,1024]{1,0:T(8,128)(2,1)S(1)}, u32[]{:S(2)}, u32[]{:S(2)}) collective-permute-start(bf16[64,1024]{1,0:T(8,128)(2,1)S(1)} %join.12), channel_id=1, source_target_pairs={{0,8},{2,10},{4,12},{6,14},{8,0},{10,2},{12,4},{14,6},{16,24},{18,... | collective-permute-start | bytes 393224 | tf_op jit(solution)/shard_map/ppermute | solution.py:36
  32.6 5.6 %collective-permute-start.6 = (bf16[64,1024]{1,0:T(8,128)(2,1)S(1)}, bf16[64,1024]{1,0:T(8,128)(2,1)S(1)}, u32[]{:S(2)}, u32[]{:S(2)}) collective-permute-start(bf16[64,1024]{1,0:T(8,128)(2,1)S(1)} %join.11), channel_id=1, source_target_pairs={{0,4},{2,6},{4,0},{6,2},{8,12},{10,14},{12,8},{14,10},{16,20},{18,... | collective-permute-start | bytes 393224 | tf_op jit(solution)/shard_map/ppermute | solution.py:36
  37.1 11.9 %copy-start.6 = (f32[8]{0:T(128)S(1)}, f32[8]{0:T(128)}, u32[]{:S(2)}) copy-start(f32[8]{0:T(128)} %scales.1) | copy-start | bytes 100
  38.2 1.3 %collective-permute-start.9 = (bf16[64,1024]{1,0:T(8,128)(2,1)S(1)}, bf16[64,1024]{1,0:T(8,128)(2,1)S(1)}, u32[]{:S(2)}, u32[]{:S(2)}) collective-permute-start(bf16[64,1024]{1,0:T(8,128)(2,1)S(1)} %collective-permute-done.6.refs_0_), channel_id=1, source_target_pairs={{0,2},{2,0},{4,6},{6,4},{8,10},{10,8},{12,14},{14,12},{16,18},{18,... | collective-permute-start | bytes 393224 | tf_op jit(solution)/shard_map/ppermute | solution.py:36
  38.2 1.5 %collective-permute-start.10 = (bf16[64,1024]{1,0:T(8,128)(2,1)S(1)}, bf16[64,1024]{1,0:T(8,128)(2,1)S(1)}, u32[]{:S(2)}, u32[]{:S(2)}) collective-permute-start(bf16[64,1024]{1,0:T(8,128)(2,1)S(1)} %collective-permute-done.7.refs_6_), channel_id=1, source_target_pairs={{0,2},{2,0},{4,6},{6,4},{8,10},{10,8},{12,14},{14,12},{16,18},{18,... | collective-permute-start | bytes 393224 | tf_op jit(solution)/shard_map/ppermute | solution.py:36
  44.5 4.6 %collective-permute-start.11 = (f32[8,2304]{1,0:T(8,128)S(1)}, f32[8,2304]{1,0:T(8,128)S(1)}, u32[]{:S(2)}, u32[]{:S(2)}) collective-permute-start(f32[8,2304]{1,0:T(8,128)S(1)} %get-tuple-element.75.own), channel_id=1, source_target_pairs={{0,1},{1,0},{2,3},{3,2},{4,5},{5,4},{6,7},{7,6},{8,9},{9,8},{10,11... | collective-permute-start | bytes 221192 | tf_op jit(solution)/shard_map/ppermute | solution.py:36
  52.4 2.4 %collective-permute-start.12 = (bf16[96,2560]{1,0:T(8,128)(2,1)S(1)}, bf16[96,2560]{1,0:T(8,128)(2,1)S(1)}, u32[]{:S(2)}, u32[]{:S(2)}) collective-permute-start(bf16[96,2560]{1,0:T(8,128)(2,1)S(1)} %get-tuple-element.82), channel_id=1, source_target_pairs={{0,2},{2,0},{4,6},{6,4},{8,10},{10,8},{12,14},{14,12},{16,18},{18,... | collective-permute-start | bytes 1474568 | tf_op jit(solution)/shard_map/ppermute | solution.py:36
  54.2 22.7 %copy-start.1 = (bf16[64,1024]{1,0:T(8,128)(2,1)S(1)}, bf16[64,1024]{1,0:T(8,128)(2,1)}, u32[]{:S(2)}) copy-start(bf16[64,1024]{1,0:T(8,128)(2,1)} %chol.1) | copy-start | bytes 393220
  54.2 5.0 %collective-permute-start.13 = (bf16[64,2560]{1,0:T(8,128)(2,1)S(1)}, bf16[64,2560]{1,0:T(8,128)(2,1)S(1)}, u32[]{:S(2)}, u32[]{:S(2)}) collective-permute-start(bf16[64,2560]{1,0:T(8,128)(2,1)S(1)} %get-tuple-element.88), channel_id=1, source_target_pairs={{0,2},{2,0},{4,6},{6,4},{8,10},{10,8},{12,14},{14,12},{16,18},{18,... | collective-permute-start | bytes 983048 | tf_op jit(solution)/shard_map/ppermute | solution.py:36
  55.0 7.8 %collective-permute-start.14 = (bf16[64,1024]{1,0:T(8,128)(2,1)S(1)}, bf16[64,1024]{1,0:T(8,128)(2,1)S(1)}, u32[]{:S(2)}, u32[]{:S(2)}) collective-permute-start(bf16[64,1024]{1,0:T(8,128)(2,1)S(1)} %get-tuple-element.89), channel_id=1, source_target_pairs={{0,4},{2,6},{4,0},{6,2},{8,12},{10,14},{12,8},{14,10},{16,20},{18,... | collective-permute-start | bytes 393224 | tf_op jit(solution)/shard_map/ppermute | solution.py:36
  56.6 6.2 %collective-permute-start.15 = (f32[16,1024]{1,0:T(8,128)S(1)}, f32[16,1024]{1,0:T(8,128)S(1)}, u32[]{:S(2)}, u32[]{:S(2)}) collective-permute-start(f32[16,1024]{1,0:T(8,128)S(1)} %get-tuple-element.90), channel_id=1, source_target_pairs={{0,16},{2,18},{4,20},{6,22},{8,24},{10,26},{12,28},{14,30},{16,0},... | collective-permute-start | bytes 196616 | tf_op jit(solution)/shard_map/ppermute | solution.py:36
  58.7 7.7 %collective-permute-start.16 = (bf16[128,1024]{1,0:T(8,128)(2,1)S(1)}, bf16[128,1024]{1,0:T(8,128)(2,1)S(1)}, u32[]{:S(2)}, u32[]{:S(2)}) collective-permute-start(bf16[128,1024]{1,0:T(8,128)(2,1)S(1)} %get-tuple-element.92), channel_id=1, source_target_pairs={{0,4},{2,6},{4,0},{6,2},{8,12},{10,14},{12,8},{14,10},{16,20},{18,... | collective-permute-start | bytes 786440 | tf_op jit(solution)/shard_map/ppermute | solution.py:36
  62.9 5.7 %collective-permute-start.17 = (bf16[96,1024]{1,0:T(8,128)(2,1)S(1)}, bf16[96,1024]{1,0:T(8,128)(2,1)S(1)}, u32[]{:S(2)}, u32[]{:S(2)}) collective-permute-start(bf16[96,1024]{1,0:T(8,128)(2,1)S(1)} %get-tuple-element.93), channel_id=1, source_target_pairs={{0,8},{2,10},{4,12},{6,14},{8,0},{10,2},{12,4},{14,6},{16,24},{18,... | collective-permute-start | bytes 589832 | tf_op jit(solution)/shard_map/ppermute | solution.py:36
  68.7 8.2 %collective-permute-start.20 = (bf16[96,1024]{1,0:T(8,128)(2,1)S(1)}, bf16[96,1024]{1,0:T(8,128)(2,1)S(1)}, u32[]{:S(2)}, u32[]{:S(2)}) collective-permute-start(bf16[96,1024]{1,0:T(8,128)(2,1)S(1)} %get-tuple-element.97), channel_id=1, source_target_pairs={{0,4},{2,6},{4,0},{6,2},{8,12},{10,14},{12,8},{14,10},{16,20},{18,... | collective-permute-start | bytes 589832 | tf_op jit(solution)/shard_map/ppermute | solution.py:36
  69.3 7.4 %collective-permute-start.18 = (bf16[64,1024]{1,0:T(8,128)(2,1)S(1)}, bf16[64,1024]{1,0:T(8,128)(2,1)S(1)}, u32[]{:S(2)}, u32[]{:S(2)}) collective-permute-start(bf16[64,1024]{1,0:T(8,128)(2,1)S(1)} %get-tuple-element.95), channel_id=1, source_target_pairs={{0,16},{2,18},{4,20},{6,22},{8,24},{10,26},{12,28},{14,30},{16,0},... | collective-permute-start | bytes 393224 | tf_op jit(solution)/shard_map/ppermute | solution.py:36
  71.6 5.4 %collective-permute-start.19 = (bf16[64,1024]{1,0:T(8,128)(2,1)S(1)}, bf16[64,1024]{1,0:T(8,128)(2,1)S(1)}, u32[]{:S(2)}, u32[]{:S(2)}) collective-permute-start(bf16[64,1024]{1,0:T(8,128)(2,1)S(1)} %get-tuple-element.96), channel_id=1, source_target_pairs={{0,8},{2,10},{4,12},{6,14},{8,0},{10,2},{12,4},{14,6},{16,24},{18,... | collective-permute-start | bytes 393224 | tf_op jit(solution)/shard_map/ppermute | solution.py:36

commit v8 on v7

--- a/solution.py
+++ b/solution.py
@@ -214,11 +214,11 @@
     @pl.loop(0, ROWS_DEV // COL)
     def _(step):
         columns = pl.ds(pl.multiple_of(step * COL, COL), COL)
-        for k in range(0, turned.shape[0], 256):
-            part = dot(turned[k : k + 256, :], kt[:, columns])
+        for k in range(0, turned.shape[0], 512):
+            part = dot(turned[k : k + 512, :], kt[:, columns])
             if number > 0:
-                part = part + start[k : k + 256, columns]
-            total[k : k + 256, columns] = part
+                part = part + start[k : k + 512, columns]
+            total[k : k + 512, columns] = part
 
 
 def covary_kernel(nz, last, last_places, places, kt, start, means, *refs):
@@ -236,10 +236,10 @@
     def _(step):
         columns = pl.ds(pl.multiple_of(step * COL, COL), COL)
         square = jnp.zeros((1, COL), f32)
-        for k in range(0, width, 512):
-            part = start[k : k + 512, columns] + dot(last_turned[k : k + 512, :], kt[:, columns])
+        for k in range(0, width, 1024):
+            part = start[k : k + 1024, columns] + dot(last_turned[k : k + 1024, :], kt[:, columns])
             square = square - jnp.sum(part * part, axis=0, keepdims=True)
-            ab[k : k + 512, columns] = part.astype(bf16)
+            ab[k : k + 1024, columns] = part.astype(bf16)
         for l in range(0, width, 256):
             rows = turned[l : l + 256, l:]
             if l == 0:

time: 78.3 us -> 78.3 us (level)
  no operation moved by 1% of the time
where the time goes in v8:
time: 78.3 us; the launch traced here: 77.9 us
  waiting for transfers between devices  24.8 us (32%)
  starting transfers between devices  24.7 us (32%)
  Pallas kernels  21.6 us (28%)
  local copies, waits for them, and re-layouts  5.95 us (8%)
  between operations  0.86 us (1%)
    ppermute x21, waiting for transfers between devices, swap(): return lax.ppermute(value, axis, [(i, i ^ bit) for i in range(size)])  24.8 us
    ppermute x21, starting transfers between devices, swap(): return lax.ppermute(value, axis, [(i, i ^ bit) for i in range(size)])  24.7 us
    unnamed x22, local copies, waits for them, and re-layouts  5.95 us
    pallas_call x2, Pallas kernels, whiten(): pl.pallas_call(functools.partial(whiten_kernel, nz, number, places), out_...  5.32 us
    pallas_call x1, Pallas kernels, body(): pl.pallas_call(functools.partial(covary_kernel, nz, last, last_places, ch...  4.73 us
    pallas_call x1, Pallas kernels, body(): pl.pallas_call(functools.partial(slope_kernel, nz), out_shape=[jax.ShapeD...  3.37 us
    pallas_call x1, Pallas kernels, body(): pl.pallas_call(functools.partial(first_rows_kernel, nz), out_shape=[cover...  2.93 us
    pallas_call x1, Pallas kernels, body(): pl.pallas_call(functools.partial(more_rows_kernel, nz), out_shape=covered...  2.04 us
  transfers between devices with their start and end apart: 21, of which 15 were waited for; matrix products, arithmetic and copies ran while one was open for 0% of the time, Pallas kernels for 16%

profile of v8, /device:TPU:0, one launch (start us, length us, event | category | flops | bytes accessed | tf_op | source)
XLA Modules:
  0.0 77.9 jit_solution(18005933495635275135)
XLA Ops:
  0.6 0.0 copy-start
  0.6 0.9 %copy-done = bf16[64,1024]{1,0:T(8,128)(2,1)S(1)} copy-done((bf16[64,1024]{1,0:T(8,128)(2,1)S(1)}, bf16[64,1024]{1,0:T(8,128)(2,1)}, u32[]{:S(2)}) %copy-start) | copy-done | bytes 131096
  1.5 0.9 %copy-done.2 = bf16[64,1024]{1,0:T(8,128)(2,1)S(1)} copy-done((bf16[64,1024]{1,0:T(8,128)(2,1)S(1)}, bf16[64,1024]{1,0:T(8,128)(2,1)}, u32[]{:S(2)}) %copy-start.2) | copy-done | bytes 131096
  2.5 4.1 %collective-permute-start.2 = (bf16[128,1024]{1,0:T(8,128)(2,1)S(1)}, bf16[128,1024]{1,0:T(8,128)(2,1)S(1)}, u32[]{:S(2)}, u32[]{:S(2)}) collective-permute-start(bf16[128,1024]{1,0:T(8,128)(2,1)S(1)} %join.7.refs_0_), channel_id=1, source_target_pairs={{0,16},{2,18},{4,20},{6,22},{8,24},{10,26},{12,28},{14,30},{16,0},... | collective-permute-start | bytes 786440 | tf_op jit(solution)/shard_map/ppermute | solution.py:36
  6.6 1.6 %collective-permute-start.1 = (bf16[128,1024]{1,0:T(8,128)(2,1)S(1)}, bf16[128,1024]{1,0:T(8,128)(2,1)S(1)}, u32[]{:S(2)}, u32[]{:S(2)}) collective-permute-start(bf16[128,1024]{1,0:T(8,128)(2,1)S(1)} %join.7.refs_0_), channel_id=1, source_target_pairs={{0,8},{2,10},{4,12},{6,14},{8,0},{10,2},{12,4},{14,6},{16,24},{18,... | collective-permute-start | bytes 786440 | tf_op jit(solution)/shard_map/ppermute | solution.py:36
  8.1 1.5 %collective-permute-start = (bf16[128,1024]{1,0:T(8,128)(2,1)S(1)}, bf16[128,1024]{1,0:T(8,128)(2,1)S(1)}, u32[]{:S(2)}, u32[]{:S(2)}) collective-permute-start(bf16[128,1024]{1,0:T(8,128)(2,1)S(1)} %join.7.refs_0_), channel_id=1, source_target_pairs={{0,4},{2,6},{4,0},{6,2},{8,12},{10,14},{12,8},{14,10},{16,20},{18,... | collective-permute-start | bytes 786440 | tf_op jit(solution)/shard_map/ppermute | solution.py:36
  9.6 0.7 copy-done.4
  10.4 0.7 copy-done.5
  11.1 0.0 copy-start.7
  11.1 0.7 copy-done.7
  11.8 0.7 copy-done.8
  12.5 0.7 copy-done.9
  13.2 0.7 copy-done.10
  13.8 2.9 %first_rows.1 = (bf16[512,2048]{1,0:T(8,128)(2,1)S(1)}, s32[1,2048]{1,0:T(1,128)S(1)}, f32[1,2048]{1,0:T(1,128)S(1)}, f32[1024,8]{1,0:T(8,128)S(1)}, f32[8,2048]{1,0:T(8,128)S(1)}, /*index=5*/f32[8,8]{1,0:T(8,128)S(1)}) custom-call(f32[3,2048]{1,0:T(4,128)S(1)} %stack.1.arrived, f32[2,1024]{1,0:T(2,128)S(1)} %copy-done.7, s32[1,1024]{1,0:T(1,128)S(1)} %bitcast.3, ...), custom_call_target="tpu_custom_call" | custom-call | flops 20971520 | bytes 2097152 | tf_op jit(solution)/shard_map/first_rows/pallas_call | solution.py:508
  16.8 1.8 %collective-permute-done.2.refs_0_.refs_3_ = bf16[128,1024]{1,0:T(8,128)(2,1)S(1)} collective-permute-done((bf16[128,1024]{1,0:T(8,128)(2,1)S(1)}, bf16[128,1024]{1,0:T(8,128)(2,1)S(1)}, u32[]{:S(2)}, u32[]{:S(2)}) %collective-permute-start.2) | collective-permute-done | bytes 262176 | tf_op jit(solution)/shard_map/ppermute | solution.py:36
  18.6 0.2 collective-permute-done.1.refs_1_.refs_2_
  18.8 0.0 collective-permute-done.refs_1_
  18.8 0.1 join.10.refs_0_.refs_2_
  18.9 0.1 collective-permute-start.5
  19.0 1.6 %collective-permute-start.4 = (bf16[192,1024]{1,0:T(8,128)(2,1)S(1)}, bf16[192,1024]{1,0:T(8,128)(2,1)S(1)}, u32[]{:S(2)}, u32[]{:S(2)}) collective-permute-start(bf16[192,1024]{1,0:T(8,128)(2,1)S(1)} %join.9), channel_id=1, source_target_pairs={{0,8},{2,10},{4,12},{6,14},{8,0},{10,2},{12,4},{14,6},{16,24},{18,... | collective-permute-start | bytes 1179656 | tf_op jit(solution)/shard_map/ppermute | solution.py:36
  20.6 1.5 %collective-permute-start.3 = (bf16[192,1024]{1,0:T(8,128)(2,1)S(1)}, bf16[192,1024]{1,0:T(8,128)(2,1)S(1)}, u32[]{:S(2)}, u32[]{:S(2)}) collective-permute-start(bf16[192,1024]{1,0:T(8,128)(2,1)S(1)} %join.8), channel_id=1, source_target_pairs={{0,4},{2,6},{4,0},{6,2},{8,12},{10,14},{12,8},{14,10},{16,20},{18,... | collective-permute-start | bytes 1179656 | tf_op jit(solution)/shard_map/ppermute | solution.py:36
  22.1 2.0 %more_rows.1 = (bf16[384,2048]{1,0:T(8,128)(2,1)S(1)}, bf16[128,2048]{1,0:T(8,128)(2,1)S(1)}) custom-call(f32[1024,8]{1,0:T(8,128)S(1)} %get-tuple-element.62.columns, f32[8,2048]{1,0:T(8,128)S(1)} %get-tuple-element.63.table, f32[8,8]{1,0:T(8,128)S(1)} %get-tuple-element.64.mix), custom_call_target="tpu_custom_call" | custom-call | flops 20971520 | bytes 2097152 | tf_op jit(solution)/shard_map/more_rows/pallas_call | solution.py:532
  24.1 0.0 collective-permute-done.5.refs_1_.refs_3_
  24.1 2.5 %whiten.2.refs_0_ = f32[1024,2048]{1,0:T(8,128)S(1)} custom-call(bf16[512,2048]{1,0:T(8,128)(2,1)S(1)} %get-tuple-element.61.kt, bf16[512,1024]{1,0:T(8,128)(2,1)S(1)} %join.10.refs_0_.refs_2_, bf16[512,1024]{1,0:T(8,128)(2,1)S(1)} %collective-permute-done.5.refs_1_.refs_3_), custom_call_target="tpu_custom_call" | custom-call | flops 2147483648 | bytes 10485760 | tf_op jit(solution)/shard_map/whiten/pallas_call | solution.py:547
  26.6 4.0 %collective-permute-done.4.refs_0_.refs_1_ = bf16[192,1024]{1,0:T(8,128)(2,1)S(1)} collective-permute-done((bf16[192,1024]{1,0:T(8,128)(2,1)S(1)}, bf16[192,1024]{1,0:T(8,128)(2,1)S(1)}, u32[]{:S(2)}, u32[]{:S(2)}) %collective-permute-start.4) | collective-permute-done | bytes 393248 | tf_op jit(solution)/shard_map/ppermute | solution.py:36
  30.6 1.2 %collective-permute-done.3.refs_0_ = bf16[192,1024]{1,0:T(8,128)(2,1)S(1)} collective-permute-done((bf16[192,1024]{1,0:T(8,128)(2,1)S(1)}, bf16[192,1024]{1,0:T(8,128)(2,1)S(1)}, u32[]{:S(2)}, u32[]{:S(2)}) %collective-permute-start.3) | collective-permute-done | bytes 393248 | tf_op jit(solution)/shard_map/ppermute | solution.py:36
  31.8 0.1 join.13.refs_1_.refs_4_
  31.9 0.1 collective-permute-start.8
  32.0 0.0 copy-start.3
  32.0 0.6 collective-permute-start.7
  32.6 1.5 %collective-permute-start.6 = (bf16[64,1024]{1,0:T(8,128)(2,1)S(1)}, bf16[64,1024]{1,0:T(8,128)(2,1)S(1)}, u32[]{:S(2)}, u32[]{:S(2)}) collective-permute-start(bf16[64,1024]{1,0:T(8,128)(2,1)S(1)} %join.11), channel_id=1, source_target_pairs={{0,4},{2,6},{4,0},{6,2},{8,12},{10,14},{12,8},{14,10},{16,20},{18,... | collective-permute-start | bytes 393224 | tf_op jit(solution)/shard_map/ppermute | solution.py:36
  34.1 0.1 collective-permute-done.8.refs_2_.refs_5_
  34.2 2.8 %whiten.3.start = f32[1024,2048]{1,0:T(8,128)S(1)} custom-call(bf16[384,2048]{1,0:T(8,128)(2,1)S(1)} %get-tuple-element.70.kt, f32[1024,2048]{1,0:T(8,128)S(1)} %whiten.2.refs_0_, bf16[384,1024]{1,0:T(8,128)(2,1)S(1)} %join.13.refs_1_.refs_4_, bf16[384,1024]{1,0:T(8,128)(2,1)S(1)} %collective-permute-done.8.refs_2_.refs_5_), custom_call_target="tpu_custom_call", output_to_operand_aliasing={{}: (1, {})} | custom-call | flops 1610612736 | bytes 10485760 | tf_op jit(solution)/shard_map/whiten/pallas_call | solution.py:547
  37.0 0.0 copy-start.6
  37.1 0.9 %collective-permute-done.7.refs_6_ = bf16[64,1024]{1,0:T(8,128)(2,1)S(1)} collective-permute-done((bf16[64,1024]{1,0:T(8,128)(2,1)S(1)}, bf16[64,1024]{1,0:T(8,128)(2,1)S(1)}, u32[]{:S(2)}, u32[]{:S(2)}) %collective-permute-start.7) | collective-permute-done | bytes 131104 | tf_op jit(solution)/shard_map/ppermute | solution.py:36
  37.9 0.3 collective-permute-done.6.refs_0_
  38.2 0.5 collective-permute-start.10
  38.7 0.8 %collective-permute-done.9.refs_1_ = bf16[64,1024]{1,0:T(8,128)(2,1)S(1)} collective-permute-done((bf16[64,1024]{1,0:T(8,128)(2,1)S(1)}, bf16[64,1024]{1,0:T(8,128)(2,1)S(1)}, u32[]{:S(2)}, u32[]{:S(2)}) %collective-permute-start.9) | collective-permute-done | bytes 131104 | tf_op jit(solution)/shard_map/ppermute | solution.py:36
  39.5 0.2 collective-permute-done.10.refs_7_
  39.7 4.7 %covary.1 = (bf16[1024,2048]{1,0:T(8,128)(2,1)S(1)}, bf16[1024,2048]{1,0:T(8,128)(2,1)S(1)}, f32[8,2304]{1,0:T(8,128)S(1)}) custom-call(bf16[128,2048]{1,0:T(8,128)(2,1)S(1)} %get-tuple-element.67.kt, f32[1024,2048]{1,0:T(8,128)S(1)} %whiten.3.start, bf16[8,1024]{1,0:T(8,128)(2,1)S(1)} %copy-done.3, bf16[64,1024]{1,0:T(8,128)(2,1)S(1)} %collective-permute-done.6.refs_0_, ...), custom_call_target="tpu_custom_call" | custom-call | flops 2147483648 | bytes 10485760 | tf_op jit(solution)/shard_map/covary/pallas_call | solution.py:571
  44.5 1.6 %collective-permute-start.11 = (f32[8,2304]{1,0:T(8,128)S(1)}, f32[8,2304]{1,0:T(8,128)S(1)}, u32[]{:S(2)}, u32[]{:S(2)}) collective-permute-start(f32[8,2304]{1,0:T(8,128)S(1)} %get-tuple-element.75.own), channel_id=1, source_target_pairs={{0,1},{1,0},{2,3},{3,2},{4,5},{5,4},{6,7},{7,6},{8,9},{9,8},{10,11... | collective-permute-start | bytes 221192 | tf_op jit(solution)/shard_map/ppermute | solution.py:36
  46.1 2.9 %collective-permute-done.11.other = f32[8,2304]{1,0:T(8,128)S(1)} collective-permute-done((f32[8,2304]{1,0:T(8,128)S(1)}, f32[8,2304]{1,0:T(8,128)S(1)}, u32[]{:S(2)}, u32[]{:S(2)}) %collective-permute-start.11) | collective-permute-done | bytes 73760 | tf_op jit(solution)/shard_map/ppermute | solution.py:36
  49.0 3.4 %slopes.1 = (f32[8,2048]{1,0:T(8,128)}, f32[8,3072]{1,0:T(8,128)S(1)}, bf16[1024,2048]{1,0:T(8,128)(2,1)S(1)}, f32[64,2560]{1,0:T(8,128)S(1)}, bf16[96,2560]{1,0:T(8,128)(2,1)S(1)}) custom-call(f32[8,2304]{1,0:T(8,128)S(1)} %get-tuple-element.75.own, f32[8,2304]{1,0:T(8,128)S(1)} %collective-permute-done.11.other, f32[8]{0:T(128)S(1)} %copy-done.6, ...), custom_call_target="tpu_custom_call" | custom-call | tf_op jit(solution)/shard_map/slopes/pallas_call | solution.py:605
  52.4 0.1 collective-permute-start.12
  52.5 1.7 %near_outer.1 = (f32[64,2560]{1,0:T(8,128)S(1)}, bf16[64,2560]{1,0:T(8,128)(2,1)S(1)}) custom-call(bf16[1024,2048]{1,0:T(8,128)(2,1)S(1)} %get-tuple-element.78.ab, bf16[1024,2048]{1,0:T(8,128)(2,1)S(1)} %get-tuple-element.86.heavy), custom_call_target="tpu_custom_call" | custom-call | tf_op jit(solution)/shard_map/near_outer/pallas_call | solution.py:620
  54.2 0.0 copy-start.1
  54.2 0.6 collective-permute-start.13
  54.8 0.1 add_pair.1
  54.9 0.1 add_level.3
  55.0 1.6 %collective-permute-start.14 = (bf16[64,1024]{1,0:T(8,128)(2,1)S(1)}, bf16[64,1024]{1,0:T(8,128)(2,1)S(1)}, u32[]{:S(2)}, u32[]{:S(2)}) collective-permute-start(bf16[64,1024]{1,0:T(8,128)(2,1)S(1)} %get-tuple-element.89), channel_id=1, source_target_pairs={{0,4},{2,6},{4,0},{6,2},{8,12},{10,14},{12,8},{14,10},{16,20},{18,... | collective-permute-start | bytes 393224 | tf_op jit(solution)/shard_map/ppermute | solution.py:36
  56.6 2.1 %collective-permute-start.15 = (f32[16,1024]{1,0:T(8,128)S(1)}, f32[16,1024]{1,0:T(8,128)S(1)}, u32[]{:S(2)}, u32[]{:S(2)}) collective-permute-start(f32[16,1024]{1,0:T(8,128)S(1)} %get-tuple-element.90), channel_id=1, source_target_pairs={{0,16},{2,18},{4,20},{6,22},{8,24},{10,26},{12,28},{14,30},{16,0},... | collective-permute-start | bytes 196616 | tf_op jit(solution)/shard_map/ppermute | solution.py:36
  58.7 0.5 collective-permute-start.16
  59.2 0.1 add_near_pair.1.near
  59.3 3.5 %collective-permute-done.15.refs_1_ = f32[16,1024]{1,0:T(8,128)S(1)} collective-permute-done((f32[16,1024]{1,0:T(8,128)S(1)}, f32[16,1024]{1,0:T(8,128)S(1)}, u32[]{:S(2)}, u32[]{:S(2)}) %collective-permute-start.15) | collective-permute-done | bytes 65568 | tf_op jit(solution)/shard_map/ppermute | solution.py:36
  62.9 0.6 collective-permute-start.17
  63.4 2.9 %collective-permute-done.16.refs_0_ = bf16[128,1024]{1,0:T(8,128)(2,1)S(1)} collective-permute-done((bf16[128,1024]{1,0:T(8,128)(2,1)S(1)}, bf16[128,1024]{1,0:T(8,128)(2,1)S(1)}, u32[]{:S(2)}, u32[]{:S(2)}) %collective-permute-start.16) | collective-permute-done | bytes 262176 | tf_op jit(solution)/shard_map/ppermute | solution.py:36
  66.3 2.3 %collective-permute-done.17.refs_1_ = bf16[96,1024]{1,0:T(8,128)(2,1)S(1)} collective-permute-done((bf16[96,1024]{1,0:T(8,128)(2,1)S(1)}, bf16[96,1024]{1,0:T(8,128)(2,1)S(1)}, u32[]{:S(2)}, u32[]{:S(2)}) %collective-permute-start.17) | collective-permute-done | bytes 196640 | tf_op jit(solution)/shard_map/ppermute | solution.py:36
  68.6 0.1 add_level.5
  68.7 0.6 collective-permute-start.20
  69.3 2.2 %collective-permute-start.18 = (bf16[64,1024]{1,0:T(8,128)(2,1)S(1)}, bf16[64,1024]{1,0:T(8,128)(2,1)S(1)}, u32[]{:S(2)}, u32[]{:S(2)}) collective-permute-start(bf16[64,1024]{1,0:T(8,128)(2,1)S(1)} %get-tuple-element.95), channel_id=1, source_target_pairs={{0,16},{2,18},{4,20},{6,22},{8,24},{10,26},{12,28},{14,30},{16,0},... | collective-permute-start | bytes 393224 | tf_op jit(solution)/shard_map/ppermute | solution.py:36
  71.6 1.7 %collective-permute-start.19 = (bf16[64,1024]{1,0:T(8,128)(2,1)S(1)}, bf16[64,1024]{1,0:T(8,128)(2,1)S(1)}, u32[]{:S(2)}, u32[]{:S(2)}) collective-permute-start(bf16[64,1024]{1,0:T(8,128)(2,1)S(1)} %get-tuple-element.96), channel_id=1, source_target_pairs={{0,8},{2,10},{4,12},{6,14},{8,0},{10,2},{12,4},{14,6},{16,24},{18,... | collective-permute-start | bytes 393224 | tf_op jit(solution)/shard_map/ppermute | solution.py:36
  73.3 3.4 %collective-permute-done.18.refs_0_ = bf16[64,1024]{1,0:T(8,128)(2,1)S(1)} collective-permute-done((bf16[64,1024]{1,0:T(8,128)(2,1)S(1)}, bf16[64,1024]{1,0:T(8,128)(2,1)S(1)}, u32[]{:S(2)}, u32[]{:S(2)}) %collective-permute-start.18) | collective-permute-done | bytes 131104 | tf_op jit(solution)/shard_map/ppermute | solution.py:36
  76.7 0.3 collective-permute-done.19.refs_1_
  77.0 0.9 %finish.1 = (f32[64,1024]{1,0:T(8,128)}, f32[8,1024]{1,0:T(8,128)}, f32[8,2048]{1,0:T(8,128)}) custom-call(f32[8,3072]{1,0:T(8,128)S(1)} %get-tuple-element.94.state, f32[64,2560]{1,0:T(8,128)S(1)} %add_near_pair.1.near, bf16[64,1024]{1,0:T(8,128)(2,1)S(1)} %copy-done.1, bf16[8,1024]{1,0:T(8,128)(2,1)S(1)} %copy-done.3, ...), custom_call_target="tpu_custom_call" | custom-call | tf_op jit(solution)/shard_map/finish/pallas_call | solution.py:663
  (21 shorter events, 0.2 us)
Async XLA Ops:
  0.6 0.9 %copy-start = (bf16[64,1024]{1,0:T(8,128)(2,1)S(1)}, bf16[64,1024]{1,0:T(8,128)(2,1)}, u32[]{:S(2)}) copy-start(bf16[64,1024]{1,0:T(8,128)(2,1)} %chol.1) | copy-start | bytes 393220
  1.5 0.9 %copy-start.2 = (bf16[64,1024]{1,0:T(8,128)(2,1)S(1)}, bf16[64,1024]{1,0:T(8,128)(2,1)}, u32[]{:S(2)}) copy-start(bf16[64,1024]{1,0:T(8,128)(2,1)} %refs_0_.1) | copy-start | bytes 393220
  2.5 16.1 %collective-permute-start.2 = (bf16[128,1024]{1,0:T(8,128)(2,1)S(1)}, bf16[128,1024]{1,0:T(8,128)(2,1)S(1)}, u32[]{:S(2)}, u32[]{:S(2)}) collective-permute-start(bf16[128,1024]{1,0:T(8,128)(2,1)S(1)} %join.7.refs_0_), channel_id=1, source_target_pairs={{0,16},{2,18},{4,20},{6,22},{8,24},{10,26},{12,28},{14,30},{16,0},... | collective-permute-start | bytes 786440 | tf_op jit(solution)/shard_map/ppermute | solution.py:36
  6.6 12.2 %collective-permute-start.1 = (bf16[128,1024]{1,0:T(8,128)(2,1)S(1)}, bf16[128,1024]{1,0:T(8,128)(2,1)S(1)}, u32[]{:S(2)}, u32[]{:S(2)}) collective-permute-start(bf16[128,1024]{1,0:T(8,128)(2,1)S(1)} %join.7.refs_0_), channel_id=1, source_target_pairs={{0,8},{2,10},{4,12},{6,14},{8,0},{10,2},{12,4},{14,6},{16,24},{18,... | collective-permute-start | bytes 786440 | tf_op jit(solution)/shard_map/ppermute | solution.py:36
  8.1 10.6 %collective-permute-start = (bf16[128,1024]{1,0:T(8,128)(2,1)S(1)}, bf16[128,1024]{1,0:T(8,128)(2,1)S(1)}, u32[]{:S(2)}, u32[]{:S(2)}) collective-permute-start(bf16[128,1024]{1,0:T(8,128)(2,1)S(1)} %join.7.refs_0_), channel_id=1, source_target_pairs={{0,4},{2,6},{4,0},{6,2},{8,12},{10,14},{12,8},{14,10},{16,20},{18,... | collective-permute-start | bytes 786440 | tf_op jit(solution)/shard_map/ppermute | solution.py:36
  9.6 0.7 copy-start.4
  10.4 0.7 copy-start.5
  11.1 0.7 copy-start.7
  11.8 0.7 copy-start.8
  12.5 0.7 copy-start.9
  13.2 0.7 copy-start.10
  18.9 5.2 %collective-permute-start.5 = (bf16[512,1024]{1,0:T(8,128)(2,1)S(1)}, bf16[512,1024]{1,0:T(8,128)(2,1)S(1)}, u32[]{:S(2)}, u32[]{:S(2)}) collective-permute-start(bf16[512,1024]{1,0:T(8,128)(2,1)S(1)} %join.10.refs_0_.refs_2_), channel_id=1, source_target_pairs={{0,2},{2,0},{4,6},{6,4},{8,10},{10,8},{12,14},{14,12},{16,18},{18,... | collective-permute-start | bytes 3145736 | tf_op jit(solution)/shard_map/ppermute | solution.py:36
  19.0 11.6 %collective-permute-start.4 = (bf16[192,1024]{1,0:T(8,128)(2,1)S(1)}, bf16[192,1024]{1,0:T(8,128)(2,1)S(1)}, u32[]{:S(2)}, u32[]{:S(2)}) collective-permute-start(bf16[192,1024]{1,0:T(8,128)(2,1)S(1)} %join.9), channel_id=1, source_target_pairs={{0,8},{2,10},{4,12},{6,14},{8,0},{10,2},{12,4},{14,6},{16,24},{18,... | collective-permute-start | bytes 1179656 | tf_op jit(solution)/shard_map/ppermute | solution.py:36
  20.6 11.2 %collective-permute-start.3 = (bf16[192,1024]{1,0:T(8,128)(2,1)S(1)}, bf16[192,1024]{1,0:T(8,128)(2,1)S(1)}, u32[]{:S(2)}, u32[]{:S(2)}) collective-permute-start(bf16[192,1024]{1,0:T(8,128)(2,1)S(1)} %join.8), channel_id=1, source_target_pairs={{0,4},{2,6},{4,0},{6,2},{8,12},{10,14},{12,8},{14,10},{16,20},{18,... | collective-permute-start | bytes 1179656 | tf_op jit(solution)/shard_map/ppermute | solution.py:36
  31.9 2.4 %collective-permute-start.8 = (bf16[384,1024]{1,0:T(8,128)(2,1)S(1)}, bf16[384,1024]{1,0:T(8,128)(2,1)S(1)}, u32[]{:S(2)}, u32[]{:S(2)}) collective-permute-start(bf16[384,1024]{1,0:T(8,128)(2,1)S(1)} %join.13.refs_1_.refs_4_), channel_id=1, source_target_pairs={{0,2},{2,0},{4,6},{6,4},{8,10},{10,8},{12,14},{14,12},{16,18},{18,... | collective-permute-start | bytes 2359304 | tf_op jit(solution)/shard_map/ppermute | solution.py:36
  32.0 7.8 %copy-start.3 = (bf16[8,1024]{1,0:T(8,128)(2,1)S(1)}, bf16[8,1024]{1,0:T(8,128)(2,1)}, u32[]{:S(2)}) copy-start(bf16[8,1024]{1,0:T(8,128)(2,1)} %means.3) | copy-start | bytes 49156
  32.0 6.0 %collective-permute-start.7 = (bf16[64,1024]{1,0:T(8,128)(2,1)S(1)}, bf16[64,1024]{1,0:T(8,128)(2,1)S(1)}, u32[]{:S(2)}, u32[]{:S(2)}) collective-permute-start(bf16[64,1024]{1,0:T(8,128)(2,1)S(1)} %join.12), channel_id=1, source_target_pairs={{0,8},{2,10},{4,12},{6,14},{8,0},{10,2},{12,4},{14,6},{16,24},{18,... | collective-permute-start | bytes 393224 | tf_op jit(solution)/shard_map/ppermute | solution.py:36
  32.6 5.6 %collective-permute-start.6 = (bf16[64,1024]{1,0:T(8,128)(2,1)S(1)}, bf16[64,1024]{1,0:T(8,128)(2,1)S(1)}, u32[]{:S(2)}, u32[]{:S(2)}) collective-permute-start(bf16[64,1024]{1,0:T(8,128)(2,1)S(1)} %join.11), channel_id=1, source_target_pairs={{0,4},{2,6},{4,0},{6,2},{8,12},{10,14},{12,8},{14,10},{16,20},{18,... | collective-permute-start | bytes 393224 | tf_op jit(solution)/shard_map/ppermute | solution.py:36
  37.0 12.0 %copy-start.6 = (f32[8]{0:T(128)S(1)}, f32[8]{0:T(128)}, u32[]{:S(2)}) copy-start(f32[8]{0:T(128)} %scales.1) | copy-start | bytes 100
  38.2 1.3 %collective-permute-start.9 = (bf16[64,1024]{1,0:T(8,128)(2,1)S(1)}, bf16[64,1024]{1,0:T(8,128)(2,1)S(1)}, u32[]{:S(2)}, u32[]{:S(2)}) collective-permute-start(bf16[64,1024]{1,0:T(8,128)(2,1)S(1)} %collective-permute-done.6.refs_0_), channel_id=1, source_target_pairs={{0,2},{2,0},{4,6},{6,4},{8,10},{10,8},{12,14},{14,12},{16,18},{18,... | collective-permute-start | bytes 393224 | tf_op jit(solution)/shard_map/ppermute | solution.py:36
  38.2 1.5 %collective-permute-start.10 = (bf16[64,1024]{1,0:T(8,128)(2,1)S(1)}, bf16[64,1024]{1,0:T(8,128)(2,1)S(1)}, u32[]{:S(2)}, u32[]{:S(2)}) collective-permute-start(bf16[64,1024]{1,0:T(8,128)(2,1)S(1)} %collective-permute-done.7.refs_6_), channel_id=1, source_target_pairs={{0,2},{2,0},{4,6},{6,4},{8,10},{10,8},{12,14},{14,12},{16,18},{18,... | collective-permute-start | bytes 393224 | tf_op jit(solution)/shard_map/ppermute | solution.py:36
  44.5 4.6 %collective-permute-start.11 = (f32[8,2304]{1,0:T(8,128)S(1)}, f32[8,2304]{1,0:T(8,128)S(1)}, u32[]{:S(2)}, u32[]{:S(2)}) collective-permute-start(f32[8,2304]{1,0:T(8,128)S(1)} %get-tuple-element.75.own), channel_id=1, source_target_pairs={{0,1},{1,0},{2,3},{3,2},{4,5},{5,4},{6,7},{7,6},{8,9},{9,8},{10,11... | collective-permute-start | bytes 221192 | tf_op jit(solution)/shard_map/ppermute | solution.py:36
  52.4 2.4 %collective-permute-start.12 = (bf16[96,2560]{1,0:T(8,128)(2,1)S(1)}, bf16[96,2560]{1,0:T(8,128)(2,1)S(1)}, u32[]{:S(2)}, u32[]{:S(2)}) collective-permute-start(bf16[96,2560]{1,0:T(8,128)(2,1)S(1)} %get-tuple-element.82), channel_id=1, source_target_pairs={{0,2},{2,0},{4,6},{6,4},{8,10},{10,8},{12,14},{14,12},{16,18},{18,... | collective-permute-start | bytes 1474568 | tf_op jit(solution)/shard_map/ppermute | solution.py:36
  54.2 22.7 %copy-start.1 = (bf16[64,1024]{1,0:T(8,128)(2,1)S(1)}, bf16[64,1024]{1,0:T(8,128)(2,1)}, u32[]{:S(2)}) copy-start(bf16[64,1024]{1,0:T(8,128)(2,1)} %chol.1) | copy-start | bytes 393220
  54.2 5.0 %collective-permute-start.13 = (bf16[64,2560]{1,0:T(8,128)(2,1)S(1)}, bf16[64,2560]{1,0:T(8,128)(2,1)S(1)}, u32[]{:S(2)}, u32[]{:S(2)}) collective-permute-start(bf16[64,2560]{1,0:T(8,128)(2,1)S(1)} %get-tuple-element.88), channel_id=1, source_target_pairs={{0,2},{2,0},{4,6},{6,4},{8,10},{10,8},{12,14},{14,12},{16,18},{18,... | collective-permute-start | bytes 983048 | tf_op jit(solution)/shard_map/ppermute | solution.py:36
  55.0 7.8 %collective-permute-start.14 = (bf16[64,1024]{1,0:T(8,128)(2,1)S(1)}, bf16[64,1024]{1,0:T(8,128)(2,1)S(1)}, u32[]{:S(2)}, u32[]{:S(2)}) collective-permute-start(bf16[64,1024]{1,0:T(8,128)(2,1)S(1)} %get-tuple-element.89), channel_id=1, source_target_pairs={{0,4},{2,6},{4,0},{6,2},{8,12},{10,14},{12,8},{14,10},{16,20},{18,... | collective-permute-start | bytes 393224 | tf_op jit(solution)/shard_map/ppermute | solution.py:36
  56.6 6.2 %collective-permute-start.15 = (f32[16,1024]{1,0:T(8,128)S(1)}, f32[16,1024]{1,0:T(8,128)S(1)}, u32[]{:S(2)}, u32[]{:S(2)}) collective-permute-start(f32[16,1024]{1,0:T(8,128)S(1)} %get-tuple-element.90), channel_id=1, source_target_pairs={{0,16},{2,18},{4,20},{6,22},{8,24},{10,26},{12,28},{14,30},{16,0},... | collective-permute-start | bytes 196616 | tf_op jit(solution)/shard_map/ppermute | solution.py:36
  58.7 7.7 %collective-permute-start.16 = (bf16[128,1024]{1,0:T(8,128)(2,1)S(1)}, bf16[128,1024]{1,0:T(8,128)(2,1)S(1)}, u32[]{:S(2)}, u32[]{:S(2)}) collective-permute-start(bf16[128,1024]{1,0:T(8,128)(2,1)S(1)} %get-tuple-element.92), channel_id=1, source_target_pairs={{0,4},{2,6},{4,0},{6,2},{8,12},{10,14},{12,8},{14,10},{16,20},{18,... | collective-permute-start | bytes 786440 | tf_op jit(solution)/shard_map/ppermute | solution.py:36
  62.9 5.7 %collective-permute-start.17 = (bf16[96,1024]{1,0:T(8,128)(2,1)S(1)}, bf16[96,1024]{1,0:T(8,128)(2,1)S(1)}, u32[]{:S(2)}, u32[]{:S(2)}) collective-permute-start(bf16[96,1024]{1,0:T(8,128)(2,1)S(1)} %get-tuple-element.93), channel_id=1, source_target_pairs={{0,8},{2,10},{4,12},{6,14},{8,0},{10,2},{12,4},{14,6},{16,24},{18,... | collective-permute-start | bytes 589832 | tf_op jit(solution)/shard_map/ppermute | solution.py:36
  68.7 8.2 %collective-permute-start.20 = (bf16[96,1024]{1,0:T(8,128)(2,1)S(1)}, bf16[96,1024]{1,0:T(8,128)(2,1)S(1)}, u32[]{:S(2)}, u32[]{:S(2)}) collective-permute-start(bf16[96,1024]{1,0:T(8,128)(2,1)S(1)} %get-tuple-element.97), channel_id=1, source_target_pairs={{0,4},{2,6},{4,0},{6,2},{8,12},{10,14},{12,8},{14,10},{16,20},{18,... | collective-permute-start | bytes 589832 | tf_op jit(solution)/shard_map/ppermute | solution.py:36
  69.3 7.4 %collective-permute-start.18 = (bf16[64,1024]{1,0:T(8,128)(2,1)S(1)}, bf16[64,1024]{1,0:T(8,128)(2,1)S(1)}, u32[]{:S(2)}, u32[]{:S(2)}) collective-permute-start(bf16[64,1024]{1,0:T(8,128)(2,1)S(1)} %get-tuple-element.95), channel_id=1, source_target_pairs={{0,16},{2,18},{4,20},{6,22},{8,24},{10,26},{12,28},{14,30},{16,0},... | collective-permute-start | bytes 393224 | tf_op jit(solution)/shard_map/ppermute | solution.py:36
  71.6 5.4 %collective-permute-start.19 = (bf16[64,1024]{1,0:T(8,128)(2,1)S(1)}, bf16[64,1024]{1,0:T(8,128)(2,1)S(1)}, u32[]{:S(2)}, u32[]{:S(2)}) collective-permute-start(bf16[64,1024]{1,0:T(8,128)(2,1)S(1)} %get-tuple-element.96), channel_id=1, source_target_pairs={{0,8},{2,10},{4,12},{6,14},{8,0},{10,2},{12,4},{14,6},{16,24},{18,... | collective-permute-start | bytes 393224 | tf_op jit(solution)/shard_map/ppermute | solution.py:36
